TPU v7x, 128 devices: a whole 4x4x4 slice. The times are simulated.
128 devices in a mesh: seq: 64 (over x_lo, z, y, core), samp: 2 (over x_hi).
Axes of the slice: x: 4 (x_hi: 2, x_lo: 2; x = x_hi * 2 + x_lo), y: 4, z: 4, core: 2. Of those that a mesh axis runs over, the one named last changes fastest.
Arguments:
- trunk: bfloat16 [2, 16384, 768], P('samp', 'seq'), may hold values from -6 to 6
- conv_weight: bfloat16 [3, 3, 768, 768], replicated, may hold values from -0.125 to 0.125
- head_weight: bfloat16 [768, 2688], replicated, may hold values from -0.21875 to 0.21875
- targets: int32 [2, 16384, 2688], P('samp', 'seq'), may hold values from 0 to 8
- error_mask: int32 [2, 16384], P('samp', 'seq'), may hold values 0 or 1
- upweight: int32 [2, 16384], P('samp', 'seq'), may hold values from 1 to 16, as said below
Outputs:
- loss: float32 [], replicated
- grad_conv: float32 [3, 2304, 768], P(None, 'seq', 'samp')
- grad_head: float32 [768, 2688], P('seq', 'samp')
- trunk_input_gradient: bfloat16 [2, 16384, 768], P('samp', 'seq')
Inputs may be any that keep to these rules, and one draw needn't show every extreme that they name: upweight is 1 at the first bin of each window and 16 at the last; at bin p it is at most 1 + (15 p) // 16383.
All inputs are finite; a program needn't handle non-finite values. No bound on the sum of `error_mask` on one device may be relied on, other than what follows from the above.
Results may differ from a plain program's by a relative error of at most 0.015.
Values may be sent and summed in bfloat16 or wider, within the bound.
No kernel may reach another device: no remote copies, remote signals or barrier semaphores. Data moves between devices by JAX's collectives and lax.ppermute only.
A program may use at most 192 MiB of HBM per device.

v0:
```python
import jax
import jax.numpy as jnp
from jax import lax
from jax.sharding import Mesh
from jax.sharding import PartitionSpec as P

OUTPUT_TRACKS = 2688
LAYERS = 3
BASE_DILATION = 64
AXES = ("xl", "z", "y", "c", "xh")
BF = jnp.bfloat16
F32 = jnp.float32


def perm_of(target):
    pairs = []
    for xl in range(2):
        for z in range(4):
            for y in range(4):
                for c in range(2):
                    for xh in range(2):
                        goal = target(xl, z, y, c, xh)
                        pairs.append((lin(xl, z, y, c, xh), lin(*goal)))
    return pairs


def lin(xl, z, y, c, xh):
    return (((xl * 4 + z) * 4 + y) * 2 + c) * 2 + xh


CORE = perm_of(lambda xl, z, y, c, xh: (xl, z, y, 1 - c, xh))
NEXT_CHIP = [(a * 2 + xh, (a + 1) * 2 + xh) for a in range(1, 63, 2) for xh in range(2)]
NEXT_CHIP = NEXT_CHIP + [(b, a) for a, b in NEXT_CHIP]
ALONG_X = perm_of(lambda xl, z, y, c, xh: (1 - xl, z, y, c, xh))


def last_hop(dx, m):
    return perm_of(lambda xl, z, y, c, xh: (xl ^ dx, z, y, xh ^ m, c))


def send(v, pairs):
    return lax.ppermute(v, AXES, pairs)


def edges(shard, width, c):
    first, last = shard[:width], shard[shard.shape[0] - width :]
    if width == shard.shape[0]:
        inner = outer = shard
    else:
        inner = jnp.where(c == 0, last, first)
        outer = jnp.where(c == 0, first, last)
    outer = send(outer, NEXT_CHIP)
    inner = send(inner, CORE)
    return jnp.where(c == 0, outer, inner), jnp.where(c == 0, inner, outer)


def extended(shard, width, c):
    before, after = edges(shard, width, c)
    return jnp.concatenate([before, shard, after], axis=0)


def after_all(value, *others):
    return lax.optimization_barrier((value,) + others)[0]


def smooth(values):
    return jax.nn.gelu(values, approximate=True)


def pick(blocks, place):
    return lax.dynamic_index_in_dim(blocks, place, 0, keepdims=False)


def swap_xl(part, xl):
    halves = part.reshape(2, part.shape[0] // 2, part.shape[1])
    got = send(pick(halves, 1 - xl), ALONG_X)
    return (pick(halves, xl).astype(F32) + got.astype(F32)).astype(BF)


def plane_sum(blocks):
    got = lax.all_to_all(blocks, ("z", "y"), 0, 0, tiled=True)
    return jnp.sum(got.astype(F32), axis=0).astype(BF)


def last_sum(block, extra, xl, xh, at):
    near = jnp.concatenate([block[:, :at], pick(extra, xl), block[:, at:]], axis=1)
    rest = pick(extra, 1 - xl)
    total = sum(send(pick(near, xh ^ m), last_hop(0, m)).astype(F32) for m in range(2))
    more = sum(send(pick(rest, xh ^ m), last_hop(1, m)).astype(F32) for m in range(2))
    return jnp.concatenate(
        [total[:at], total[at : at + more.shape[0]] + more, total[at + more.shape[0] :]], axis=0
    )


def per_device(trunk, conv_weight, head_weight, targets, error_mask, upweight):
    _, positions, channels = trunk.shape
    xl, z, y, c, xh = (lax.axis_index(axis) for axis in AXES)
    bins_all = positions * lax.axis_size(AXES)
    bin_weight = jnp.where(error_mask == 1, upweight, 1).astype(F32).reshape(positions, 1)
    weight_part = jnp.sum(bin_weight)
    first, last = (xl + z + y + c == 0), (xl == 1) & (z == 3) & (y == 3) & (c == 1)

    def inside(v, width):
        row = lax.broadcasted_iota(jnp.int32, (v.shape[0], 1), 0)
        out = (first & (row < width)) | (last & (row >= v.shape[0] - width))
        return jnp.where(out, jnp.zeros_like(v), v)

    def conv(rows, weights, d, count):
        total = jnp.dot(rows[d : d + count], weights[1], preferred_element_type=F32)
        total = total + jnp.dot(rows[:count], weights[0], preferred_element_type=F32)
        return total + jnp.dot(
            rows[2 * d : 2 * d + count], weights[2], preferred_element_type=F32
        )

    def conv_back(rows, weights, d, count):
        total = jnp.dot(rows[d : d + count], weights[1].T, preferred_element_type=F32)
        total = total + jnp.dot(
            rows[2 * d : 2 * d + count], weights[0].T, preferred_element_type=F32
        )
        return total + jnp.dot(rows[:count], weights[2].T, preferred_element_type=F32)

    def activate(v):
        return smooth(v.astype(F32)).astype(BF)

    def through(v, grad):
        return jax.vjp(smooth, v.astype(F32))[1](grad)[0]

    wide0 = extended(trunk[0], 192, c)
    act0 = activate(wide0)
    wide1 = (wide0[64:576].astype(F32) + conv(act0, conv_weight[0], 64, 512)).astype(BF)
    wide1 = inside(wide1, 128)
    act1 = activate(wide1)
    stream2 = (wide1[128:384].astype(F32) + conv(act1, conv_weight[1], 128, 256)).astype(BF)
    act2 = extended(activate(stream2), 256, c)
    stream = (stream2.astype(F32) + conv(act2, conv_weight[2], 256, 256)).astype(BF)
    padded_acts = [act0[128:512], act1, act2]
    logits = jnp.dot(stream, head_weight, preferred_element_type=F32)
    predicted = jax.nn.softplus(logits)
    slope = jax.nn.sigmoid(logits)
    counts = targets[0].astype(F32)
    partial_loss = jnp.sum(bin_weight * (predicted - counts * jnp.log(predicted)))
    logit_grad = (bin_weight * (1.0 - counts / predicted) * slope).astype(BF)
    lanes = lax.broadcasted_iota(jnp.int32, (1, 1408), 1)
    spare = lanes - 1344 * (1 - c)

    def with_scalars(v, scalars):
        for n, s in enumerate(scalars):
            inside = (spare >= 32 * n) & (spare < 32 * n + 32)
            v = jnp.where(inside, s * (1.0 + (spare - 32 * n).astype(F32) / 32), v)
        return v

    def halves(v, width):
        low, high = v[:, :width], v[:, v.shape[1] - width :]
        return jnp.where(c == 0, low, high), jnp.where(c == 0, high, low)

    def pair_dot(a, b, far_a, far_b):
        return jnp.dot(a.T, b, preferred_element_type=F32) + jnp.dot(
            far_a.T, far_b, preferred_element_type=F32
        )

    near, far = halves(logit_grad, 1408)
    scal = jnp.stack([weight_part, partial_loss])
    scal = scal + send(scal, CORE)
    head_half = pair_dot(stream, near, send(stream, CORE), send(far, CORE))
    head_half = with_scalars(head_half, (scal[0], scal[1])).astype(BF)
    head_sum = swap_xl(head_half, xl)
    g_top = jnp.dot(logit_grad, head_weight.T, preferred_element_type=F32)

    def conv_grad(layer, grad_bf):
        d = BASE_DILATION * 2**layer
        padded = padded_acts[layer]
        far_padded = send(padded, CORE)
        near, far = halves(grad_bf, 384)
        far = send(far, CORE)
        return jnp.concatenate(
            [
                pair_dot(padded[rows], near, far_padded[rows], far).astype(BF)
                for rows in (slice(tap * d, tap * d + positions) for tap in range(3))
            ],
            axis=0,
        )

    gb2 = g_top.astype(BF)
    before, after = edges(gb2, 256, c)
    half2 = conv_grad(2, gb2)
    sum2 = swap_xl(half2, xl)
    before = after_all(before, head_half, half2)
    wide = jnp.concatenate([before, gb2, after], axis=0)
    g2 = g_top + through(stream2, conv_back(wide, conv_weight[2], 256, 256))
    gb1 = g2.astype(BF)
    before, after = edges(gb1, 192, c)
    half1 = conv_grad(1, gb1)
    sum1 = swap_xl(half1, xl)
    head_plane = plane_sum(head_sum.reshape(16, 24, 1408))
    plane2 = plane_sum(sum2.reshape(16, 72, 384))
    before = after_all(before, half1, head_sum, sum2)
    wide = jnp.concatenate([before, gb1, after], axis=0)
    g_in = jnp.concatenate([before[128:].astype(F32), g2, after[:64].astype(F32)], axis=0)
    g1 = g_in + through(wide1[64:448], conv_back(wide, conv_weight[1], 128, 384))
    gb0 = inside(g1.astype(BF), 64)
    half0 = conv_grad(0, gb0[64:320])
    plane0 = plane_sum(half0.reshape(2, 16, 72, 384).transpose(1, 0, 2, 3))
    plane1 = plane_sum(sum1.reshape(16, 72, 384))
    gb0 = after_all(gb0, half0)
    g0 = g1[64:320] + through(trunk[0], conv_back(gb0, conv_weight[0], 64, 256))

    def by_core(v, rows):
        v = v.reshape(v.shape[:-2] + (2, rows, 384))
        return jnp.pad(v, ((0, 0),) * (v.ndim - 2) + ((0, 4), (0, 0)))

    head_rows = jnp.pad(head_plane.reshape(2, 12, 1408), ((0, 0), (0, 0), (0, 128)))
    message = jnp.concatenate(
        [by_core(plane1, 36), by_core(plane2, 36)]
        + [head_rows[..., 384 * k : 384 * k + 384] for k in range(4)],
        axis=1,
    )
    total = last_sum(message, by_core(plane0, 36), xl, xh, 0)
    conv_total = jnp.stack([total[40 * k : 40 * k + 36] for k in range(LAYERS)])
    head_total = jnp.concatenate([total[120 + 12 * k : 132 + 12 * k] for k in range(4)], axis=1)
    low = head_total[:, :1344]
    high = head_total[:, 64:1408]
    row = head_total[0]
    found = jnp.where(xh == 0, row[1344:1408], row[:64])
    weight_sum = jnp.sum(found[:32]) / 47.5
    loss_sum = jnp.sum(found[32:]) / 47.5
    factor = bins_all / weight_sum
    loss = loss_sum / (OUTPUT_TRACKS * weight_sum)
    return (
        loss,
        conv_total * factor,
        jnp.where(xh == 0, low, high) * factor,
        (g0 * factor).astype(BF)[None],
    )


def solution(mesh):
    parts = Mesh(mesh.devices.reshape(2, 4, 4, 2, 2), ("xl", "z", "y", "c", "xh"))
    seq = ("xl", "z", "y", "c")
    return jax.shard_map(
        per_device,
        mesh=parts,
        in_specs=(
            P("xh", seq, None),
            P(),
            P(),
            P("xh", seq, None),
            P("xh", seq),
            P("xh", seq),
        ),
        out_specs=(P(), P(None, seq, "xh"), P(seq, "xh"), P("xh", seq, None)),
        check_vma=False,
    )
```

profile of v0, /device:TPU:1, one launch (start us, length us, event | category | flops | bytes accessed | tf_op | source)
XLA Modules:
  0.0 222.8 jit_solution(5703949016116921067)
XLA Ops:
  1.8 4.6 %collective-permute-start = (bf16[192,768]{1,0:T(8,128)(2,1)S(1)}, bf16[192,768]{1,0:T(8,128)(2,1)S(1)}, u32[]{:S(2)}, u32[]{:S(2)}) collective-permute-start(bf16[192,768]{1,0:T(8,128)(2,1)S(1)} %get-tuple-element.30), channel_id=1, source_target_pairs={{2,4},{3,5},{6,8},{7,9},{10,12},{11,13},{14,16},{15,17},{18,20},{1... | collective-permute-start | bytes 884744 | tf_op jit(solution)/shard_map/ppermute | solution.py:42
  7.9 2.9 %collective-permute-done = bf16[192,768]{1,0:T(8,128)(2,1)S(1)} collective-permute-done((bf16[192,768]{1,0:T(8,128)(2,1)S(1)}, bf16[192,768]{1,0:T(8,128)(2,1)S(1)}, u32[]{:S(2)}, u32[]{:S(2)}) %collective-permute-start) | collective-permute-done | bytes 294944 | tf_op jit(solution)/shard_map/ppermute | solution.py:42
  19.4 3.6 %collective-permute-start.2 = (bf16[256,768]{1,0:T(8,128)(2,1)S(1)}, bf16[256,768]{1,0:T(8,128)(2,1)S(1)}, u32[]{:S(2)}, u32[]{:S(2)}) collective-permute-start(bf16[256,768]{1,0:T(8,128)(2,1)S(1)} %get-tuple-element.50), channel_id=1, source_target_pairs={{2,4},{3,5},{6,8},{7,9},{10,12},{11,13},{14,16},{15,17},{18,20},{1... | collective-permute-start | bytes 1179656 | tf_op jit(solution)/shard_map/ppermute | solution.py:42
  25.2 3.2 %collective-permute-done.2 = bf16[256,768]{1,0:T(8,128)(2,1)S(1)} collective-permute-done((bf16[256,768]{1,0:T(8,128)(2,1)S(1)}, bf16[256,768]{1,0:T(8,128)(2,1)S(1)}, u32[]{:S(2)}, u32[]{:S(2)}) %collective-permute-start.2) | collective-permute-done | bytes 393248 | tf_op jit(solution)/shard_map/ppermute | solution.py:42
  31.6 4.6 %fusion.5 = (f32[]{:T(128)}, bf16[256,2688]{1,0:T(8,128)(2,1)S(1)}) fusion(s32[1,256,2688]{2,1,0:T(8,128)S(1)} %copy-done.13, f32[256]{0:T(256)S(1)} %bitcast.185, bf16[256,768]{1,0:T(8,128)(2,1)S(1)} %fusion.35, bf16[768,2688]{1,0:T(8,128)(2,1)S(1)} %copy-done.12), kind=kOutput, calls=%fused_computation.13 | convolution fusion | flops 1070039040 | bytes 8651780 | tf_op jit(solution)/shard_map/dot_general | solution.py:137
  38.5 3.9 %collective-permute-start.5 = (bf16[256,768]{1,0:T(8,128)(2,1)S(1)}, bf16[256,768]{1,0:T(8,128)(2,1)S(1)}, u32[]{:S(2)}, u32[]{:S(2)}) collective-permute-start(bf16[256,768]{1,0:T(8,128)(2,1)S(1)} %get-tuple-element.52), channel_id=1, source_target_pairs={{2,4},{3,5},{6,8},{7,9},{10,12},{11,13},{14,16},{15,17},{18,20},{1... | collective-permute-start | bytes 1179656 | tf_op jit(solution)/shard_map/ppermute | solution.py:42
  52.5 14.0 %collective-permute-start.15 = (bf16[384,1408]{1,0:T(8,128)(2,1)S(1)}, bf16[384,1408]{1,0:T(8,128)(2,1)S(1)}, u32[]{:S(2)}, u32[]{:S(2)}) collective-permute-start(bf16[384,1408]{1,0:T(8,128)(2,1)S(1)} %dynamic-slice_bitcast_fusion), channel_id=1, source_target_pairs={{0,64},{1,65},{2,66},{3,67},{4,68},{5,69},{6,70},{7,71},{8,72},{9,... | collective-permute-start | bytes 3244040 | tf_op jit(solution)/shard_map/ppermute | solution.py:42
  75.5 4.0 %collective-permute-start.16 = (bf16[1152,384]{1,0:T(8,128)(2,1)}, bf16[1152,384]{1,0:T(8,128)(2,1)}, u32[]{:S(2)}, u32[]{:S(2)}) collective-permute-start(bf16[1152,384]{1,0:T(8,128)(2,1)} %dynamic-slice_bitcast_fusion.2), channel_id=1, source_target_pairs={{0,64},{1,65},{2,66},{3,67},{4,68},{5,69},{6,70},{7,71},{8,72},{9,... | collective-permute-start | bytes 2654216 | tf_op jit(solution)/shard_map/ppermute | solution.py:42
  85.3 5.3 %collective-permute-done.15 = bf16[384,1408]{1,0:T(8,128)(2,1)S(1)} collective-permute-done((bf16[384,1408]{1,0:T(8,128)(2,1)S(1)}, bf16[384,1408]{1,0:T(8,128)(2,1)S(1)}, u32[]{:S(2)}, u32[]{:S(2)}) %collective-permute-start.15) | collective-permute-done | bytes 1081376 | tf_op jit(solution)/shard_map/ppermute | solution.py:42
  91.9 16.0 %all-to-all-start.3 = ((bf16[16,24,1408]{2,1,0:T(8,128)(2,1)}), bf16[16,24,1408]{2,1,0:T(8,128)(2,1)}, u32[]{:S(2)}, u32[]{:S(2)}) async-start(bf16[16,24,1408]{2,1,0:T(8,128)(2,1)} %bitcast.178), calls=%async_computation.3 | async-start | bytes 2162688 | tf_op jit(solution)/shard_map/all_to_all | solution.py:81
  109.7 2.6 %fusion.15 = bf16[1152,384]{1,0:T(8,128)(2,1)} fusion(bf16[1152,384]{1,0:T(8,128)(2,1)} %collective-permute-done.16, bf16[2,1152,384]{2,1,0:T(8,128)(2,1)} %bitcast.174, s32[]{:T(128)S(6)} %select_n.205), kind=kLoop, calls=%fused_computation.37 | loop fusion | flops 1769472 | bytes 2654212 | tf_op jit(solution)/shard_map/convert_element_type | solution.py:77
  114.6 3.7 %convert_select_fusion = (bf16[384,768]{1,0:T(8,128)(2,1)S(1)}, f32[384,768]{1,0:T(8,128)}) fusion(pred[384]{0:T(512)(128)(4,1)S(1)} %fusion.175, bf16[512,768]{1,0:T(8,128)(2,1)S(1)} %copy-done.16, f32[384,768]{1,0:T(8,128)S(1)} %fusion.52, f32[384,768]{1,0:T(8,128)S(1)} %copy-done.14, bf16[3,3,768,768]{3,2,1,0:T(8,128)(2,1)} %param.7, ...), kind=kOutput, calls=%fused_computation.185 | convolution fusion | flops 462716928 | bytes 8061312 | tf_op jit(solution)/shard_map/dot_general | solution.py:116
  120.5 7.5 %collective-permute-start.18 = (bf16[256,384]{1,0:T(8,128)(2,1)}, bf16[256,384]{1,0:T(8,128)(2,1)S(1)}, u32[]{:S(2)}, u32[]{:S(2)}) collective-permute-start(bf16[256,384]{1,0:T(8,128)(2,1)} %get-tuple-element.18), channel_id=1, source_target_pairs={{0,2},{1,3},{2,0},{3,1},{4,6},{5,7},{6,4},{7,5},{8,10},{9,11},{10,... | collective-permute-start | bytes 589832 | tf_op jit(solution)/shard_map/ppermute | solution.py:42
  129.5 4.3 %all-to-all-start.2 = ((bf16[16,72,384]{2,1,0:T(8,128)(2,1)}), bf16[16,72,384]{2,1,0:T(8,128)(2,1)}, u32[]{:S(2)}, u32[]{:S(2)}) async-start(bf16[16,72,384]{2,1,0:T(8,128)(2,1)} %bitcast.179), calls=%async_computation.2 | async-start | bytes 1769472 | tf_op jit(solution)/shard_map/all_to_all | solution.py:81
  136.7 2.4 %fusion.14 = bf16[1152,384]{1,0:T(8,128)(2,1)} fusion(bf16[1152,384]{1,0:T(8,128)(2,1)} %collective-permute-done.19, bf16[2,1152,384]{2,1,0:T(8,128)(2,1)S(1)} %bitcast.172, s32[]{:T(128)S(6)} %select_n.205), kind=kLoop, calls=%fused_computation.35 | loop fusion | flops 1769472 | bytes 2654212 | tf_op jit(solution)/shard_map/convert_element_type | solution.py:77
  139.1 11.3 %all-to-all-done.2 = bf16[16,72,384]{2,1,0:T(8,128)(2,1)} async-done(((bf16[16,72,384]{2,1,0:T(8,128)(2,1)}), bf16[16,72,384]{2,1,0:T(8,128)(2,1)}, u32[]{:S(2)}, u32[]{:S(2)}) %all-to-all-start.2) | async-done | bytes 884768 | tf_op jit(solution)/shard_map/all_to_all | solution.py:81
  150.4 3.6 %all-to-all-start.1 = ((bf16[16,72,384]{2,1,0:T(8,128)(2,1)}), bf16[16,72,384]{2,1,0:T(8,128)(2,1)S(1)}, u32[]{:S(2)}, u32[]{:S(2)}) async-start(bf16[16,72,384]{2,1,0:T(8,128)(2,1)} %bitcast.30), calls=%async_computation.1 | async-start | bytes 1769472 | tf_op jit(solution)/shard_map/all_to_all | solution.py:81
  158.9 9.5 %all-to-all-done.1 = bf16[16,72,384]{2,1,0:T(8,128)(2,1)S(1)} async-done(((bf16[16,72,384]{2,1,0:T(8,128)(2,1)}), bf16[16,72,384]{2,1,0:T(8,128)(2,1)S(1)}, u32[]{:S(2)}, u32[]{:S(2)}) %all-to-all-start.1) | async-done | bytes 884768 | tf_op jit(solution)/shard_map/all_to_all | solution.py:81
  168.4 3.8 %all-to-all-start = ((bf16[16,2,72,384]{3,2,1,0:T(8,128)(2,1)}), bf16[16,2,72,384]{3,2,1,0:T(8,128)(2,1)S(1)}, u32[]{:S(2)}, u32[]{:S(2)}) async-start(bf16[16,2,72,384]{3,2,1,0:T(8,128)(2,1)} %bitcast.165), calls=%async_computation | async-start | bytes 3538944 | tf_op jit(solution)/shard_map/all_to_all | solution.py:81
  172.2 2.8 %fusion.67 = f32[256,768]{1,0:T(8,128)} fusion(bf16[3,3,768,768]{3,2,1,0:T(8,128)(2,1)} %param.7, bf16[384,768]{1,0:T(8,128)(2,1)} %copy-done.5), kind=kOutput, calls=%fused_computation.120 | convolution fusion | flops 301989888 | bytes 2359296 | tf_op jit(solution)/shard_map/dot_general | solution.py:116
  179.8 15.0 %all-to-all-done = bf16[16,2,72,384]{3,2,1,0:T(8,128)(2,1)S(1)} async-done(((bf16[16,2,72,384]{3,2,1,0:T(8,128)(2,1)}), bf16[16,2,72,384]{3,2,1,0:T(8,128)(2,1)S(1)}, u32[]{:S(2)}, u32[]{:S(2)}) %all-to-all-start) | async-done | bytes 1769504 | tf_op jit(solution)/shard_map/all_to_all | solution.py:81
  196.9 4.9 %concatenate.42 = bf16[2,168,384]{2,1,0:T(8,128)(2,1)S(1)} concatenate(bf16[2,40,384]{2,1,0:T(8,128)(2,1)S(1)} %bitcast.182, bf16[2,40,384]{2,1,0:T(8,128)(2,1)} %pad.16, bf16[2,40,384]{2,1,0:T(8,128)(2,1)} %pad.17, bf16[2,12,384]{2,1,0:T(8,128)(2,1)} %get-tuple-element.45, bf16[2,12,384]{2,1,0:T(8,128)(2,1)} %get-tuple-element.44, bf16[2,12,384]{2,1,0:T(8,128)(2,1)} %get-tuple-element.43, ...), dimensions={1} | concatenate | bytes 516096 | tf_op jit(solution)/shard_map/concatenate | solution.py:86
  201.8 9.0 %collective-permute-start.20 = (bf16[168,384]{1,0:T(8,128)(2,1)S(1)}, bf16[168,384]{1,0:T(8,128)(2,1)S(1)}, u32[]{:S(2)}, u32[]{:S(2)}) collective-permute-start(bf16[168,384]{1,0:T(8,128)(2,1)S(1)} %get-tuple-element.38), channel_id=1, source_target_pairs={{0,0},{1,2},{2,1},{3,3},{4,4},{5,6},{6,5},{7,7},{8,8},{9,10},{10,9... | collective-permute-start | bytes 387080 | tf_op jit(solution)/shard_map/ppermute | solution.py:42
  216.4 3.1 %fusion.122 = bf16[1,256,768]{2,1,0:T(8,128)(2,1)} fusion(f32[256,768]{1,0:T(8,128)S(1)} %convolution_add_fusion.11, bf16[3,3,768,768]{3,2,1,0:T(8,128)(2,1)} %param.7, f32[384,768]{1,0:T(8,128)} %get-tuple-element.57, f32[]{:T(128)S(6)} %div.31, bf16[384,768]{1,0:T(8,128)(2,1)S(1)} %copy-done.6, bf16[1,256,768]{2,1,0:T(8,128)(2,1)S(1)} %copy-done.1), kind=kOutput, calls=%fused_computation.171 | convolution fusion | flops 306708480 | bytes 3932164 | tf_op jit(solution)/shard_map/dot_general | solution.py:120
  (170 shorter events, 72.2 us)
Async XLA Ops:
  1.8 9.0 %collective-permute-start = (bf16[192,768]{1,0:T(8,128)(2,1)S(1)}, bf16[192,768]{1,0:T(8,128)(2,1)S(1)}, u32[]{:S(2)}, u32[]{:S(2)}) collective-permute-start(bf16[192,768]{1,0:T(8,128)(2,1)S(1)} %get-tuple-element.30), channel_id=1, source_target_pairs={{2,4},{3,5},{6,8},{7,9},{10,12},{11,13},{14,16},{15,17},{18,20},{1... | collective-permute-start | bytes 884744 | tf_op jit(solution)/shard_map/ppermute | solution.py:42
  6.4 4.4 %collective-permute-start.1 = (bf16[192,768]{1,0:T(8,128)(2,1)S(1)}, bf16[192,768]{1,0:T(8,128)(2,1)S(1)}, u32[]{:S(2)}, u32[]{:S(2)}) collective-permute-start(bf16[192,768]{1,0:T(8,128)(2,1)S(1)} %get-tuple-element.31), channel_id=1, source_target_pairs={{0,2},{1,3},{2,0},{3,1},{4,6},{5,7},{6,4},{7,5},{8,10},{9,11},{10,... | collective-permute-start | bytes 884744 | tf_op jit(solution)/shard_map/ppermute | solution.py:42
  19.4 9.1 %collective-permute-start.2 = (bf16[256,768]{1,0:T(8,128)(2,1)S(1)}, bf16[256,768]{1,0:T(8,128)(2,1)S(1)}, u32[]{:S(2)}, u32[]{:S(2)}) collective-permute-start(bf16[256,768]{1,0:T(8,128)(2,1)S(1)} %get-tuple-element.50), channel_id=1, source_target_pairs={{2,4},{3,5},{6,8},{7,9},{10,12},{11,13},{14,16},{15,17},{18,20},{1... | collective-permute-start | bytes 1179656 | tf_op jit(solution)/shard_map/ppermute | solution.py:42
  23.0 5.4 %collective-permute-start.3 = (bf16[256,768]{1,0:T(8,128)(2,1)S(1)}, bf16[256,768]{1,0:T(8,128)(2,1)S(1)}, u32[]{:S(2)}, u32[]{:S(2)}) collective-permute-start(bf16[256,768]{1,0:T(8,128)(2,1)S(1)} %get-tuple-element.50), channel_id=1, source_target_pairs={{0,2},{1,3},{2,0},{3,1},{4,6},{5,7},{6,4},{7,5},{8,10},{9,11},{10,... | collective-permute-start | bytes 1179656 | tf_op jit(solution)/shard_map/ppermute | solution.py:42
  23.1 51.9 %collective-permute-start.13 = (bf16[512,768]{1,0:T(8,128)(2,1)S(1)}, bf16[512,768]{1,0:T(8,128)(2,1)S(1)}, u32[]{:S(2)}, u32[]{:S(2)}) collective-permute-start(bf16[512,768]{1,0:T(8,128)(2,1)S(1)} %get-tuple-element.48), channel_id=1, source_target_pairs={{0,2},{1,3},{2,0},{3,1},{4,6},{5,7},{6,4},{7,5},{8,10},{9,11},{10,... | collective-permute-start | bytes 2359304 | tf_op jit(solution)/shard_map/ppermute | solution.py:42
  24.5 110.8 %collective-permute-start.17 = (bf16[384,768]{1,0:T(8,128)(2,1)}, bf16[384,768]{1,0:T(8,128)(2,1)}, u32[]{:S(2)}, u32[]{:S(2)}) collective-permute-start(bf16[384,768]{1,0:T(8,128)(2,1)} %slice.382), channel_id=1, source_target_pairs={{0,2},{1,3},{2,0},{3,1},{4,6},{5,7},{6,4},{7,5},{8,10},{9,11},{10,... | collective-permute-start | bytes 1769480 | tf_op jit(solution)/shard_map/ppermute | solution.py:42
  38.4 11.1 %collective-permute-start.4 = (bf16[256,768]{1,0:T(8,128)(2,1)S(1)}, bf16[256,768]{1,0:T(8,128)(2,1)S(1)}, u32[]{:S(2)}, u32[]{:S(2)}) collective-permute-start(bf16[256,768]{1,0:T(8,128)(2,1)S(1)} %get-tuple-element.52), channel_id=1, source_target_pairs={{0,2},{1,3},{2,0},{3,1},{4,6},{5,7},{6,4},{7,5},{8,10},{9,11},{10,... | collective-permute-start | bytes 1179656 | tf_op jit(solution)/shard_map/ppermute | solution.py:42
  38.5 11.4 %collective-permute-start.5 = (bf16[256,768]{1,0:T(8,128)(2,1)S(1)}, bf16[256,768]{1,0:T(8,128)(2,1)S(1)}, u32[]{:S(2)}, u32[]{:S(2)}) collective-permute-start(bf16[256,768]{1,0:T(8,128)(2,1)S(1)} %get-tuple-element.52), channel_id=1, source_target_pairs={{2,4},{3,5},{6,8},{7,9},{10,12},{11,13},{14,16},{15,17},{18,20},{1... | collective-permute-start | bytes 1179656 | tf_op jit(solution)/shard_map/ppermute | solution.py:42
  46.0 5.6 %collective-permute-start.8 = (bf16[256,1408]{1,0:T(8,128)(2,1)S(1)}, bf16[256,1408]{1,0:T(8,128)(2,1)S(1)}, u32[]{:S(2)}, u32[]{:S(2)}) collective-permute-start(bf16[256,1408]{1,0:T(8,128)(2,1)S(1)} %broadcast_select_fusion), channel_id=1, source_target_pairs={{0,2},{1,3},{2,0},{3,1},{4,6},{5,7},{6,4},{7,5},{8,10},{9,11},{10,... | collective-permute-start | bytes 2162696 | tf_op jit(solution)/shard_map/ppermute | solution.py:42
  49.9 16.7 %collective-permute-start.9 = (bf16[768,768]{1,0:T(8,128)(2,1)S(1)}, bf16[768,768]{1,0:T(8,128)(2,1)S(1)}, u32[]{:S(2)}, u32[]{:S(2)}) collective-permute-start(bf16[768,768]{1,0:T(8,128)(2,1)S(1)} %pad_maximum_fusion.3), channel_id=1, source_target_pairs={{0,2},{1,3},{2,0},{3,1},{4,6},{5,7},{6,4},{7,5},{8,10},{9,11},{10,... | collective-permute-start | bytes 3538952 | tf_op jit(solution)/shard_map/ppermute | solution.py:42
  51.3 15.3 %collective-permute-start.10 = (bf16[256,384]{1,0:T(8,128)(2,1)S(1)}, bf16[256,384]{1,0:T(8,128)(2,1)S(1)}, u32[]{:S(2)}, u32[]{:S(2)}) collective-permute-start(bf16[256,384]{1,0:T(8,128)(2,1)S(1)} %get-tuple-element.29), channel_id=1, source_target_pairs={{0,2},{1,3},{2,0},{3,1},{4,6},{5,7},{6,4},{7,5},{8,10},{9,11},{10,... | collective-permute-start | bytes 589832 | tf_op jit(solution)/shard_map/ppermute | solution.py:42
  52.5 38.1 %collective-permute-start.15 = (bf16[384,1408]{1,0:T(8,128)(2,1)S(1)}, bf16[384,1408]{1,0:T(8,128)(2,1)S(1)}, u32[]{:S(2)}, u32[]{:S(2)}) collective-permute-start(bf16[384,1408]{1,0:T(8,128)(2,1)S(1)} %dynamic-slice_bitcast_fusion), channel_id=1, source_target_pairs={{0,64},{1,65},{2,66},{3,67},{4,68},{5,69},{6,70},{7,71},{8,72},{9,... | collective-permute-start | bytes 3244040 | tf_op jit(solution)/shard_map/ppermute | solution.py:42
  70.7 11.3 %collective-permute-start.11 = (bf16[192,768]{1,0:T(8,128)(2,1)S(1)}, bf16[192,768]{1,0:T(8,128)(2,1)S(1)}, u32[]{:S(2)}, u32[]{:S(2)}) collective-permute-start(bf16[192,768]{1,0:T(8,128)(2,1)S(1)} %get-tuple-element.26), channel_id=1, source_target_pairs={{2,4},{3,5},{6,8},{7,9},{10,12},{11,13},{14,16},{15,17},{18,20},{1... | collective-permute-start | bytes 884744 | tf_op jit(solution)/shard_map/ppermute | solution.py:42
  75.0 7.1 %collective-permute-start.12 = (bf16[192,768]{1,0:T(8,128)(2,1)S(1)}, bf16[192,768]{1,0:T(8,128)(2,1)S(1)}, u32[]{:S(2)}, u32[]{:S(2)}) collective-permute-start(bf16[192,768]{1,0:T(8,128)(2,1)S(1)} %get-tuple-element.27), channel_id=1, source_target_pairs={{0,2},{1,3},{2,0},{3,1},{4,6},{5,7},{6,4},{7,5},{8,10},{9,11},{10,... | collective-permute-start | bytes 884744 | tf_op jit(solution)/shard_map/ppermute | solution.py:42
  75.5 34.2 %collective-permute-start.16 = (bf16[1152,384]{1,0:T(8,128)(2,1)}, bf16[1152,384]{1,0:T(8,128)(2,1)}, u32[]{:S(2)}, u32[]{:S(2)}) collective-permute-start(bf16[1152,384]{1,0:T(8,128)(2,1)} %dynamic-slice_bitcast_fusion.2), channel_id=1, source_target_pairs={{0,64},{1,65},{2,66},{3,67},{4,68},{5,69},{6,70},{7,71},{8,72},{9,... | collective-permute-start | bytes 2654216 | tf_op jit(solution)/shard_map/ppermute | solution.py:42
  82.0 54.6 %collective-permute-start.19 = (bf16[1152,384]{1,0:T(8,128)(2,1)}, bf16[1152,384]{1,0:T(8,128)(2,1)}, u32[]{:S(2)}, u32[]{:S(2)}) collective-permute-start(bf16[1152,384]{1,0:T(8,128)(2,1)} %dynamic-slice_bitcast_fusion.1), channel_id=1, source_target_pairs={{0,64},{1,65},{2,66},{3,67},{4,68},{5,69},{6,70},{7,71},{8,72},{9,... | collective-permute-start | bytes 2654216 | tf_op jit(solution)/shard_map/ppermute | solution.py:42
  91.9 37.6 %all-to-all-start.3 = ((bf16[16,24,1408]{2,1,0:T(8,128)(2,1)}), bf16[16,24,1408]{2,1,0:T(8,128)(2,1)}, u32[]{:S(2)}, u32[]{:S(2)}) async-start(bf16[16,24,1408]{2,1,0:T(8,128)(2,1)} %bitcast.178), calls=%async_computation.3 | async-start | bytes 2162688 | tf_op jit(solution)/shard_map/all_to_all | solution.py:81
  120.5 14.8 %collective-permute-start.18 = (bf16[256,384]{1,0:T(8,128)(2,1)}, bf16[256,384]{1,0:T(8,128)(2,1)S(1)}, u32[]{:S(2)}, u32[]{:S(2)}) collective-permute-start(bf16[256,384]{1,0:T(8,128)(2,1)} %get-tuple-element.18), channel_id=1, source_target_pairs={{0,2},{1,3},{2,0},{3,1},{4,6},{5,7},{6,4},{7,5},{8,10},{9,11},{10,... | collective-permute-start | bytes 589832 | tf_op jit(solution)/shard_map/ppermute | solution.py:42
  129.5 20.9 %all-to-all-start.2 = ((bf16[16,72,384]{2,1,0:T(8,128)(2,1)}), bf16[16,72,384]{2,1,0:T(8,128)(2,1)}, u32[]{:S(2)}, u32[]{:S(2)}) async-start(bf16[16,72,384]{2,1,0:T(8,128)(2,1)} %bitcast.179), calls=%async_computation.2 | async-start | bytes 1769472 | tf_op jit(solution)/shard_map/all_to_all | solution.py:81
  150.4 18.0 %all-to-all-start.1 = ((bf16[16,72,384]{2,1,0:T(8,128)(2,1)}), bf16[16,72,384]{2,1,0:T(8,128)(2,1)S(1)}, u32[]{:S(2)}, u32[]{:S(2)}) async-start(bf16[16,72,384]{2,1,0:T(8,128)(2,1)} %bitcast.30), calls=%async_computation.1 | async-start | bytes 1769472 | tf_op jit(solution)/shard_map/all_to_all | solution.py:81
  168.4 26.4 %all-to-all-start = ((bf16[16,2,72,384]{3,2,1,0:T(8,128)(2,1)}), bf16[16,2,72,384]{3,2,1,0:T(8,128)(2,1)S(1)}, u32[]{:S(2)}, u32[]{:S(2)}) async-start(bf16[16,2,72,384]{3,2,1,0:T(8,128)(2,1)} %bitcast.165), calls=%async_computation | async-start | bytes 3538944 | tf_op jit(solution)/shard_map/all_to_all | solution.py:81
  201.8 11.7 %collective-permute-start.20 = (bf16[168,384]{1,0:T(8,128)(2,1)S(1)}, bf16[168,384]{1,0:T(8,128)(2,1)S(1)}, u32[]{:S(2)}, u32[]{:S(2)}) collective-permute-start(bf16[168,384]{1,0:T(8,128)(2,1)S(1)} %get-tuple-element.38), channel_id=1, source_target_pairs={{0,0},{1,2},{2,1},{3,3},{4,4},{5,6},{6,5},{7,7},{8,8},{9,10},{10,9... | collective-permute-start | bytes 387080 | tf_op jit(solution)/shard_map/ppermute | solution.py:42
  212.9 7.9 %collective-permute-start.22 = (bf16[40,384]{1,0:T(8,128)(2,1)S(1)}, bf16[40,384]{1,0:T(8,128)(2,1)S(1)}, u32[]{:S(2)}, u32[]{:S(2)}) collective-permute-start(bf16[40,384]{1,0:T(8,128)(2,1)S(1)} %bitcast.183), channel_id=1, source_target_pairs={{0,64},{1,66},{2,65},{3,67},{4,68},{5,70},{6,69},{7,71},{8,72},{9,... | collective-permute-start | bytes 92168 | tf_op jit(solution)/shard_map/ppermute | solution.py:42
  213.1 7.8 %collective-permute-start.23 = (bf16[40,384]{1,0:T(8,128)(2,1)S(1)}, bf16[40,384]{1,0:T(8,128)(2,1)S(1)}, u32[]{:S(2)}, u32[]{:S(2)}) collective-permute-start(bf16[40,384]{1,0:T(8,128)(2,1)S(1)} %bitcast.184), channel_id=1, source_target_pairs={{0,66},{1,64},{2,67},{3,65},{4,70},{5,68},{6,71},{7,69},{8,74},{9,... | collective-permute-start | bytes 92168 | tf_op jit(solution)/shard_map/ppermute | solution.py:42
  (22 other events, 120.8 us)
where the time goes:
time: 225 us; the launch traced here: 223 us
  starting transfers between devices  79.6 us (35%)
  waiting for transfers between devices  51.5 us (23%)
  matrix products  48.7 us (22%)
  other arithmetic  22.8 us (10%)
  local copies, waits for them, and re-layouts  15.5 us (7%)
  between operations  4.68 us (2%)
    ppermute x24, starting transfers between devices, send(): return lax.ppermute(v, AXES, pairs)  51.8 us
    all_to_all x4, waiting for transfers between devices, plane_sum(): got = lax.all_to_all(blocks, ('z', 'y'), 0, 0, tiled=True)  35.8 us
    all_to_all x4, starting transfers between devices, plane_sum(): got = lax.all_to_all(blocks, ('z', 'y'), 0, 0, tiled=True)  27.7 us
    ppermute x24, waiting for transfers between devices, send(): return lax.ppermute(v, AXES, pairs)  15.8 us
    dot_general x10, matrix products, pair_dot(): jnp.dot(far_a.T, far_b, preferred_element_type=F32)  7.88 us
    dot_general x10, matrix products, pair_dot(): jnp.dot(a.T, b, preferred_element_type=F32)  7.65 us
    dot_general x3, matrix products, conv_back(): jnp.dot(rows[:count], weights[2].T, preferred_element_type=F32)  7.02 us
    dot_general x3, matrix products, conv_back(): total = jnp.dot(rows[d:d + count], weights[1].T, preferred_element_type=F32)  6.97 us
  transfers between devices with their start and end apart: 28, of which 11 were waited for; matrix products, arithmetic and copies ran while one was open for 30% of the time, Pallas kernels for 0%

commit v1 on v0

--- a/solution.py
+++ b/solution.py
@@ -32,6 +32,8 @@
 NEXT_CHIP = [(a * 2 + xh, (a + 1) * 2 + xh) for a in range(1, 63, 2) for xh in range(2)]
 NEXT_CHIP = NEXT_CHIP + [(b, a) for a, b in NEXT_CHIP]
 ALONG_X = perm_of(lambda xl, z, y, c, xh: (1 - xl, z, y, c, xh))
+ALONG_Y = [perm_of(lambda xl, z, y, c, xh, k=k: (xl, z, y ^ k, c, xh)) for k in range(4)]
+ALONG_Z = [perm_of(lambda xl, z, y, c, xh, k=k: (xl, z ^ k, y, c, xh)) for k in range(4)]
 
 
 def last_hop(dx, m):
@@ -59,22 +61,30 @@
     return jnp.concatenate([before, shard, after], axis=0)
 
 
-def after_all(value, *others):
-    return lax.optimization_barrier((value,) + others)[0]
-
-
 def smooth(values):
     return jax.nn.gelu(values, approximate=True)
 
 
-def pick(blocks, place):
-    return lax.dynamic_index_in_dim(blocks, place, 0, keepdims=False)
-
-
-def swap_xl(part, xl):
-    halves = part.reshape(2, part.shape[0] // 2, part.shape[1])
-    got = send(pick(halves, 1 - xl), ALONG_X)
-    return (pick(halves, xl).astype(F32) + got.astype(F32)).astype(BF)
+def pick(blocks, place, axis=0):
+    return lax.dynamic_index_in_dim(blocks, place, axis, keepdims=False)
+
+
+def give(part, bit, route, outer=1):
+    rows, lanes = part.shape
+    halves = part.reshape(outer, 2, rows // (2 * outer), lanes)
+    return send(pick(halves, 1 - bit, 1), route)
+
+
+def take(part, got, bit):
+    rows, lanes = part.shape
+    outer = got.shape[0]
+    halves = part.reshape(outer, 2, rows // (2 * outer), lanes)
+    total = pick(halves, bit, 1).astype(F32) + got.astype(F32)
+    return total.astype(BF).reshape(rows // 2, lanes)
+
+
+def halve(part, bit, route, outer=1):
+    return take(part, give(part, bit, route, outer), bit)
 
 
 def plane_sum(blocks):
@@ -82,14 +92,11 @@
     return jnp.sum(got.astype(F32), axis=0).astype(BF)
 
 
-def last_sum(block, extra, xl, xh, at):
-    near = jnp.concatenate([block[:, :at], pick(extra, xl), block[:, at:]], axis=1)
-    rest = pick(extra, 1 - xl)
-    total = sum(send(pick(near, xh ^ m), last_hop(0, m)).astype(F32) for m in range(2))
-    more = sum(send(pick(rest, xh ^ m), last_hop(1, m)).astype(F32) for m in range(2))
-    return jnp.concatenate(
-        [total[:at], total[at : at + more.shape[0]] + more, total[at + more.shape[0] :]], axis=0
-    )
+def last_sum(near, rest):
+    total = sum(send(near, last_hop(0, m)).astype(F32) for m in range(2))
+    more = sum(send(rest, last_hop(1, m)).astype(F32) for m in range(2))
+    count = rest.shape[0]
+    return total[:count] + more, total[count:]
 
 
 def per_device(trunk, conv_weight, head_weight, targets, error_mask, upweight):
@@ -131,7 +138,12 @@
     wide1 = inside(wide1, 128)
     act1 = activate(wide1)
     stream2 = (wide1[128:384].astype(F32) + conv(act1, conv_weight[1], 128, 256)).astype(BF)
-    act2 = extended(activate(stream2), 256, c)
+    act2 = activate(stream2)
+    before, after = edges(act2, 256, c)
+    far_acts = [send(act0[128:512], CORE), send(act1, CORE)]
+    before, far_acts[0], far_acts[1] = lax.optimization_barrier((before, *far_acts))
+    act2 = jnp.concatenate([before, act2, after], axis=0)
+    far_acts.append(send(act2, CORE))
     stream = (stream2.astype(F32) + conv(act2, conv_weight[2], 256, 256)).astype(BF)
     padded_acts = [act0[128:512], act1, act2]
     logits = jnp.dot(stream, head_weight, preferred_element_type=F32)
@@ -140,6 +152,7 @@
     counts = targets[0].astype(F32)
     partial_loss = jnp.sum(bin_weight * (predicted - counts * jnp.log(predicted)))
     logit_grad = (bin_weight * (1.0 - counts / predicted) * slope).astype(BF)
+    logit_grad, far_acts[2] = lax.optimization_barrier((logit_grad, far_acts[2]))
     lanes = lax.broadcasted_iota(jnp.int32, (1, 1408), 1)
     spare = lanes - 1344 * (1 - c)
 
@@ -163,13 +176,13 @@
     scal = scal + send(scal, CORE)
     head_half = pair_dot(stream, near, send(stream, CORE), send(far, CORE))
     head_half = with_scalars(head_half, (scal[0], scal[1])).astype(BF)
-    head_sum = swap_xl(head_half, xl)
+    head_got = give(head_half, xl, ALONG_X)
     g_top = jnp.dot(logit_grad, head_weight.T, preferred_element_type=F32)
 
     def conv_grad(layer, grad_bf):
         d = BASE_DILATION * 2**layer
         padded = padded_acts[layer]
-        far_padded = send(padded, CORE)
+        far_padded = far_acts[layer]
         near, far = halves(grad_bf, 384)
         far = send(far, CORE)
         return jnp.concatenate(
@@ -183,40 +196,57 @@
     gb2 = g_top.astype(BF)
     before, after = edges(gb2, 256, c)
     half2 = conv_grad(2, gb2)
-    sum2 = swap_xl(half2, xl)
-    before = after_all(before, head_half, half2)
+    got2 = give(half2, z // 2, ALONG_Z[3], 2)
+    before, head_half, half2 = lax.optimization_barrier((before, head_half, half2))
     wide = jnp.concatenate([before, gb2, after], axis=0)
     g2 = g_top + through(stream2, conv_back(wide, conv_weight[2], 256, 256))
     gb1 = g2.astype(BF)
     before, after = edges(gb1, 192, c)
     half1 = conv_grad(1, gb1)
-    sum1 = swap_xl(half1, xl)
-    head_plane = plane_sum(head_sum.reshape(16, 24, 1408))
-    plane2 = plane_sum(sum2.reshape(16, 72, 384))
-    before = after_all(before, half1, head_sum, sum2)
+    head_x = take(head_half, head_got, xl)
+    part2_z = take(half2, got2, z // 2)
+    half1, head_x, part2_z = lax.optimization_barrier((half1, head_x, part2_z))
+    got1 = give(half1, xl, ALONG_X)
+    head_got = give(head_x, z // 2, ALONG_Z[3])
+    got2 = give(part2_z, z % 2, ALONG_Z[1], 2)
+    before, half1, head_x, part2_z = lax.optimization_barrier((before, half1, head_x, part2_z))
     wide = jnp.concatenate([before, gb1, after], axis=0)
     g_in = jnp.concatenate([before[128:].astype(F32), g2, after[:64].astype(F32)], axis=0)
     g1 = g_in + through(wide1[64:448], conv_back(wide, conv_weight[1], 128, 384))
     gb0 = inside(g1.astype(BF), 64)
+    head_z = take(head_x, head_got, z // 2)
+    part2_zz = take(part2_z, got2, z % 2)
+    head_got = give(head_z, z % 2, ALONG_Z[1])
+    got2 = give(part2_zz, xl, ALONG_X)
+    gb0, head_z, part2_zz = lax.optimization_barrier((gb0, head_z, part2_zz))
     half0 = conv_grad(0, gb0[64:320])
     plane0 = plane_sum(half0.reshape(2, 16, 72, 384).transpose(1, 0, 2, 3))
-    plane1 = plane_sum(sum1.reshape(16, 72, 384))
-    gb0 = after_all(gb0, half0)
+    head_zz = take(head_z, head_got, z % 2)
+    part2 = take(part2_zz, got2, xl)
+    part1_x = take(half1, got1, xl)
+    part1_z = halve(part1_x, z // 2, ALONG_Z[3])
+    part1 = halve(part1_z, z % 2, ALONG_Z[1])
     g0 = g1[64:320] + through(trunk[0], conv_back(gb0, conv_weight[0], 64, 256))
-
-    def by_core(v, rows):
-        v = v.reshape(v.shape[:-2] + (2, rows, 384))
-        return jnp.pad(v, ((0, 0),) * (v.ndim - 2) + ((0, 4), (0, 0)))
-
-    head_rows = jnp.pad(head_plane.reshape(2, 12, 1408), ((0, 0), (0, 0), (0, 128)))
-    message = jnp.concatenate(
-        [by_core(plane1, 36), by_core(plane2, 36)]
+    g0 = lax.optimization_barrier(g0)
+    head_rows = jnp.pad(head_zz, ((0, 0), (0, 128))).reshape(4, 24, 1536)
+    early = jnp.concatenate(
+        [part1.reshape(4, 72, 384), part2.reshape(4, 72, 384)]
         + [head_rows[..., 384 * k : 384 * k + 384] for k in range(4)],
         axis=1,
+    ).reshape(960, 384)
+    early = halve(early, y // 2, ALONG_Y[3])
+    early = halve(early, y % 2, ALONG_Y[1])
+    near = jnp.concatenate([pick(plane0, xl), early], axis=0)
+    part0, early = last_sum(near, pick(plane0, 1 - xl))
+
+    def own(v):
+        half = v.shape[0] // 2
+        return jnp.where(c == 0, v[:half], v[half:])
+
+    conv_total = jnp.stack([own(part0), own(early[:72]), own(early[72:144])])
+    head_total = jnp.concatenate(
+        [own(early[144 + 24 * k : 168 + 24 * k]) for k in range(4)], axis=1
     )
-    total = last_sum(message, by_core(plane0, 36), xl, xh, 0)
-    conv_total = jnp.stack([total[40 * k : 40 * k + 36] for k in range(LAYERS)])
-    head_total = jnp.concatenate([total[120 + 12 * k : 132 + 12 * k] for k in range(4)], axis=1)
     low = head_total[:, :1344]
     high = head_total[:, 64:1408]
     row = head_total[0]

time: 225 us -> 215 us (0.956)
  waiting for transfers between devices: 51.5 us -> 68 us
  local copies, waits for them, and re-layouts: 15.5 us -> 5.17 us
  starting transfers between devices: 79.6 us -> 70.2 us
  other arithmetic: 22.8 us -> 18.6 us
    ppermute x24 -> x32, waiting for transfers between devices: 15.8 us -> 68 us  [send(): return lax.ppermute(v, AXES, pairs)]
    all_to_all x4 -> x1, waiting for transfers between devices: 35.8 us -> 0.01 us  [plane_sum(): got = lax.all_to_all(blocks, ('z', 'y'), 0, 0, tiled=True)]
    all_to_all x4 -> x1, starting transfers between devices: 27.7 us -> 6.76 us  [plane_sum(): got = lax.all_to_all(blocks, ('z', 'y'), 0, 0, tiled=True)]
    ppermute x24 -> x32, starting transfers between devices: 51.8 us -> 63.5 us  [send(): return lax.ppermute(v, AXES, pairs)]
    concatenate x1, local copies, waits for them, and re-layouts: 4.87 us -> 0.02 us  [per_device(): jnp.concatenate([part1.reshape(4, 72, 384), part2.reshape(4, 72, 384)] +...]
    dot_general x3, matrix products: 2.47 us -> 7.28 us  [conv(): jnp.dot(rows[2 * d:2 * d + count], weights[2], preferred_element_type=F32)]
    dot_general x10, matrix products: 7.88 us -> 4.4 us  [pair_dot(): jnp.dot(far_a.T, far_b, preferred_element_type=F32)]
    reduce_sum x4 -> x1, other arithmetic: 3.71 us -> 0.25 us  [plane_sum(): return jnp.sum(got.astype(F32), axis=0).astype(BF)]
  transfers between devices with their start and end apart: 28 -> 33, of which waited for: 11 -> 14; matrix products, arithmetic and copies ran while one was open for 30% -> 27% of each run, Pallas kernels for 0% -> 0%
where the time goes in v1:
time: 215 us; the launch traced here: 214 us
  starting transfers between devices  70.2 us (33%)
  waiting for transfers between devices  68 us (32%)
  matrix products  46.8 us (22%)
  other arithmetic  18.6 us (9%)
  local copies, waits for them, and re-layouts  5.17 us (2%)
  between operations  4.83 us (2%)
    ppermute x32, waiting for transfers between devices, send(): return lax.ppermute(v, AXES, pairs)  68 us
    ppermute x32, starting transfers between devices, send(): return lax.ppermute(v, AXES, pairs)  63.5 us
    dot_general x3, matrix products, conv(): jnp.dot(rows[2 * d:2 * d + count], weights[2], preferred_element_type=F32)  7.28 us
    all_to_all x1, starting transfers between devices, plane_sum(): got = lax.all_to_all(blocks, ('z', 'y'), 0, 0, tiled=True)  6.76 us
    dot_general x3, matrix products, conv(): total = jnp.dot(rows[d:d + count], weights[1], preferred_element_type=F32)  6.12 us
    dot_general x3, matrix products, conv(): jnp.dot(rows[:count], weights[0], preferred_element_type=F32)  5.72 us
    dot_general x3, matrix products, conv_back(): total = jnp.dot(rows[d:d + count], weights[1].T, preferred_element_type=F32)  4.88 us
    dot_general x1, matrix products, per_device(): logits = jnp.dot(stream, head_weight, preferred_element_type=F32)  4.61 us
  transfers between devices with their start and end apart: 33, of which 14 were waited for; matrix products, arithmetic and copies ran while one was open for 27% of the time, Pallas kernels for 0%

profile of v1, /device:TPU:1, one launch (start us, length us, event | category | flops | bytes accessed | tf_op | source)
XLA Modules:
  0.0 213.7 jit_solution(13889379950127663406)
XLA Ops:
  1.8 4.6 %collective-permute-start = (bf16[192,768]{1,0:T(8,128)(2,1)S(1)}, bf16[192,768]{1,0:T(8,128)(2,1)S(1)}, u32[]{:S(2)}, u32[]{:S(2)}) collective-permute-start(bf16[192,768]{1,0:T(8,128)(2,1)S(1)} %get-tuple-element.66), channel_id=1, source_target_pairs={{2,4},{3,5},{6,8},{7,9},{10,12},{11,13},{14,16},{15,17},{18,20},{1... | collective-permute-start | bytes 884744 | tf_op jit(solution)/shard_map/ppermute | solution.py:44
  7.9 2.9 %collective-permute-done = bf16[192,768]{1,0:T(8,128)(2,1)S(1)} collective-permute-done((bf16[192,768]{1,0:T(8,128)(2,1)S(1)}, bf16[192,768]{1,0:T(8,128)(2,1)S(1)}, u32[]{:S(2)}, u32[]{:S(2)}) %collective-permute-start) | collective-permute-done | bytes 294944 | tf_op jit(solution)/shard_map/ppermute | solution.py:44
  15.7 2.6 %fusion.22 = (bf16[512,768]{1,0:T(8,128)(2,1)S(1)}, bf16[512,768]{1,0:T(8,128)(2,1)S(1)}) fusion(bf16[3,3,768,768]{3,2,1,0:T(8,128)(2,1)} %param.7, bf16[640,768]{1,0:T(8,128)(2,1)S(1)} %fusion.13, f32[512,768]{1,0:T(8,128)S(1)} %fusion.69, f32[512,768]{1,0:T(8,128)S(1)} %fusion.65, bf16[640,768]{1,0:T(8,128)(2,1)S(1)} %pad_maximum_fusion.4, ...), kind=kOutput, calls=%fused_computation.51 | convolution fusion | flops 610271232 | bytes 7471616 | tf_op jit(solution)/shard_map/dot_general | solution.py:118
  22.2 2.8 %fusion.112 = (bf16[256,768]{1,0:T(8,128)(2,1)}, bf16[256,768]{1,0:T(8,128)(2,1)}) fusion(f32[256,768]{1,0:T(8,128)S(1)} %convolution_add_fusion.17, bf16[3,3,768,768]{3,2,1,0:T(8,128)(2,1)} %param.7, bf16[512,768]{1,0:T(8,128)(2,1)S(1)} %get-tuple-element.72, bf16[512,768]{1,0:T(8,128)(2,1)S(1)} %get-tuple-element.73), kind=kOutput, calls=%fused_computation.170 | convolution fusion | flops 304742400 | bytes 3538944 | tf_op jit(solution)/shard_map/dot_general | solution.py:118
  25.0 3.7 %collective-permute-start.2 = (bf16[256,768]{1,0:T(8,128)(2,1)}, bf16[256,768]{1,0:T(8,128)(2,1)}, u32[]{:S(2)}, u32[]{:S(2)}) collective-permute-start(bf16[256,768]{1,0:T(8,128)(2,1)} %get-tuple-element.74), channel_id=1, source_target_pairs={{2,4},{3,5},{6,8},{7,9},{10,12},{11,13},{14,16},{15,17},{18,20},{1... | collective-permute-start | bytes 1179656 | tf_op jit(solution)/shard_map/ppermute | solution.py:44
  41.5 4.6 %fusion.5 = (f32[]{:T(128)}, bf16[256,2688]{1,0:T(8,128)(2,1)S(1)}) fusion(s32[1,256,2688]{2,1,0:T(8,128)S(1)} %copy-done.9, f32[256]{0:T(256)S(1)} %bitcast.250, bf16[256,768]{1,0:T(8,128)(2,1)S(1)} %fusion.35, bf16[768,2688]{1,0:T(8,128)(2,1)S(1)} %copy-done.8), kind=kOutput, calls=%fused_computation.13 | convolution fusion | flops 1070039040 | bytes 8651780 | tf_op jit(solution)/shard_map/dot_general | solution.py:149
  54.6 3.8 %collective-permute-start.8 = (bf16[256,768]{1,0:T(8,128)(2,1)S(1)}, bf16[256,768]{1,0:T(8,128)(2,1)S(1)}, u32[]{:S(2)}, u32[]{:S(2)}) collective-permute-start(bf16[256,768]{1,0:T(8,128)(2,1)S(1)} %get-tuple-element.76), channel_id=1, source_target_pairs={{2,4},{3,5},{6,8},{7,9},{10,12},{11,13},{14,16},{15,17},{18,20},{1... | collective-permute-start | bytes 1179656 | tf_op jit(solution)/shard_map/ppermute | solution.py:44
  62.8 8.5 %collective-permute-start.17 = (bf16[2,576,384]{2,1,0:T(8,128)(2,1)S(1)}, bf16[2,576,384]{2,1,0:T(8,128)(2,1)S(1)}, u32[]{:S(2)}, u32[]{:S(2)}) collective-permute-start(bf16[2,576,384]{2,1,0:T(8,128)(2,1)S(1)} %dynamic-slice_bitcast_fusion.2), channel_id=1, source_target_pairs={{0,48},{1,49},{2,50},{3,51},{4,52},{5,53},{6,54},{7,55},{8,56},{9,... | collective-permute-start | bytes 2654216 | tf_op jit(solution)/shard_map/ppermute | solution.py:44
  76.8 12.6 %collective-permute-start.16 = (bf16[1,384,1408]{2,1,0:T(8,128)(2,1)S(1)}, bf16[1,384,1408]{2,1,0:T(8,128)(2,1)S(1)}, u32[]{:S(2)}, u32[]{:S(2)}) collective-permute-start(bf16[1,384,1408]{2,1,0:T(8,128)(2,1)S(1)} %dynamic-slice_bitcast_fusion), channel_id=1, source_target_pairs={{0,64},{1,65},{2,66},{3,67},{4,68},{5,69},{6,70},{7,71},{8,72},{9,... | collective-permute-start | bytes 3244040 | tf_op jit(solution)/shard_map/ppermute | solution.py:44
  93.3 20.5 %collective-permute-done.16 = bf16[1,384,1408]{2,1,0:T(8,128)(2,1)S(1)} collective-permute-done((bf16[1,384,1408]{2,1,0:T(8,128)(2,1)S(1)}, bf16[1,384,1408]{2,1,0:T(8,128)(2,1)S(1)}, u32[]{:S(2)}, u32[]{:S(2)}) %collective-permute-start.16) | collective-permute-done | bytes 1081376 | tf_op jit(solution)/shard_map/ppermute | solution.py:44
  116.4 2.4 %convert_select_fusion = (bf16[384,768]{1,0:T(8,128)(2,1)S(1)}, f32[384,768]{1,0:T(8,128)}) fusion(pred[384]{0:T(512)(128)(4,1)S(1)} %fusion.184, bf16[512,768]{1,0:T(8,128)(2,1)S(1)} %copy-done.11, f32[384,768]{1,0:T(8,128)S(1)} %fusion.52, f32[384,768]{1,0:T(8,128)S(1)} %fusion.55, bf16[3,3,768,768]{3,2,1,0:T(8,128)(2,1)S(1)} %bitcast.228, ...), kind=kOutput, calls=%fused_computation.192 | convolution fusion | flops 462716928 | bytes 8061440 | tf_op jit(solution)/shard_map/dot_general | solution.py:123
  118.8 4.5 %collective-permute-done.19 = bf16[2,288,384]{2,1,0:T(8,128)(2,1)S(1)} collective-permute-done((bf16[2,288,384]{2,1,0:T(8,128)(2,1)S(1)}, bf16[2,288,384]{2,1,0:T(8,128)(2,1)S(1)}, u32[]{:S(2)}, u32[]{:S(2)}) %collective-permute-start.19) | collective-permute-done | bytes 442400 | tf_op jit(solution)/shard_map/ppermute | solution.py:44
  123.5 2.9 %collective-permute-start.24 = (bf16[1,288,384]{2,1,0:T(8,128)(2,1)S(1)}, bf16[1,288,384]{2,1,0:T(8,128)(2,1)S(1)}, u32[]{:S(2)}, u32[]{:S(2)}) collective-permute-start(bf16[1,288,384]{2,1,0:T(8,128)(2,1)S(1)} %constant_dynamic-slice_fusion), channel_id=1, source_target_pairs={{0,64},{1,65},{2,66},{3,67},{4,68},{5,69},{6,70},{7,71},{8,72},{9,... | collective-permute-start | bytes 663560 | tf_op jit(solution)/shard_map/ppermute | solution.py:44
  127.9 4.5 %collective-permute-start.20 = (bf16[256,384]{1,0:T(8,128)(2,1)S(1)}, bf16[256,384]{1,0:T(8,128)(2,1)S(1)}, u32[]{:S(2)}, u32[]{:S(2)}) collective-permute-start(bf16[256,384]{1,0:T(8,128)(2,1)S(1)} %get-tuple-element.48), channel_id=1, source_target_pairs={{0,2},{1,3},{2,0},{3,1},{4,6},{5,7},{6,4},{7,5},{8,10},{9,11},{10,... | collective-permute-start | bytes 589832 | tf_op jit(solution)/shard_map/ppermute | solution.py:44
  133.1 4.8 %collective-permute-done.24 = bf16[1,288,384]{2,1,0:T(8,128)(2,1)S(1)} collective-permute-done((bf16[1,288,384]{2,1,0:T(8,128)(2,1)S(1)}, bf16[1,288,384]{2,1,0:T(8,128)(2,1)S(1)}, u32[]{:S(2)}, u32[]{:S(2)}) %collective-permute-start.24) | collective-permute-done | bytes 221216 | tf_op jit(solution)/shard_map/ppermute | solution.py:44
  140.0 2.4 %collective-permute-start.22 = (bf16[1,576,384]{2,1,0:T(8,128)(2,1)}, bf16[1,576,384]{2,1,0:T(8,128)(2,1)}, u32[]{:S(2)}, u32[]{:S(2)}) collective-permute-start(bf16[1,576,384]{2,1,0:T(8,128)(2,1)} %dynamic-slice_bitcast_fusion.4), channel_id=1, source_target_pairs={{0,48},{1,49},{2,50},{3,51},{4,52},{5,53},{6,54},{7,55},{8,56},{9,... | collective-permute-start | bytes 1327112 | tf_op jit(solution)/shard_map/ppermute | solution.py:44
  144.3 6.8 %all-to-all-start = ((bf16[16,2,72,384]{3,2,1,0:T(8,128)(2,1)}), bf16[16,2,72,384]{3,2,1,0:T(8,128)(2,1)S(1)}, u32[]{:S(2)}, u32[]{:S(2)}) async-start(bf16[16,2,72,384]{3,2,1,0:T(8,128)(2,1)} %bitcast.217), calls=%async_computation | async-start | bytes 3538944 | tf_op jit(solution)/shard_map/all_to_all | solution.py:91
  154.8 20.7 %collective-permute-done.23 = bf16[1,288,384]{2,1,0:T(8,128)(2,1)S(1)} collective-permute-done((bf16[1,288,384]{2,1,0:T(8,128)(2,1)S(1)}, bf16[1,288,384]{2,1,0:T(8,128)(2,1)S(1)}, u32[]{:S(2)}, u32[]{:S(2)}) %collective-permute-start.23) | collective-permute-done | bytes 221216 | tf_op jit(solution)/shard_map/ppermute | solution.py:44
  175.8 3.2 %collective-permute-start.26 = (bf16[1,480,384]{2,1,0:T(8,128)(2,1)S(1)}, bf16[1,480,384]{2,1,0:T(8,128)(2,1)}, u32[]{:S(2)}, u32[]{:S(2)}) collective-permute-start(bf16[1,480,384]{2,1,0:T(8,128)(2,1)S(1)} %dynamic-slice_bitcast_fusion.6), channel_id=1, source_target_pairs={{0,12},{1,13},{2,14},{3,15},{4,8},{5,9},{6,10},{7,11},{8,4},{9,5},... | collective-permute-start | bytes 1105928 | tf_op jit(solution)/shard_map/ppermute | solution.py:44
  181.0 4.7 %collective-permute-done.26 = bf16[1,480,384]{2,1,0:T(8,128)(2,1)} collective-permute-done((bf16[1,480,384]{2,1,0:T(8,128)(2,1)S(1)}, bf16[1,480,384]{2,1,0:T(8,128)(2,1)}, u32[]{:S(2)}, u32[]{:S(2)}) %collective-permute-start.26) | collective-permute-done | bytes 368672 | tf_op jit(solution)/shard_map/ppermute | solution.py:44
  187.4 2.7 %convolution_add_fusion.11 = f32[256,768]{1,0:T(8,128)} fusion(f32[256,768]{1,0:T(8,128)S(1)} %fusion.67, bf16[3,3,768,768]{3,2,1,0:T(8,128)(2,1)} %param.7, bf16[384,768]{1,0:T(8,128)(2,1)S(1)} %copy-done.5), kind=kOutput, calls=%fused_computation.78 | convolution fusion | flops 302186496 | bytes 3145728 | tf_op jit(solution)/shard_map/dot_general | solution.py:124
  192.1 8.6 %collective-permute-start.28 = (bf16[312,384]{1,0:T(8,128)(2,1)S(1)}, bf16[312,384]{1,0:T(8,128)(2,1)S(1)}, u32[]{:S(2)}, u32[]{:S(2)}) collective-permute-start(bf16[312,384]{1,0:T(8,128)(2,1)S(1)} %pad_maximum_fusion.13), channel_id=1, source_target_pairs={{0,0},{1,2},{2,1},{3,3},{4,4},{5,6},{6,5},{7,7},{8,8},{9,10},{10,9... | collective-permute-start | bytes 718856 | tf_op jit(solution)/shard_map/ppermute | solution.py:44
  200.9 2.6 %fusion.102 = f32[256,768]{1,0:T(8,128)S(1)} fusion(f32[384,768]{1,0:T(8,128)} %get-tuple-element.81, f32[256,768]{1,0:T(8,128)} %convolution_add_fusion.11, bf16[3,3,768,768]{3,2,1,0:T(8,128)(2,1)} %param.7, bf16[384,768]{1,0:T(8,128)(2,1)S(1)} %copy-done.6, bf16[1,256,768]{2,1,0:T(8,128)(2,1)S(1)} %copy-done), kind=kOutput, calls=%fused_computation.160 | convolution fusion | flops 306315264 | bytes 4325376 | tf_op jit(solution)/shard_map/dot_general | solution.py:127
  204.6 2.9 %collective-permute-done.29 = bf16[312,384]{1,0:T(8,128)(2,1)S(1)} collective-permute-done((bf16[312,384]{1,0:T(8,128)(2,1)S(1)}, bf16[312,384]{1,0:T(8,128)(2,1)S(1)}, u32[]{:S(2)}, u32[]{:S(2)}) %collective-permute-start.29) | collective-permute-done | bytes 239648 | tf_op jit(solution)/shard_map/ppermute | solution.py:44
  (184 shorter events, 68.5 us)
Async XLA Ops:
  1.8 9.0 %collective-permute-start = (bf16[192,768]{1,0:T(8,128)(2,1)S(1)}, bf16[192,768]{1,0:T(8,128)(2,1)S(1)}, u32[]{:S(2)}, u32[]{:S(2)}) collective-permute-start(bf16[192,768]{1,0:T(8,128)(2,1)S(1)} %get-tuple-element.66), channel_id=1, source_target_pairs={{2,4},{3,5},{6,8},{7,9},{10,12},{11,13},{14,16},{15,17},{18,20},{1... | collective-permute-start | bytes 884744 | tf_op jit(solution)/shard_map/ppermute | solution.py:44
  20.3 15.3 %collective-permute-start.5 = (bf16[512,768]{1,0:T(8,128)(2,1)S(1)}, bf16[512,768]{1,0:T(8,128)(2,1)S(1)}, u32[]{:S(2)}, u32[]{:S(2)}) collective-permute-start(bf16[512,768]{1,0:T(8,128)(2,1)S(1)} %get-tuple-element.72), channel_id=1, source_target_pairs={{0,2},{1,3},{2,0},{3,1},{4,6},{5,7},{6,4},{7,5},{8,10},{9,11},{10,... | collective-permute-start | bytes 2359304 | tf_op jit(solution)/shard_map/ppermute | solution.py:44
  25.0 9.5 %collective-permute-start.2 = (bf16[256,768]{1,0:T(8,128)(2,1)}, bf16[256,768]{1,0:T(8,128)(2,1)}, u32[]{:S(2)}, u32[]{:S(2)}) collective-permute-start(bf16[256,768]{1,0:T(8,128)(2,1)} %get-tuple-element.74), channel_id=1, source_target_pairs={{2,4},{3,5},{6,8},{7,9},{10,12},{11,13},{14,16},{15,17},{18,20},{1... | collective-permute-start | bytes 1179656 | tf_op jit(solution)/shard_map/ppermute | solution.py:44
  36.9 15.1 %collective-permute-start.6 = (bf16[768,768]{1,0:T(8,128)(2,1)S(1)}, bf16[768,768]{1,0:T(8,128)(2,1)S(1)}, u32[]{:S(2)}, u32[]{:S(2)}) collective-permute-start(bf16[768,768]{1,0:T(8,128)(2,1)S(1)} %pad_maximum_fusion.3), channel_id=1, source_target_pairs={{0,2},{1,3},{2,0},{3,1},{4,6},{5,7},{6,4},{7,5},{8,10},{9,11},{10,... | collective-permute-start | bytes 3538952 | tf_op jit(solution)/shard_map/ppermute | solution.py:44
  40.9 31.0 %collective-permute-start.10 = (bf16[256,768]{1,0:T(8,128)(2,1)S(1)}, bf16[256,768]{1,0:T(8,128)(2,1)S(1)}, u32[]{:S(2)}, u32[]{:S(2)}) collective-permute-start(bf16[256,768]{1,0:T(8,128)(2,1)S(1)} %fusion.35), channel_id=1, source_target_pairs={{0,2},{1,3},{2,0},{3,1},{4,6},{5,7},{6,4},{7,5},{8,10},{9,11},{10,... | collective-permute-start | bytes 1179656 | tf_op jit(solution)/shard_map/ppermute | solution.py:44
  54.4 17.0 %collective-permute-start.7 = (bf16[256,768]{1,0:T(8,128)(2,1)S(1)}, bf16[256,768]{1,0:T(8,128)(2,1)S(1)}, u32[]{:S(2)}, u32[]{:S(2)}) collective-permute-start(bf16[256,768]{1,0:T(8,128)(2,1)S(1)} %get-tuple-element.76), channel_id=1, source_target_pairs={{0,2},{1,3},{2,0},{3,1},{4,6},{5,7},{6,4},{7,5},{8,10},{9,11},{10,... | collective-permute-start | bytes 1179656 | tf_op jit(solution)/shard_map/ppermute | solution.py:44
  54.6 16.7 %collective-permute-start.8 = (bf16[256,768]{1,0:T(8,128)(2,1)S(1)}, bf16[256,768]{1,0:T(8,128)(2,1)S(1)}, u32[]{:S(2)}, u32[]{:S(2)}) collective-permute-start(bf16[256,768]{1,0:T(8,128)(2,1)S(1)} %get-tuple-element.76), channel_id=1, source_target_pairs={{2,4},{3,5},{6,8},{7,9},{10,12},{11,13},{14,16},{15,17},{18,20},{1... | collective-permute-start | bytes 1179656 | tf_op jit(solution)/shard_map/ppermute | solution.py:44
  59.1 12.8 %collective-permute-start.11 = (bf16[256,1408]{1,0:T(8,128)(2,1)S(1)}, bf16[256,1408]{1,0:T(8,128)(2,1)S(1)}, u32[]{:S(2)}, u32[]{:S(2)}) collective-permute-start(bf16[256,1408]{1,0:T(8,128)(2,1)S(1)} %broadcast_select_fusion), channel_id=1, source_target_pairs={{0,2},{1,3},{2,0},{3,1},{4,6},{5,7},{6,4},{7,5},{8,10},{9,11},{10,... | collective-permute-start | bytes 2162696 | tf_op jit(solution)/shard_map/ppermute | solution.py:44
  62.8 30.2 %collective-permute-start.17 = (bf16[2,576,384]{2,1,0:T(8,128)(2,1)S(1)}, bf16[2,576,384]{2,1,0:T(8,128)(2,1)S(1)}, u32[]{:S(2)}, u32[]{:S(2)}) collective-permute-start(bf16[2,576,384]{2,1,0:T(8,128)(2,1)S(1)} %dynamic-slice_bitcast_fusion.2), channel_id=1, source_target_pairs={{0,48},{1,49},{2,50},{3,51},{4,52},{5,53},{6,54},{7,55},{8,56},{9,... | collective-permute-start | bytes 2654216 | tf_op jit(solution)/shard_map/ppermute | solution.py:44
  74.6 17.7 %collective-permute-start.13 = (bf16[192,768]{1,0:T(8,128)(2,1)S(1)}, bf16[192,768]{1,0:T(8,128)(2,1)S(1)}, u32[]{:S(2)}, u32[]{:S(2)}) collective-permute-start(bf16[192,768]{1,0:T(8,128)(2,1)S(1)} %get-tuple-element.61), channel_id=1, source_target_pairs={{2,4},{3,5},{6,8},{7,9},{10,12},{11,13},{14,16},{15,17},{18,20},{1... | collective-permute-start | bytes 884744 | tf_op jit(solution)/shard_map/ppermute | solution.py:44
  76.7 15.7 %collective-permute-start.14 = (bf16[192,768]{1,0:T(8,128)(2,1)S(1)}, bf16[192,768]{1,0:T(8,128)(2,1)S(1)}, u32[]{:S(2)}, u32[]{:S(2)}) collective-permute-start(bf16[192,768]{1,0:T(8,128)(2,1)S(1)} %get-tuple-element.60), channel_id=1, source_target_pairs={{0,2},{1,3},{2,0},{3,1},{4,6},{5,7},{6,4},{7,5},{8,10},{9,11},{10,... | collective-permute-start | bytes 884744 | tf_op jit(solution)/shard_map/ppermute | solution.py:44
  76.8 37.0 %collective-permute-start.16 = (bf16[1,384,1408]{2,1,0:T(8,128)(2,1)S(1)}, bf16[1,384,1408]{2,1,0:T(8,128)(2,1)S(1)}, u32[]{:S(2)}, u32[]{:S(2)}) collective-permute-start(bf16[1,384,1408]{2,1,0:T(8,128)(2,1)S(1)} %dynamic-slice_bitcast_fusion), channel_id=1, source_target_pairs={{0,64},{1,65},{2,66},{3,67},{4,68},{5,69},{6,70},{7,71},{8,72},{9,... | collective-permute-start | bytes 3244040 | tf_op jit(solution)/shard_map/ppermute | solution.py:44
  114.9 11.6 %collective-permute-start.18 = (bf16[1,192,1408]{2,1,0:T(8,128)(2,1)S(1)}, bf16[1,192,1408]{2,1,0:T(8,128)(2,1)S(1)}, u32[]{:S(2)}, u32[]{:S(2)}) collective-permute-start(bf16[1,192,1408]{2,1,0:T(8,128)(2,1)S(1)} %dynamic-slice_bitcast_fusion.3), channel_id=1, source_target_pairs={{0,48},{1,49},{2,50},{3,51},{4,52},{5,53},{6,54},{7,55},{8,56},{9,... | collective-permute-start | bytes 1622024 | tf_op jit(solution)/shard_map/ppermute | solution.py:44
  115.1 8.3 %collective-permute-start.19 = (bf16[2,288,384]{2,1,0:T(8,128)(2,1)S(1)}, bf16[2,288,384]{2,1,0:T(8,128)(2,1)S(1)}, u32[]{:S(2)}, u32[]{:S(2)}) collective-permute-start(bf16[2,288,384]{2,1,0:T(8,128)(2,1)S(1)} %dynamic-slice_bitcast_fusion.5), channel_id=1, source_target_pairs={{0,16},{1,17},{2,18},{3,19},{4,20},{5,21},{6,22},{7,23},{8,24},{9,... | collective-permute-start | bytes 1327112 | tf_op jit(solution)/shard_map/ppermute | solution.py:44
  115.3 23.6 %collective-permute-start.21 = (bf16[1,1152,384]{2,1,0:T(8,128)(2,1)S(1)}, bf16[1,1152,384]{2,1,0:T(8,128)(2,1)S(1)}, u32[]{:S(2)}, u32[]{:S(2)}) collective-permute-start(bf16[1,1152,384]{2,1,0:T(8,128)(2,1)S(1)} %dynamic-slice_bitcast_fusion.1), channel_id=1, source_target_pairs={{0,64},{1,65},{2,66},{3,67},{4,68},{5,69},{6,70},{7,71},{8,72},{9,... | collective-permute-start | bytes 2654216 | tf_op jit(solution)/shard_map/ppermute | solution.py:44
  123.5 14.4 %collective-permute-start.24 = (bf16[1,288,384]{2,1,0:T(8,128)(2,1)S(1)}, bf16[1,288,384]{2,1,0:T(8,128)(2,1)S(1)}, u32[]{:S(2)}, u32[]{:S(2)}) collective-permute-start(bf16[1,288,384]{2,1,0:T(8,128)(2,1)S(1)} %constant_dynamic-slice_fusion), channel_id=1, source_target_pairs={{0,64},{1,65},{2,66},{3,67},{4,68},{5,69},{6,70},{7,71},{8,72},{9,... | collective-permute-start | bytes 663560 | tf_op jit(solution)/shard_map/ppermute | solution.py:44
  127.9 10.1 %collective-permute-start.20 = (bf16[256,384]{1,0:T(8,128)(2,1)S(1)}, bf16[256,384]{1,0:T(8,128)(2,1)S(1)}, u32[]{:S(2)}, u32[]{:S(2)}) collective-permute-start(bf16[256,384]{1,0:T(8,128)(2,1)S(1)} %get-tuple-element.48), channel_id=1, source_target_pairs={{0,2},{1,3},{2,0},{3,1},{4,6},{5,7},{6,4},{7,5},{8,10},{9,11},{10,... | collective-permute-start | bytes 589832 | tf_op jit(solution)/shard_map/ppermute | solution.py:44
  133.1 20.6 %collective-permute-start.25 = (bf16[1,96,1408]{2,1,0:T(8,128)(2,1)}, bf16[1,96,1408]{2,1,0:T(8,128)(2,1)}, u32[]{:S(2)}, u32[]{:S(2)}) collective-permute-start(bf16[1,96,1408]{2,1,0:T(8,128)(2,1)} %dynamic-slice_bitcast_fusion.7), channel_id=1, source_target_pairs={{0,16},{1,17},{2,18},{3,19},{4,20},{5,21},{6,22},{7,23},{8,24},{9,... | collective-permute-start | bytes 811016 | tf_op jit(solution)/shard_map/ppermute | solution.py:44
  140.0 11.1 %collective-permute-start.22 = (bf16[1,576,384]{2,1,0:T(8,128)(2,1)}, bf16[1,576,384]{2,1,0:T(8,128)(2,1)}, u32[]{:S(2)}, u32[]{:S(2)}) collective-permute-start(bf16[1,576,384]{2,1,0:T(8,128)(2,1)} %dynamic-slice_bitcast_fusion.4), channel_id=1, source_target_pairs={{0,48},{1,49},{2,50},{3,51},{4,52},{5,53},{6,54},{7,55},{8,56},{9,... | collective-permute-start | bytes 1327112 | tf_op jit(solution)/shard_map/ppermute | solution.py:44
  144.3 47.5 %all-to-all-start = ((bf16[16,2,72,384]{3,2,1,0:T(8,128)(2,1)}), bf16[16,2,72,384]{3,2,1,0:T(8,128)(2,1)S(1)}, u32[]{:S(2)}, u32[]{:S(2)}) async-start(bf16[16,2,72,384]{3,2,1,0:T(8,128)(2,1)} %bitcast.217), calls=%async_computation | async-start | bytes 3538944 | tf_op jit(solution)/shard_map/all_to_all | solution.py:91
  152.3 23.2 %collective-permute-start.23 = (bf16[1,288,384]{2,1,0:T(8,128)(2,1)S(1)}, bf16[1,288,384]{2,1,0:T(8,128)(2,1)S(1)}, u32[]{:S(2)}, u32[]{:S(2)}) collective-permute-start(bf16[1,288,384]{2,1,0:T(8,128)(2,1)S(1)} %dynamic-slice_bitcast_fusion.8), channel_id=1, source_target_pairs={{0,16},{1,17},{2,18},{3,19},{4,20},{5,21},{6,22},{7,23},{8,24},{9,... | collective-permute-start | bytes 663560 | tf_op jit(solution)/shard_map/ppermute | solution.py:44
  175.8 9.9 %collective-permute-start.26 = (bf16[1,480,384]{2,1,0:T(8,128)(2,1)S(1)}, bf16[1,480,384]{2,1,0:T(8,128)(2,1)}, u32[]{:S(2)}, u32[]{:S(2)}) collective-permute-start(bf16[1,480,384]{2,1,0:T(8,128)(2,1)S(1)} %dynamic-slice_bitcast_fusion.6), channel_id=1, source_target_pairs={{0,12},{1,13},{2,14},{3,15},{4,8},{5,9},{6,10},{7,11},{8,4},{9,5},... | collective-permute-start | bytes 1105928 | tf_op jit(solution)/shard_map/ppermute | solution.py:44
  192.1 12.4 %collective-permute-start.28 = (bf16[312,384]{1,0:T(8,128)(2,1)S(1)}, bf16[312,384]{1,0:T(8,128)(2,1)S(1)}, u32[]{:S(2)}, u32[]{:S(2)}) collective-permute-start(bf16[312,384]{1,0:T(8,128)(2,1)S(1)} %pad_maximum_fusion.13), channel_id=1, source_target_pairs={{0,0},{1,2},{2,1},{3,3},{4,4},{5,6},{6,5},{7,7},{8,8},{9,10},{10,9... | collective-permute-start | bytes 718856 | tf_op jit(solution)/shard_map/ppermute | solution.py:44
  203.4 7.1 %collective-permute-start.30 = (bf16[72,384]{1,0:T(8,128)(2,1)S(1)}, bf16[72,384]{1,0:T(8,128)(2,1)S(1)}, u32[]{:S(2)}, u32[]{:S(2)}) collective-permute-start(bf16[72,384]{1,0:T(8,128)(2,1)S(1)} %get-tuple-element.68), channel_id=1, source_target_pairs={{0,64},{1,66},{2,65},{3,67},{4,68},{5,70},{6,69},{7,71},{8,72},{9,... | collective-permute-start | bytes 165896 | tf_op jit(solution)/shard_map/ppermute | solution.py:44
  (24 other events, 162.1 us)

commit v2 on v0

--- a/solution.py
+++ b/solution.py
@@ -31,11 +31,9 @@
 CORE = perm_of(lambda xl, z, y, c, xh: (xl, z, y, 1 - c, xh))
 NEXT_CHIP = [(a * 2 + xh, (a + 1) * 2 + xh) for a in range(1, 63, 2) for xh in range(2)]
 NEXT_CHIP = NEXT_CHIP + [(b, a) for a, b in NEXT_CHIP]
-ALONG_X = perm_of(lambda xl, z, y, c, xh: (1 - xl, z, y, c, xh))
-
-
-def last_hop(dx, m):
-    return perm_of(lambda xl, z, y, c, xh: (xl ^ dx, z, y, xh ^ m, c))
+
+def last_hop(m):
+    return perm_of(lambda xl, z, y, c, xh: (xl, z, y, xh ^ m, c))
 
 
 def send(v, pairs):
@@ -59,37 +57,17 @@
     return jnp.concatenate([before, shard, after], axis=0)
 
 
-def after_all(value, *others):
-    return lax.optimization_barrier((value,) + others)[0]
-
-
 def smooth(values):
     return jax.nn.gelu(values, approximate=True)
 
 
-def pick(blocks, place):
-    return lax.dynamic_index_in_dim(blocks, place, 0, keepdims=False)
-
-
-def swap_xl(part, xl):
-    halves = part.reshape(2, part.shape[0] // 2, part.shape[1])
-    got = send(pick(halves, 1 - xl), ALONG_X)
-    return (pick(halves, xl).astype(F32) + got.astype(F32)).astype(BF)
-
-
-def plane_sum(blocks):
-    got = lax.all_to_all(blocks, ("z", "y"), 0, 0, tiled=True)
+def over_chips(blocks):
+    got = lax.all_to_all(blocks, ("xl", "z", "y"), 0, 0, tiled=True)
     return jnp.sum(got.astype(F32), axis=0).astype(BF)
 
 
-def last_sum(block, extra, xl, xh, at):
-    near = jnp.concatenate([block[:, :at], pick(extra, xl), block[:, at:]], axis=1)
-    rest = pick(extra, 1 - xl)
-    total = sum(send(pick(near, xh ^ m), last_hop(0, m)).astype(F32) for m in range(2))
-    more = sum(send(pick(rest, xh ^ m), last_hop(1, m)).astype(F32) for m in range(2))
-    return jnp.concatenate(
-        [total[:at], total[at : at + more.shape[0]] + more, total[at + more.shape[0] :]], axis=0
-    )
+def over_halves(v):
+    return sum(send(v, last_hop(m)).astype(F32) for m in range(2))
 
 
 def per_device(trunk, conv_weight, head_weight, targets, error_mask, upweight):
@@ -131,7 +109,12 @@
     wide1 = inside(wide1, 128)
     act1 = activate(wide1)
     stream2 = (wide1[128:384].astype(F32) + conv(act1, conv_weight[1], 128, 256)).astype(BF)
-    act2 = extended(activate(stream2), 256, c)
+    act2 = activate(stream2)
+    before, after = edges(act2, 256, c)
+    far_acts = [send(act0[128:512], CORE), send(act1, CORE)]
+    before, far_acts[0], far_acts[1] = lax.optimization_barrier((before, *far_acts))
+    act2 = jnp.concatenate([before, act2, after], axis=0)
+    far_acts.append(send(act2, CORE))
     stream = (stream2.astype(F32) + conv(act2, conv_weight[2], 256, 256)).astype(BF)
     padded_acts = [act0[128:512], act1, act2]
     logits = jnp.dot(stream, head_weight, preferred_element_type=F32)
@@ -140,6 +123,7 @@
     counts = targets[0].astype(F32)
     partial_loss = jnp.sum(bin_weight * (predicted - counts * jnp.log(predicted)))
     logit_grad = (bin_weight * (1.0 - counts / predicted) * slope).astype(BF)
+    logit_grad, far_acts[2] = lax.optimization_barrier((logit_grad, far_acts[2]))
     lanes = lax.broadcasted_iota(jnp.int32, (1, 1408), 1)
     spare = lanes - 1344 * (1 - c)
 
@@ -163,13 +147,12 @@
     scal = scal + send(scal, CORE)
     head_half = pair_dot(stream, near, send(stream, CORE), send(far, CORE))
     head_half = with_scalars(head_half, (scal[0], scal[1])).astype(BF)
-    head_sum = swap_xl(head_half, xl)
     g_top = jnp.dot(logit_grad, head_weight.T, preferred_element_type=F32)
 
     def conv_grad(layer, grad_bf):
         d = BASE_DILATION * 2**layer
         padded = padded_acts[layer]
-        far_padded = send(padded, CORE)
+        far_padded = far_acts[layer]
         near, far = halves(grad_bf, 384)
         far = send(far, CORE)
         return jnp.concatenate(
@@ -183,40 +166,41 @@
     gb2 = g_top.astype(BF)
     before, after = edges(gb2, 256, c)
     half2 = conv_grad(2, gb2)
-    sum2 = swap_xl(half2, xl)
-    before = after_all(before, head_half, half2)
+    head_rows = jnp.pad(head_half, ((0, 0), (0, 128))).reshape(32, 24, 1536)
+    early = jnp.concatenate(
+        [half2.reshape(32, 72, 384)]
+        + [head_rows[..., 384 * k : 384 * k + 384] for k in range(4)],
+        axis=1,
+    )
+    before, early = lax.optimization_barrier((before, early))
+    early = over_chips(early)
     wide = jnp.concatenate([before, gb2, after], axis=0)
     g2 = g_top + through(stream2, conv_back(wide, conv_weight[2], 256, 256))
     gb1 = g2.astype(BF)
     before, after = edges(gb1, 192, c)
     half1 = conv_grad(1, gb1)
-    sum1 = swap_xl(half1, xl)
-    head_plane = plane_sum(head_sum.reshape(16, 24, 1408))
-    plane2 = plane_sum(sum2.reshape(16, 72, 384))
-    before = after_all(before, half1, head_sum, sum2)
+    before, half1 = lax.optimization_barrier((before, half1))
     wide = jnp.concatenate([before, gb1, after], axis=0)
     g_in = jnp.concatenate([before[128:].astype(F32), g2, after[:64].astype(F32)], axis=0)
     g1 = g_in + through(wide1[64:448], conv_back(wide, conv_weight[1], 128, 384))
     gb0 = inside(g1.astype(BF), 64)
     half0 = conv_grad(0, gb0[64:320])
-    plane0 = plane_sum(half0.reshape(2, 16, 72, 384).transpose(1, 0, 2, 3))
-    plane1 = plane_sum(sum1.reshape(16, 72, 384))
-    gb0 = after_all(gb0, half0)
+    late = jnp.concatenate([half0.reshape(32, 72, 384), half1.reshape(32, 72, 384)], axis=1)
+    gb0, late, early = lax.optimization_barrier((gb0, late, early))
+    late = over_chips(late)
     g0 = g1[64:320] + through(trunk[0], conv_back(gb0, conv_weight[0], 64, 256))
-
-    def by_core(v, rows):
-        v = v.reshape(v.shape[:-2] + (2, rows, 384))
-        return jnp.pad(v, ((0, 0),) * (v.ndim - 2) + ((0, 4), (0, 0)))
-
-    head_rows = jnp.pad(head_plane.reshape(2, 12, 1408), ((0, 0), (0, 0), (0, 128)))
-    message = jnp.concatenate(
-        [by_core(plane1, 36), by_core(plane2, 36)]
-        + [head_rows[..., 384 * k : 384 * k + 384] for k in range(4)],
-        axis=1,
-    )
-    total = last_sum(message, by_core(plane0, 36), xl, xh, 0)
-    conv_total = jnp.stack([total[40 * k : 40 * k + 36] for k in range(LAYERS)])
-    head_total = jnp.concatenate([total[120 + 12 * k : 132 + 12 * k] for k in range(4)], axis=1)
+    g0 = lax.optimization_barrier(g0)
+    early = over_halves(early)
+    late = over_halves(late)
+
+    def own(v):
+        half = v.shape[0] // 2
+        return jnp.where(c == 0, v[:half], v[half:])
+
+    conv_total = jnp.stack([own(late[:72]), own(late[72:]), own(early[:72])])
+    head_total = jnp.concatenate(
+        [own(early[72 + 24 * k : 96 + 24 * k]) for k in range(4)], axis=1
+    )
     low = head_total[:, :1344]
     high = head_total[:, 64:1408]
     row = head_total[0]

time: 225 us -> 219 us (0.973)
  waiting for transfers between devices: 51.5 us -> 77.9 us
  starting transfers between devices: 79.6 us -> 55.9 us
  local copies, waits for them, and re-layouts: 15.5 us -> 5.45 us
  other arithmetic: 22.8 us -> 26 us
  matrix products: 48.7 us -> 45.7 us
    ppermute x24 -> x21, waiting for transfers between devices: 15.8 us -> 44 us  [send(): return lax.ppermute(v, AXES, pairs)]
    ppermute x24 -> x21, starting transfers between devices: 51.8 us -> 29.9 us  [send(): return lax.ppermute(v, AXES, pairs)]
    convert_element_type x3 -> x0, other arithmetic: 6.31 us -> none  [swap_xl(): return (pick(halves, xl).astype(F32) + got.astype(F32)).astype(BF)]
    concatenate x1, local copies, waits for them, and re-layouts: 4.87 us -> 0.1 us  [per_device(): jnp.concatenate([half2.reshape(32, 72, 384)] + [head_rows[..., 384 * k:38...]
    concatenate x1 -> x3, other arithmetic: 0.01 us -> 2.99 us  [the longest x1 2.11 us: per_device(): jnp.concatenate([half0.reshape(32, 72, 384), half1.reshape(32, 72, 384)],...]
    unnamed x39 -> x46, local copies, waits for them, and re-layouts: 2.14 us -> 4.55 us
    squeeze x4 -> x0, local copies, waits for them, and re-layouts: 2.3 us -> none  [pick(): return lax.dynamic_index_in_dim(blocks, place, 0, keepdims=False)]
    all_to_all x4 -> x2, waiting for transfers between devices: 35.8 us -> 33.8 us  [over_chips(): got = lax.all_to_all(blocks, ('xl', 'z', 'y'), 0, 0, tiled=True)]
  transfers between devices with their start and end apart: 28 -> 23, of which waited for: 11 -> 7; matrix products, arithmetic and copies ran while one was open for 30% -> 24% of each run, Pallas kernels for 0% -> 0%
where the time goes in v2:
time: 219 us; the launch traced here: 216 us
  waiting for transfers between devices  77.9 us (36%)
  starting transfers between devices  55.9 us (26%)
  matrix products  45.7 us (21%)
  other arithmetic  26 us (12%)
  local copies, waits for them, and re-layouts  5.45 us (2%)
  between operations  4.75 us (2%)
    ppermute x21, waiting for transfers between devices, send(): return lax.ppermute(v, AXES, pairs)  44 us
    all_to_all x2, waiting for transfers between devices, over_chips(): got = lax.all_to_all(blocks, ('xl', 'z', 'y'), 0, 0, tiled=True)  33.8 us
    ppermute x21, starting transfers between devices, send(): return lax.ppermute(v, AXES, pairs)  29.9 us
    all_to_all x2, starting transfers between devices, over_chips(): got = lax.all_to_all(blocks, ('xl', 'z', 'y'), 0, 0, tiled=True)  25.9 us
    dot_general x3, matrix products, conv_back(): jnp.dot(rows[:count], weights[2].T, preferred_element_type=F32)  7.25 us
    dot_general x10, matrix products, pair_dot(): jnp.dot(far_a.T, far_b, preferred_element_type=F32)  7.14 us
    dot_general x3, matrix products, conv_back(): total = jnp.dot(rows[d:d + count], weights[1].T, preferred_element_type=F32)  6.14 us
    dot_general x10, matrix products, pair_dot(): jnp.dot(a.T, b, preferred_element_type=F32)  5.56 us
  transfers between devices with their start and end apart: 23, of which 7 were waited for; matrix products, arithmetic and copies ran while one was open for 24% of the time, Pallas kernels for 0%

profile of v2, /device:TPU:1, one launch (start us, length us, event | category | flops | bytes accessed | tf_op | source)
XLA Modules:
  0.0 215.6 jit_solution(268204616004789235)
XLA Ops:
  1.8 4.6 %collective-permute-start = (bf16[192,768]{1,0:T(8,128)(2,1)S(1)}, bf16[192,768]{1,0:T(8,128)(2,1)S(1)}, u32[]{:S(2)}, u32[]{:S(2)}) collective-permute-start(bf16[192,768]{1,0:T(8,128)(2,1)S(1)} %get-tuple-element.48), channel_id=1, source_target_pairs={{2,4},{3,5},{6,8},{7,9},{10,12},{11,13},{14,16},{15,17},{18,20},{1... | collective-permute-start | bytes 884744 | tf_op jit(solution)/shard_map/ppermute | solution.py:40
  7.9 2.9 %collective-permute-done = bf16[192,768]{1,0:T(8,128)(2,1)S(1)} collective-permute-done((bf16[192,768]{1,0:T(8,128)(2,1)S(1)}, bf16[192,768]{1,0:T(8,128)(2,1)S(1)}, u32[]{:S(2)}, u32[]{:S(2)}) %collective-permute-start) | collective-permute-done | bytes 294944 | tf_op jit(solution)/shard_map/ppermute | solution.py:40
  11.5 2.3 %fusion.62 = f32[512,768]{1,0:T(8,128)S(1)} fusion(bf16[3,3,768,768]{3,2,1,0:T(8,128)(2,1)} %param.7, bf16[640,768]{1,0:T(8,128)(2,1)S(1)} %fusion.12), kind=kOutput, calls=%fused_computation.112 | convolution fusion | flops 603979776 | bytes 3538944 | tf_op jit(solution)/shard_map/dot_general | solution.py:88
  13.9 2.4 %fusion.66 = f32[512,768]{1,0:T(8,128)S(1)} fusion(bf16[3,3,768,768]{3,2,1,0:T(8,128)(2,1)} %param.7, bf16[640,768]{1,0:T(8,128)(2,1)S(1)} %fusion.12), kind=kOutput, calls=%fused_computation.116 | convolution fusion | flops 603979776 | bytes 3538944 | tf_op jit(solution)/shard_map/dot_general | solution.py:87
  19.4 3.7 %collective-permute-start.2 = (bf16[256,768]{1,0:T(8,128)(2,1)S(1)}, bf16[256,768]{1,0:T(8,128)(2,1)S(1)}, u32[]{:S(2)}, u32[]{:S(2)}) collective-permute-start(bf16[256,768]{1,0:T(8,128)(2,1)S(1)} %get-tuple-element.60), channel_id=1, source_target_pairs={{2,4},{3,5},{6,8},{7,9},{10,12},{11,13},{14,16},{15,17},{18,20},{1... | collective-permute-start | bytes 1179656 | tf_op jit(solution)/shard_map/ppermute | solution.py:40
  24.5 4.1 %collective-permute-done.2 = bf16[256,768]{1,0:T(8,128)(2,1)S(1)} collective-permute-done((bf16[256,768]{1,0:T(8,128)(2,1)S(1)}, bf16[256,768]{1,0:T(8,128)(2,1)S(1)}, u32[]{:S(2)}, u32[]{:S(2)}) %collective-permute-start.2) | collective-permute-done | bytes 393248 | tf_op jit(solution)/shard_map/ppermute | solution.py:40
  33.5 4.6 %fusion.5 = (f32[]{:T(128)}, bf16[256,2688]{1,0:T(8,128)(2,1)S(1)}) fusion(s32[1,256,2688]{2,1,0:T(8,128)S(1)} %copy-done.16, f32[256]{0:T(256)S(1)} %bitcast.141, bf16[256,768]{1,0:T(8,128)(2,1)S(1)} %fusion.32, bf16[768,2688]{1,0:T(8,128)(2,1)S(1)} %copy-done.15), kind=kOutput, calls=%fused_computation.14 | convolution fusion | flops 1070039040 | bytes 8651780 | tf_op jit(solution)/shard_map/dot_general | solution.py:120
  46.7 3.8 %collective-permute-start.8 = (bf16[256,768]{1,0:T(8,128)(2,1)S(1)}, bf16[256,768]{1,0:T(8,128)(2,1)S(1)}, u32[]{:S(2)}, u32[]{:S(2)}) collective-permute-start(bf16[256,768]{1,0:T(8,128)(2,1)S(1)} %get-tuple-element.62), channel_id=1, source_target_pairs={{2,4},{3,5},{6,8},{7,9},{10,12},{11,13},{14,16},{15,17},{18,20},{1... | collective-permute-start | bytes 1179656 | tf_op jit(solution)/shard_map/ppermute | solution.py:40
  58.1 2.2 %fusion.186 = (bf16[256,768]{1,0:T(8,128)(2,1)S(1)}, f32[256,768]{1,0:T(8,128)}) fusion(f32[256,768]{1,0:T(8,128)S(1)} %get-tuple-element.63, bf16[256,768]{1,0:T(8,128)(2,1)S(1)} %get-tuple-element.61, f32[256,768]{1,0:T(8,128)S(1)} %convolution_add_fusion.13, bf16[256,768]{1,0:T(8,128)(2,1)S(1)} %broadcast_select_fusion.1, ...), kind=kOutput, calls=%fused_computation.279 | convolution fusion | flops 306511872 | bytes 4718592 | tf_op jit(solution)/shard_map/dot_general | solution.py:98
  62.7 4.3 %collective-permute-start.13 = (bf16[192,768]{1,0:T(8,128)(2,1)}, bf16[192,768]{1,0:T(8,128)(2,1)}, u32[]{:S(2)}, u32[]{:S(2)}) collective-permute-start(bf16[192,768]{1,0:T(8,128)(2,1)} %get-tuple-element.44), channel_id=1, source_target_pairs={{2,4},{3,5},{6,8},{7,9},{10,12},{11,13},{14,16},{15,17},{18,20},{1... | collective-permute-start | bytes 884744 | tf_op jit(solution)/shard_map/ppermute | solution.py:40
  67.7 19.0 %all-to-all-start = ((bf16[32,168,384]{2,1,0:T(8,128)(2,1)}), bf16[32,168,384]{2,1,0:T(8,128)(2,1)}, u32[]{:S(2)}, u32[]{:S(2)}) async-start(bf16[32,168,384]{2,1,0:T(8,128)(2,1)} %copy-done), calls=%async_computation | async-start | bytes 8257536 | tf_op jit(solution)/shard_map/all_to_all | solution.py:65
  93.5 1.9 fusion.52
  95.5 2.0 fusion.49
  97.6 3.7 %convert_select_fusion = (bf16[384,768]{1,0:T(8,128)(2,1)S(1)}, f32[384,768]{1,0:T(8,128)}) fusion(pred[384]{0:T(512)(128)(4,1)S(1)} %fusion.170, bf16[512,768]{1,0:T(8,128)(2,1)S(1)} %copy-done.18, f32[384,768]{1,0:T(8,128)S(1)} %fusion.49, f32[384,768]{1,0:T(8,128)S(1)} %fusion.52, bf16[3,3,768,768]{3,2,1,0:T(8,128)(2,1)} %param.7, ...), kind=kOutput, calls=%fused_computation.178 | convolution fusion | flops 462716928 | bytes 8061312 | tf_op jit(solution)/shard_map/dot_general | solution.py:94
  105.2 2.1 pad_maximum_fusion
  107.3 33.8 %all-to-all-done = bf16[32,168,384]{2,1,0:T(8,128)(2,1)} async-done(((bf16[32,168,384]{2,1,0:T(8,128)(2,1)}), bf16[32,168,384]{2,1,0:T(8,128)(2,1)}, u32[]{:S(2)}, u32[]{:S(2)}) %all-to-all-start) | async-done | bytes 4128800 | tf_op jit(solution)/shard_map/all_to_all | solution.py:65
  141.1 3.5 %reduce_sum.62 = bf16[168,384]{1,0:T(8,128)(2,1)} reduce(bf16[32,168,384]{2,1,0:T(8,128)(2,1)} %all-to-all-done, bf16[]{:T(256)} %constant.37.clone.1), dimensions={0}, to_apply=%region_2.3 | reduce | flops 1999872 | bytes 4257794 | tf_op jit(solution)/shard_map/reduce_sum | solution.py:66
  144.6 7.0 %all-to-all-start.1 = ((bf16[32,144,384]{2,1,0:T(8,128)(2,1)}), bf16[32,144,384]{2,1,0:T(8,128)(2,1)S(1)}, u32[]{:S(2)}, u32[]{:S(2)}) async-start(bf16[32,144,384]{2,1,0:T(8,128)(2,1)} %pad_maximum_fusion), calls=%async_computation.1 | async-start | bytes 7077888 | tf_op jit(solution)/shard_map/all_to_all | solution.py:65
  151.6 6.3 %collective-permute-start.17 = (bf16[168,384]{1,0:T(8,128)(2,1)}, bf16[168,384]{1,0:T(8,128)(2,1)S(1)}, u32[]{:S(2)}, u32[]{:S(2)}) collective-permute-start(bf16[168,384]{1,0:T(8,128)(2,1)} %reduce_sum.62), channel_id=1, source_target_pairs={{0,0},{1,2},{2,1},{3,3},{4,4},{5,6},{6,5},{7,7},{8,8},{9,10},{10,9... | collective-permute-start | bytes 387080 | tf_op jit(solution)/shard_map/ppermute | solution.py:40
  161.9 3.0 %fusion.95 = f32[256,768]{1,0:T(8,128)} fusion(f32[384,768]{1,0:T(8,128)S(1)} %copy-done.20, f32[256,768]{1,0:T(8,128)S(1)} %convolution_add_fusion.11, bf16[3,3,768,768]{3,2,1,0:T(8,128)(2,1)} %param.7, bf16[384,768]{1,0:T(8,128)(2,1)S(1)} %copy-done.12, bf16[1,256,768]{2,1,0:T(8,128)(2,1)S(1)} %copy-done.2), kind=kOutput, calls=%fused_computation.144 | convolution fusion | flops 306315264 | bytes 4325376 | tf_op jit(solution)/shard_map/dot_general | solution.py:98
  165.0 32.0 %collective-permute-done.17 = bf16[168,384]{1,0:T(8,128)(2,1)S(1)} collective-permute-done((bf16[168,384]{1,0:T(8,128)(2,1)}, bf16[168,384]{1,0:T(8,128)(2,1)S(1)}, u32[]{:S(2)}, u32[]{:S(2)}) %collective-permute-start.17) | collective-permute-done | bytes 129056 | tf_op jit(solution)/shard_map/ppermute | solution.py:40
  202.1 1.9 fusion.127
  206.0 2.9 %collective-permute-start.19 = (bf16[144,384]{1,0:T(8,128)(2,1)}, bf16[144,384]{1,0:T(8,128)(2,1)S(1)}, u32[]{:S(2)}, u32[]{:S(2)}) collective-permute-start(bf16[144,384]{1,0:T(8,128)(2,1)} %reduce_sum.65), channel_id=1, source_target_pairs={{0,0},{1,2},{2,1},{3,3},{4,4},{5,6},{6,5},{7,7},{8,8},{9,10},{10,9... | collective-permute-start | bytes 331784 | tf_op jit(solution)/shard_map/ppermute | solution.py:40
  211.4 2.4 %collective-permute-done.19 = bf16[144,384]{1,0:T(8,128)(2,1)S(1)} collective-permute-done((bf16[144,384]{1,0:T(8,128)(2,1)}, bf16[144,384]{1,0:T(8,128)(2,1)S(1)}, u32[]{:S(2)}, u32[]{:S(2)}) %collective-permute-start.19) | collective-permute-done | bytes 110624 | tf_op jit(solution)/shard_map/ppermute | solution.py:40
  (151 shorter events, 54.1 us)
Async XLA Ops:
  1.8 9.0 %collective-permute-start = (bf16[192,768]{1,0:T(8,128)(2,1)S(1)}, bf16[192,768]{1,0:T(8,128)(2,1)S(1)}, u32[]{:S(2)}, u32[]{:S(2)}) collective-permute-start(bf16[192,768]{1,0:T(8,128)(2,1)S(1)} %get-tuple-element.48), channel_id=1, source_target_pairs={{2,4},{3,5},{6,8},{7,9},{10,12},{11,13},{14,16},{15,17},{18,20},{1... | collective-permute-start | bytes 884744 | tf_op jit(solution)/shard_map/ppermute | solution.py:40
  6.4 4.4 %collective-permute-start.1 = (bf16[192,768]{1,0:T(8,128)(2,1)S(1)}, bf16[192,768]{1,0:T(8,128)(2,1)S(1)}, u32[]{:S(2)}, u32[]{:S(2)}) collective-permute-start(bf16[192,768]{1,0:T(8,128)(2,1)S(1)} %get-tuple-element.49), channel_id=1, source_target_pairs={{0,2},{1,3},{2,0},{3,1},{4,6},{5,7},{6,4},{7,5},{8,10},{9,11},{10,... | collective-permute-start | bytes 884744 | tf_op jit(solution)/shard_map/ppermute | solution.py:40
  17.7 44.6 %copy-start.4 = (bf16[512,768]{1,0:T(8,128)(2,1)}, bf16[512,768]{1,0:T(8,128)(2,1)S(1)}, u32[]{:S(2)}) copy-start(bf16[512,768]{1,0:T(8,128)(2,1)S(1)} %get-tuple-element.58) | copy-start | bytes 2359300
  18.2 10.5 %collective-permute-start.5 = (bf16[512,768]{1,0:T(8,128)(2,1)S(1)}, bf16[512,768]{1,0:T(8,128)(2,1)S(1)}, u32[]{:S(2)}, u32[]{:S(2)}) collective-permute-start(bf16[512,768]{1,0:T(8,128)(2,1)S(1)} %get-tuple-element.58), channel_id=1, source_target_pairs={{0,2},{1,3},{2,0},{3,1},{4,6},{5,7},{6,4},{7,5},{8,10},{9,11},{10,... | collective-permute-start | bytes 2359304 | tf_op jit(solution)/shard_map/ppermute | solution.py:40
  19.4 9.2 %collective-permute-start.2 = (bf16[256,768]{1,0:T(8,128)(2,1)S(1)}, bf16[256,768]{1,0:T(8,128)(2,1)S(1)}, u32[]{:S(2)}, u32[]{:S(2)}) collective-permute-start(bf16[256,768]{1,0:T(8,128)(2,1)S(1)} %get-tuple-element.60), channel_id=1, source_target_pairs={{2,4},{3,5},{6,8},{7,9},{10,12},{11,13},{14,16},{15,17},{18,20},{1... | collective-permute-start | bytes 1179656 | tf_op jit(solution)/shard_map/ppermute | solution.py:40
  23.2 5.4 %collective-permute-start.3 = (bf16[256,768]{1,0:T(8,128)(2,1)S(1)}, bf16[256,768]{1,0:T(8,128)(2,1)S(1)}, u32[]{:S(2)}, u32[]{:S(2)}) collective-permute-start(bf16[256,768]{1,0:T(8,128)(2,1)S(1)} %get-tuple-element.60), channel_id=1, source_target_pairs={{0,2},{1,3},{2,0},{3,1},{4,6},{5,7},{6,4},{7,5},{8,10},{9,11},{10,... | collective-permute-start | bytes 1179656 | tf_op jit(solution)/shard_map/ppermute | solution.py:40
  23.3 5.4 %collective-permute-start.4 = (bf16[384,768]{1,0:T(8,128)(2,1)S(1)}, bf16[384,768]{1,0:T(8,128)(2,1)S(1)}, u32[]{:S(2)}, u32[]{:S(2)}) collective-permute-start(bf16[384,768]{1,0:T(8,128)(2,1)S(1)} %slice.397), channel_id=1, source_target_pairs={{0,2},{1,3},{2,0},{3,1},{4,6},{5,7},{6,4},{7,5},{8,10},{9,11},{10,... | collective-permute-start | bytes 1769480 | tf_op jit(solution)/shard_map/ppermute | solution.py:40
  31.5 12.5 %collective-permute-start.6 = (bf16[768,768]{1,0:T(8,128)(2,1)S(1)}, bf16[768,768]{1,0:T(8,128)(2,1)S(1)}, u32[]{:S(2)}, u32[]{:S(2)}) collective-permute-start(bf16[768,768]{1,0:T(8,128)(2,1)S(1)} %pad_maximum_fusion.4), channel_id=1, source_target_pairs={{0,2},{1,3},{2,0},{3,1},{4,6},{5,7},{6,4},{7,5},{8,10},{9,11},{10,... | collective-permute-start | bytes 3538952 | tf_op jit(solution)/shard_map/ppermute | solution.py:40
  31.6 25.0 %collective-permute-start.11 = (bf16[256,768]{1,0:T(8,128)(2,1)S(1)}, bf16[256,768]{1,0:T(8,128)(2,1)S(1)}, u32[]{:S(2)}, u32[]{:S(2)}) collective-permute-start(bf16[256,768]{1,0:T(8,128)(2,1)S(1)} %fusion.32), channel_id=1, source_target_pairs={{0,2},{1,3},{2,0},{3,1},{4,6},{5,7},{6,4},{7,5},{8,10},{9,11},{10,... | collective-permute-start | bytes 1179656 | tf_op jit(solution)/shard_map/ppermute | solution.py:40
  39.6 1.1 collective-permute-start.10
  46.3 9.7 %collective-permute-start.7 = (bf16[256,768]{1,0:T(8,128)(2,1)S(1)}, bf16[256,768]{1,0:T(8,128)(2,1)S(1)}, u32[]{:S(2)}, u32[]{:S(2)}) collective-permute-start(bf16[256,768]{1,0:T(8,128)(2,1)S(1)} %get-tuple-element.62), channel_id=1, source_target_pairs={{0,2},{1,3},{2,0},{3,1},{4,6},{5,7},{6,4},{7,5},{8,10},{9,11},{10,... | collective-permute-start | bytes 1179656 | tf_op jit(solution)/shard_map/ppermute | solution.py:40
  46.7 9.3 %collective-permute-start.8 = (bf16[256,768]{1,0:T(8,128)(2,1)S(1)}, bf16[256,768]{1,0:T(8,128)(2,1)S(1)}, u32[]{:S(2)}, u32[]{:S(2)}) collective-permute-start(bf16[256,768]{1,0:T(8,128)(2,1)S(1)} %get-tuple-element.62), channel_id=1, source_target_pairs={{2,4},{3,5},{6,8},{7,9},{10,12},{11,13},{14,16},{15,17},{18,20},{1... | collective-permute-start | bytes 1179656 | tf_op jit(solution)/shard_map/ppermute | solution.py:40
  51.1 5.5 %collective-permute-start.12 = (bf16[256,1408]{1,0:T(8,128)(2,1)S(1)}, bf16[256,1408]{1,0:T(8,128)(2,1)S(1)}, u32[]{:S(2)}, u32[]{:S(2)}) collective-permute-start(bf16[256,1408]{1,0:T(8,128)(2,1)S(1)} %broadcast_select_fusion), channel_id=1, source_target_pairs={{0,2},{1,3},{2,0},{3,1},{4,6},{5,7},{6,4},{7,5},{8,10},{9,11},{10,... | collective-permute-start | bytes 2162696 | tf_op jit(solution)/shard_map/ppermute | solution.py:40
  51.2 2.5 %collective-permute-start.9 = (bf16[256,384]{1,0:T(8,128)(2,1)S(1)}, bf16[256,384]{1,0:T(8,128)(2,1)S(1)}, u32[]{:S(2)}, u32[]{:S(2)}) collective-permute-start(bf16[256,384]{1,0:T(8,128)(2,1)S(1)} %get-tuple-element.47), channel_id=1, source_target_pairs={{0,2},{1,3},{2,0},{3,1},{4,6},{5,7},{6,4},{7,5},{8,10},{9,11},{10,... | collective-permute-start | bytes 589832 | tf_op jit(solution)/shard_map/ppermute | solution.py:40
  62.7 29.6 %collective-permute-start.13 = (bf16[192,768]{1,0:T(8,128)(2,1)}, bf16[192,768]{1,0:T(8,128)(2,1)}, u32[]{:S(2)}, u32[]{:S(2)}) collective-permute-start(bf16[192,768]{1,0:T(8,128)(2,1)} %get-tuple-element.44), channel_id=1, source_target_pairs={{2,4},{3,5},{6,8},{7,9},{10,12},{11,13},{14,16},{15,17},{18,20},{1... | collective-permute-start | bytes 884744 | tf_op jit(solution)/shard_map/ppermute | solution.py:40
  67.1 25.2 %collective-permute-start.14 = (bf16[192,768]{1,0:T(8,128)(2,1)}, bf16[192,768]{1,0:T(8,128)(2,1)}, u32[]{:S(2)}, u32[]{:S(2)}) collective-permute-start(bf16[192,768]{1,0:T(8,128)(2,1)} %get-tuple-element.45), channel_id=1, source_target_pairs={{0,2},{1,3},{2,0},{3,1},{4,6},{5,7},{6,4},{7,5},{8,10},{9,11},{10,... | collective-permute-start | bytes 884744 | tf_op jit(solution)/shard_map/ppermute | solution.py:40
  67.2 20.9 %collective-permute-start.15 = (bf16[256,384]{1,0:T(8,128)(2,1)}, bf16[256,384]{1,0:T(8,128)(2,1)}, u32[]{:S(2)}, u32[]{:S(2)}) collective-permute-start(bf16[256,384]{1,0:T(8,128)(2,1)} %get-tuple-element.42), channel_id=1, source_target_pairs={{0,2},{1,3},{2,0},{3,1},{4,6},{5,7},{6,4},{7,5},{8,10},{9,11},{10,... | collective-permute-start | bytes 589832 | tf_op jit(solution)/shard_map/ppermute | solution.py:40
  67.7 73.4 %all-to-all-start = ((bf16[32,168,384]{2,1,0:T(8,128)(2,1)}), bf16[32,168,384]{2,1,0:T(8,128)(2,1)}, u32[]{:S(2)}, u32[]{:S(2)}) async-start(bf16[32,168,384]{2,1,0:T(8,128)(2,1)} %copy-done), calls=%async_computation | async-start | bytes 8257536 | tf_op jit(solution)/shard_map/all_to_all | solution.py:65
  101.3 2.2 %collective-permute-start.16 = (bf16[256,384]{1,0:T(8,128)(2,1)S(1)}, bf16[256,384]{1,0:T(8,128)(2,1)S(1)}, u32[]{:S(2)}, u32[]{:S(2)}) collective-permute-start(bf16[256,384]{1,0:T(8,128)(2,1)S(1)} %get-tuple-element.36), channel_id=1, source_target_pairs={{0,2},{1,3},{2,0},{3,1},{4,6},{5,7},{6,4},{7,5},{8,10},{9,11},{10,... | collective-permute-start | bytes 589832 | tf_op jit(solution)/shard_map/ppermute | solution.py:40
  144.6 60.2 %all-to-all-start.1 = ((bf16[32,144,384]{2,1,0:T(8,128)(2,1)}), bf16[32,144,384]{2,1,0:T(8,128)(2,1)S(1)}, u32[]{:S(2)}, u32[]{:S(2)}) async-start(bf16[32,144,384]{2,1,0:T(8,128)(2,1)} %pad_maximum_fusion), calls=%async_computation.1 | async-start | bytes 7077888 | tf_op jit(solution)/shard_map/all_to_all | solution.py:65
  151.6 45.4 %collective-permute-start.17 = (bf16[168,384]{1,0:T(8,128)(2,1)}, bf16[168,384]{1,0:T(8,128)(2,1)S(1)}, u32[]{:S(2)}, u32[]{:S(2)}) collective-permute-start(bf16[168,384]{1,0:T(8,128)(2,1)} %reduce_sum.62), channel_id=1, source_target_pairs={{0,0},{1,2},{2,1},{3,3},{4,4},{5,6},{6,5},{7,7},{8,8},{9,10},{10,9... | collective-permute-start | bytes 387080 | tf_op jit(solution)/shard_map/ppermute | solution.py:40
  158.0 39.0 %collective-permute-start.18 = (bf16[168,384]{1,0:T(8,128)(2,1)}, bf16[168,384]{1,0:T(8,128)(2,1)S(1)}, u32[]{:S(2)}, u32[]{:S(2)}) collective-permute-start(bf16[168,384]{1,0:T(8,128)(2,1)} %reduce_sum.62), channel_id=1, source_target_pairs={{0,2},{1,0},{2,3},{3,1},{4,6},{5,4},{6,7},{7,5},{8,10},{9,8},{10,1... | collective-permute-start | bytes 387080 | tf_op jit(solution)/shard_map/ppermute | solution.py:40
  206.0 7.8 %collective-permute-start.19 = (bf16[144,384]{1,0:T(8,128)(2,1)}, bf16[144,384]{1,0:T(8,128)(2,1)S(1)}, u32[]{:S(2)}, u32[]{:S(2)}) collective-permute-start(bf16[144,384]{1,0:T(8,128)(2,1)} %reduce_sum.65), channel_id=1, source_target_pairs={{0,0},{1,2},{2,1},{3,3},{4,4},{5,6},{6,5},{7,7},{8,8},{9,10},{10,9... | collective-permute-start | bytes 331784 | tf_op jit(solution)/shard_map/ppermute | solution.py:40
  208.9 4.8 %collective-permute-start.20 = (bf16[144,384]{1,0:T(8,128)(2,1)}, bf16[144,384]{1,0:T(8,128)(2,1)S(1)}, u32[]{:S(2)}, u32[]{:S(2)}) collective-permute-start(bf16[144,384]{1,0:T(8,128)(2,1)} %reduce_sum.65), channel_id=1, source_target_pairs={{0,2},{1,0},{2,3},{3,1},{4,6},{5,4},{6,7},{7,5},{8,10},{9,8},{10,1... | collective-permute-start | bytes 331784 | tf_op jit(solution)/shard_map/ppermute | solution.py:40
  (20 other events, 50.1 us)

commit v3 on v2

--- a/solution.py
+++ b/solution.py
@@ -32,8 +32,11 @@
 NEXT_CHIP = [(a * 2 + xh, (a + 1) * 2 + xh) for a in range(1, 63, 2) for xh in range(2)]
 NEXT_CHIP = NEXT_CHIP + [(b, a) for a, b in NEXT_CHIP]
 
-def last_hop(m):
-    return perm_of(lambda xl, z, y, c, xh: (xl, z, y, xh ^ m, c))
+ALONG_X = perm_of(lambda xl, z, y, c, xh: (1 - xl, z, y, c, xh))
+
+
+def last_hop(dx, m):
+    return perm_of(lambda xl, z, y, c, xh: (xl ^ dx, z, y, xh ^ m, c))
 
 
 def send(v, pairs):
@@ -61,13 +64,20 @@
     return jax.nn.gelu(values, approximate=True)
 
 
-def over_chips(blocks):
-    got = lax.all_to_all(blocks, ("xl", "z", "y"), 0, 0, tiled=True)
+def pick(blocks, place):
+    return lax.dynamic_index_in_dim(blocks, place, 0, keepdims=False)
+
+
+def over_plane(blocks):
+    got = lax.all_to_all(blocks, ("z", "y"), 0, 0, tiled=True)
     return jnp.sum(got.astype(F32), axis=0).astype(BF)
 
 
-def over_halves(v):
-    return sum(send(v, last_hop(m)).astype(F32) for m in range(2))
+def last_sum(near, rest):
+    total = sum(send(near, last_hop(0, m)).astype(F32) for m in range(2))
+    more = sum(send(rest, last_hop(1, m)).astype(F32) for m in range(2))
+    count = rest.shape[0]
+    return jnp.concatenate([total[:count] + more, total[count:]], axis=0)
 
 
 def per_device(trunk, conv_weight, head_weight, targets, error_mask, upweight):
@@ -172,26 +182,35 @@
         + [head_rows[..., 384 * k : 384 * k + 384] for k in range(4)],
         axis=1,
     )
+    early = early.reshape(2, 16, 168, 384).transpose(1, 0, 2, 3).reshape(16 * 336, 384)
     before, early = lax.optimization_barrier((before, early))
-    early = over_chips(early)
+    early = lax.psum_scatter(early, ("z", "y"), scatter_dimension=0, tiled=True)
     wide = jnp.concatenate([before, gb2, after], axis=0)
     g2 = g_top + through(stream2, conv_back(wide, conv_weight[2], 256, 256))
     gb1 = g2.astype(BF)
     before, after = edges(gb1, 192, c)
     half1 = conv_grad(1, gb1)
+    half1 = half1.reshape(2, 1152, 384)
+    got1 = send(pick(half1, 1 - xl), ALONG_X)
     before, half1 = lax.optimization_barrier((before, half1))
     wide = jnp.concatenate([before, gb1, after], axis=0)
     g_in = jnp.concatenate([before[128:].astype(F32), g2, after[:64].astype(F32)], axis=0)
     g1 = g_in + through(wide1[64:448], conv_back(wide, conv_weight[1], 128, 384))
     gb0 = inside(g1.astype(BF), 64)
     half0 = conv_grad(0, gb0[64:320])
-    late = jnp.concatenate([half0.reshape(32, 72, 384), half1.reshape(32, 72, 384)], axis=1)
-    gb0, late, early = lax.optimization_barrier((gb0, late, early))
-    late = over_chips(late)
+    half1 = (pick(half1, xl).astype(F32) + got1.astype(F32)).astype(BF).reshape(16, 72, 384)
+    half0 = half0.reshape(2, 16, 72, 384)
+    late = jnp.concatenate([half0[0], half0[1], half1], axis=1)
+    gb0, late = lax.optimization_barrier((gb0, late))
+    late = over_plane(late)
     g0 = g1[64:320] + through(trunk[0], conv_back(gb0, conv_weight[0], 64, 256))
-    g0 = lax.optimization_barrier(g0)
-    early = over_halves(early)
-    late = over_halves(late)
+    g0, late = lax.optimization_barrier((g0, late))
+    early = early.reshape(2, 168, 384)
+    half0, half1 = late[:144].reshape(2, 72, 384), late[144:]
+    near = jnp.concatenate([pick(early, xl), pick(half0, xl), half1], axis=0)
+    rest = jnp.concatenate([pick(early, 1 - xl), pick(half0, 1 - xl)], axis=0)
+    total = last_sum(near, rest)
+    early, late = total[:168], total[168:]
 
     def own(v):
         half = v.shape[0] // 2

time: 219 us -> 241 us (1.10)
  matrix products: 45.7 us -> 62.3 us
  between operations: 4.75 us -> 18.1 us
  waiting for transfers between devices: 77.9 us -> 86.7 us
  starting transfers between devices: 55.9 us -> 47.2 us
  other arithmetic: 26 us -> 18.9 us
    unnamed x0 -> x2, waiting for transfers between devices: none -> 23.6 us
    all_to_all x2 -> x1, starting transfers between devices: 25.9 us -> 3.74 us  [over_plane(): got = lax.all_to_all(blocks, ('z', 'y'), 0, 0, tiled=True)]
    ppermute x21 -> x22, waiting for transfers between devices: 44 us -> 25.2 us  [send(): return lax.ppermute(v, AXES, pairs)]
    ppermute x21 -> x22, starting transfers between devices: 29.9 us -> 43.4 us  [send(): return lax.ppermute(v, AXES, pairs)]
    dot_general x3, matrix products: 2.44 us -> 7.01 us  [conv(): jnp.dot(rows[2 * d:2 * d + count], weights[2], preferred_element_type=F32)]
    reduce_sum x2 -> x1, other arithmetic: 4.69 us -> 0.4 us  [over_plane(): return jnp.sum(got.astype(F32), axis=0).astype(BF)]
    all_to_all x2 -> x1, waiting for transfers between devices: 33.8 us -> 37.9 us  [over_plane(): got = lax.all_to_all(blocks, ('z', 'y'), 0, 0, tiled=True)]
    unnamed x46 -> x40, local copies, waits for them, and re-layouts: 4.55 us -> 0.87 us
  transfers between devices with their start and end apart: 23 -> 24, of which waited for: 7 -> 10; matrix products, arithmetic and copies ran while one was open for 24% -> 25% of each run, Pallas kernels for 0% -> 0%
where the time goes in v3:
time: 241 us; the launch traced here: 239 us
  waiting for transfers between devices  86.7 us (36%)
  matrix products  62.3 us (26%)
  starting transfers between devices  47.2 us (20%)
  other arithmetic  18.9 us (8%)
  between operations  18.1 us (8%)
  local copies, waits for them, and re-layouts  6.31 us (3%)
    ppermute x22, starting transfers between devices, send(): return lax.ppermute(v, AXES, pairs)  43.4 us
    all_to_all x1, waiting for transfers between devices, over_plane(): got = lax.all_to_all(blocks, ('z', 'y'), 0, 0, tiled=True)  37.9 us
    ppermute x22, waiting for transfers between devices, send(): return lax.ppermute(v, AXES, pairs)  25.2 us
    unnamed x2, waiting for transfers between devices  23.6 us
    dot_general x3, matrix products, conv_back(): jnp.dot(rows[:count], weights[2].T, preferred_element_type=F32)  8.42 us
    dot_general x3, matrix products, conv_back(): total = jnp.dot(rows[d:d + count], weights[1].T, preferred_element_type=F32)  7.48 us
    dot_general x10, matrix products, pair_dot(): jnp.dot(far_a.T, far_b, preferred_element_type=F32)  7.35 us
    dot_general x3, matrix products, conv(): jnp.dot(rows[2 * d:2 * d + count], weights[2], preferred_element_type=F32)  7.01 us
  transfers between devices with their start and end apart: 24, of which 10 were waited for; matrix products, arithmetic and copies ran while one was open for 25% of the time, Pallas kernels for 0%

profile of v3, /device:TPU:1, one launch (start us, length us, event | category | flops | bytes accessed | tf_op | source)
XLA Modules:
  0.0 239.5 jit_solution(1137919056137828653)
XLA Ops:
  8.4 4.6 %collective-permute-start = (bf16[192,768]{1,0:T(8,128)(2,1)S(1)}, bf16[192,768]{1,0:T(8,128)(2,1)S(1)}, u32[]{:S(2)}, u32[]{:S(2)}) collective-permute-start(bf16[192,768]{1,0:T(8,128)(2,1)S(1)} %get-tuple-element.56), channel_id=1, source_target_pairs={{2,4},{3,5},{6,8},{7,9},{10,12},{11,13},{14,16},{15,17},{18,20},{1... | collective-permute-start | bytes 884744 | tf_op jit(solution)/shard_map/ppermute | solution.py:43
  14.4 2.9 %collective-permute-done = bf16[192,768]{1,0:T(8,128)(2,1)S(1)} collective-permute-done((bf16[192,768]{1,0:T(8,128)(2,1)S(1)}, bf16[192,768]{1,0:T(8,128)(2,1)S(1)}, u32[]{:S(2)}, u32[]{:S(2)}) %collective-permute-start) | collective-permute-done | bytes 294944 | tf_op jit(solution)/shard_map/ppermute | solution.py:43
  22.3 2.6 %fusion.20 = (bf16[512,768]{1,0:T(8,128)(2,1)S(1)}, bf16[512,768]{1,0:T(8,128)(2,1)S(1)}) fusion(bf16[3,3,768,768]{3,2,1,0:T(8,128)(2,1)} %param.7, bf16[640,768]{1,0:T(8,128)(2,1)S(1)} %fusion.12, f32[512,768]{1,0:T(8,128)S(1)} %fusion.67, f32[512,768]{1,0:T(8,128)S(1)} %fusion.63, bf16[640,768]{1,0:T(8,128)(2,1)S(1)} %pad_maximum_fusion.4, ...), kind=kOutput, calls=%fused_computation.46 | convolution fusion | flops 610271232 | bytes 7471616 | tf_op jit(solution)/shard_map/dot_general | solution.py:99
  24.9 2.3 fusion.57
  29.1 2.7 %fusion.106 = (bf16[256,768]{1,0:T(8,128)(2,1)}, bf16[256,768]{1,0:T(8,128)(2,1)S(1)}) fusion(f32[256,768]{1,0:T(8,128)S(1)} %convolution_add_fusion.17, bf16[3,3,768,768]{3,2,1,0:T(8,128)(2,1)} %param.7, bf16[512,768]{1,0:T(8,128)(2,1)S(1)} %get-tuple-element.70, bf16[512,768]{1,0:T(8,128)(2,1)S(1)} %get-tuple-element.71), kind=kOutput, calls=%fused_computation.158 | convolution fusion | flops 304742400 | bytes 3538944 | tf_op jit(solution)/shard_map/dot_general | solution.py:99
  31.7 3.7 %collective-permute-start.2 = (bf16[256,768]{1,0:T(8,128)(2,1)}, bf16[256,768]{1,0:T(8,128)(2,1)}, u32[]{:S(2)}, u32[]{:S(2)}) collective-permute-start(bf16[256,768]{1,0:T(8,128)(2,1)} %get-tuple-element.72), channel_id=1, source_target_pairs={{2,4},{3,5},{6,8},{7,9},{10,12},{11,13},{14,16},{15,17},{18,20},{1... | collective-permute-start | bytes 1179656 | tf_op jit(solution)/shard_map/ppermute | solution.py:43
  38.9 2.4 collective-permute-done.2
  48.2 4.6 %fusion.5 = (f32[]{:T(128)}, bf16[256,2688]{1,0:T(8,128)(2,1)S(1)}) fusion(s32[1,256,2688]{2,1,0:T(8,128)S(1)} %copy-done.13, f32[256]{0:T(256)S(1)} %bitcast.173, bf16[256,768]{1,0:T(8,128)(2,1)S(1)} %fusion.33, bf16[768,2688]{1,0:T(8,128)(2,1)S(1)} %copy-done.12), kind=kOutput, calls=%fused_computation.13 | convolution fusion | flops 1070039040 | bytes 8651780 | tf_op jit(solution)/shard_map/dot_general | solution.py:130
  59.7 2.2 fusion.187
  62.0 3.7 %collective-permute-start.7 = (bf16[256,768]{1,0:T(8,128)(2,1)S(1)}, bf16[256,768]{1,0:T(8,128)(2,1)S(1)}, u32[]{:S(2)}, u32[]{:S(2)}) collective-permute-start(bf16[256,768]{1,0:T(8,128)(2,1)S(1)} %get-tuple-element.74), channel_id=1, source_target_pairs={{2,4},{3,5},{6,8},{7,9},{10,12},{11,13},{14,16},{15,17},{18,20},{1... | collective-permute-start | bytes 1179656 | tf_op jit(solution)/shard_map/ppermute | solution.py:43
  72.7 2.7 %convolution_add_fusion.13 = f32[256,768]{1,0:T(8,128)} fusion(f32[256,768]{1,0:T(8,128)S(1)} %fusion.46, bf16[3,3,768,768]{3,2,1,0:T(8,128)(2,1)} %param.7, bf16[256,768]{1,0:T(8,128)(2,1)S(1)} %collective-permute-done.8, bf16[256,768]{1,0:T(8,128)(2,1)S(1)} %collective-permute-done.7, pred[]{:T(512)S(6)} %eq.19), kind=kOutput, calls=%fused_computation.75 | convolution fusion | flops 302383104 | bytes 3538945 | tf_op jit(solution)/shard_map/dot_general | solution.py:105
  77.2 2.3 copy.21
  79.6 3.3 %fusion.188 = (bf16[256,768]{1,0:T(8,128)(2,1)S(1)}, f32[256,768]{1,0:T(8,128)}) fusion(f32[256,768]{1,0:T(8,128)} %get-tuple-element.75, bf16[256,768]{1,0:T(8,128)(2,1)S(1)} %copy-done.11, f32[256,768]{1,0:T(8,128)S(1)} %copy-done.9, bf16[256,768]{1,0:T(8,128)(2,1)S(1)} %broadcast_select_fusion.1, bf16[3,3,768,768]{3,2,1,0:T(8,128)(2,1)} %param.7), kind=kOutput, calls=%fused_computation.290 | convolution fusion | flops 306511872 | bytes 4718592 | tf_op jit(solution)/shard_map/dot_general | solution.py:108
  86.3 4.6 %collective-permute-start.13 = (bf16[192,768]{1,0:T(8,128)(2,1)}, bf16[192,768]{1,0:T(8,128)(2,1)}, u32[]{:S(2)}, u32[]{:S(2)}) collective-permute-start(bf16[192,768]{1,0:T(8,128)(2,1)} %get-tuple-element.52), channel_id=1, source_target_pairs={{2,4},{3,5},{6,8},{7,9},{10,12},{11,13},{14,16},{15,17},{18,20},{1... | collective-permute-start | bytes 884744 | tf_op jit(solution)/shard_map/ppermute | solution.py:43
  97.5 15.9 %collective-permute-start.17 = (bf16[1152,384]{1,0:T(8,128)(2,1)S(1)}, bf16[1152,384]{1,0:T(8,128)(2,1)S(1)}, u32[]{:S(2)}, u32[]{:S(2)}) collective-permute-start(bf16[1152,384]{1,0:T(8,128)(2,1)S(1)} %dynamic-slice_bitcast_fusion), channel_id=1, source_target_pairs={{0,64},{1,65},{2,66},{3,67},{4,68},{5,69},{6,70},{7,71},{8,72},{9,... | collective-permute-start | bytes 2654216 | tf_op jit(solution)/shard_map/ppermute | solution.py:43
  118.6 3.7 %convert_select_fusion = (bf16[384,768]{1,0:T(8,128)(2,1)S(1)}, f32[384,768]{1,0:T(8,128)}) fusion(pred[384]{0:T(512)(128)(4,1)S(1)} %fusion.174, bf16[512,768]{1,0:T(8,128)(2,1)S(1)} %copy-done.15, f32[384,768]{1,0:T(8,128)S(1)} %fusion.50, f32[384,768]{1,0:T(8,128)S(1)} %fusion.53, bf16[3,3,768,768]{3,2,1,0:T(8,128)(2,1)} %param.7, ...), kind=kOutput, calls=%fused_computation.178 | convolution fusion | flops 462716928 | bytes 8061312 | tf_op jit(solution)/shard_map/dot_general | solution.py:104
  126.0 7.2 %collective-permute-done.17 = bf16[1152,384]{1,0:T(8,128)(2,1)S(1)} collective-permute-done((bf16[1152,384]{1,0:T(8,128)(2,1)S(1)}, bf16[1152,384]{1,0:T(8,128)(2,1)S(1)}, u32[]{:S(2)}, u32[]{:S(2)}) %collective-permute-start.17) | collective-permute-done | bytes 884768 | tf_op jit(solution)/shard_map/ppermute | solution.py:43
  135.3 3.7 %all-to-all-start = ((bf16[16,216,384]{2,1,0:T(8,128)(2,1)}), bf16[16,216,384]{2,1,0:T(8,128)(2,1)S(1)}, u32[]{:S(2)}, u32[]{:S(2)}) async-start(bf16[16,216,384]{2,1,0:T(8,128)(2,1)} %pad_maximum_fusion), calls=%async_computation | async-start | bytes 5308416 | tf_op jit(solution)/shard_map/all_to_all | solution.py:72
  143.0 3.1 %fusion.96 = f32[256,768]{1,0:T(8,128)} fusion(f32[384,768]{1,0:T(8,128)S(1)} %copy-done.17, f32[256,768]{1,0:T(8,128)S(1)} %convolution_add_fusion.11, bf16[3,3,768,768]{3,2,1,0:T(8,128)(2,1)} %param.7, bf16[384,768]{1,0:T(8,128)(2,1)S(1)} %copy-done.7, bf16[1,256,768]{2,1,0:T(8,128)(2,1)S(1)} %copy-done), kind=kOutput, calls=%fused_computation.148 | convolution fusion | flops 306315264 | bytes 4325376 | tf_op jit(solution)/shard_map/dot_general | solution.py:108
  146.0 37.9 %all-to-all-done = bf16[16,216,384]{2,1,0:T(8,128)(2,1)S(1)} async-done(((bf16[16,216,384]{2,1,0:T(8,128)(2,1)}), bf16[16,216,384]{2,1,0:T(8,128)(2,1)S(1)}, u32[]{:S(2)}, u32[]{:S(2)}) %all-to-all-start) | async-done | bytes 2654240 | tf_op jit(solution)/shard_map/all_to_all | solution.py:72
  184.4 23.6 %reduce-scatter.4.cloned.1.call-done = bf16[336,384]{1,0:T(8,128)(2,1)} async-done(((bf16[5376,384]{1,0:T(8,128)(2,1)}), bf16[336,384]{1,0:T(8,128)(2,1)}) %reduce-scatter.4.cloned.1.call-update) | async-done | bytes 258064
  209.0 6.6 %collective-permute-start.18 = (bf16[312,384]{1,0:T(8,128)(2,1)S(1)}, bf16[312,384]{1,0:T(8,128)(2,1)S(1)}, u32[]{:S(2)}, u32[]{:S(2)}) collective-permute-start(bf16[312,384]{1,0:T(8,128)(2,1)S(1)} %pad_maximum_fusion.15), channel_id=1, source_target_pairs={{0,0},{1,2},{2,1},{3,3},{4,4},{5,6},{6,5},{7,7},{8,8},{9,10},{10,9... | collective-permute-start | bytes 718856 | tf_op jit(solution)/shard_map/ppermute | solution.py:43
  216.3 4.8 %collective-permute-done.18 = bf16[312,384]{1,0:T(8,128)(2,1)S(1)} collective-permute-done((bf16[312,384]{1,0:T(8,128)(2,1)S(1)}, bf16[312,384]{1,0:T(8,128)(2,1)S(1)}, u32[]{:S(2)}, u32[]{:S(2)}) %collective-permute-start.18) | collective-permute-done | bytes 239648 | tf_op jit(solution)/shard_map/ppermute | solution.py:43
  221.0 3.9 %collective-permute-done.19 = bf16[312,384]{1,0:T(8,128)(2,1)S(1)} collective-permute-done((bf16[312,384]{1,0:T(8,128)(2,1)S(1)}, bf16[312,384]{1,0:T(8,128)(2,1)S(1)}, u32[]{:S(2)}, u32[]{:S(2)}) %collective-permute-start.19) | collective-permute-done | bytes 239648 | tf_op jit(solution)/shard_map/ppermute | solution.py:43
  (158 shorter events, 66.3 us)
Async XLA Ops:
  7.2 200.8 %reduce-scatter.4.cloned.1.call-start = ((), (), s32[]{:S(2)}) async-start(), calls=%async_computation.2 | async-start | bytes 4386816
  8.4 9.0 %collective-permute-start = (bf16[192,768]{1,0:T(8,128)(2,1)S(1)}, bf16[192,768]{1,0:T(8,128)(2,1)S(1)}, u32[]{:S(2)}, u32[]{:S(2)}) collective-permute-start(bf16[192,768]{1,0:T(8,128)(2,1)S(1)} %get-tuple-element.56), channel_id=1, source_target_pairs={{2,4},{3,5},{6,8},{7,9},{10,12},{11,13},{14,16},{15,17},{18,20},{1... | collective-permute-start | bytes 884744 | tf_op jit(solution)/shard_map/ppermute | solution.py:43
  13.0 4.4 %collective-permute-start.1 = (bf16[192,768]{1,0:T(8,128)(2,1)S(1)}, bf16[192,768]{1,0:T(8,128)(2,1)S(1)}, u32[]{:S(2)}, u32[]{:S(2)}) collective-permute-start(bf16[192,768]{1,0:T(8,128)(2,1)S(1)} %get-tuple-element.57), channel_id=1, source_target_pairs={{0,2},{1,3},{2,0},{3,1},{4,6},{5,7},{6,4},{7,5},{8,10},{9,11},{10,... | collective-permute-start | bytes 884744 | tf_op jit(solution)/shard_map/ppermute | solution.py:43
  27.2 15.2 %collective-permute-start.5 = (bf16[512,768]{1,0:T(8,128)(2,1)S(1)}, bf16[512,768]{1,0:T(8,128)(2,1)}, u32[]{:S(2)}, u32[]{:S(2)}) collective-permute-start(bf16[512,768]{1,0:T(8,128)(2,1)S(1)} %get-tuple-element.70), channel_id=1, source_target_pairs={{0,2},{1,3},{2,0},{3,1},{4,6},{5,7},{6,4},{7,5},{8,10},{9,11},{10,... | collective-permute-start | bytes 2359304 | tf_op jit(solution)/shard_map/ppermute | solution.py:43
  31.7 9.5 %collective-permute-start.2 = (bf16[256,768]{1,0:T(8,128)(2,1)}, bf16[256,768]{1,0:T(8,128)(2,1)}, u32[]{:S(2)}, u32[]{:S(2)}) collective-permute-start(bf16[256,768]{1,0:T(8,128)(2,1)} %get-tuple-element.72), channel_id=1, source_target_pairs={{2,4},{3,5},{6,8},{7,9},{10,12},{11,13},{14,16},{15,17},{18,20},{1... | collective-permute-start | bytes 1179656 | tf_op jit(solution)/shard_map/ppermute | solution.py:43
  35.5 5.8 %collective-permute-start.3 = (bf16[256,768]{1,0:T(8,128)(2,1)}, bf16[256,768]{1,0:T(8,128)(2,1)}, u32[]{:S(2)}, u32[]{:S(2)}) collective-permute-start(bf16[256,768]{1,0:T(8,128)(2,1)} %get-tuple-element.72), channel_id=1, source_target_pairs={{0,2},{1,3},{2,0},{3,1},{4,6},{5,7},{6,4},{7,5},{8,10},{9,11},{10,... | collective-permute-start | bytes 1179656 | tf_op jit(solution)/shard_map/ppermute | solution.py:43
  36.4 6.0 %collective-permute-start.4 = (bf16[384,768]{1,0:T(8,128)(2,1)}, bf16[384,768]{1,0:T(8,128)(2,1)S(1)}, u32[]{:S(2)}, u32[]{:S(2)}) collective-permute-start(bf16[384,768]{1,0:T(8,128)(2,1)} %slice.435), channel_id=1, source_target_pairs={{0,2},{1,3},{2,0},{3,1},{4,6},{5,7},{6,4},{7,5},{8,10},{9,11},{10,... | collective-permute-start | bytes 1769480 | tf_op jit(solution)/shard_map/ppermute | solution.py:43
  43.8 15.0 %collective-permute-start.6 = (bf16[768,768]{1,0:T(8,128)(2,1)S(1)}, bf16[768,768]{1,0:T(8,128)(2,1)S(1)}, u32[]{:S(2)}, u32[]{:S(2)}) collective-permute-start(bf16[768,768]{1,0:T(8,128)(2,1)S(1)} %pad_maximum_fusion.3), channel_id=1, source_target_pairs={{0,2},{1,3},{2,0},{3,1},{4,6},{5,7},{6,4},{7,5},{8,10},{9,11},{10,... | collective-permute-start | bytes 3538952 | tf_op jit(solution)/shard_map/ppermute | solution.py:43
  47.6 27.9 %collective-permute-start.11 = (bf16[256,768]{1,0:T(8,128)(2,1)S(1)}, bf16[256,768]{1,0:T(8,128)(2,1)S(1)}, u32[]{:S(2)}, u32[]{:S(2)}) collective-permute-start(bf16[256,768]{1,0:T(8,128)(2,1)S(1)} %fusion.33), channel_id=1, source_target_pairs={{0,2},{1,3},{2,0},{3,1},{4,6},{5,7},{6,4},{7,5},{8,10},{9,11},{10,... | collective-permute-start | bytes 1179656 | tf_op jit(solution)/shard_map/ppermute | solution.py:43
  54.2 1.3 collective-permute-start.10
  62.0 10.7 %collective-permute-start.7 = (bf16[256,768]{1,0:T(8,128)(2,1)S(1)}, bf16[256,768]{1,0:T(8,128)(2,1)S(1)}, u32[]{:S(2)}, u32[]{:S(2)}) collective-permute-start(bf16[256,768]{1,0:T(8,128)(2,1)S(1)} %get-tuple-element.74), channel_id=1, source_target_pairs={{2,4},{3,5},{6,8},{7,9},{10,12},{11,13},{14,16},{15,17},{18,20},{1... | collective-permute-start | bytes 1179656 | tf_op jit(solution)/shard_map/ppermute | solution.py:43
  65.7 6.9 %collective-permute-start.8 = (bf16[256,768]{1,0:T(8,128)(2,1)S(1)}, bf16[256,768]{1,0:T(8,128)(2,1)S(1)}, u32[]{:S(2)}, u32[]{:S(2)}) collective-permute-start(bf16[256,768]{1,0:T(8,128)(2,1)S(1)} %get-tuple-element.74), channel_id=1, source_target_pairs={{0,2},{1,3},{2,0},{3,1},{4,6},{5,7},{6,4},{7,5},{8,10},{9,11},{10,... | collective-permute-start | bytes 1179656 | tf_op jit(solution)/shard_map/ppermute | solution.py:43
  67.6 7.9 %collective-permute-start.12 = (bf16[256,1408]{1,0:T(8,128)(2,1)S(1)}, bf16[256,1408]{1,0:T(8,128)(2,1)S(1)}, u32[]{:S(2)}, u32[]{:S(2)}) collective-permute-start(bf16[256,1408]{1,0:T(8,128)(2,1)S(1)} %broadcast_select_fusion), channel_id=1, source_target_pairs={{0,2},{1,3},{2,0},{3,1},{4,6},{5,7},{6,4},{7,5},{8,10},{9,11},{10,... | collective-permute-start | bytes 2162696 | tf_op jit(solution)/shard_map/ppermute | solution.py:43
  68.2 2.1 collective-permute-start.9
  86.3 27.1 %collective-permute-start.13 = (bf16[192,768]{1,0:T(8,128)(2,1)}, bf16[192,768]{1,0:T(8,128)(2,1)}, u32[]{:S(2)}, u32[]{:S(2)}) collective-permute-start(bf16[192,768]{1,0:T(8,128)(2,1)} %get-tuple-element.52), channel_id=1, source_target_pairs={{2,4},{3,5},{6,8},{7,9},{10,12},{11,13},{14,16},{15,17},{18,20},{1... | collective-permute-start | bytes 884744 | tf_op jit(solution)/shard_map/ppermute | solution.py:43
  90.9 22.5 %collective-permute-start.14 = (bf16[192,768]{1,0:T(8,128)(2,1)}, bf16[192,768]{1,0:T(8,128)(2,1)}, u32[]{:S(2)}, u32[]{:S(2)}) collective-permute-start(bf16[192,768]{1,0:T(8,128)(2,1)} %get-tuple-element.53), channel_id=1, source_target_pairs={{0,2},{1,3},{2,0},{3,1},{4,6},{5,7},{6,4},{7,5},{8,10},{9,11},{10,... | collective-permute-start | bytes 884744 | tf_op jit(solution)/shard_map/ppermute | solution.py:43
  91.0 2.1 collective-permute-start.15
  97.5 35.7 %collective-permute-start.17 = (bf16[1152,384]{1,0:T(8,128)(2,1)S(1)}, bf16[1152,384]{1,0:T(8,128)(2,1)S(1)}, u32[]{:S(2)}, u32[]{:S(2)}) collective-permute-start(bf16[1152,384]{1,0:T(8,128)(2,1)S(1)} %dynamic-slice_bitcast_fusion), channel_id=1, source_target_pairs={{0,64},{1,65},{2,66},{3,67},{4,68},{5,69},{6,70},{7,71},{8,72},{9,... | collective-permute-start | bytes 2654216 | tf_op jit(solution)/shard_map/ppermute | solution.py:43
  122.4 1.9 collective-permute-start.16
  135.3 48.7 %all-to-all-start = ((bf16[16,216,384]{2,1,0:T(8,128)(2,1)}), bf16[16,216,384]{2,1,0:T(8,128)(2,1)S(1)}, u32[]{:S(2)}, u32[]{:S(2)}) async-start(bf16[16,216,384]{2,1,0:T(8,128)(2,1)} %pad_maximum_fusion), calls=%async_computation | async-start | bytes 5308416 | tf_op jit(solution)/shard_map/all_to_all | solution.py:72
  209.0 12.0 %collective-permute-start.18 = (bf16[312,384]{1,0:T(8,128)(2,1)S(1)}, bf16[312,384]{1,0:T(8,128)(2,1)S(1)}, u32[]{:S(2)}, u32[]{:S(2)}) collective-permute-start(bf16[312,384]{1,0:T(8,128)(2,1)S(1)} %pad_maximum_fusion.15), channel_id=1, source_target_pairs={{0,0},{1,2},{2,1},{3,3},{4,4},{5,6},{6,5},{7,7},{8,8},{9,10},{10,9... | collective-permute-start | bytes 718856 | tf_op jit(solution)/shard_map/ppermute | solution.py:43
  215.7 9.3 %collective-permute-start.19 = (bf16[312,384]{1,0:T(8,128)(2,1)S(1)}, bf16[312,384]{1,0:T(8,128)(2,1)S(1)}, u32[]{:S(2)}, u32[]{:S(2)}) collective-permute-start(bf16[312,384]{1,0:T(8,128)(2,1)S(1)} %pad_maximum_fusion.15), channel_id=1, source_target_pairs={{0,2},{1,0},{2,3},{3,1},{4,6},{5,4},{6,7},{7,5},{8,10},{9,8},{10,1... | collective-permute-start | bytes 718856 | tf_op jit(solution)/shard_map/ppermute | solution.py:43
  215.8 9.2 %collective-permute-start.20 = (bf16[240,384]{1,0:T(8,128)(2,1)S(1)}, bf16[240,384]{1,0:T(8,128)(2,1)S(1)}, u32[]{:S(2)}, u32[]{:S(2)}) collective-permute-start(bf16[240,384]{1,0:T(8,128)(2,1)S(1)} %pad_maximum_fusion.16), channel_id=1, source_target_pairs={{0,64},{1,66},{2,65},{3,67},{4,68},{5,70},{6,69},{7,71},{8,72},{9,... | collective-permute-start | bytes 552968 | tf_op jit(solution)/shard_map/ppermute | solution.py:43
  215.9 10.5 %collective-permute-start.21 = (bf16[240,384]{1,0:T(8,128)(2,1)S(1)}, bf16[240,384]{1,0:T(8,128)(2,1)S(1)}, u32[]{:S(2)}, u32[]{:S(2)}) collective-permute-start(bf16[240,384]{1,0:T(8,128)(2,1)S(1)} %pad_maximum_fusion.16), channel_id=1, source_target_pairs={{0,66},{1,64},{2,67},{3,65},{4,70},{5,68},{6,71},{7,69},{8,74},{9,... | collective-permute-start | bytes 552968 | tf_op jit(solution)/shard_map/ppermute | solution.py:43
  (18 other events, 101.7 us)
Sparse Core Ops, SparseCore 0:
  91.6 116.3 reduce-scatter.3

commit v4 on v1

--- a/solution.py
+++ b/solution.py
@@ -31,7 +31,6 @@
 CORE = perm_of(lambda xl, z, y, c, xh: (xl, z, y, 1 - c, xh))
 NEXT_CHIP = [(a * 2 + xh, (a + 1) * 2 + xh) for a in range(1, 63, 2) for xh in range(2)]
 NEXT_CHIP = NEXT_CHIP + [(b, a) for a, b in NEXT_CHIP]
-ALONG_X = perm_of(lambda xl, z, y, c, xh: (1 - xl, z, y, c, xh))
 ALONG_Y = [perm_of(lambda xl, z, y, c, xh, k=k: (xl, z, y ^ k, c, xh)) for k in range(4)]
 ALONG_Z = [perm_of(lambda xl, z, y, c, xh, k=k: (xl, z ^ k, y, c, xh)) for k in range(4)]
 
@@ -83,10 +82,6 @@
     return total.astype(BF).reshape(rows // 2, lanes)
 
 
-def halve(part, bit, route, outer=1):
-    return take(part, give(part, bit, route, outer), bit)
-
-
 def plane_sum(blocks):
     got = lax.all_to_all(blocks, ("z", "y"), 0, 0, tiled=True)
     return jnp.sum(got.astype(F32), axis=0).astype(BF)
@@ -94,9 +89,7 @@
 
 def last_sum(near, rest):
     total = sum(send(near, last_hop(0, m)).astype(F32) for m in range(2))
-    more = sum(send(rest, last_hop(1, m)).astype(F32) for m in range(2))
-    count = rest.shape[0]
-    return total[:count] + more, total[count:]
+    return total + sum(send(rest, last_hop(1, m)).astype(F32) for m in range(2))
 
 
 def per_device(trunk, conv_weight, head_weight, targets, error_mask, upweight):
@@ -171,13 +164,17 @@
             far_a.T, far_b, preferred_element_type=F32
         )
 
+    g_top = jnp.dot(logit_grad, head_weight.T, preferred_element_type=F32)
+    gb2 = g_top.astype(BF)
+    gb2, logit_grad, partial_loss, far_stream = lax.optimization_barrier(
+        (gb2, logit_grad, partial_loss, send(stream, CORE))
+    )
     near, far = halves(logit_grad, 1408)
     scal = jnp.stack([weight_part, partial_loss])
     scal = scal + send(scal, CORE)
-    head_half = pair_dot(stream, near, send(stream, CORE), send(far, CORE))
+    head_half = pair_dot(stream, near, far_stream, send(far, CORE))
     head_half = with_scalars(head_half, (scal[0], scal[1])).astype(BF)
-    head_got = give(head_half, xl, ALONG_X)
-    g_top = jnp.dot(logit_grad, head_weight.T, preferred_element_type=F32)
+    head_got = give(head_half, z // 2, ALONG_Z[3], 2)
 
     def conv_grad(layer, grad_bf):
         d = BASE_DILATION * 2**layer
@@ -193,7 +190,6 @@
             axis=0,
         )
 
-    gb2 = g_top.astype(BF)
     before, after = edges(gb2, 256, c)
     half2 = conv_grad(2, gb2)
     got2 = give(half2, z // 2, ALONG_Z[3], 2)
@@ -203,41 +199,38 @@
     gb1 = g2.astype(BF)
     before, after = edges(gb1, 192, c)
     half1 = conv_grad(1, gb1)
-    head_x = take(head_half, head_got, xl)
-    part2_z = take(half2, got2, z // 2)
-    half1, head_x, part2_z = lax.optimization_barrier((half1, head_x, part2_z))
-    got1 = give(half1, xl, ALONG_X)
-    head_got = give(head_x, z // 2, ALONG_Z[3])
-    got2 = give(part2_z, z % 2, ALONG_Z[1], 2)
-    before, half1, head_x, part2_z = lax.optimization_barrier((before, half1, head_x, part2_z))
+    got1 = give(half1, z // 2, ALONG_Z[3], 2)
+    before, half1 = lax.optimization_barrier((before, half1))
     wide = jnp.concatenate([before, gb1, after], axis=0)
     g_in = jnp.concatenate([before[128:].astype(F32), g2, after[:64].astype(F32)], axis=0)
     g1 = g_in + through(wide1[64:448], conv_back(wide, conv_weight[1], 128, 384))
     gb0 = inside(g1.astype(BF), 64)
-    head_z = take(head_x, head_got, z // 2)
-    part2_zz = take(part2_z, got2, z % 2)
-    head_got = give(head_z, z % 2, ALONG_Z[1])
-    got2 = give(part2_zz, xl, ALONG_X)
-    gb0, head_z, part2_zz = lax.optimization_barrier((gb0, head_z, part2_zz))
+    head_z = take(head_half, head_got, z // 2)
+    part2_z = take(half2, got2, z // 2)
+    head_got = give(head_z, z % 2, ALONG_Z[1], 2)
+    got2 = give(part2_z, z % 2, ALONG_Z[1], 2)
+    gb0, head_z, part2_z = lax.optimization_barrier((gb0, head_z, part2_z))
     half0 = conv_grad(0, gb0[64:320])
-    plane0 = plane_sum(half0.reshape(2, 16, 72, 384).transpose(1, 0, 2, 3))
+    half0 = half0.reshape(2, 16, 72, 384).transpose(1, 0, 2, 3)
+    half0, half1, part2_z, head_z = lax.optimization_barrier((half0, half1, part2_z, head_z))
+    plane0 = plane_sum(half0)
+    part1_z = take(half1, got1, z // 2)
     head_zz = take(head_z, head_got, z % 2)
-    part2 = take(part2_zz, got2, xl)
-    part1_x = take(half1, got1, xl)
-    part1_z = halve(part1_x, z // 2, ALONG_Z[3])
-    part1 = halve(part1_z, z % 2, ALONG_Z[1])
+    part2 = take(part2_z, got2, z % 2)
+    part1 = take(part1_z, give(part1_z, z % 2, ALONG_Z[1], 2), z % 2)
     g0 = g1[64:320] + through(trunk[0], conv_back(gb0, conv_weight[0], 64, 256))
     g0 = lax.optimization_barrier(g0)
-    head_rows = jnp.pad(head_zz, ((0, 0), (0, 128))).reshape(4, 24, 1536)
+    head_rows = jnp.pad(head_zz, ((0, 0), (0, 128))).reshape(2, 4, 24, 1536)
     early = jnp.concatenate(
-        [part1.reshape(4, 72, 384), part2.reshape(4, 72, 384)]
+        [part1.reshape(2, 4, 72, 384), part2.reshape(2, 4, 72, 384)]
         + [head_rows[..., 384 * k : 384 * k + 384] for k in range(4)],
-        axis=1,
-    ).reshape(960, 384)
-    early = halve(early, y // 2, ALONG_Y[3])
-    early = halve(early, y % 2, ALONG_Y[1])
-    near = jnp.concatenate([pick(plane0, xl), early], axis=0)
-    part0, early = last_sum(near, pick(plane0, 1 - xl))
+        axis=2,
+    )
+    got = [send(pick(early, y ^ k, 1), ALONG_Y[k]) for k in (1, 3, 2)]
+    early = sum((g.astype(F32) for g in got), pick(early, y, 1).astype(F32)).astype(BF)
+    both = jnp.concatenate([plane0, early], axis=1)
+    total = last_sum(pick(both, xl), pick(both, 1 - xl))
+    part0, early = total[:72], total[72:]
 
     def own(v):
         half = v.shape[0] // 2

time: 215 us -> 215 us (level)
  starting transfers between devices: 70.2 us -> 60.9 us
  waiting for transfers between devices: 68 us -> 75.5 us
  local copies, waits for them, and re-layouts: 5.17 us -> 7.62 us
    ppermute x32 -> x30, starting transfers between devices: 63.5 us -> 50 us  [send(): return lax.ppermute(v, AXES, pairs)]
    ppermute x32 -> x30, waiting for transfers between devices: 68 us -> 75.5 us  [send(): return lax.ppermute(v, AXES, pairs)]
    all_to_all x1, starting transfers between devices: 6.76 us -> 10.9 us  [plane_sum(): got = lax.all_to_all(blocks, ('z', 'y'), 0, 0, tiled=True)]
    convert_element_type x8 -> x6, other arithmetic: 3.28 us -> 4.41 us  [take(): return total.astype(BF).reshape(rows // 2, lanes)]
  transfers between devices with their start and end apart: 33 -> 31, of which waited for: 14 -> 13; matrix products, arithmetic and copies ran while one was open for 27% -> 26% of each run, Pallas kernels for 0% -> 0%
where the time goes in v4:
time: 215 us; the launch traced here: 214 us
  waiting for transfers between devices  75.5 us (35%)
  starting transfers between devices  60.9 us (28%)
  matrix products  46.5 us (22%)
  other arithmetic  19 us (9%)
  local copies, waits for them, and re-layouts  7.62 us (4%)
  between operations  4.76 us (2%)
    ppermute x30, waiting for transfers between devices, send(): return lax.ppermute(v, AXES, pairs)  75.5 us
    ppermute x30, starting transfers between devices, send(): return lax.ppermute(v, AXES, pairs)  50 us
    all_to_all x1, starting transfers between devices, plane_sum(): got = lax.all_to_all(blocks, ('z', 'y'), 0, 0, tiled=True)  10.9 us
    dot_general x3, matrix products, conv(): jnp.dot(rows[2 * d:2 * d + count], weights[2], preferred_element_type=F32)  7.14 us
    dot_general x3, matrix products, conv(): total = jnp.dot(rows[d:d + count], weights[1], preferred_element_type=F32)  6.12 us
    dot_general x3, matrix products, conv(): jnp.dot(rows[:count], weights[0], preferred_element_type=F32)  5.72 us
    dot_general x3, matrix products, conv_back(): total = jnp.dot(rows[d:d + count], weights[1].T, preferred_element_type=F32)  5.11 us
    dot_general x1, matrix products, per_device(): logits = jnp.dot(stream, head_weight, preferred_element_type=F32)  4.59 us
  transfers between devices with their start and end apart: 31, of which 13 were waited for; matrix products, arithmetic and copies ran while one was open for 26% of the time, Pallas kernels for 0%

profile of v4, /device:TPU:1, one launch (start us, length us, event | category | flops | bytes accessed | tf_op | source)
XLA Modules:
  0.0 214.3 jit_solution(1065488022719065697)
XLA Ops:
  1.8 4.6 %collective-permute-start = (bf16[192,768]{1,0:T(8,128)(2,1)S(1)}, bf16[192,768]{1,0:T(8,128)(2,1)S(1)}, u32[]{:S(2)}, u32[]{:S(2)}) collective-permute-start(bf16[192,768]{1,0:T(8,128)(2,1)S(1)} %get-tuple-element.78), channel_id=1, source_target_pairs={{2,4},{3,5},{6,8},{7,9},{10,12},{11,13},{14,16},{15,17},{18,20},{1... | collective-permute-start | bytes 884744 | tf_op jit(solution)/shard_map/ppermute | solution.py:43
  7.9 2.9 %collective-permute-done = bf16[192,768]{1,0:T(8,128)(2,1)S(1)} collective-permute-done((bf16[192,768]{1,0:T(8,128)(2,1)S(1)}, bf16[192,768]{1,0:T(8,128)(2,1)S(1)}, u32[]{:S(2)}, u32[]{:S(2)}) %collective-permute-start) | collective-permute-done | bytes 294944 | tf_op jit(solution)/shard_map/ppermute | solution.py:43
  15.7 2.6 %fusion.22 = (bf16[512,768]{1,0:T(8,128)(2,1)S(1)}, bf16[512,768]{1,0:T(8,128)(2,1)S(1)}) fusion(bf16[3,3,768,768]{3,2,1,0:T(8,128)(2,1)} %param.7, bf16[640,768]{1,0:T(8,128)(2,1)S(1)} %fusion.13, f32[512,768]{1,0:T(8,128)S(1)} %fusion.71, f32[512,768]{1,0:T(8,128)S(1)} %fusion.67, bf16[640,768]{1,0:T(8,128)(2,1)S(1)} %pad_maximum_fusion.4, ...), kind=kOutput, calls=%fused_computation.51 | convolution fusion | flops 610271232 | bytes 7471616 | tf_op jit(solution)/shard_map/dot_general | solution.py:111
  22.2 2.8 %fusion.113 = (bf16[256,768]{1,0:T(8,128)(2,1)}, bf16[256,768]{1,0:T(8,128)(2,1)}) fusion(f32[256,768]{1,0:T(8,128)S(1)} %convolution_add_fusion.16, bf16[3,3,768,768]{3,2,1,0:T(8,128)(2,1)} %param.7, bf16[512,768]{1,0:T(8,128)(2,1)S(1)} %get-tuple-element.82, bf16[512,768]{1,0:T(8,128)(2,1)S(1)} %get-tuple-element.83), kind=kOutput, calls=%fused_computation.170 | convolution fusion | flops 304742400 | bytes 3538944 | tf_op jit(solution)/shard_map/dot_general | solution.py:111
  25.0 3.7 %collective-permute-start.2 = (bf16[256,768]{1,0:T(8,128)(2,1)}, bf16[256,768]{1,0:T(8,128)(2,1)}, u32[]{:S(2)}, u32[]{:S(2)}) collective-permute-start(bf16[256,768]{1,0:T(8,128)(2,1)} %get-tuple-element.84), channel_id=1, source_target_pairs={{2,4},{3,5},{6,8},{7,9},{10,12},{11,13},{14,16},{15,17},{18,20},{1... | collective-permute-start | bytes 1179656 | tf_op jit(solution)/shard_map/ppermute | solution.py:43
  32.2 2.3 %collective-permute-done.2 = bf16[256,768]{1,0:T(8,128)(2,1)} collective-permute-done((bf16[256,768]{1,0:T(8,128)(2,1)}, bf16[256,768]{1,0:T(8,128)(2,1)}, u32[]{:S(2)}, u32[]{:S(2)}) %collective-permute-start.2) | collective-permute-done | bytes 393248 | tf_op jit(solution)/shard_map/ppermute | solution.py:43
  41.5 4.6 %fusion.5 = (f32[]{:T(128)}, bf16[256,2688]{1,0:T(8,128)(2,1)S(1)}) fusion(s32[1,256,2688]{2,1,0:T(8,128)S(1)} %copy-done.10, f32[256]{0:T(256)S(1)} %bitcast.222, bf16[256,768]{1,0:T(8,128)(2,1)S(1)} %fusion.36, bf16[768,2688]{1,0:T(8,128)(2,1)S(1)} %copy-done.9), kind=kOutput, calls=%fused_computation.13 | convolution fusion | flops 1070039040 | bytes 8651780 | tf_op jit(solution)/shard_map/dot_general | solution.py:142
  48.5 4.2 %collective-permute-start.9 = (bf16[256,768]{1,0:T(8,128)(2,1)S(1)}, bf16[256,768]{1,0:T(8,128)(2,1)S(1)}, u32[]{:S(2)}, u32[]{:S(2)}) collective-permute-start(bf16[256,768]{1,0:T(8,128)(2,1)S(1)} %get-tuple-element.27), channel_id=1, source_target_pairs={{2,4},{3,5},{6,8},{7,9},{10,12},{11,13},{14,16},{15,17},{18,20},{1... | collective-permute-start | bytes 1179656 | tf_op jit(solution)/shard_map/ppermute | solution.py:43
  61.8 8.5 %collective-permute-start.17 = (bf16[2,576,384]{2,1,0:T(8,128)(2,1)S(1)}, bf16[2,576,384]{2,1,0:T(8,128)(2,1)S(1)}, u32[]{:S(2)}, u32[]{:S(2)}) collective-permute-start(bf16[2,576,384]{2,1,0:T(8,128)(2,1)S(1)} %dynamic-slice_bitcast_fusion.2), channel_id=1, source_target_pairs={{0,48},{1,49},{2,50},{3,51},{4,52},{5,53},{6,54},{7,55},{8,56},{9,... | collective-permute-start | bytes 2654216 | tf_op jit(solution)/shard_map/ppermute | solution.py:43
  81.0 2.2 %collective-permute-start.19 = (bf16[2,576,384]{2,1,0:T(8,128)(2,1)S(1)}, bf16[2,576,384]{2,1,0:T(8,128)(2,1)S(1)}, u32[]{:S(2)}, u32[]{:S(2)}) collective-permute-start(bf16[2,576,384]{2,1,0:T(8,128)(2,1)S(1)} %dynamic-slice_bitcast_fusion.1), channel_id=1, source_target_pairs={{0,48},{1,49},{2,50},{3,51},{4,52},{5,53},{6,54},{7,55},{8,56},{9,... | collective-permute-start | bytes 2654216 | tf_op jit(solution)/shard_map/ppermute | solution.py:43
  85.6 2.4 %convert_select_fusion = (bf16[384,768]{1,0:T(8,128)(2,1)S(1)}, f32[384,768]{1,0:T(8,128)}) fusion(pred[384]{0:T(512)(128)(4,1)S(1)} %fusion.185, bf16[512,768]{1,0:T(8,128)(2,1)S(1)} %copy-done.12, f32[384,768]{1,0:T(8,128)S(1)} %fusion.54, f32[384,768]{1,0:T(8,128)S(1)} %fusion.57, bf16[3,3,768,768]{3,2,1,0:T(8,128)(2,1)S(1)} %bitcast.214, ...), kind=kOutput, calls=%fused_computation.196 | convolution fusion | flops 462716928 | bytes 8061440 | tf_op jit(solution)/shard_map/dot_general | solution.py:116
  88.0 2.3 %collective-permute-done.17 = bf16[2,576,384]{2,1,0:T(8,128)(2,1)S(1)} collective-permute-done((bf16[2,576,384]{2,1,0:T(8,128)(2,1)S(1)}, bf16[2,576,384]{2,1,0:T(8,128)(2,1)S(1)}, u32[]{:S(2)}, u32[]{:S(2)}) %collective-permute-start.17) | collective-permute-done | bytes 884768 | tf_op jit(solution)/shard_map/ppermute | solution.py:43
  92.9 20.5 %collective-permute-done.16 = bf16[2,192,1408]{2,1,0:T(8,128)(2,1)S(1)} collective-permute-done((bf16[2,192,1408]{2,1,0:T(8,128)(2,1)S(1)}, bf16[2,192,1408]{2,1,0:T(8,128)(2,1)S(1)}, u32[]{:S(2)}, u32[]{:S(2)}) %collective-permute-start.16) | collective-permute-done | bytes 1081376 | tf_op jit(solution)/shard_map/ppermute | solution.py:43
  121.7 10.7 %collective-permute-done.19 = bf16[2,576,384]{2,1,0:T(8,128)(2,1)S(1)} collective-permute-done((bf16[2,576,384]{2,1,0:T(8,128)(2,1)S(1)}, bf16[2,576,384]{2,1,0:T(8,128)(2,1)S(1)}, u32[]{:S(2)}, u32[]{:S(2)}) %collective-permute-start.19) | collective-permute-done | bytes 884768 | tf_op jit(solution)/shard_map/ppermute | solution.py:43
  135.8 10.9 %all-to-all-start = ((bf16[16,2,72,384]{3,2,1,0:T(8,128)(2,1)}), bf16[16,2,72,384]{3,2,1,0:T(8,128)(2,1)S(1)}, u32[]{:S(2)}, u32[]{:S(2)}) async-start(bf16[16,2,72,384]{3,2,1,0:T(8,128)(2,1)} %bitcast.197), calls=%async_computation | async-start | bytes 3538944 | tf_op jit(solution)/shard_map/all_to_all | solution.py:86
  156.6 2.7 %convolution_add_fusion.11 = f32[256,768]{1,0:T(8,128)} fusion(f32[256,768]{1,0:T(8,128)S(1)} %fusion.69, bf16[3,3,768,768]{3,2,1,0:T(8,128)(2,1)} %param.7, bf16[384,768]{1,0:T(8,128)(2,1)S(1)} %copy-done.7), kind=kOutput, calls=%fused_computation.78 | convolution fusion | flops 302186496 | bytes 3145728 | tf_op jit(solution)/shard_map/dot_general | solution.py:117
  159.3 15.8 %collective-permute-done.23 = bf16[2,240,384]{2,1,0:T(8,128)(2,1)S(1)} collective-permute-done((bf16[2,240,384]{2,1,0:T(8,128)(2,1)S(1)}, bf16[2,240,384]{2,1,0:T(8,128)(2,1)S(1)}, u32[]{:S(2)}, u32[]{:S(2)}) %collective-permute-start.23) | collective-permute-done | bytes 368672 | tf_op jit(solution)/shard_map/ppermute | solution.py:43
  175.1 2.2 %collective-permute-done.24 = bf16[2,240,384]{2,1,0:T(8,128)(2,1)S(1)} collective-permute-done((bf16[2,240,384]{2,1,0:T(8,128)(2,1)S(1)}, bf16[2,240,384]{2,1,0:T(8,128)(2,1)S(1)}, u32[]{:S(2)}, u32[]{:S(2)}) %collective-permute-start.24) | collective-permute-done | bytes 368672 | tf_op jit(solution)/shard_map/ppermute | solution.py:43
  177.3 7.6 %collective-permute-done.25 = bf16[2,240,384]{2,1,0:T(8,128)(2,1)S(1)} collective-permute-done((bf16[2,240,384]{2,1,0:T(8,128)(2,1)S(1)}, bf16[2,240,384]{2,1,0:T(8,128)(2,1)S(1)}, u32[]{:S(2)}, u32[]{:S(2)}) %collective-permute-start.25) | collective-permute-done | bytes 368672 | tf_op jit(solution)/shard_map/ppermute | solution.py:43
  185.5 7.0 %collective-permute-start.26 = (bf16[312,384]{1,0:T(8,128)(2,1)S(1)}, bf16[312,384]{1,0:T(8,128)(2,1)S(1)}, u32[]{:S(2)}, u32[]{:S(2)}) collective-permute-start(bf16[312,384]{1,0:T(8,128)(2,1)S(1)} %get-tuple-element.70), channel_id=1, source_target_pairs={{0,0},{1,2},{2,1},{3,3},{4,4},{5,6},{6,5},{7,7},{8,8},{9,10},{10,9... | collective-permute-start | bytes 718856 | tf_op jit(solution)/shard_map/ppermute | solution.py:43
  192.5 3.8 %collective-permute-start.28 = (bf16[312,384]{1,0:T(8,128)(2,1)S(1)}, bf16[312,384]{1,0:T(8,128)(2,1)S(1)}, u32[]{:S(2)}, u32[]{:S(2)}) collective-permute-start(bf16[312,384]{1,0:T(8,128)(2,1)S(1)} %get-tuple-element.71), channel_id=1, source_target_pairs={{0,64},{1,66},{2,65},{3,67},{4,68},{5,70},{6,69},{7,71},{8,72},{9,... | collective-permute-start | bytes 718856 | tf_op jit(solution)/shard_map/ppermute | solution.py:43
  196.4 2.6 %fusion.103 = f32[256,768]{1,0:T(8,128)S(1)} fusion(f32[384,768]{1,0:T(8,128)} %get-tuple-element.91, f32[256,768]{1,0:T(8,128)} %convolution_add_fusion.11, bf16[3,3,768,768]{3,2,1,0:T(8,128)(2,1)} %param.7, bf16[384,768]{1,0:T(8,128)(2,1)S(1)} %copy-done.7, bf16[1,256,768]{2,1,0:T(8,128)(2,1)S(1)} %copy-done), kind=kOutput, calls=%fused_computation.160 | convolution fusion | flops 306315264 | bytes 4325376 | tf_op jit(solution)/shard_map/dot_general | solution.py:120
  199.0 3.5 %collective-permute-done.28 = bf16[312,384]{1,0:T(8,128)(2,1)S(1)} collective-permute-done((bf16[312,384]{1,0:T(8,128)(2,1)S(1)}, bf16[312,384]{1,0:T(8,128)(2,1)S(1)}, u32[]{:S(2)}, u32[]{:S(2)}) %collective-permute-start.28) | collective-permute-done | bytes 239648 | tf_op jit(solution)/shard_map/ppermute | solution.py:43
  202.5 5.4 %collective-permute-done.29 = bf16[312,384]{1,0:T(8,128)(2,1)S(1)} collective-permute-done((bf16[312,384]{1,0:T(8,128)(2,1)S(1)}, bf16[312,384]{1,0:T(8,128)(2,1)S(1)}, u32[]{:S(2)}, u32[]{:S(2)}) %collective-permute-start.29) | collective-permute-done | bytes 239648 | tf_op jit(solution)/shard_map/ppermute | solution.py:43
  (171 shorter events, 73.6 us)
Async XLA Ops:
  1.8 9.0 %collective-permute-start = (bf16[192,768]{1,0:T(8,128)(2,1)S(1)}, bf16[192,768]{1,0:T(8,128)(2,1)S(1)}, u32[]{:S(2)}, u32[]{:S(2)}) collective-permute-start(bf16[192,768]{1,0:T(8,128)(2,1)S(1)} %get-tuple-element.78), channel_id=1, source_target_pairs={{2,4},{3,5},{6,8},{7,9},{10,12},{11,13},{14,16},{15,17},{18,20},{1... | collective-permute-start | bytes 884744 | tf_op jit(solution)/shard_map/ppermute | solution.py:43
  20.3 15.3 %collective-permute-start.5 = (bf16[512,768]{1,0:T(8,128)(2,1)S(1)}, bf16[512,768]{1,0:T(8,128)(2,1)S(1)}, u32[]{:S(2)}, u32[]{:S(2)}) collective-permute-start(bf16[512,768]{1,0:T(8,128)(2,1)S(1)} %get-tuple-element.82), channel_id=1, source_target_pairs={{0,2},{1,3},{2,0},{3,1},{4,6},{5,7},{6,4},{7,5},{8,10},{9,11},{10,... | collective-permute-start | bytes 2359304 | tf_op jit(solution)/shard_map/ppermute | solution.py:43
  25.0 9.5 %collective-permute-start.2 = (bf16[256,768]{1,0:T(8,128)(2,1)}, bf16[256,768]{1,0:T(8,128)(2,1)}, u32[]{:S(2)}, u32[]{:S(2)}) collective-permute-start(bf16[256,768]{1,0:T(8,128)(2,1)} %get-tuple-element.84), channel_id=1, source_target_pairs={{2,4},{3,5},{6,8},{7,9},{10,12},{11,13},{14,16},{15,17},{18,20},{1... | collective-permute-start | bytes 1179656 | tf_op jit(solution)/shard_map/ppermute | solution.py:43
  37.0 9.0 %collective-permute-start.6 = (bf16[768,768]{1,0:T(8,128)(2,1)S(1)}, bf16[768,768]{1,0:T(8,128)(2,1)S(1)}, u32[]{:S(2)}, u32[]{:S(2)}) collective-permute-start(bf16[768,768]{1,0:T(8,128)(2,1)S(1)} %pad_maximum_fusion.3), channel_id=1, source_target_pairs={{0,2},{1,3},{2,0},{3,1},{4,6},{5,7},{6,4},{7,5},{8,10},{9,11},{10,... | collective-permute-start | bytes 3538952 | tf_op jit(solution)/shard_map/ppermute | solution.py:43
  40.9 6.5 %collective-permute-start.7 = (bf16[256,768]{1,0:T(8,128)(2,1)S(1)}, bf16[256,768]{1,0:T(8,128)(2,1)S(1)}, u32[]{:S(2)}, u32[]{:S(2)}) collective-permute-start(bf16[256,768]{1,0:T(8,128)(2,1)S(1)} %fusion.36), channel_id=1, source_target_pairs={{0,2},{1,3},{2,0},{3,1},{4,6},{5,7},{6,4},{7,5},{8,10},{9,11},{10,... | collective-permute-start | bytes 1179656 | tf_op jit(solution)/shard_map/ppermute | solution.py:43
  48.3 22.0 %collective-permute-start.8 = (bf16[256,768]{1,0:T(8,128)(2,1)S(1)}, bf16[256,768]{1,0:T(8,128)(2,1)S(1)}, u32[]{:S(2)}, u32[]{:S(2)}) collective-permute-start(bf16[256,768]{1,0:T(8,128)(2,1)S(1)} %get-tuple-element.27), channel_id=1, source_target_pairs={{0,2},{1,3},{2,0},{3,1},{4,6},{5,7},{6,4},{7,5},{8,10},{9,11},{10,... | collective-permute-start | bytes 1179656 | tf_op jit(solution)/shard_map/ppermute | solution.py:43
  48.5 21.9 %collective-permute-start.9 = (bf16[256,768]{1,0:T(8,128)(2,1)S(1)}, bf16[256,768]{1,0:T(8,128)(2,1)S(1)}, u32[]{:S(2)}, u32[]{:S(2)}) collective-permute-start(bf16[256,768]{1,0:T(8,128)(2,1)S(1)} %get-tuple-element.27), channel_id=1, source_target_pairs={{2,4},{3,5},{6,8},{7,9},{10,12},{11,13},{14,16},{15,17},{18,20},{1... | collective-permute-start | bytes 1179656 | tf_op jit(solution)/shard_map/ppermute | solution.py:43
  52.6 6.9 %collective-permute-start.12 = (bf16[256,384]{1,0:T(8,128)(2,1)S(1)}, bf16[256,384]{1,0:T(8,128)(2,1)S(1)}, u32[]{:S(2)}, u32[]{:S(2)}) collective-permute-start(bf16[256,384]{1,0:T(8,128)(2,1)S(1)} %get-tuple-element.77), channel_id=1, source_target_pairs={{0,2},{1,3},{2,0},{3,1},{4,6},{5,7},{6,4},{7,5},{8,10},{9,11},{10,... | collective-permute-start | bytes 589832 | tf_op jit(solution)/shard_map/ppermute | solution.py:43
  55.4 15.6 %collective-permute-start.11 = (bf16[256,1408]{1,0:T(8,128)(2,1)S(1)}, bf16[256,1408]{1,0:T(8,128)(2,1)S(1)}, u32[]{:S(2)}, u32[]{:S(2)}) collective-permute-start(bf16[256,1408]{1,0:T(8,128)(2,1)S(1)} %broadcast_select_fusion), channel_id=1, source_target_pairs={{0,2},{1,3},{2,0},{3,1},{4,6},{5,7},{6,4},{7,5},{8,10},{9,11},{10,... | collective-permute-start | bytes 2162696 | tf_op jit(solution)/shard_map/ppermute | solution.py:43
  61.8 28.4 %collective-permute-start.17 = (bf16[2,576,384]{2,1,0:T(8,128)(2,1)S(1)}, bf16[2,576,384]{2,1,0:T(8,128)(2,1)S(1)}, u32[]{:S(2)}, u32[]{:S(2)}) collective-permute-start(bf16[2,576,384]{2,1,0:T(8,128)(2,1)S(1)} %dynamic-slice_bitcast_fusion.2), channel_id=1, source_target_pairs={{0,48},{1,49},{2,50},{3,51},{4,52},{5,53},{6,54},{7,55},{8,56},{9,... | collective-permute-start | bytes 2654216 | tf_op jit(solution)/shard_map/ppermute | solution.py:43
  74.3 39.2 %collective-permute-start.16 = (bf16[2,192,1408]{2,1,0:T(8,128)(2,1)S(1)}, bf16[2,192,1408]{2,1,0:T(8,128)(2,1)S(1)}, u32[]{:S(2)}, u32[]{:S(2)}) collective-permute-start(bf16[2,192,1408]{2,1,0:T(8,128)(2,1)S(1)} %dynamic-slice_bitcast_fusion), channel_id=1, source_target_pairs={{0,48},{1,49},{2,50},{3,51},{4,52},{5,53},{6,54},{7,55},{8,56},{9,... | collective-permute-start | bytes 3244040 | tf_op jit(solution)/shard_map/ppermute | solution.py:43
  75.4 8.3 %collective-permute-start.13 = (bf16[192,768]{1,0:T(8,128)(2,1)S(1)}, bf16[192,768]{1,0:T(8,128)(2,1)S(1)}, u32[]{:S(2)}, u32[]{:S(2)}) collective-permute-start(bf16[192,768]{1,0:T(8,128)(2,1)S(1)} %get-tuple-element.72), channel_id=1, source_target_pairs={{2,4},{3,5},{6,8},{7,9},{10,12},{11,13},{14,16},{15,17},{18,20},{1... | collective-permute-start | bytes 884744 | tf_op jit(solution)/shard_map/ppermute | solution.py:43
  81.0 51.4 %collective-permute-start.19 = (bf16[2,576,384]{2,1,0:T(8,128)(2,1)S(1)}, bf16[2,576,384]{2,1,0:T(8,128)(2,1)S(1)}, u32[]{:S(2)}, u32[]{:S(2)}) collective-permute-start(bf16[2,576,384]{2,1,0:T(8,128)(2,1)S(1)} %dynamic-slice_bitcast_fusion.1), channel_id=1, source_target_pairs={{0,48},{1,49},{2,50},{3,51},{4,52},{5,53},{6,54},{7,55},{8,56},{9,... | collective-permute-start | bytes 2654216 | tf_op jit(solution)/shard_map/ppermute | solution.py:43
  91.4 55.3 %collective-permute-start.21 = (bf16[2,288,384]{2,1,0:T(8,128)(2,1)}, bf16[2,288,384]{2,1,0:T(8,128)(2,1)}, u32[]{:S(2)}, u32[]{:S(2)}) collective-permute-start(bf16[2,288,384]{2,1,0:T(8,128)(2,1)} %dynamic-slice_bitcast_fusion.4), channel_id=1, source_target_pairs={{0,16},{1,17},{2,18},{3,19},{4,20},{5,21},{6,22},{7,23},{8,24},{9,... | collective-permute-start | bytes 1327112 | tf_op jit(solution)/shard_map/ppermute | solution.py:43
  116.5 31.5 %collective-permute-start.22 = (bf16[2,96,1408]{2,1,0:T(8,128)(2,1)}, bf16[2,96,1408]{2,1,0:T(8,128)(2,1)}, u32[]{:S(2)}, u32[]{:S(2)}) collective-permute-start(bf16[2,96,1408]{2,1,0:T(8,128)(2,1)} %dynamic-slice_bitcast_fusion.3), channel_id=1, source_target_pairs={{0,16},{1,17},{2,18},{3,19},{4,20},{5,21},{6,22},{7,23},{8,24},{9,... | collective-permute-start | bytes 1622024 | tf_op jit(solution)/shard_map/ppermute | solution.py:43
  134.5 14.9 %collective-permute-start.20 = (bf16[2,288,384]{2,1,0:T(8,128)(2,1)}, bf16[2,288,384]{2,1,0:T(8,128)(2,1)}, u32[]{:S(2)}, u32[]{:S(2)}) collective-permute-start(bf16[2,288,384]{2,1,0:T(8,128)(2,1)} %dynamic-slice_bitcast_fusion.5), channel_id=1, source_target_pairs={{0,16},{1,17},{2,18},{3,19},{4,20},{5,21},{6,22},{7,23},{8,24},{9,... | collective-permute-start | bytes 1327112 | tf_op jit(solution)/shard_map/ppermute | solution.py:43
  135.8 49.3 %all-to-all-start = ((bf16[16,2,72,384]{3,2,1,0:T(8,128)(2,1)}), bf16[16,2,72,384]{3,2,1,0:T(8,128)(2,1)S(1)}, u32[]{:S(2)}, u32[]{:S(2)}) async-start(bf16[16,2,72,384]{3,2,1,0:T(8,128)(2,1)} %bitcast.197), calls=%async_computation | async-start | bytes 3538944 | tf_op jit(solution)/shard_map/all_to_all | solution.py:86
  150.9 24.1 %collective-permute-start.23 = (bf16[2,240,384]{2,1,0:T(8,128)(2,1)S(1)}, bf16[2,240,384]{2,1,0:T(8,128)(2,1)S(1)}, u32[]{:S(2)}, u32[]{:S(2)}) collective-permute-start(bf16[2,240,384]{2,1,0:T(8,128)(2,1)S(1)} %get-tuple-element.52), channel_id=1, source_target_pairs={{0,4},{1,5},{2,6},{3,7},{4,0},{5,1},{6,2},{7,3},{8,12},{9,13},{10,... | collective-permute-start | bytes 1105928 | tf_op jit(solution)/shard_map/ppermute | solution.py:43
  152.4 24.9 %collective-permute-start.24 = (bf16[2,240,384]{2,1,0:T(8,128)(2,1)S(1)}, bf16[2,240,384]{2,1,0:T(8,128)(2,1)S(1)}, u32[]{:S(2)}, u32[]{:S(2)}) collective-permute-start(bf16[2,240,384]{2,1,0:T(8,128)(2,1)S(1)} %get-tuple-element.54), channel_id=1, source_target_pairs={{0,12},{1,13},{2,14},{3,15},{4,8},{5,9},{6,10},{7,11},{8,4},{9,5},... | collective-permute-start | bytes 1105928 | tf_op jit(solution)/shard_map/ppermute | solution.py:43
  154.2 30.7 %collective-permute-start.25 = (bf16[2,240,384]{2,1,0:T(8,128)(2,1)S(1)}, bf16[2,240,384]{2,1,0:T(8,128)(2,1)S(1)}, u32[]{:S(2)}, u32[]{:S(2)}) collective-permute-start(bf16[2,240,384]{2,1,0:T(8,128)(2,1)S(1)} %get-tuple-element.53), channel_id=1, source_target_pairs={{0,8},{1,9},{2,10},{3,11},{4,12},{5,13},{6,14},{7,15},{8,0},{9,1},... | collective-permute-start | bytes 1105928 | tf_op jit(solution)/shard_map/ppermute | solution.py:43
  185.5 13.5 %collective-permute-start.26 = (bf16[312,384]{1,0:T(8,128)(2,1)S(1)}, bf16[312,384]{1,0:T(8,128)(2,1)S(1)}, u32[]{:S(2)}, u32[]{:S(2)}) collective-permute-start(bf16[312,384]{1,0:T(8,128)(2,1)S(1)} %get-tuple-element.70), channel_id=1, source_target_pairs={{0,0},{1,2},{2,1},{3,3},{4,4},{5,6},{6,5},{7,7},{8,8},{9,10},{10,9... | collective-permute-start | bytes 718856 | tf_op jit(solution)/shard_map/ppermute | solution.py:43
  192.4 6.6 %collective-permute-start.27 = (bf16[312,384]{1,0:T(8,128)(2,1)S(1)}, bf16[312,384]{1,0:T(8,128)(2,1)S(1)}, u32[]{:S(2)}, u32[]{:S(2)}) collective-permute-start(bf16[312,384]{1,0:T(8,128)(2,1)S(1)} %get-tuple-element.70), channel_id=1, source_target_pairs={{0,2},{1,0},{2,3},{3,1},{4,6},{5,4},{6,7},{7,5},{8,10},{9,8},{10,1... | collective-permute-start | bytes 718856 | tf_op jit(solution)/shard_map/ppermute | solution.py:43
  192.5 10.0 %collective-permute-start.28 = (bf16[312,384]{1,0:T(8,128)(2,1)S(1)}, bf16[312,384]{1,0:T(8,128)(2,1)S(1)}, u32[]{:S(2)}, u32[]{:S(2)}) collective-permute-start(bf16[312,384]{1,0:T(8,128)(2,1)S(1)} %get-tuple-element.71), channel_id=1, source_target_pairs={{0,64},{1,66},{2,65},{3,67},{4,68},{5,70},{6,69},{7,71},{8,72},{9,... | collective-permute-start | bytes 718856 | tf_op jit(solution)/shard_map/ppermute | solution.py:43
  196.4 11.6 %collective-permute-start.29 = (bf16[312,384]{1,0:T(8,128)(2,1)S(1)}, bf16[312,384]{1,0:T(8,128)(2,1)S(1)}, u32[]{:S(2)}, u32[]{:S(2)}) collective-permute-start(bf16[312,384]{1,0:T(8,128)(2,1)S(1)} %get-tuple-element.71), channel_id=1, source_target_pairs={{0,66},{1,64},{2,67},{3,65},{4,70},{5,68},{6,71},{7,69},{8,74},{9,... | collective-permute-start | bytes 718856 | tf_op jit(solution)/shard_map/ppermute | solution.py:43
  (23 other events, 160.5 us)

commit v5 on v4

--- a/solution.py
+++ b/solution.py
@@ -31,6 +31,7 @@
 CORE = perm_of(lambda xl, z, y, c, xh: (xl, z, y, 1 - c, xh))
 NEXT_CHIP = [(a * 2 + xh, (a + 1) * 2 + xh) for a in range(1, 63, 2) for xh in range(2)]
 NEXT_CHIP = NEXT_CHIP + [(b, a) for a, b in NEXT_CHIP]
+ALONG_X = perm_of(lambda xl, z, y, c, xh: (1 - xl, z, y, c, xh))
 ALONG_Y = [perm_of(lambda xl, z, y, c, xh, k=k: (xl, z, y ^ k, c, xh)) for k in range(4)]
 ALONG_Z = [perm_of(lambda xl, z, y, c, xh, k=k: (xl, z ^ k, y, c, xh)) for k in range(4)]
 
@@ -89,7 +90,8 @@
 
 def last_sum(near, rest):
     total = sum(send(near, last_hop(0, m)).astype(F32) for m in range(2))
-    return total + sum(send(rest, last_hop(1, m)).astype(F32) for m in range(2))
+    more = sum(send(rest, last_hop(1, m)).astype(F32) for m in range(2))
+    return total[: rest.shape[0]] + more, total[rest.shape[0] :]
 
 
 def per_device(trunk, conv_weight, head_weight, targets, error_mask, upweight):
@@ -174,7 +176,7 @@
     scal = scal + send(scal, CORE)
     head_half = pair_dot(stream, near, far_stream, send(far, CORE))
     head_half = with_scalars(head_half, (scal[0], scal[1])).astype(BF)
-    head_got = give(head_half, z // 2, ALONG_Z[3], 2)
+    head_got = give(head_half, xl, ALONG_X)
 
     def conv_grad(layer, grad_bf):
         d = BASE_DILATION * 2**layer
@@ -199,47 +201,46 @@
     gb1 = g2.astype(BF)
     before, after = edges(gb1, 192, c)
     half1 = conv_grad(1, gb1)
-    got1 = give(half1, z // 2, ALONG_Z[3], 2)
+    half1 = half1.reshape(2, 4, 288, 384)
+    got1 = send(jnp.stack([pick(half1, z ^ 1, 1), pick(half1, z ^ 2, 1)]), ALONG_Z[1])
     before, half1 = lax.optimization_barrier((before, half1))
     wide = jnp.concatenate([before, gb1, after], axis=0)
     g_in = jnp.concatenate([before[128:].astype(F32), g2, after[:64].astype(F32)], axis=0)
     g1 = g_in + through(wide1[64:448], conv_back(wide, conv_weight[1], 128, 384))
     gb0 = inside(g1.astype(BF), 64)
-    head_z = take(head_half, head_got, z // 2)
     part2_z = take(half2, got2, z // 2)
-    head_got = give(head_z, z % 2, ALONG_Z[1], 2)
     got2 = give(part2_z, z % 2, ALONG_Z[1], 2)
-    gb0, head_z, part2_z = lax.optimization_barrier((gb0, head_z, part2_z))
+    gb0, part2_z = lax.optimization_barrier((gb0, part2_z))
     half0 = conv_grad(0, gb0[64:320])
-    half0 = half0.reshape(2, 16, 72, 384).transpose(1, 0, 2, 3)
-    half0, half1, part2_z, head_z = lax.optimization_barrier((half0, half1, part2_z, head_z))
-    plane0 = plane_sum(half0)
-    part1_z = take(half1, got1, z // 2)
-    head_zz = take(head_z, head_got, z % 2)
+    head_x = take(head_half, head_got, xl)
+    head_rows = jnp.pad(head_x, ((0, 0), (0, 128))).reshape(16, 24, 1536)
+    half0 = half0.reshape(2, 16, 72, 384)
+    late = jnp.concatenate(
+        [half0[0], half0[1]] + [head_rows[..., 384 * k : 384 * k + 384] for k in range(4)], axis=1
+    )
+    late, half1, part2_z = lax.optimization_barrier((late, half1, part2_z))
+    late = plane_sum(late)
+    keep1 = jnp.stack([pick(half1, z, 1), pick(half1, z ^ 3, 1)])
+    keep1 = (keep1.astype(F32) + got1.astype(F32)).astype(BF)
+    got1 = send(keep1[1], ALONG_Z[3])
+    part1 = (keep1[0].astype(F32) + got1.astype(F32)).astype(BF)
     part2 = take(part2_z, got2, z % 2)
-    part1 = take(part1_z, give(part1_z, z % 2, ALONG_Z[1], 2), z % 2)
     g0 = g1[64:320] + through(trunk[0], conv_back(gb0, conv_weight[0], 64, 256))
     g0 = lax.optimization_barrier(g0)
-    head_rows = jnp.pad(head_zz, ((0, 0), (0, 128))).reshape(2, 4, 24, 1536)
-    early = jnp.concatenate(
-        [part1.reshape(2, 4, 72, 384), part2.reshape(2, 4, 72, 384)]
-        + [head_rows[..., 384 * k : 384 * k + 384] for k in range(4)],
-        axis=2,
-    )
+    early = jnp.concatenate([part1.reshape(2, 4, 72, 384), part2.reshape(2, 4, 72, 384)], axis=2)
     got = [send(pick(early, y ^ k, 1), ALONG_Y[k]) for k in (1, 3, 2)]
     early = sum((g.astype(F32) for g in got), pick(early, y, 1).astype(F32)).astype(BF)
-    both = jnp.concatenate([plane0, early], axis=1)
-    total = last_sum(pick(both, xl), pick(both, 1 - xl))
-    part0, early = total[:72], total[72:]
+    both = jnp.concatenate([late[:144].reshape(2, 72, 384), early], axis=1)
+    conv_sum, head_sum = last_sum(
+        jnp.concatenate([pick(both, xl), late[144:]], axis=0), pick(both, 1 - xl)
+    )
 
     def own(v):
         half = v.shape[0] // 2
         return jnp.where(c == 0, v[:half], v[half:])
 
-    conv_total = jnp.stack([own(part0), own(early[:72]), own(early[72:144])])
-    head_total = jnp.concatenate(
-        [own(early[144 + 24 * k : 168 + 24 * k]) for k in range(4)], axis=1
-    )
+    conv_total = jnp.stack([own(conv_sum[72 * k : 72 * k + 72]) for k in range(LAYERS)])
+    head_total = jnp.concatenate([own(head_sum[24 * k : 24 * k + 24]) for k in range(4)], axis=1)
     low = head_total[:, :1344]
     high = head_total[:, 64:1408]
     row = head_total[0]

time: 215 us -> 201 us (0.935)
  waiting for transfers between devices: 75.5 us -> 60.8 us
  starting transfers between devices: 60.9 us -> 56.7 us
  local copies, waits for them, and re-layouts: 7.62 us -> 10.1 us
    ppermute x30 -> x29, waiting for transfers between devices: 75.5 us -> 60.8 us  [send(): return lax.ppermute(v, AXES, pairs)]
    all_to_all x1, starting transfers between devices: 10.9 us -> 6.82 us  [plane_sum(): got = lax.all_to_all(blocks, ('z', 'y'), 0, 0, tiled=True)]
    unnamed x37 -> x31, local copies, waits for them, and re-layouts: 1.63 us -> 5.06 us
    convert_element_type x6 -> x2, other arithmetic: 4.41 us -> 1.35 us  [take(): return total.astype(BF).reshape(rows // 2, lanes)]
    ppermute x30 -> x29, starting transfers between devices: 50 us -> 49.9 us  [send(): return lax.ppermute(v, AXES, pairs)]
  transfers between devices with their start and end apart: 31 -> 30, of which waited for: 13 -> 10; matrix products, arithmetic and copies ran while one was open for 26% -> 31% of each run, Pallas kernels for 0% -> 0%
where the time goes in v5:
time: 201 us; the launch traced here: 200 us
  waiting for transfers between devices  60.8 us (30%)
  starting transfers between devices  56.7 us (28%)
  matrix products  46.6 us (23%)
  other arithmetic  20.8 us (10%)
  local copies, waits for them, and re-layouts  10.1 us (5%)
  between operations  4.7 us (2%)
    ppermute x29, waiting for transfers between devices, send(): return lax.ppermute(v, AXES, pairs)  60.8 us
    ppermute x29, starting transfers between devices, send(): return lax.ppermute(v, AXES, pairs)  49.9 us
    dot_general x3, matrix products, conv(): jnp.dot(rows[2 * d:2 * d + count], weights[2], preferred_element_type=F32)  7.14 us
    all_to_all x1, starting transfers between devices, plane_sum(): got = lax.all_to_all(blocks, ('z', 'y'), 0, 0, tiled=True)  6.82 us
    dot_general x3, matrix products, conv(): total = jnp.dot(rows[d:d + count], weights[1], preferred_element_type=F32)  6.12 us
    dot_general x3, matrix products, conv(): jnp.dot(rows[:count], weights[0], preferred_element_type=F32)  5.72 us
    dot_general x3, matrix products, conv_back(): total = jnp.dot(rows[d:d + count], weights[1].T, preferred_element_type=F32)  5.14 us
    unnamed x31, local copies, waits for them, and re-layouts  5.06 us
  transfers between devices with their start and end apart: 30, of which 10 were waited for; matrix products, arithmetic and copies ran while one was open for 31% of the time, Pallas kernels for 0%

profile of v5, /device:TPU:1, one launch (start us, length us, event | category | flops | bytes accessed | tf_op | source)
XLA Modules:
  0.0 199.7 jit_solution(15454862144765730481)
XLA Ops:
  1.8 4.6 %collective-permute-start = (bf16[192,768]{1,0:T(8,128)(2,1)S(1)}, bf16[192,768]{1,0:T(8,128)(2,1)S(1)}, u32[]{:S(2)}, u32[]{:S(2)}) collective-permute-start(bf16[192,768]{1,0:T(8,128)(2,1)S(1)} %get-tuple-element.75), channel_id=1, source_target_pairs={{2,4},{3,5},{6,8},{7,9},{10,12},{11,13},{14,16},{15,17},{18,20},{1... | collective-permute-start | bytes 884744 | tf_op jit(solution)/shard_map/ppermute | solution.py:44
  7.9 2.9 %collective-permute-done = bf16[192,768]{1,0:T(8,128)(2,1)S(1)} collective-permute-done((bf16[192,768]{1,0:T(8,128)(2,1)S(1)}, bf16[192,768]{1,0:T(8,128)(2,1)S(1)}, u32[]{:S(2)}, u32[]{:S(2)}) %collective-permute-start) | collective-permute-done | bytes 294944 | tf_op jit(solution)/shard_map/ppermute | solution.py:44
  11.5 2.1 %fusion.66 = f32[512,768]{1,0:T(8,128)S(1)} fusion(bf16[3,3,768,768]{3,2,1,0:T(8,128)(2,1)} %param.7, bf16[640,768]{1,0:T(8,128)(2,1)S(1)} %fusion.13), kind=kOutput, calls=%fused_computation.124 | convolution fusion | flops 603979776 | bytes 3538944 | tf_op jit(solution)/shard_map/dot_general | solution.py:112
  13.6 2.1 %fusion.70 = f32[512,768]{1,0:T(8,128)S(1)} fusion(bf16[3,3,768,768]{3,2,1,0:T(8,128)(2,1)} %param.7, bf16[640,768]{1,0:T(8,128)(2,1)S(1)} %fusion.13), kind=kOutput, calls=%fused_computation.128 | convolution fusion | flops 603979776 | bytes 3538944 | tf_op jit(solution)/shard_map/dot_general | solution.py:111
  15.7 2.6 %fusion.21 = (bf16[512,768]{1,0:T(8,128)(2,1)S(1)}, bf16[512,768]{1,0:T(8,128)(2,1)S(1)}) fusion(bf16[3,3,768,768]{3,2,1,0:T(8,128)(2,1)} %param.7, bf16[640,768]{1,0:T(8,128)(2,1)S(1)} %fusion.13, f32[512,768]{1,0:T(8,128)S(1)} %fusion.70, f32[512,768]{1,0:T(8,128)S(1)} %fusion.66, bf16[640,768]{1,0:T(8,128)(2,1)S(1)} %pad_maximum_fusion.3, ...), kind=kOutput, calls=%fused_computation.48 | convolution fusion | flops 610271232 | bytes 7471616 | tf_op jit(solution)/shard_map/dot_general | solution.py:113
  22.2 2.8 %fusion.112 = (bf16[256,768]{1,0:T(8,128)(2,1)}, bf16[256,768]{1,0:T(8,128)(2,1)}) fusion(f32[256,768]{1,0:T(8,128)S(1)} %convolution_add_fusion.16, bf16[3,3,768,768]{3,2,1,0:T(8,128)(2,1)} %param.7, bf16[512,768]{1,0:T(8,128)(2,1)S(1)} %get-tuple-element.84, bf16[512,768]{1,0:T(8,128)(2,1)S(1)} %get-tuple-element.85), kind=kOutput, calls=%fused_computation.176 | convolution fusion | flops 304742400 | bytes 3538944 | tf_op jit(solution)/shard_map/dot_general | solution.py:113
  25.0 3.7 %collective-permute-start.2 = (bf16[256,768]{1,0:T(8,128)(2,1)}, bf16[256,768]{1,0:T(8,128)(2,1)}, u32[]{:S(2)}, u32[]{:S(2)}) collective-permute-start(bf16[256,768]{1,0:T(8,128)(2,1)} %get-tuple-element.86), channel_id=1, source_target_pairs={{2,4},{3,5},{6,8},{7,9},{10,12},{11,13},{14,16},{15,17},{18,20},{1... | collective-permute-start | bytes 1179656 | tf_op jit(solution)/shard_map/ppermute | solution.py:44
  32.3 2.3 %collective-permute-done.2 = bf16[256,768]{1,0:T(8,128)(2,1)} collective-permute-done((bf16[256,768]{1,0:T(8,128)(2,1)}, bf16[256,768]{1,0:T(8,128)(2,1)}, u32[]{:S(2)}, u32[]{:S(2)}) %collective-permute-start.2) | collective-permute-done | bytes 393248 | tf_op jit(solution)/shard_map/ppermute | solution.py:44
  41.3 4.6 %fusion.5 = (f32[]{:T(128)}, bf16[256,2688]{1,0:T(8,128)(2,1)S(1)}) fusion(s32[1,256,2688]{2,1,0:T(8,128)S(1)} %copy-done.7, f32[256]{0:T(256)S(1)} %bitcast.214, bf16[256,768]{1,0:T(8,128)(2,1)S(1)} %fusion.35, bf16[768,2688]{1,0:T(8,128)(2,1)S(1)} %copy-done.6), kind=kOutput, calls=%fused_computation.13 | convolution fusion | flops 1070039040 | bytes 8651780 | tf_op jit(solution)/shard_map/dot_general | solution.py:144
  48.4 4.1 %collective-permute-start.9 = (bf16[256,768]{1,0:T(8,128)(2,1)S(1)}, bf16[256,768]{1,0:T(8,128)(2,1)S(1)}, u32[]{:S(2)}, u32[]{:S(2)}) collective-permute-start(bf16[256,768]{1,0:T(8,128)(2,1)S(1)} %get-tuple-element.25), channel_id=1, source_target_pairs={{2,4},{3,5},{6,8},{7,9},{10,12},{11,13},{14,16},{15,17},{18,20},{1... | collective-permute-start | bytes 1179656 | tf_op jit(solution)/shard_map/ppermute | solution.py:44
  61.7 8.5 %collective-permute-start.16 = (bf16[2,576,384]{2,1,0:T(8,128)(2,1)S(1)}, bf16[2,576,384]{2,1,0:T(8,128)(2,1)S(1)}, u32[]{:S(2)}, u32[]{:S(2)}) collective-permute-start(bf16[2,576,384]{2,1,0:T(8,128)(2,1)S(1)} %dynamic-slice_bitcast_fusion.1), channel_id=1, source_target_pairs={{0,48},{1,49},{2,50},{3,51},{4,52},{5,53},{6,54},{7,55},{8,56},{9,... | collective-permute-start | bytes 2654216 | tf_op jit(solution)/shard_map/ppermute | solution.py:44
  74.1 2.2 %collective-permute-start.13 = (bf16[192,768]{1,0:T(8,128)(2,1)S(1)}, bf16[192,768]{1,0:T(8,128)(2,1)S(1)}, u32[]{:S(2)}, u32[]{:S(2)}) collective-permute-start(bf16[192,768]{1,0:T(8,128)(2,1)S(1)} %get-tuple-element.71), channel_id=1, source_target_pairs={{2,4},{3,5},{6,8},{7,9},{10,12},{11,13},{14,16},{15,17},{18,20},{1... | collective-permute-start | bytes 884744 | tf_op jit(solution)/shard_map/ppermute | solution.py:44
  76.9 6.8 %collective-permute-start.18 = (bf16[1,384,1408]{2,1,0:T(8,128)(2,1)S(1)}, bf16[1,384,1408]{2,1,0:T(8,128)(2,1)S(1)}, u32[]{:S(2)}, u32[]{:S(2)}) collective-permute-start(bf16[1,384,1408]{2,1,0:T(8,128)(2,1)S(1)} %dynamic-slice_bitcast_fusion), channel_id=1, source_target_pairs={{0,64},{1,65},{2,66},{3,67},{4,68},{5,69},{6,70},{7,71},{8,72},{9,... | collective-permute-start | bytes 3244040 | tf_op jit(solution)/shard_map/ppermute | solution.py:44
  89.0 2.4 %convert_select_fusion = (bf16[384,768]{1,0:T(8,128)(2,1)S(1)}, f32[384,768]{1,0:T(8,128)}) fusion(pred[384]{0:T(512)(128)(4,1)S(1)} %fusion.192, bf16[512,768]{1,0:T(8,128)(2,1)S(1)} %copy-done.9, f32[384,768]{1,0:T(8,128)S(1)} %fusion.53, f32[384,768]{1,0:T(8,128)S(1)} %fusion.56, bf16[3,3,768,768]{3,2,1,0:T(8,128)(2,1)S(1)} %bitcast.212, ...), kind=kOutput, calls=%fused_computation.196 | convolution fusion | flops 462716928 | bytes 8061440 | tf_op jit(solution)/shard_map/dot_general | solution.py:118
  98.8 9.5 %collective-permute-done.18 = bf16[1,384,1408]{2,1,0:T(8,128)(2,1)S(1)} collective-permute-done((bf16[1,384,1408]{2,1,0:T(8,128)(2,1)S(1)}, bf16[1,384,1408]{2,1,0:T(8,128)(2,1)S(1)}, u32[]{:S(2)}, u32[]{:S(2)}) %collective-permute-start.18) | collective-permute-done | bytes 1081376 | tf_op jit(solution)/shard_map/ppermute | solution.py:44
  111.8 6.8 %all-to-all-start = ((bf16[16,240,384]{2,1,0:T(8,128)(2,1)}), bf16[16,240,384]{2,1,0:T(8,128)(2,1)S(1)}, u32[]{:S(2)}, u32[]{:S(2)}) async-start(bf16[16,240,384]{2,1,0:T(8,128)(2,1)} %slice_dynamic-update-slice_fusion), calls=%async_computation | async-start | bytes 5898240 | tf_op jit(solution)/shard_map/all_to_all | solution.py:87
  127.6 34.0 %collective-permute-done.21 = bf16[2,288,384]{2,1,0:T(8,128)(2,1)S(1)} collective-permute-done((bf16[2,288,384]{2,1,0:T(8,128)(2,1)S(1)}, bf16[2,288,384]{2,1,0:T(8,128)(2,1)S(1)}, u32[]{:S(2)}, u32[]{:S(2)}) %collective-permute-start.21) | collective-permute-done | bytes 442400 | tf_op jit(solution)/shard_map/ppermute | solution.py:44
  161.9 2.3 %collective-permute-start.22 = (bf16[2,144,384]{2,1,0:T(8,128)(2,1)S(1)}, bf16[2,144,384]{2,1,0:T(8,128)(2,1)S(1)}, u32[]{:S(2)}, u32[]{:S(2)}) collective-permute-start(bf16[2,144,384]{2,1,0:T(8,128)(2,1)S(1)} %get-tuple-element.52), channel_id=1, source_target_pairs={{0,4},{1,5},{2,6},{3,7},{4,0},{5,1},{6,2},{7,3},{8,12},{9,13},{10,... | collective-permute-start | bytes 663560 | tf_op jit(solution)/shard_map/ppermute | solution.py:44
  164.2 2.7 %collective-permute-start.23 = (bf16[2,144,384]{2,1,0:T(8,128)(2,1)S(1)}, bf16[2,144,384]{2,1,0:T(8,128)(2,1)S(1)}, u32[]{:S(2)}, u32[]{:S(2)}) collective-permute-start(bf16[2,144,384]{2,1,0:T(8,128)(2,1)S(1)} %get-tuple-element.53), channel_id=1, source_target_pairs={{0,12},{1,13},{2,14},{3,15},{4,8},{5,9},{6,10},{7,11},{8,4},{9,5},... | collective-permute-start | bytes 663560 | tf_op jit(solution)/shard_map/ppermute | solution.py:44
  166.9 2.7 %convolution_add_fusion.11 = f32[256,768]{1,0:T(8,128)} fusion(f32[256,768]{1,0:T(8,128)S(1)} %fusion.68, bf16[3,3,768,768]{3,2,1,0:T(8,128)(2,1)} %param.7, bf16[384,768]{1,0:T(8,128)(2,1)S(1)} %copy-done.4), kind=kOutput, calls=%fused_computation.75 | convolution fusion | flops 302186496 | bytes 3145728 | tf_op jit(solution)/shard_map/dot_general | solution.py:119
  169.6 6.5 %collective-permute-done.23 = bf16[2,144,384]{2,1,0:T(8,128)(2,1)S(1)} collective-permute-done((bf16[2,144,384]{2,1,0:T(8,128)(2,1)S(1)}, bf16[2,144,384]{2,1,0:T(8,128)(2,1)S(1)}, u32[]{:S(2)}, u32[]{:S(2)}) %collective-permute-start.23) | collective-permute-done | bytes 221216 | tf_op jit(solution)/shard_map/ppermute | solution.py:44
  178.4 6.5 %collective-permute-start.25 = (bf16[312,384]{1,0:T(8,128)(2,1)S(1)}, bf16[312,384]{1,0:T(8,128)(2,1)S(1)}, u32[]{:S(2)}, u32[]{:S(2)}) collective-permute-start(bf16[312,384]{1,0:T(8,128)(2,1)S(1)} %pad_maximum_fusion.15), channel_id=1, source_target_pairs={{0,0},{1,2},{2,1},{3,3},{4,4},{5,6},{6,5},{7,7},{8,8},{9,10},{10,9... | collective-permute-start | bytes 718856 | tf_op jit(solution)/shard_map/ppermute | solution.py:44
  185.0 2.7 %fusion.102 = f32[256,768]{1,0:T(8,128)S(1)} fusion(f32[384,768]{1,0:T(8,128)} %get-tuple-element.93, f32[256,768]{1,0:T(8,128)} %convolution_add_fusion.11, bf16[3,3,768,768]{3,2,1,0:T(8,128)(2,1)} %param.7, bf16[384,768]{1,0:T(8,128)(2,1)} %copy-done.3, bf16[1,256,768]{2,1,0:T(8,128)(2,1)S(1)} %copy-done.1), kind=kOutput, calls=%fused_computation.166 | convolution fusion | flops 306315264 | bytes 4325376 | tf_op jit(solution)/shard_map/dot_general | solution.py:122
  193.8 2.7 %collective-permute-done.28 = bf16[216,384]{1,0:T(8,128)(2,1)S(1)} collective-permute-done((bf16[216,384]{1,0:T(8,128)(2,1)S(1)}, bf16[216,384]{1,0:T(8,128)(2,1)S(1)}, u32[]{:S(2)}, u32[]{:S(2)}) %collective-permute-start.28) | collective-permute-done | bytes 165920 | tf_op jit(solution)/shard_map/ppermute | solution.py:44
  (166 shorter events, 67.1 us)
Async XLA Ops:
  1.8 9.0 %collective-permute-start = (bf16[192,768]{1,0:T(8,128)(2,1)S(1)}, bf16[192,768]{1,0:T(8,128)(2,1)S(1)}, u32[]{:S(2)}, u32[]{:S(2)}) collective-permute-start(bf16[192,768]{1,0:T(8,128)(2,1)S(1)} %get-tuple-element.75), channel_id=1, source_target_pairs={{2,4},{3,5},{6,8},{7,9},{10,12},{11,13},{14,16},{15,17},{18,20},{1... | collective-permute-start | bytes 884744 | tf_op jit(solution)/shard_map/ppermute | solution.py:44
  20.4 15.3 %collective-permute-start.5 = (bf16[512,768]{1,0:T(8,128)(2,1)S(1)}, bf16[512,768]{1,0:T(8,128)(2,1)S(1)}, u32[]{:S(2)}, u32[]{:S(2)}) collective-permute-start(bf16[512,768]{1,0:T(8,128)(2,1)S(1)} %get-tuple-element.84), channel_id=1, source_target_pairs={{0,2},{1,3},{2,0},{3,1},{4,6},{5,7},{6,4},{7,5},{8,10},{9,11},{10,... | collective-permute-start | bytes 2359304 | tf_op jit(solution)/shard_map/ppermute | solution.py:44
  25.0 9.5 %collective-permute-start.2 = (bf16[256,768]{1,0:T(8,128)(2,1)}, bf16[256,768]{1,0:T(8,128)(2,1)}, u32[]{:S(2)}, u32[]{:S(2)}) collective-permute-start(bf16[256,768]{1,0:T(8,128)(2,1)} %get-tuple-element.86), channel_id=1, source_target_pairs={{2,4},{3,5},{6,8},{7,9},{10,12},{11,13},{14,16},{15,17},{18,20},{1... | collective-permute-start | bytes 1179656 | tf_op jit(solution)/shard_map/ppermute | solution.py:44
  37.0 9.0 %collective-permute-start.6 = (bf16[768,768]{1,0:T(8,128)(2,1)S(1)}, bf16[768,768]{1,0:T(8,128)(2,1)S(1)}, u32[]{:S(2)}, u32[]{:S(2)}) collective-permute-start(bf16[768,768]{1,0:T(8,128)(2,1)S(1)} %pad_maximum_fusion.2), channel_id=1, source_target_pairs={{0,2},{1,3},{2,0},{3,1},{4,6},{5,7},{6,4},{7,5},{8,10},{9,11},{10,... | collective-permute-start | bytes 3538952 | tf_op jit(solution)/shard_map/ppermute | solution.py:44
  40.8 6.5 %collective-permute-start.7 = (bf16[256,768]{1,0:T(8,128)(2,1)S(1)}, bf16[256,768]{1,0:T(8,128)(2,1)S(1)}, u32[]{:S(2)}, u32[]{:S(2)}) collective-permute-start(bf16[256,768]{1,0:T(8,128)(2,1)S(1)} %fusion.35), channel_id=1, source_target_pairs={{0,2},{1,3},{2,0},{3,1},{4,6},{5,7},{6,4},{7,5},{8,10},{9,11},{10,... | collective-permute-start | bytes 1179656 | tf_op jit(solution)/shard_map/ppermute | solution.py:44
  48.2 22.0 %collective-permute-start.8 = (bf16[256,768]{1,0:T(8,128)(2,1)S(1)}, bf16[256,768]{1,0:T(8,128)(2,1)S(1)}, u32[]{:S(2)}, u32[]{:S(2)}) collective-permute-start(bf16[256,768]{1,0:T(8,128)(2,1)S(1)} %get-tuple-element.25), channel_id=1, source_target_pairs={{0,2},{1,3},{2,0},{3,1},{4,6},{5,7},{6,4},{7,5},{8,10},{9,11},{10,... | collective-permute-start | bytes 1179656 | tf_op jit(solution)/shard_map/ppermute | solution.py:44
  48.4 21.9 %collective-permute-start.9 = (bf16[256,768]{1,0:T(8,128)(2,1)S(1)}, bf16[256,768]{1,0:T(8,128)(2,1)S(1)}, u32[]{:S(2)}, u32[]{:S(2)}) collective-permute-start(bf16[256,768]{1,0:T(8,128)(2,1)S(1)} %get-tuple-element.25), channel_id=1, source_target_pairs={{2,4},{3,5},{6,8},{7,9},{10,12},{11,13},{14,16},{15,17},{18,20},{1... | collective-permute-start | bytes 1179656 | tf_op jit(solution)/shard_map/ppermute | solution.py:44
  52.5 6.9 %collective-permute-start.12 = (bf16[256,384]{1,0:T(8,128)(2,1)S(1)}, bf16[256,384]{1,0:T(8,128)(2,1)S(1)}, u32[]{:S(2)}, u32[]{:S(2)}) collective-permute-start(bf16[256,384]{1,0:T(8,128)(2,1)S(1)} %get-tuple-element.74), channel_id=1, source_target_pairs={{0,2},{1,3},{2,0},{3,1},{4,6},{5,7},{6,4},{7,5},{8,10},{9,11},{10,... | collective-permute-start | bytes 589832 | tf_op jit(solution)/shard_map/ppermute | solution.py:44
  55.3 15.6 %collective-permute-start.11 = (bf16[256,1408]{1,0:T(8,128)(2,1)S(1)}, bf16[256,1408]{1,0:T(8,128)(2,1)S(1)}, u32[]{:S(2)}, u32[]{:S(2)}) collective-permute-start(bf16[256,1408]{1,0:T(8,128)(2,1)S(1)} %broadcast_select_fusion), channel_id=1, source_target_pairs={{0,2},{1,3},{2,0},{3,1},{4,6},{5,7},{6,4},{7,5},{8,10},{9,11},{10,... | collective-permute-start | bytes 2162696 | tf_op jit(solution)/shard_map/ppermute | solution.py:44
  61.7 29.7 %collective-permute-start.16 = (bf16[2,576,384]{2,1,0:T(8,128)(2,1)S(1)}, bf16[2,576,384]{2,1,0:T(8,128)(2,1)S(1)}, u32[]{:S(2)}, u32[]{:S(2)}) collective-permute-start(bf16[2,576,384]{2,1,0:T(8,128)(2,1)S(1)} %dynamic-slice_bitcast_fusion.1), channel_id=1, source_target_pairs={{0,48},{1,49},{2,50},{3,51},{4,52},{5,53},{6,54},{7,55},{8,56},{9,... | collective-permute-start | bytes 2654216 | tf_op jit(solution)/shard_map/ppermute | solution.py:44
  74.1 13.0 %collective-permute-start.13 = (bf16[192,768]{1,0:T(8,128)(2,1)S(1)}, bf16[192,768]{1,0:T(8,128)(2,1)S(1)}, u32[]{:S(2)}, u32[]{:S(2)}) collective-permute-start(bf16[192,768]{1,0:T(8,128)(2,1)S(1)} %get-tuple-element.71), channel_id=1, source_target_pairs={{2,4},{3,5},{6,8},{7,9},{10,12},{11,13},{14,16},{15,17},{18,20},{1... | collective-permute-start | bytes 884744 | tf_op jit(solution)/shard_map/ppermute | solution.py:44
  76.3 10.9 %collective-permute-start.14 = (bf16[192,768]{1,0:T(8,128)(2,1)S(1)}, bf16[192,768]{1,0:T(8,128)(2,1)S(1)}, u32[]{:S(2)}, u32[]{:S(2)}) collective-permute-start(bf16[192,768]{1,0:T(8,128)(2,1)S(1)} %get-tuple-element.72), channel_id=1, source_target_pairs={{0,2},{1,3},{2,0},{3,1},{4,6},{5,7},{6,4},{7,5},{8,10},{9,11},{10,... | collective-permute-start | bytes 884744 | tf_op jit(solution)/shard_map/ppermute | solution.py:44
  76.4 7.8 %collective-permute-start.15 = (bf16[256,384]{1,0:T(8,128)(2,1)S(1)}, bf16[256,384]{1,0:T(8,128)(2,1)S(1)}, u32[]{:S(2)}, u32[]{:S(2)}) collective-permute-start(bf16[256,384]{1,0:T(8,128)(2,1)S(1)} %get-tuple-element.69), channel_id=1, source_target_pairs={{0,2},{1,3},{2,0},{3,1},{4,6},{5,7},{6,4},{7,5},{8,10},{9,11},{10,... | collective-permute-start | bytes 589832 | tf_op jit(solution)/shard_map/ppermute | solution.py:44
  76.9 31.3 %collective-permute-start.18 = (bf16[1,384,1408]{2,1,0:T(8,128)(2,1)S(1)}, bf16[1,384,1408]{2,1,0:T(8,128)(2,1)S(1)}, u32[]{:S(2)}, u32[]{:S(2)}) collective-permute-start(bf16[1,384,1408]{2,1,0:T(8,128)(2,1)S(1)} %dynamic-slice_bitcast_fusion), channel_id=1, source_target_pairs={{0,64},{1,65},{2,66},{3,67},{4,68},{5,69},{6,70},{7,71},{8,72},{9,... | collective-permute-start | bytes 3244040 | tf_op jit(solution)/shard_map/ppermute | solution.py:44
  87.1 35.2 %collective-permute-start.19 = (bf16[2,2,288,384]{3,2,1,0:T(8,128)(2,1)}, bf16[2,2,288,384]{3,2,1,0:T(8,128)(2,1)}, u32[]{:S(2)}, u32[]{:S(2)}) collective-permute-start(bf16[2,2,288,384]{3,2,1,0:T(8,128)(2,1)} %pad_maximum_fusion.6), channel_id=1, source_target_pairs={{0,16},{1,17},{2,18},{3,19},{4,20},{5,21},{6,22},{7,23},{8,24},{9,... | collective-permute-start | bytes 2654216 | tf_op jit(solution)/shard_map/ppermute | solution.py:44
  111.8 65.1 %all-to-all-start = ((bf16[16,240,384]{2,1,0:T(8,128)(2,1)}), bf16[16,240,384]{2,1,0:T(8,128)(2,1)S(1)}, u32[]{:S(2)}, u32[]{:S(2)}) async-start(bf16[16,240,384]{2,1,0:T(8,128)(2,1)} %slice_dynamic-update-slice_fusion), calls=%async_computation | async-start | bytes 5898240 | tf_op jit(solution)/shard_map/all_to_all | solution.py:87
  119.7 41.9 %collective-permute-start.21 = (bf16[2,288,384]{2,1,0:T(8,128)(2,1)S(1)}, bf16[2,288,384]{2,1,0:T(8,128)(2,1)S(1)}, u32[]{:S(2)}, u32[]{:S(2)}) collective-permute-start(bf16[2,288,384]{2,1,0:T(8,128)(2,1)S(1)} %dynamic-slice_bitcast_fusion.2), channel_id=1, source_target_pairs={{0,16},{1,17},{2,18},{3,19},{4,20},{5,21},{6,22},{7,23},{8,24},{9,... | collective-permute-start | bytes 1327112 | tf_op jit(solution)/shard_map/ppermute | solution.py:44
  123.9 37.8 %collective-permute-start.20 = (bf16[2,288,384]{2,1,0:T(8,128)(2,1)S(1)}, bf16[2,288,384]{2,1,0:T(8,128)(2,1)S(1)}, u32[]{:S(2)}, u32[]{:S(2)}) collective-permute-start(bf16[2,288,384]{2,1,0:T(8,128)(2,1)S(1)} %slice_bitcast_fusion), channel_id=1, source_target_pairs={{0,48},{1,49},{2,50},{3,51},{4,52},{5,53},{6,54},{7,55},{8,56},{9,... | collective-permute-start | bytes 1327112 | tf_op jit(solution)/shard_map/ppermute | solution.py:44
  161.9 7.6 %collective-permute-start.22 = (bf16[2,144,384]{2,1,0:T(8,128)(2,1)S(1)}, bf16[2,144,384]{2,1,0:T(8,128)(2,1)S(1)}, u32[]{:S(2)}, u32[]{:S(2)}) collective-permute-start(bf16[2,144,384]{2,1,0:T(8,128)(2,1)S(1)} %get-tuple-element.52), channel_id=1, source_target_pairs={{0,4},{1,5},{2,6},{3,7},{4,0},{5,1},{6,2},{7,3},{8,12},{9,13},{10,... | collective-permute-start | bytes 663560 | tf_op jit(solution)/shard_map/ppermute | solution.py:44
  164.2 11.8 %collective-permute-start.23 = (bf16[2,144,384]{2,1,0:T(8,128)(2,1)S(1)}, bf16[2,144,384]{2,1,0:T(8,128)(2,1)S(1)}, u32[]{:S(2)}, u32[]{:S(2)}) collective-permute-start(bf16[2,144,384]{2,1,0:T(8,128)(2,1)S(1)} %get-tuple-element.53), channel_id=1, source_target_pairs={{0,12},{1,13},{2,14},{3,15},{4,8},{5,9},{6,10},{7,11},{8,4},{9,5},... | collective-permute-start | bytes 663560 | tf_op jit(solution)/shard_map/ppermute | solution.py:44
  166.9 9.2 %collective-permute-start.24 = (bf16[2,144,384]{2,1,0:T(8,128)(2,1)S(1)}, bf16[2,144,384]{2,1,0:T(8,128)(2,1)S(1)}, u32[]{:S(2)}, u32[]{:S(2)}) collective-permute-start(bf16[2,144,384]{2,1,0:T(8,128)(2,1)S(1)} %get-tuple-element.54), channel_id=1, source_target_pairs={{0,8},{1,9},{2,10},{3,11},{4,12},{5,13},{6,14},{7,15},{8,0},{9,1},... | collective-permute-start | bytes 663560 | tf_op jit(solution)/shard_map/ppermute | solution.py:44
  178.4 10.8 %collective-permute-start.25 = (bf16[312,384]{1,0:T(8,128)(2,1)S(1)}, bf16[312,384]{1,0:T(8,128)(2,1)S(1)}, u32[]{:S(2)}, u32[]{:S(2)}) collective-permute-start(bf16[312,384]{1,0:T(8,128)(2,1)S(1)} %pad_maximum_fusion.15), channel_id=1, source_target_pairs={{0,0},{1,2},{2,1},{3,3},{4,4},{5,6},{6,5},{7,7},{8,8},{9,10},{10,9... | collective-permute-start | bytes 718856 | tf_op jit(solution)/shard_map/ppermute | solution.py:44
  187.7 6.1 %collective-permute-start.27 = (bf16[216,384]{1,0:T(8,128)(2,1)S(1)}, bf16[216,384]{1,0:T(8,128)(2,1)S(1)}, u32[]{:S(2)}, u32[]{:S(2)}) collective-permute-start(bf16[216,384]{1,0:T(8,128)(2,1)S(1)} %get-tuple-element.80), channel_id=1, source_target_pairs={{0,64},{1,66},{2,65},{3,67},{4,68},{5,70},{6,69},{7,71},{8,72},{9,... | collective-permute-start | bytes 497672 | tf_op jit(solution)/shard_map/ppermute | solution.py:44
  189.0 7.5 %collective-permute-start.28 = (bf16[216,384]{1,0:T(8,128)(2,1)S(1)}, bf16[216,384]{1,0:T(8,128)(2,1)S(1)}, u32[]{:S(2)}, u32[]{:S(2)}) collective-permute-start(bf16[216,384]{1,0:T(8,128)(2,1)S(1)} %get-tuple-element.80), channel_id=1, source_target_pairs={{0,66},{1,64},{2,67},{3,65},{4,70},{5,68},{6,71},{7,69},{8,74},{9,... | collective-permute-start | bytes 497672 | tf_op jit(solution)/shard_map/ppermute | solution.py:44
  (19 other events, 133.7 us)

commit v6 on v5

--- a/solution.py
+++ b/solution.py
@@ -1,6 +1,8 @@
 import jax
 import jax.numpy as jnp
 from jax import lax
+from jax.experimental import pallas as pl
+from jax.experimental.pallas import tpu as pltpu
 from jax.sharding import Mesh
 from jax.sharding import PartitionSpec as P
 
@@ -56,9 +58,146 @@
     return jnp.where(c == 0, outer, inner), jnp.where(c == 0, inner, outer)
 
 
-def extended(shard, width, c):
-    before, after = edges(shard, width, c)
-    return jnp.concatenate([before, shard, after], axis=0)
+def copies_in(w_ref, scratch, sems, layers):
+    order = [(n, layer, tap) for n, layer in enumerate(layers) for tap in (1, 0, 2)]
+    made = {
+        (n, tap): pltpu.make_async_copy(
+            w_ref.at[layer, tap], scratch.at[n, tap], sems.at[n, tap]
+        )
+        for n, layer, tap in order
+    }
+    for n, layer, tap in order:
+        made[n, tap].start()
+    return made
+
+
+def three_taps(rows, weights, n, d, start, count, cols, back):
+    total = None
+    for tap in (1, 0, 2):
+        at = start + (2 - tap if back else tap) * d
+        left = rows[at : at + count, :]
+        if back:
+            part = lax.dot_general(
+                left, weights[n, tap, cols, :], (((1,), (1,)), ((), ())), preferred_element_type=F32
+            )
+        else:
+            part = jnp.dot(left, weights[n, tap, :, cols], preferred_element_type=F32)
+        total = part if total is None else total + part
+    return total
+
+
+def tanh_gelu(x):
+    return 0.5 * x * (1.0 + jnp.tanh(0.7978845608028654 * (x + 0.044715 * x * x * x)))
+
+
+def tanh_gelu_slope(x):
+    t = jnp.tanh(0.7978845608028654 * (x + 0.044715 * x * x * x))
+    return 0.5 * (1.0 + t) + 0.5 * x * (1.0 - t * t) * 0.7978845608028654 * (
+        1.0 + 0.134145 * x * x
+    )
+
+
+def zero_outside(v, flags, start, width, total):
+    row = start + lax.broadcasted_iota(jnp.int32, v.shape, 0)
+    out = ((flags[0] == 1) & (row < width)) | ((flags[1] == 1) & (row >= total - width))
+    return jnp.where(out, 0.0, v)
+
+
+COLS = [slice(256 * n, 256 * n + 256) for n in range(3)]
+
+
+def front_kernel(flags, before, own, after, w_ref, act0, wide1, act1, stream2, act2, wide, acts, weights, sems):
+    made = copies_in(w_ref, weights, sems, (0, 1))
+    wide[0:192, :] = before[...]
+    wide[192:448, :] = own[...]
+    wide[448:640, :] = after[...]
+    for r in range(0, 640, 64):
+        acts[r : r + 64, :] = tanh_gelu(wide[r : r + 64, :].astype(F32)).astype(BF)
+    act0[...] = acts[128:512, :]
+    for tap in (1, 0, 2):
+        made[0, tap].wait()
+    for start in (0, 256):
+        for cols in COLS:
+            conv = three_taps(acts, weights, 0, 64, start, 256, cols, False)
+            stream = (wide[start + 64 : start + 320, cols].astype(F32) + conv).astype(BF)
+            stream = zero_outside(stream.astype(F32), flags, start, 128, 512)
+            wide1[start : start + 256, cols] = stream.astype(BF)
+            act1[start : start + 256, cols] = tanh_gelu(stream).astype(BF)
+    for tap in (1, 0, 2):
+        made[1, tap].wait()
+    for cols in COLS:
+        conv = three_taps(act1, weights, 1, 128, 0, 256, cols, False)
+        stream = (wide1[128:384, cols].astype(F32) + conv).astype(BF)
+        stream2[:, cols] = stream
+        act2[:, cols] = tanh_gelu(stream.astype(F32)).astype(BF)
+
+
+def middle_kernel(before, own, after, stream, w_ref, padded, out, weights, sems):
+    made = copies_in(w_ref, weights, sems, (2,))
+    padded[0:256, :] = before[...]
+    padded[256:512, :] = own[...]
+    padded[512:768, :] = after[...]
+    for tap in (1, 0, 2):
+        made[0, tap].wait()
+    for cols in COLS:
+        conv = three_taps(padded, weights, 0, 256, 0, 256, cols, False)
+        out[:, cols] = (stream[:, cols].astype(F32) + conv).astype(BF)
+
+
+def back2_kernel(before, own, after, stream, grad, w_ref, out, out_bf, wide, weights, sems):
+    made = copies_in(w_ref, weights, sems, (2,))
+    wide[0:256, :] = before[...]
+    wide[256:512, :] = own[...]
+    wide[512:768, :] = after[...]
+    for tap in (1, 0, 2):
+        made[0, tap].wait()
+    for cols in COLS:
+        act_grad = three_taps(wide, weights, 0, 256, 0, 256, cols, True)
+        total = grad[:, cols] + tanh_gelu_slope(stream[:, cols].astype(F32)) * act_grad
+        out[:, cols] = total
+        out_bf[:, cols] = total.astype(BF)
+
+
+def back1_kernel(flags, before, own, after, stream, grad, w_ref, out, out_bf, wide, g_in, weights, sems):
+    made = copies_in(w_ref, weights, sems, (1,))
+    wide[0:192, :] = before[...]
+    wide[192:448, :] = own[...]
+    wide[448:640, :] = after[...]
+    g_in[0:64, :] = before[128:192, :].astype(F32)
+    g_in[64:320, :] = grad[...]
+    g_in[320:384, :] = after[0:64, :].astype(F32)
+    for tap in (1, 0, 2):
+        made[0, tap].wait()
+    for start in (0, 192):
+        for cols in COLS:
+            act_grad = three_taps(wide, weights, 0, 128, start, 192, cols, True)
+            slope = tanh_gelu_slope(stream[start + 64 : start + 256, cols].astype(F32))
+            total = g_in[start : start + 192, cols] + slope * act_grad
+            g_in[start : start + 192, cols] = total
+            out_bf[start : start + 192, cols] = zero_outside(total, flags, start, 64, 384).astype(BF)
+    out[...] = g_in[64:320, :]
+
+
+def on_core(kernel, outs, scratch, count, flops, *operands):
+    def place(v):
+        if v.ndim == 4:
+            return pl.BlockSpec(memory_space=pl.ANY)
+        if v.ndim == 1:
+            return pl.BlockSpec(memory_space=pltpu.SMEM)
+        return pl.BlockSpec(memory_space=pltpu.VMEM)
+
+    return pl.pallas_call(
+        kernel,
+        out_shape=[jax.ShapeDtypeStruct((rows, 768), kind) for rows, kind in outs],
+        in_specs=[place(v) for v in operands],
+        out_specs=[pl.BlockSpec(memory_space=pltpu.VMEM) for _ in outs],
+        scratch_shapes=[pltpu.VMEM((rows, 768), kind) for rows, kind in scratch]
+        + [pltpu.VMEM((count, 3, 768, 768), BF), pltpu.SemaphoreType.DMA((count, 3))],
+        compiler_params=pltpu.CompilerParams(vmem_limit_bytes=36 * 2**20),
+        cost_estimate=pl.CostEstimate(
+            flops=flops, bytes_accessed=count * 3 * 768 * 768 * 2, transcendentals=0
+        ),
+    )(*operands)
 
 
 def smooth(values):
@@ -102,18 +241,6 @@
     weight_part = jnp.sum(bin_weight)
     first, last = (xl + z + y + c == 0), (xl == 1) & (z == 3) & (y == 3) & (c == 1)
 
-    def inside(v, width):
-        row = lax.broadcasted_iota(jnp.int32, (v.shape[0], 1), 0)
-        out = (first & (row < width)) | (last & (row >= v.shape[0] - width))
-        return jnp.where(out, jnp.zeros_like(v), v)
-
-    def conv(rows, weights, d, count):
-        total = jnp.dot(rows[d : d + count], weights[1], preferred_element_type=F32)
-        total = total + jnp.dot(rows[:count], weights[0], preferred_element_type=F32)
-        return total + jnp.dot(
-            rows[2 * d : 2 * d + count], weights[2], preferred_element_type=F32
-        )
-
     def conv_back(rows, weights, d, count):
         total = jnp.dot(rows[d : d + count], weights[1].T, preferred_element_type=F32)
         total = total + jnp.dot(
@@ -121,26 +248,33 @@
         )
         return total + jnp.dot(rows[:count], weights[2].T, preferred_element_type=F32)
 
-    def activate(v):
-        return smooth(v.astype(F32)).astype(BF)
-
     def through(v, grad):
         return jax.vjp(smooth, v.astype(F32))[1](grad)[0]
 
-    wide0 = extended(trunk[0], 192, c)
-    act0 = activate(wide0)
-    wide1 = (wide0[64:576].astype(F32) + conv(act0, conv_weight[0], 64, 512)).astype(BF)
-    wide1 = inside(wide1, 128)
-    act1 = activate(wide1)
-    stream2 = (wide1[128:384].astype(F32) + conv(act1, conv_weight[1], 128, 256)).astype(BF)
-    act2 = activate(stream2)
+    flags = jnp.stack([first, last]).astype(jnp.int32)
+    tap_flops = 2 * 768 * 768 * 3
+    before, after = edges(trunk[0], 192, c)
+    act0, wide1, act1, stream2, act2 = on_core(
+        front_kernel,
+        [(384, BF), (512, BF), (512, BF), (256, BF), (256, BF)],
+        [(640, BF), (640, BF)],
+        2,
+        768 * tap_flops,
+        *(flags, before, trunk[0], after, conv_weight),
+    )
     before, after = edges(act2, 256, c)
-    far_acts = [send(act0[128:512], CORE), send(act1, CORE)]
+    far_acts = [send(act0, CORE), send(act1, CORE)]
     before, far_acts[0], far_acts[1] = lax.optimization_barrier((before, *far_acts))
-    act2 = jnp.concatenate([before, act2, after], axis=0)
+    act2, stream = on_core(
+        middle_kernel,
+        [(768, BF), (256, BF)],
+        [],
+        1,
+        256 * tap_flops,
+        *(before, act2, after, stream2, conv_weight),
+    )
     far_acts.append(send(act2, CORE))
-    stream = (stream2.astype(F32) + conv(act2, conv_weight[2], 256, 256)).astype(BF)
-    padded_acts = [act0[128:512], act1, act2]
+    padded_acts = [act0, act1, act2]
     logits = jnp.dot(stream, head_weight, preferred_element_type=F32)
     predicted = jax.nn.softplus(logits)
     slope = jax.nn.sigmoid(logits)
@@ -196,18 +330,27 @@
     half2 = conv_grad(2, gb2)
     got2 = give(half2, z // 2, ALONG_Z[3], 2)
     before, head_half, half2 = lax.optimization_barrier((before, head_half, half2))
-    wide = jnp.concatenate([before, gb2, after], axis=0)
-    g2 = g_top + through(stream2, conv_back(wide, conv_weight[2], 256, 256))
-    gb1 = g2.astype(BF)
+    g2, gb1 = on_core(
+        back2_kernel,
+        [(256, F32), (256, BF)],
+        [(768, BF)],
+        1,
+        256 * tap_flops,
+        *(before, gb2, after, stream2, g_top, conv_weight),
+    )
     before, after = edges(gb1, 192, c)
     half1 = conv_grad(1, gb1)
     half1 = half1.reshape(2, 4, 288, 384)
     got1 = send(jnp.stack([pick(half1, z ^ 1, 1), pick(half1, z ^ 2, 1)]), ALONG_Z[1])
     before, half1 = lax.optimization_barrier((before, half1))
-    wide = jnp.concatenate([before, gb1, after], axis=0)
-    g_in = jnp.concatenate([before[128:].astype(F32), g2, after[:64].astype(F32)], axis=0)
-    g1 = g_in + through(wide1[64:448], conv_back(wide, conv_weight[1], 128, 384))
-    gb0 = inside(g1.astype(BF), 64)
+    g1, gb0 = on_core(
+        back1_kernel,
+        [(256, F32), (384, BF)],
+        [(640, BF), (384, F32)],
+        1,
+        384 * tap_flops,
+        *(flags, before, gb1, after, wide1, g2, conv_weight),
+    )
     part2_z = take(half2, got2, z // 2)
     got2 = give(part2_z, z % 2, ALONG_Z[1], 2)
     gb0, part2_z = lax.optimization_barrier((gb0, part2_z))
@@ -225,7 +368,7 @@
     got1 = send(keep1[1], ALONG_Z[3])
     part1 = (keep1[0].astype(F32) + got1.astype(F32)).astype(BF)
     part2 = take(part2_z, got2, z % 2)
-    g0 = g1[64:320] + through(trunk[0], conv_back(gb0, conv_weight[0], 64, 256))
+    g0 = g1 + through(trunk[0], conv_back(gb0, conv_weight[0], 64, 256))
     g0 = lax.optimization_barrier(g0)
     early = jnp.concatenate([part1.reshape(2, 4, 72, 384), part2.reshape(2, 4, 72, 384)], axis=2)
     got = [send(pick(early, y ^ k, 1), ALONG_Y[k]) for k in (1, 3, 2)]

time: 201 us -> 203 us (level)
  matrix products: 46.6 us -> 24.1 us
  Pallas kernels: 0 us -> 15 us
  local copies, waits for them, and re-layouts: 10.1 us -> 16.5 us
    dot_general x9 -> x0, matrix products: 19 us -> none  [the longest x3 7.14 us: conv(): jnp.dot(rows[2 * d:2 * d + count], weights[2], preferred_element_type=F32)]
    pallas_call x0 -> x4, Pallas kernels: none -> 15 us  [on_core(): pl.pallas_call(kernel, out_shape=[jax.ShapeDtypeStruct((rows, 768), kind)...]
    unnamed x31 -> x27, local copies, waits for them, and re-layouts: 5.06 us -> 12.5 us
    dot_general x3 -> x1, matrix products: 5.14 us -> 1.77 us  [conv_back(): total = jnp.dot(rows[d:d + count], weights[1].T, preferred_element_type=F32)]
    dot_general x10, matrix products: 4.4 us -> 7.31 us  [pair_dot(): jnp.dot(far_a.T, far_b, preferred_element_type=F32)]
    dot_general x3 -> x1, matrix products: 3.86 us -> 1.78 us  [conv_back(): jnp.dot(rows[:count], weights[2].T, preferred_element_type=F32)]
    dot_general x3 -> x1, matrix products: 3.84 us -> 1.78 us  [conv_back(): jnp.dot(rows[2 * d:2 * d + count], weights[0].T, preferred_element_type=F32)]
  transfers between devices with their start and end apart: 30 -> 30, of which waited for: 10 -> 8; matrix products, arithmetic and copies ran while one was open for 31% -> 25% of each run, Pallas kernels for 0% -> 3%
where the time goes in v6:
time: 203 us; the launch traced here: 200 us
  waiting for transfers between devices  60.6 us (30%)
  starting transfers between devices  58.2 us (29%)
  matrix products  24.1 us (12%)
  other arithmetic  21.1 us (10%)
  local copies, waits for them, and re-layouts  16.5 us (8%)
  Pallas kernels  15 us (7%)
  between operations  4.63 us (2%)
    ppermute x29, waiting for transfers between devices, send(): return lax.ppermute(v, AXES, pairs)  60.6 us
    ppermute x29, starting transfers between devices, send(): return lax.ppermute(v, AXES, pairs)  51.6 us
    pallas_call x4, Pallas kernels, on_core(): pl.pallas_call(kernel, out_shape=[jax.ShapeDtypeStruct((rows, 768), kind)...  15 us
    unnamed x27, local copies, waits for them, and re-layouts  12.5 us
    dot_general x10, matrix products, pair_dot(): jnp.dot(far_a.T, far_b, preferred_element_type=F32)  7.31 us
    all_to_all x1, starting transfers between devices, plane_sum(): got = lax.all_to_all(blocks, ('z', 'y'), 0, 0, tiled=True)  6.61 us
    dot_general x1, matrix products, per_device(): logits = jnp.dot(stream, head_weight, preferred_element_type=F32)  5.82 us
    dot_general x10, matrix products, pair_dot(): jnp.dot(a.T, b, preferred_element_type=F32)  4.37 us
  transfers between devices with their start and end apart: 30, of which 8 were waited for; matrix products, arithmetic and copies ran while one was open for 25% of the time, Pallas kernels for 3%

profile of v6, /device:TPU:1, one launch (start us, length us, event | category | flops | bytes accessed | tf_op | source)
XLA Modules:
  0.0 200.2 jit_solution(6280420738394806917)
XLA Ops:
  1.8 4.6 %collective-permute-start = (bf16[192,768]{1,0:T(8,128)(2,1)S(1)}, bf16[192,768]{1,0:T(8,128)(2,1)S(1)}, u32[]{:S(2)}, u32[]{:S(2)}) collective-permute-start(bf16[192,768]{1,0:T(8,128)(2,1)S(1)} %get-tuple-element.100), channel_id=1, source_target_pairs={{2,4},{3,5},{6,8},{7,9},{10,12},{11,13},{14,16},{15,17},{18,20},{1... | collective-permute-start | bytes 884744 | tf_op jit(solution)/shard_map/ppermute | solution.py:46
  6.6 4.2 %collective-permute-done = bf16[192,768]{1,0:T(8,128)(2,1)S(1)} collective-permute-done((bf16[192,768]{1,0:T(8,128)(2,1)S(1)}, bf16[192,768]{1,0:T(8,128)(2,1)S(1)}, u32[]{:S(2)}, u32[]{:S(2)}) %collective-permute-start) | collective-permute-done | bytes 294944 | tf_op jit(solution)/shard_map/ppermute | solution.py:46
  10.9 4.0 %copy-done = bf16[3,3,768,768]{3,2,1,0:T(8,128)(2,1)S(1)} copy-done((bf16[3,3,768,768]{3,2,1,0:T(8,128)(2,1)S(1)}, bf16[3,3,768,768]{3,2,1,0:T(8,128)(2,1)}, u32[]{:S(2)}) %copy-start) | copy-done | bytes 10616856
  14.9 6.7 %shard_map.93 = (bf16[384,768]{1,0:T(8,128)(2,1)S(1)}, bf16[512,768]{1,0:T(8,128)(2,1)S(1)}, bf16[512,768]{1,0:T(8,128)(2,1)S(1)}, bf16[256,768]{1,0:T(8,128)(2,1)S(1)}, bf16[256,768]{1,0:T(8,128)(2,1)S(1)}) custom-call(s32[2]{0:T(128)S(1)} %add_convert_fusion.1.flags, bf16[192,768]{1,0:T(8,128)(2,1)S(1)} %get-tuple-element.88.before, ...), custom_call_target="tpu_custom_call" | custom-call | flops 2717908992 | bytes 7077888 | tf_op jit(solution)/shard_map/pallas_call | solution.py:189
  21.7 3.7 %collective-permute-start.2 = (bf16[256,768]{1,0:T(8,128)(2,1)S(1)}, bf16[256,768]{1,0:T(8,128)(2,1)}, u32[]{:S(2)}, u32[]{:S(2)}) collective-permute-start(bf16[256,768]{1,0:T(8,128)(2,1)S(1)} %get-tuple-element.35.own), channel_id=1, source_target_pairs={{2,4},{3,5},{6,8},{7,9},{10,12},{11,13},{14,16},{15,17},{18,20},{1... | collective-permute-start | bytes 1179656 | tf_op jit(solution)/shard_map/ppermute | solution.py:46
  26.7 4.3 %collective-permute-done.2 = bf16[256,768]{1,0:T(8,128)(2,1)} collective-permute-done((bf16[256,768]{1,0:T(8,128)(2,1)S(1)}, bf16[256,768]{1,0:T(8,128)(2,1)}, u32[]{:S(2)}, u32[]{:S(2)}) %collective-permute-start.2) | collective-permute-done | bytes 393248 | tf_op jit(solution)/shard_map/ppermute | solution.py:46
  32.2 4.0 %copy-done.1 = bf16[3,3,768,768]{3,2,1,0:T(8,128)(2,1)S(1)} copy-done((bf16[3,3,768,768]{3,2,1,0:T(8,128)(2,1)S(1)}, bf16[3,3,768,768]{3,2,1,0:T(8,128)(2,1)}, u32[]{:S(2)}) %copy-start.1) | copy-done | bytes 10616856
  38.7 5.8 %fusion.5 = (f32[]{:T(128)}, bf16[256,2688]{1,0:T(8,128)(2,1)S(1)}) fusion(s32[1,256,2688]{2,1,0:T(8,128)} %param.9, f32[256]{0:T(256)S(1)} %bitcast.155, bf16[256,768]{1,0:T(8,128)(2,1)S(1)} %get-tuple-element.39, bf16[768,2688]{1,0:T(8,128)(2,1)S(1)} %copy-done.10), kind=kOutput, calls=%fused_computation.9 | convolution fusion | flops 1070039040 | bytes 8651780 | tf_op jit(solution)/shard_map/dot_general | solution.py:278
  45.9 3.6 %collective-permute-start.8 = (bf16[256,768]{1,0:T(8,128)(2,1)S(1)}, bf16[256,768]{1,0:T(8,128)(2,1)S(1)}, u32[]{:S(2)}, u32[]{:S(2)}) collective-permute-start(bf16[256,768]{1,0:T(8,128)(2,1)S(1)} %get-tuple-element.42.own), channel_id=1, source_target_pairs={{2,4},{3,5},{6,8},{7,9},{10,12},{11,13},{14,16},{15,17},{18,20},{1... | collective-permute-start | bytes 1179656 | tf_op jit(solution)/shard_map/ppermute | solution.py:46
  59.6 8.7 %collective-permute-start.16 = (bf16[2,576,384]{2,1,0:T(8,128)(2,1)}, bf16[2,576,384]{2,1,0:T(8,128)(2,1)}, u32[]{:S(2)}, u32[]{:S(2)}) collective-permute-start(bf16[2,576,384]{2,1,0:T(8,128)(2,1)} %dynamic-slice_bitcast_fusion.1), channel_id=1, source_target_pairs={{0,48},{1,49},{2,50},{3,51},{4,52},{5,53},{6,54},{7,55},{8,56},{9,... | collective-permute-start | bytes 2654216 | tf_op jit(solution)/shard_map/ppermute | solution.py:46
  70.0 2.2 %shard_map.95 = (f32[256,768]{1,0:T(8,128)S(1)}, bf16[256,768]{1,0:T(8,128)(2,1)S(1)}) custom-call(bf16[256,768]{1,0:T(8,128)(2,1)S(1)} %get-tuple-element.47.before, bf16[256,768]{1,0:T(8,128)(2,1)S(1)} %get-tuple-element.42.own, bf16[256,768]{1,0:T(8,128)(2,1)S(1)} %get-tuple-element.77.after, bf16[256,768]{1,0:T(8,128)(2,1)S(1)} %get-tuple-element.38.stream, ...), custom_call_target="tpu_custom_call" | custom-call | flops 905969664 | bytes 3538944 | tf_op jit(solution)/shard_map/pallas_call | solution.py:189
  75.0 6.5 %collective-permute-start.18 = (bf16[1,384,1408]{2,1,0:T(8,128)(2,1)S(1)}, bf16[1,384,1408]{2,1,0:T(8,128)(2,1)}, u32[]{:S(2)}, u32[]{:S(2)}) collective-permute-start(bf16[1,384,1408]{2,1,0:T(8,128)(2,1)S(1)} %dynamic-slice_bitcast_fusion), channel_id=1, source_target_pairs={{0,64},{1,65},{2,66},{3,67},{4,68},{5,69},{6,70},{7,71},{8,72},{9,... | collective-permute-start | bytes 3244040 | tf_op jit(solution)/shard_map/ppermute | solution.py:46
  87.2 4.2 %shard_map.96 = (f32[256,768]{1,0:T(8,128)S(1)}, bf16[384,768]{1,0:T(8,128)(2,1)S(1)}) custom-call(s32[2]{0:T(128)S(1)} %add_convert_fusion.1.flags, bf16[192,768]{1,0:T(8,128)(2,1)S(1)} %get-tuple-element.50.before, bf16[256,768]{1,0:T(8,128)(2,1)S(1)} %get-tuple-element.48.own, bf16[192,768]{1,0:T(8,128)(2,1)S(1)} %get-tuple-element.85.after, ...), custom_call_target="tpu_custom_call" | custom-call | flops 1358954496 | bytes 3538944 | tf_op jit(solution)/shard_map/pallas_call | solution.py:189
  91.3 2.7 %fusion.8 = bf16[2,576,384]{2,1,0:T(8,128)(2,1)} fusion(bf16[2,576,384]{2,1,0:T(8,128)(2,1)} %collective-permute-done.16, bf16[2,2,576,384]{3,2,1,0:T(8,128)(2,1)S(1)} %bitcast.139, s32[]{:T(128)S(6)} %select_n.268), kind=kLoop, calls=%fused_computation.16 | loop fusion | flops 1769472 | bytes 2654212 | tf_op jit(solution)/shard_map/convert_element_type | solution.py:222
  100.2 5.8 %collective-permute-done.18 = bf16[1,384,1408]{2,1,0:T(8,128)(2,1)} collective-permute-done((bf16[1,384,1408]{2,1,0:T(8,128)(2,1)S(1)}, bf16[1,384,1408]{2,1,0:T(8,128)(2,1)}, u32[]{:S(2)}, u32[]{:S(2)}) %collective-permute-start.18) | collective-permute-done | bytes 1081376 | tf_op jit(solution)/shard_map/ppermute | solution.py:46
  110.7 6.6 %all-to-all-start = ((bf16[16,240,384]{2,1,0:T(8,128)(2,1)}), bf16[16,240,384]{2,1,0:T(8,128)(2,1)}, u32[]{:S(2)}, u32[]{:S(2)}) async-start(bf16[16,240,384]{2,1,0:T(8,128)(2,1)} %slice_dynamic-update-slice_fusion), calls=%async_computation | async-start | bytes 5898240 | tf_op jit(solution)/shard_map/all_to_all | solution.py:226
  127.1 32.5 %collective-permute-done.21 = bf16[2,288,384]{2,1,0:T(8,128)(2,1)S(1)} collective-permute-done((bf16[2,288,384]{2,1,0:T(8,128)(2,1)S(1)}, bf16[2,288,384]{2,1,0:T(8,128)(2,1)S(1)}, u32[]{:S(2)}, u32[]{:S(2)}) %collective-permute-start.21) | collective-permute-done | bytes 442400 | tf_op jit(solution)/shard_map/ppermute | solution.py:46
  159.9 2.9 %collective-permute-start.22 = (bf16[2,144,384]{2,1,0:T(8,128)(2,1)S(1)}, bf16[2,144,384]{2,1,0:T(8,128)(2,1)S(1)}, u32[]{:S(2)}, u32[]{:S(2)}) collective-permute-start(bf16[2,144,384]{2,1,0:T(8,128)(2,1)S(1)} %get-tuple-element.74), channel_id=1, source_target_pairs={{0,4},{1,5},{2,6},{3,7},{4,0},{5,1},{6,2},{7,3},{8,12},{9,13},{10,... | collective-permute-start | bytes 663560 | tf_op jit(solution)/shard_map/ppermute | solution.py:46
  162.8 2.7 %collective-permute-start.23 = (bf16[2,144,384]{2,1,0:T(8,128)(2,1)S(1)}, bf16[2,144,384]{2,1,0:T(8,128)(2,1)S(1)}, u32[]{:S(2)}, u32[]{:S(2)}) collective-permute-start(bf16[2,144,384]{2,1,0:T(8,128)(2,1)S(1)} %get-tuple-element.75), channel_id=1, source_target_pairs={{0,12},{1,13},{2,14},{3,15},{4,8},{5,9},{6,10},{7,11},{8,4},{9,5},... | collective-permute-start | bytes 663560 | tf_op jit(solution)/shard_map/ppermute | solution.py:46
  167.3 7.3 %collective-permute-done.23 = bf16[2,144,384]{2,1,0:T(8,128)(2,1)S(1)} collective-permute-done((bf16[2,144,384]{2,1,0:T(8,128)(2,1)S(1)}, bf16[2,144,384]{2,1,0:T(8,128)(2,1)S(1)}, u32[]{:S(2)}, u32[]{:S(2)}) %collective-permute-start.23) | collective-permute-done | bytes 221216 | tf_op jit(solution)/shard_map/ppermute | solution.py:46
  174.8 2.4 %reduce_sum.50 = bf16[240,384]{1,0:T(8,128)(2,1)S(1)} reduce(bf16[16,240,384]{2,1,0:T(8,128)(2,1)} %all-to-all-done, bf16[]{:T(256)} %constant.133.clone.1), dimensions={0}, to_apply=%region_2.3 | reduce | flops 1382400 | bytes 3133442 | tf_op jit(solution)/shard_map/reduce_sum | solution.py:227
  177.3 6.5 %collective-permute-start.25 = (bf16[312,384]{1,0:T(8,128)(2,1)S(1)}, bf16[312,384]{1,0:T(8,128)(2,1)S(1)}, u32[]{:S(2)}, u32[]{:S(2)}) collective-permute-start(bf16[312,384]{1,0:T(8,128)(2,1)S(1)} %pad_maximum_fusion.5), channel_id=1, source_target_pairs={{0,0},{1,2},{2,1},{3,3},{4,4},{5,6},{6,5},{7,7},{8,8},{9,10},{10,9... | collective-permute-start | bytes 718856 | tf_op jit(solution)/shard_map/ppermute | solution.py:46
  184.5 3.0 %collective-permute-start.27 = (bf16[216,384]{1,0:T(8,128)(2,1)S(1)}, bf16[216,384]{1,0:T(8,128)(2,1)S(1)}, u32[]{:S(2)}, u32[]{:S(2)}) collective-permute-start(bf16[216,384]{1,0:T(8,128)(2,1)S(1)} %get-tuple-element.104), channel_id=1, source_target_pairs={{0,64},{1,66},{2,65},{3,67},{4,68},{5,70},{6,69},{7,71},{8,72},{9,... | collective-permute-start | bytes 497672 | tf_op jit(solution)/shard_map/ppermute | solution.py:46
  192.6 4.3 %collective-permute-done.28 = bf16[216,384]{1,0:T(8,128)(2,1)S(1)} collective-permute-done((bf16[216,384]{1,0:T(8,128)(2,1)S(1)}, bf16[216,384]{1,0:T(8,128)(2,1)S(1)}, u32[]{:S(2)}, u32[]{:S(2)}) %collective-permute-start.28) | collective-permute-done | bytes 165920 | tf_op jit(solution)/shard_map/ppermute | solution.py:46
  (144 shorter events, 56.1 us)
Async XLA Ops:
  1.8 9.0 %collective-permute-start = (bf16[192,768]{1,0:T(8,128)(2,1)S(1)}, bf16[192,768]{1,0:T(8,128)(2,1)S(1)}, u32[]{:S(2)}, u32[]{:S(2)}) collective-permute-start(bf16[192,768]{1,0:T(8,128)(2,1)S(1)} %get-tuple-element.100), channel_id=1, source_target_pairs={{2,4},{3,5},{6,8},{7,9},{10,12},{11,13},{14,16},{15,17},{18,20},{1... | collective-permute-start | bytes 884744 | tf_op jit(solution)/shard_map/ppermute | solution.py:46
  21.6 10.6 %collective-permute-start.5 = (bf16[512,768]{1,0:T(8,128)(2,1)S(1)}, bf16[512,768]{1,0:T(8,128)(2,1)}, u32[]{:S(2)}, u32[]{:S(2)}) collective-permute-start(bf16[512,768]{1,0:T(8,128)(2,1)S(1)} %get-tuple-element.36), channel_id=1, source_target_pairs={{0,2},{1,3},{2,0},{3,1},{4,6},{5,7},{6,4},{7,5},{8,10},{9,11},{10,... | collective-permute-start | bytes 2359304 | tf_op jit(solution)/shard_map/ppermute | solution.py:46
  21.7 9.3 %collective-permute-start.2 = (bf16[256,768]{1,0:T(8,128)(2,1)S(1)}, bf16[256,768]{1,0:T(8,128)(2,1)}, u32[]{:S(2)}, u32[]{:S(2)}) collective-permute-start(bf16[256,768]{1,0:T(8,128)(2,1)S(1)} %get-tuple-element.35.own), channel_id=1, source_target_pairs={{2,4},{3,5},{6,8},{7,9},{10,12},{11,13},{14,16},{15,17},{18,20},{1... | collective-permute-start | bytes 1179656 | tf_op jit(solution)/shard_map/ppermute | solution.py:46
  25.6 6.6 %collective-permute-start.4 = (bf16[384,768]{1,0:T(8,128)(2,1)S(1)}, bf16[384,768]{1,0:T(8,128)(2,1)S(1)}, u32[]{:S(2)}, u32[]{:S(2)}) collective-permute-start(bf16[384,768]{1,0:T(8,128)(2,1)S(1)} %get-tuple-element.34), channel_id=1, source_target_pairs={{0,2},{1,3},{2,0},{3,1},{4,6},{5,7},{6,4},{7,5},{8,10},{9,11},{10,... | collective-permute-start | bytes 1769480 | tf_op jit(solution)/shard_map/ppermute | solution.py:46
  38.1 6.4 %collective-permute-start.6 = (bf16[768,768]{1,0:T(8,128)(2,1)S(1)}, bf16[768,768]{1,0:T(8,128)(2,1)S(1)}, u32[]{:S(2)}, u32[]{:S(2)}) collective-permute-start(bf16[768,768]{1,0:T(8,128)(2,1)S(1)} %get-tuple-element.40), channel_id=1, source_target_pairs={{0,2},{1,3},{2,0},{3,1},{4,6},{5,7},{6,4},{7,5},{8,10},{9,11},{10,... | collective-permute-start | bytes 3538952 | tf_op jit(solution)/shard_map/ppermute | solution.py:46
  38.2 7.6 %collective-permute-start.7 = (bf16[256,768]{1,0:T(8,128)(2,1)S(1)}, bf16[256,768]{1,0:T(8,128)(2,1)S(1)}, u32[]{:S(2)}, u32[]{:S(2)}) collective-permute-start(bf16[256,768]{1,0:T(8,128)(2,1)S(1)} %get-tuple-element.39), channel_id=1, source_target_pairs={{0,2},{1,3},{2,0},{3,1},{4,6},{5,7},{6,4},{7,5},{8,10},{9,11},{10,... | collective-permute-start | bytes 1179656 | tf_op jit(solution)/shard_map/ppermute | solution.py:46
  45.9 22.3 %collective-permute-start.8 = (bf16[256,768]{1,0:T(8,128)(2,1)S(1)}, bf16[256,768]{1,0:T(8,128)(2,1)S(1)}, u32[]{:S(2)}, u32[]{:S(2)}) collective-permute-start(bf16[256,768]{1,0:T(8,128)(2,1)S(1)} %get-tuple-element.42.own), channel_id=1, source_target_pairs={{2,4},{3,5},{6,8},{7,9},{10,12},{11,13},{14,16},{15,17},{18,20},{1... | collective-permute-start | bytes 1179656 | tf_op jit(solution)/shard_map/ppermute | solution.py:46
  49.6 18.7 %collective-permute-start.9 = (bf16[256,768]{1,0:T(8,128)(2,1)S(1)}, bf16[256,768]{1,0:T(8,128)(2,1)S(1)}, u32[]{:S(2)}, u32[]{:S(2)}) collective-permute-start(bf16[256,768]{1,0:T(8,128)(2,1)S(1)} %get-tuple-element.42.own), channel_id=1, source_target_pairs={{0,2},{1,3},{2,0},{3,1},{4,6},{5,7},{6,4},{7,5},{8,10},{9,11},{10,... | collective-permute-start | bytes 1179656 | tf_op jit(solution)/shard_map/ppermute | solution.py:46
  51.8 16.6 %collective-permute-start.11 = (bf16[256,1408]{1,0:T(8,128)(2,1)S(1)}, bf16[256,1408]{1,0:T(8,128)(2,1)S(1)}, u32[]{:S(2)}, u32[]{:S(2)}) collective-permute-start(bf16[256,1408]{1,0:T(8,128)(2,1)S(1)} %broadcast_select_fusion), channel_id=1, source_target_pairs={{0,2},{1,3},{2,0},{3,1},{4,6},{5,7},{6,4},{7,5},{8,10},{9,11},{10,... | collective-permute-start | bytes 2162696 | tf_op jit(solution)/shard_map/ppermute | solution.py:46
  59.6 31.8 %collective-permute-start.16 = (bf16[2,576,384]{2,1,0:T(8,128)(2,1)}, bf16[2,576,384]{2,1,0:T(8,128)(2,1)}, u32[]{:S(2)}, u32[]{:S(2)}) collective-permute-start(bf16[2,576,384]{2,1,0:T(8,128)(2,1)} %dynamic-slice_bitcast_fusion.1), channel_id=1, source_target_pairs={{0,48},{1,49},{2,50},{3,51},{4,52},{5,53},{6,54},{7,55},{8,56},{9,... | collective-permute-start | bytes 2654216 | tf_op jit(solution)/shard_map/ppermute | solution.py:46
  72.2 9.3 %collective-permute-start.15 = (bf16[256,384]{1,0:T(8,128)(2,1)S(1)}, bf16[256,384]{1,0:T(8,128)(2,1)S(1)}, u32[]{:S(2)}, u32[]{:S(2)}) collective-permute-start(bf16[256,384]{1,0:T(8,128)(2,1)S(1)} %get-tuple-element.94), channel_id=1, source_target_pairs={{0,2},{1,3},{2,0},{3,1},{4,6},{5,7},{6,4},{7,5},{8,10},{9,11},{10,... | collective-permute-start | bytes 589832 | tf_op jit(solution)/shard_map/ppermute | solution.py:46
  72.9 14.2 %collective-permute-start.13 = (bf16[192,768]{1,0:T(8,128)(2,1)S(1)}, bf16[192,768]{1,0:T(8,128)(2,1)S(1)}, u32[]{:S(2)}, u32[]{:S(2)}) collective-permute-start(bf16[192,768]{1,0:T(8,128)(2,1)S(1)} %get-tuple-element.96), channel_id=1, source_target_pairs={{2,4},{3,5},{6,8},{7,9},{10,12},{11,13},{14,16},{15,17},{18,20},{1... | collective-permute-start | bytes 884744 | tf_op jit(solution)/shard_map/ppermute | solution.py:46
  74.8 12.3 %collective-permute-start.14 = (bf16[192,768]{1,0:T(8,128)(2,1)S(1)}, bf16[192,768]{1,0:T(8,128)(2,1)S(1)}, u32[]{:S(2)}, u32[]{:S(2)}) collective-permute-start(bf16[192,768]{1,0:T(8,128)(2,1)S(1)} %get-tuple-element.95), channel_id=1, source_target_pairs={{0,2},{1,3},{2,0},{3,1},{4,6},{5,7},{6,4},{7,5},{8,10},{9,11},{10,... | collective-permute-start | bytes 884744 | tf_op jit(solution)/shard_map/ppermute | solution.py:46
  75.0 31.0 %collective-permute-start.18 = (bf16[1,384,1408]{2,1,0:T(8,128)(2,1)S(1)}, bf16[1,384,1408]{2,1,0:T(8,128)(2,1)}, u32[]{:S(2)}, u32[]{:S(2)}) collective-permute-start(bf16[1,384,1408]{2,1,0:T(8,128)(2,1)S(1)} %dynamic-slice_bitcast_fusion), channel_id=1, source_target_pairs={{0,64},{1,65},{2,66},{3,67},{4,68},{5,69},{6,70},{7,71},{8,72},{9,... | collective-permute-start | bytes 3244040 | tf_op jit(solution)/shard_map/ppermute | solution.py:46
  95.6 26.3 %collective-permute-start.19 = (bf16[2,2,288,384]{3,2,1,0:T(8,128)(2,1)}, bf16[2,2,288,384]{3,2,1,0:T(8,128)(2,1)}, u32[]{:S(2)}, u32[]{:S(2)}) collective-permute-start(bf16[2,2,288,384]{3,2,1,0:T(8,128)(2,1)} %pad_maximum_fusion.4), channel_id=1, source_target_pairs={{0,16},{1,17},{2,18},{3,19},{4,20},{5,21},{6,22},{7,23},{8,24},{9,... | collective-permute-start | bytes 2654216 | tf_op jit(solution)/shard_map/ppermute | solution.py:46
  110.7 64.1 %all-to-all-start = ((bf16[16,240,384]{2,1,0:T(8,128)(2,1)}), bf16[16,240,384]{2,1,0:T(8,128)(2,1)}, u32[]{:S(2)}, u32[]{:S(2)}) async-start(bf16[16,240,384]{2,1,0:T(8,128)(2,1)} %slice_dynamic-update-slice_fusion), calls=%async_computation | async-start | bytes 5898240 | tf_op jit(solution)/shard_map/all_to_all | solution.py:226
  118.6 40.9 %collective-permute-start.21 = (bf16[2,288,384]{2,1,0:T(8,128)(2,1)S(1)}, bf16[2,288,384]{2,1,0:T(8,128)(2,1)S(1)}, u32[]{:S(2)}, u32[]{:S(2)}) collective-permute-start(bf16[2,288,384]{2,1,0:T(8,128)(2,1)S(1)} %dynamic-slice_bitcast_fusion.2), channel_id=1, source_target_pairs={{0,16},{1,17},{2,18},{3,19},{4,20},{5,21},{6,22},{7,23},{8,24},{9,... | collective-permute-start | bytes 1327112 | tf_op jit(solution)/shard_map/ppermute | solution.py:46
  123.4 36.3 %collective-permute-start.20 = (bf16[2,288,384]{2,1,0:T(8,128)(2,1)S(1)}, bf16[2,288,384]{2,1,0:T(8,128)(2,1)S(1)}, u32[]{:S(2)}, u32[]{:S(2)}) collective-permute-start(bf16[2,288,384]{2,1,0:T(8,128)(2,1)S(1)} %slice_bitcast_fusion), channel_id=1, source_target_pairs={{0,48},{1,49},{2,50},{3,51},{4,52},{5,53},{6,54},{7,55},{8,56},{9,... | collective-permute-start | bytes 1327112 | tf_op jit(solution)/shard_map/ppermute | solution.py:46
  159.9 7.4 %collective-permute-start.22 = (bf16[2,144,384]{2,1,0:T(8,128)(2,1)S(1)}, bf16[2,144,384]{2,1,0:T(8,128)(2,1)S(1)}, u32[]{:S(2)}, u32[]{:S(2)}) collective-permute-start(bf16[2,144,384]{2,1,0:T(8,128)(2,1)S(1)} %get-tuple-element.74), channel_id=1, source_target_pairs={{0,4},{1,5},{2,6},{3,7},{4,0},{5,1},{6,2},{7,3},{8,12},{9,13},{10,... | collective-permute-start | bytes 663560 | tf_op jit(solution)/shard_map/ppermute | solution.py:46
  162.8 11.9 %collective-permute-start.23 = (bf16[2,144,384]{2,1,0:T(8,128)(2,1)S(1)}, bf16[2,144,384]{2,1,0:T(8,128)(2,1)S(1)}, u32[]{:S(2)}, u32[]{:S(2)}) collective-permute-start(bf16[2,144,384]{2,1,0:T(8,128)(2,1)S(1)} %get-tuple-element.75), channel_id=1, source_target_pairs={{0,12},{1,13},{2,14},{3,15},{4,8},{5,9},{6,10},{7,11},{8,4},{9,5},... | collective-permute-start | bytes 663560 | tf_op jit(solution)/shard_map/ppermute | solution.py:46
  165.5 9.2 %collective-permute-start.24 = (bf16[2,144,384]{2,1,0:T(8,128)(2,1)S(1)}, bf16[2,144,384]{2,1,0:T(8,128)(2,1)S(1)}, u32[]{:S(2)}, u32[]{:S(2)}) collective-permute-start(bf16[2,144,384]{2,1,0:T(8,128)(2,1)S(1)} %get-tuple-element.76), channel_id=1, source_target_pairs={{0,8},{1,9},{2,10},{3,11},{4,12},{5,13},{6,14},{7,15},{8,0},{9,1},... | collective-permute-start | bytes 663560 | tf_op jit(solution)/shard_map/ppermute | solution.py:46
  177.3 10.4 %collective-permute-start.25 = (bf16[312,384]{1,0:T(8,128)(2,1)S(1)}, bf16[312,384]{1,0:T(8,128)(2,1)S(1)}, u32[]{:S(2)}, u32[]{:S(2)}) collective-permute-start(bf16[312,384]{1,0:T(8,128)(2,1)S(1)} %pad_maximum_fusion.5), channel_id=1, source_target_pairs={{0,0},{1,2},{2,1},{3,3},{4,4},{5,6},{6,5},{7,7},{8,8},{9,10},{10,9... | collective-permute-start | bytes 718856 | tf_op jit(solution)/shard_map/ppermute | solution.py:46
  184.5 8.1 %collective-permute-start.27 = (bf16[216,384]{1,0:T(8,128)(2,1)S(1)}, bf16[216,384]{1,0:T(8,128)(2,1)S(1)}, u32[]{:S(2)}, u32[]{:S(2)}) collective-permute-start(bf16[216,384]{1,0:T(8,128)(2,1)S(1)} %get-tuple-element.104), channel_id=1, source_target_pairs={{0,64},{1,66},{2,65},{3,67},{4,68},{5,70},{6,69},{7,71},{8,72},{9,... | collective-permute-start | bytes 497672 | tf_op jit(solution)/shard_map/ppermute | solution.py:46
  187.6 9.3 %collective-permute-start.28 = (bf16[216,384]{1,0:T(8,128)(2,1)S(1)}, bf16[216,384]{1,0:T(8,128)(2,1)S(1)}, u32[]{:S(2)}, u32[]{:S(2)}) collective-permute-start(bf16[216,384]{1,0:T(8,128)(2,1)S(1)} %get-tuple-element.104), channel_id=1, source_target_pairs={{0,66},{1,64},{2,67},{3,65},{4,70},{5,68},{6,71},{7,69},{8,74},{9,... | collective-permute-start | bytes 497672 | tf_op jit(solution)/shard_map/ppermute | solution.py:46
  (17 other events, 128.0 us)

commit v7 on v6

--- a/solution.py
+++ b/solution.py
@@ -181,7 +181,7 @@
 def on_core(kernel, outs, scratch, count, flops, *operands):
     def place(v):
         if v.ndim == 4:
-            return pl.BlockSpec(memory_space=pl.ANY)
+            return pl.BlockSpec(memory_space=pltpu.HBM)
         if v.ndim == 1:
             return pl.BlockSpec(memory_space=pltpu.SMEM)
         return pl.BlockSpec(memory_space=pltpu.VMEM)
@@ -355,34 +355,33 @@
     got2 = give(part2_z, z % 2, ALONG_Z[1], 2)
     gb0, part2_z = lax.optimization_barrier((gb0, part2_z))
     half0 = conv_grad(0, gb0[64:320])
+    got0 = give(half0, xl, ALONG_X)
+    half0, half1, head_half, part2_z = lax.optimization_barrier((half0, half1, head_half, part2_z))
     head_x = take(head_half, head_got, xl)
-    head_rows = jnp.pad(head_x, ((0, 0), (0, 128))).reshape(16, 24, 1536)
-    half0 = half0.reshape(2, 16, 72, 384)
-    late = jnp.concatenate(
-        [half0[0], half0[1]] + [head_rows[..., 384 * k : 384 * k + 384] for k in range(4)], axis=1
-    )
-    late, half1, part2_z = lax.optimization_barrier((late, half1, part2_z))
-    late = plane_sum(late)
+    head_x, half1, part2_z = lax.optimization_barrier((head_x, half1, part2_z))
+    head_plane = plane_sum(head_x.reshape(16, 24, 1408))
     keep1 = jnp.stack([pick(half1, z, 1), pick(half1, z ^ 3, 1)])
     keep1 = (keep1.astype(F32) + got1.astype(F32)).astype(BF)
     got1 = send(keep1[1], ALONG_Z[3])
+    keep1, gb0 = lax.optimization_barrier((keep1, gb0))
+    g0 = g1 + through(trunk[0], conv_back(gb0, conv_weight[0], 64, 256))
+    g0, half0, head_plane = lax.optimization_barrier((g0, half0, head_plane))
+    plane0 = plane_sum(take(half0, got0, xl).reshape(16, 72, 384))
     part1 = (keep1[0].astype(F32) + got1.astype(F32)).astype(BF)
     part2 = take(part2_z, got2, z % 2)
-    g0 = g1 + through(trunk[0], conv_back(gb0, conv_weight[0], 64, 256))
-    g0 = lax.optimization_barrier(g0)
     early = jnp.concatenate([part1.reshape(2, 4, 72, 384), part2.reshape(2, 4, 72, 384)], axis=2)
     got = [send(pick(early, y ^ k, 1), ALONG_Y[k]) for k in (1, 3, 2)]
     early = sum((g.astype(F32) for g in got), pick(early, y, 1).astype(F32)).astype(BF)
-    both = jnp.concatenate([late[:144].reshape(2, 72, 384), early], axis=1)
-    conv_sum, head_sum = last_sum(
-        jnp.concatenate([pick(both, xl), late[144:]], axis=0), pick(both, 1 - xl)
-    )
+    head_plane = jnp.pad(head_plane, ((0, 0), (0, 128)))
+    near = [pick(early, xl), plane0] + [head_plane[:, 384 * k : 384 * k + 384] for k in range(4)]
+    early, late = last_sum(jnp.concatenate(near, axis=0), pick(early, 1 - xl))
+    conv_sum, head_sum = [late[:72], early[:72], early[72:]], late[72:]
 
     def own(v):
         half = v.shape[0] // 2
         return jnp.where(c == 0, v[:half], v[half:])
 
-    conv_total = jnp.stack([own(conv_sum[72 * k : 72 * k + 72]) for k in range(LAYERS)])
+    conv_total = jnp.stack([own(v) for v in conv_sum])
     head_total = jnp.concatenate([own(head_sum[24 * k : 24 * k + 24]) for k in range(4)], axis=1)
     low = head_total[:, :1344]
     high = head_total[:, 64:1408]

time: 203 us -> 204 us (level)
  the two profiles are of different devices: /device:TPU:1 before, /device:TPU:7 now
where the time goes in v7:
time: 204 us; the launch traced here: 203 us
  starting transfers between devices  63.5 us (31%)
  waiting for transfers between devices  57.4 us (28%)
  other arithmetic  24.7 us (12%)
  matrix products  24.2 us (12%)
  Pallas kernels  15 us (7%)
  local copies, waits for them, and re-layouts  14 us (7%)
  between operations  4.51 us (2%)
    ppermute x30, waiting for transfers between devices, send(): return lax.ppermute(v, AXES, pairs)  57.4 us
    ppermute x30, starting transfers between devices, send(): return lax.ppermute(v, AXES, pairs)  51.9 us
    pallas_call x4, Pallas kernels, on_core(): pl.pallas_call(kernel, out_shape=[jax.ShapeDtypeStruct((rows, 768), kind)...  15 us
    all_to_all x2, starting transfers between devices, plane_sum(): got = lax.all_to_all(blocks, ('z', 'y'), 0, 0, tiled=True)  11.6 us
    unnamed x37, local copies, waits for them, and re-layouts  9.21 us
    dot_general x10, matrix products, pair_dot(): jnp.dot(far_a.T, far_b, preferred_element_type=F32)  7.3 us
    dot_general x1, matrix products, per_device(): logits = jnp.dot(stream, head_weight, preferred_element_type=F32)  5.82 us
    convert_element_type x3, other arithmetic, take(): return total.astype(BF).reshape(rows // 2, lanes)  4.86 us
  transfers between devices with their start and end apart: 32, of which 10 were waited for; matrix products, arithmetic and copies ran while one was open for 25% of the time, Pallas kernels for 3%

profile of v7, /device:TPU:7, one launch (start us, length us, event | category | flops | bytes accessed | tf_op | source)
XLA Modules:
  0.0 203.2 jit_solution(8380695739956360460)
XLA Ops:
  1.8 3.8 %collective-permute-start = (bf16[192,768]{1,0:T(8,128)(2,1)S(1)}, bf16[192,768]{1,0:T(8,128)(2,1)S(1)}, u32[]{:S(2)}, u32[]{:S(2)}) collective-permute-start(bf16[192,768]{1,0:T(8,128)(2,1)S(1)} %get-tuple-element.116), channel_id=1, source_target_pairs={{2,4},{3,5},{6,8},{7,9},{10,12},{11,13},{14,16},{15,17},{18,20},{1... | collective-permute-start | bytes 884744 | tf_op jit(solution)/shard_map/ppermute | solution.py:46
  5.6 5.1 %collective-permute-start.1 = (bf16[192,768]{1,0:T(8,128)(2,1)S(1)}, bf16[192,768]{1,0:T(8,128)(2,1)S(1)}, u32[]{:S(2)}, u32[]{:S(2)}) collective-permute-start(bf16[192,768]{1,0:T(8,128)(2,1)S(1)} %get-tuple-element.115), channel_id=1, source_target_pairs={{0,2},{1,3},{2,0},{3,1},{4,6},{5,7},{6,4},{7,5},{8,10},{9,11},{10,... | collective-permute-start | bytes 884744 | tf_op jit(solution)/shard_map/ppermute | solution.py:46
  11.9 4.0 %copy-done = bf16[3,3,768,768]{3,2,1,0:T(8,128)(2,1)S(1)} copy-done((bf16[3,3,768,768]{3,2,1,0:T(8,128)(2,1)S(1)}, bf16[3,3,768,768]{3,2,1,0:T(8,128)(2,1)}, u32[]{:S(2)}) %copy-start) | copy-done | bytes 10616856
  15.9 6.7 %shard_map.93 = (bf16[384,768]{1,0:T(8,128)(2,1)S(1)}, bf16[512,768]{1,0:T(8,128)(2,1)S(1)}, bf16[512,768]{1,0:T(8,128)(2,1)S(1)}, bf16[256,768]{1,0:T(8,128)(2,1)S(1)}, bf16[256,768]{1,0:T(8,128)(2,1)S(1)}) custom-call(s32[2]{0:T(128)S(1)} %add_convert_fusion.1.flags, bf16[192,768]{1,0:T(8,128)(2,1)S(1)} %get-tuple-element.104.before, ...), custom_call_target="tpu_custom_call" | custom-call | flops 2717908992 | bytes 7077888 | tf_op jit(solution)/shard_map/pallas_call | solution.py:189
  22.7 3.2 %collective-permute-start.5 = (bf16[512,768]{1,0:T(8,128)(2,1)S(1)}, bf16[512,768]{1,0:T(8,128)(2,1)}, u32[]{:S(2)}, u32[]{:S(2)}) collective-permute-start(bf16[512,768]{1,0:T(8,128)(2,1)S(1)} %get-tuple-element.45), channel_id=1, source_target_pairs={{0,2},{1,3},{2,0},{3,1},{4,6},{5,7},{6,4},{7,5},{8,10},{9,11},{10,... | collective-permute-start | bytes 2359304 | tf_op jit(solution)/shard_map/ppermute | solution.py:46
  27.8 6.0 %collective-permute-start.3 = (bf16[256,768]{1,0:T(8,128)(2,1)S(1)}, bf16[256,768]{1,0:T(8,128)(2,1)}, u32[]{:S(2)}, u32[]{:S(2)}) collective-permute-start(bf16[256,768]{1,0:T(8,128)(2,1)S(1)} %get-tuple-element.44.own), channel_id=1, source_target_pairs={{0,2},{1,3},{2,0},{3,1},{4,6},{5,7},{6,4},{7,5},{8,10},{9,11},{10,... | collective-permute-start | bytes 1179656 | tf_op jit(solution)/shard_map/ppermute | solution.py:46
  36.6 4.0 %copy-done.1 = bf16[3,3,768,768]{3,2,1,0:T(8,128)(2,1)S(1)} copy-done((bf16[3,3,768,768]{3,2,1,0:T(8,128)(2,1)S(1)}, bf16[3,3,768,768]{3,2,1,0:T(8,128)(2,1)}, u32[]{:S(2)}) %copy-start.1) | copy-done | bytes 10616856
  42.5 4.0 %collective-permute-start.6 = (bf16[768,768]{1,0:T(8,128)(2,1)S(1)}, bf16[768,768]{1,0:T(8,128)(2,1)S(1)}, u32[]{:S(2)}, u32[]{:S(2)}) collective-permute-start(bf16[768,768]{1,0:T(8,128)(2,1)S(1)} %get-tuple-element.49), channel_id=1, source_target_pairs={{0,2},{1,3},{2,0},{3,1},{4,6},{5,7},{6,4},{7,5},{8,10},{9,11},{10,... | collective-permute-start | bytes 3538952 | tf_op jit(solution)/shard_map/ppermute | solution.py:46
  46.6 5.8 %fusion.5 = (f32[]{:T(128)}, bf16[256,2688]{1,0:T(8,128)(2,1)S(1)}) fusion(s32[1,256,2688]{2,1,0:T(8,128)} %param.9, f32[256]{0:T(256)S(1)} %bitcast.154, bf16[256,768]{1,0:T(8,128)(2,1)S(1)} %get-tuple-element.48, bf16[768,2688]{1,0:T(8,128)(2,1)S(1)} %copy-done.15), kind=kOutput, calls=%fused_computation.9 | convolution fusion | flops 1070039040 | bytes 8651780 | tf_op jit(solution)/shard_map/dot_general | solution.py:278
  53.8 1.9 collective-permute-start.8
  55.8 6.4 %collective-permute-start.9 = (bf16[256,768]{1,0:T(8,128)(2,1)S(1)}, bf16[256,768]{1,0:T(8,128)(2,1)S(1)}, u32[]{:S(2)}, u32[]{:S(2)}) collective-permute-start(bf16[256,768]{1,0:T(8,128)(2,1)S(1)} %get-tuple-element.51.own), channel_id=1, source_target_pairs={{0,2},{1,3},{2,0},{3,1},{4,6},{5,7},{6,4},{7,5},{8,10},{9,11},{10,... | collective-permute-start | bytes 1179656 | tf_op jit(solution)/shard_map/ppermute | solution.py:46
  73.6 2.1 %shard_map.95 = (f32[256,768]{1,0:T(8,128)S(1)}, bf16[256,768]{1,0:T(8,128)(2,1)S(1)}) custom-call(bf16[256,768]{1,0:T(8,128)(2,1)S(1)} %get-tuple-element.56.before, bf16[256,768]{1,0:T(8,128)(2,1)S(1)} %get-tuple-element.51.own, bf16[256,768]{1,0:T(8,128)(2,1)S(1)} %get-tuple-element.95.after, bf16[256,768]{1,0:T(8,128)(2,1)S(1)} %get-tuple-element.47.stream, ...), custom_call_target="tpu_custom_call" | custom-call | flops 905969664 | bytes 3538944 | tf_op jit(solution)/shard_map/pallas_call | solution.py:189
  87.8 4.1 %shard_map.96 = (f32[256,768]{1,0:T(8,128)S(1)}, bf16[384,768]{1,0:T(8,128)(2,1)S(1)}) custom-call(s32[2]{0:T(128)S(1)} %add_convert_fusion.1.flags, bf16[192,768]{1,0:T(8,128)(2,1)S(1)} %get-tuple-element.59.before, bf16[256,768]{1,0:T(8,128)(2,1)S(1)} %get-tuple-element.57.own, bf16[192,768]{1,0:T(8,128)(2,1)S(1)} %get-tuple-element.101.after, ...), custom_call_target="tpu_custom_call" | custom-call | flops 1358954496 | bytes 3538944 | tf_op jit(solution)/shard_map/pallas_call | solution.py:189
  92.0 5.5 %collective-permute-done.16 = bf16[2,576,384]{2,1,0:T(8,128)(2,1)} collective-permute-done((bf16[2,576,384]{2,1,0:T(8,128)(2,1)}, bf16[2,576,384]{2,1,0:T(8,128)(2,1)}, u32[]{:S(2)}, u32[]{:S(2)}) %collective-permute-start.16) | collective-permute-done | bytes 884768 | tf_op jit(solution)/shard_map/ppermute | solution.py:46
  108.5 7.6 %all-to-all-start = ((bf16[16,24,1408]{2,1,0:T(8,128)(2,1)}), bf16[16,24,1408]{2,1,0:T(8,128)(2,1)}, u32[]{:S(2)}, u32[]{:S(2)}) async-start(bf16[16,24,1408]{2,1,0:T(8,128)(2,1)} %bitcast.145), calls=%async_computation | async-start | bytes 2162688 | tf_op jit(solution)/shard_map/all_to_all | solution.py:226
  116.3 24.6 %collective-permute-done.21 = bf16[2,288,384]{2,1,0:T(8,128)(2,1)} collective-permute-done((bf16[2,288,384]{2,1,0:T(8,128)(2,1)}, bf16[2,288,384]{2,1,0:T(8,128)(2,1)}, u32[]{:S(2)}, u32[]{:S(2)}) %collective-permute-start.21) | collective-permute-done | bytes 442400 | tf_op jit(solution)/shard_map/ppermute | solution.py:46
  151.1 2.0 reduce_sum.62
  153.2 2.3 %fusion.8 = bf16[1,1152,384]{2,1,0:T(8,128)(2,1)} fusion(bf16[1,1152,384]{2,1,0:T(8,128)(2,1)} %collective-permute-done.25, bf16[1,2,1152,384]{3,2,1,0:T(8,128)(2,1)S(1)} %bitcast.144, s32[]{:T(128)S(6)} %select_n.275), kind=kLoop, calls=%fused_computation.17 | loop fusion | flops 1769472 | bytes 2654212 | tf_op jit(solution)/shard_map/convert_element_type | solution.py:222
  155.5 4.1 %all-to-all-start.1 = ((bf16[16,72,384]{2,1,0:T(8,128)(2,1)}), bf16[16,72,384]{2,1,0:T(8,128)(2,1)S(1)}, u32[]{:S(2)}, u32[]{:S(2)}) async-start(bf16[16,72,384]{2,1,0:T(8,128)(2,1)} %bitcast.47), calls=%async_computation.1 | async-start | bytes 1769472 | tf_op jit(solution)/shard_map/all_to_all | solution.py:226
  164.7 9.6 %collective-permute-done.22 = bf16[2,144,384]{2,1,0:T(8,128)(2,1)S(1)} collective-permute-done((bf16[2,144,384]{2,1,0:T(8,128)(2,1)S(1)}, bf16[2,144,384]{2,1,0:T(8,128)(2,1)S(1)}, u32[]{:S(2)}, u32[]{:S(2)}) %collective-permute-start.22) | collective-permute-done | bytes 221216 | tf_op jit(solution)/shard_map/ppermute | solution.py:46
  174.3 4.3 %collective-permute-done.23 = bf16[2,144,384]{2,1,0:T(8,128)(2,1)S(1)} collective-permute-done((bf16[2,144,384]{2,1,0:T(8,128)(2,1)S(1)}, bf16[2,144,384]{2,1,0:T(8,128)(2,1)S(1)}, u32[]{:S(2)}, u32[]{:S(2)}) %collective-permute-start.23) | collective-permute-done | bytes 221216 | tf_op jit(solution)/shard_map/ppermute | solution.py:46
  181.3 4.4 %collective-permute-start.27 = (bf16[312,384]{1,0:T(8,128)(2,1)S(1)}, bf16[312,384]{1,0:T(8,128)(2,1)S(1)}, u32[]{:S(2)}, u32[]{:S(2)}) collective-permute-start(bf16[312,384]{1,0:T(8,128)(2,1)S(1)} %fusion.88), channel_id=1, source_target_pairs={{0,2},{1,0},{2,3},{3,1},{4,6},{5,4},{6,7},{7,5},{8,10},{9,8},{10,1... | collective-permute-start | bytes 718856 | tf_op jit(solution)/shard_map/ppermute | solution.py:46
  185.8 2.8 %collective-permute-start.29 = (bf16[144,384]{1,0:T(8,128)(2,1)S(1)}, bf16[144,384]{1,0:T(8,128)(2,1)S(1)}, u32[]{:S(2)}, u32[]{:S(2)}) collective-permute-start(bf16[144,384]{1,0:T(8,128)(2,1)S(1)} %dynamic-slice_bitcast_fusion.8), channel_id=1, source_target_pairs={{0,66},{1,64},{2,67},{3,65},{4,70},{5,68},{6,71},{7,69},{8,74},{9,... | collective-permute-start | bytes 331784 | tf_op jit(solution)/shard_map/ppermute | solution.py:46
  188.6 8.3 %collective-permute-done.27 = bf16[312,384]{1,0:T(8,128)(2,1)S(1)} collective-permute-done((bf16[312,384]{1,0:T(8,128)(2,1)S(1)}, bf16[312,384]{1,0:T(8,128)(2,1)S(1)}, u32[]{:S(2)}, u32[]{:S(2)}) %collective-permute-start.27) | collective-permute-done | bytes 239648 | tf_op jit(solution)/shard_map/ppermute | solution.py:46
  (158 shorter events, 65.9 us)
Async XLA Ops:
  1.8 8.9 %collective-permute-start = (bf16[192,768]{1,0:T(8,128)(2,1)S(1)}, bf16[192,768]{1,0:T(8,128)(2,1)S(1)}, u32[]{:S(2)}, u32[]{:S(2)}) collective-permute-start(bf16[192,768]{1,0:T(8,128)(2,1)S(1)} %get-tuple-element.116), channel_id=1, source_target_pairs={{2,4},{3,5},{6,8},{7,9},{10,12},{11,13},{14,16},{15,17},{18,20},{1... | collective-permute-start | bytes 884744 | tf_op jit(solution)/shard_map/ppermute | solution.py:46
  22.7 13.9 %collective-permute-start.5 = (bf16[512,768]{1,0:T(8,128)(2,1)S(1)}, bf16[512,768]{1,0:T(8,128)(2,1)}, u32[]{:S(2)}, u32[]{:S(2)}) collective-permute-start(bf16[512,768]{1,0:T(8,128)(2,1)S(1)} %get-tuple-element.45), channel_id=1, source_target_pairs={{0,2},{1,3},{2,0},{3,1},{4,6},{5,7},{6,4},{7,5},{8,10},{9,11},{10,... | collective-permute-start | bytes 2359304 | tf_op jit(solution)/shard_map/ppermute | solution.py:46
  25.9 9.5 %collective-permute-start.2 = (bf16[256,768]{1,0:T(8,128)(2,1)S(1)}, bf16[256,768]{1,0:T(8,128)(2,1)}, u32[]{:S(2)}, u32[]{:S(2)}) collective-permute-start(bf16[256,768]{1,0:T(8,128)(2,1)S(1)} %get-tuple-element.44.own), channel_id=1, source_target_pairs={{2,4},{3,5},{6,8},{7,9},{10,12},{11,13},{14,16},{15,17},{18,20},{1... | collective-permute-start | bytes 1179656 | tf_op jit(solution)/shard_map/ppermute | solution.py:46
  42.5 10.0 %collective-permute-start.6 = (bf16[768,768]{1,0:T(8,128)(2,1)S(1)}, bf16[768,768]{1,0:T(8,128)(2,1)S(1)}, u32[]{:S(2)}, u32[]{:S(2)}) collective-permute-start(bf16[768,768]{1,0:T(8,128)(2,1)S(1)} %get-tuple-element.49), channel_id=1, source_target_pairs={{0,2},{1,3},{2,0},{3,1},{4,6},{5,7},{6,4},{7,5},{8,10},{9,11},{10,... | collective-permute-start | bytes 3538952 | tf_op jit(solution)/shard_map/ppermute | solution.py:46
  53.8 18.0 %collective-permute-start.8 = (bf16[256,768]{1,0:T(8,128)(2,1)S(1)}, bf16[256,768]{1,0:T(8,128)(2,1)S(1)}, u32[]{:S(2)}, u32[]{:S(2)}) collective-permute-start(bf16[256,768]{1,0:T(8,128)(2,1)S(1)} %get-tuple-element.51.own), channel_id=1, source_target_pairs={{2,4},{3,5},{6,8},{7,9},{10,12},{11,13},{14,16},{15,17},{18,20},{1... | collective-permute-start | bytes 1179656 | tf_op jit(solution)/shard_map/ppermute | solution.py:46
  55.8 16.1 %collective-permute-start.9 = (bf16[256,768]{1,0:T(8,128)(2,1)S(1)}, bf16[256,768]{1,0:T(8,128)(2,1)S(1)}, u32[]{:S(2)}, u32[]{:S(2)}) collective-permute-start(bf16[256,768]{1,0:T(8,128)(2,1)S(1)} %get-tuple-element.51.own), channel_id=1, source_target_pairs={{0,2},{1,3},{2,0},{3,1},{4,6},{5,7},{6,4},{7,5},{8,10},{9,11},{10,... | collective-permute-start | bytes 1179656 | tf_op jit(solution)/shard_map/ppermute | solution.py:46
  64.2 7.7 %collective-permute-start.11 = (bf16[256,1408]{1,0:T(8,128)(2,1)S(1)}, bf16[256,1408]{1,0:T(8,128)(2,1)S(1)}, u32[]{:S(2)}, u32[]{:S(2)}) collective-permute-start(bf16[256,1408]{1,0:T(8,128)(2,1)S(1)} %broadcast_select_fusion), channel_id=1, source_target_pairs={{0,2},{1,3},{2,0},{3,1},{4,6},{5,7},{6,4},{7,5},{8,10},{9,11},{10,... | collective-permute-start | bytes 2162696 | tf_op jit(solution)/shard_map/ppermute | solution.py:46
  71.8 25.6 %collective-permute-start.16 = (bf16[2,576,384]{2,1,0:T(8,128)(2,1)}, bf16[2,576,384]{2,1,0:T(8,128)(2,1)}, u32[]{:S(2)}, u32[]{:S(2)}) collective-permute-start(bf16[2,576,384]{2,1,0:T(8,128)(2,1)} %dynamic-slice_bitcast_fusion.2), channel_id=1, source_target_pairs={{0,48},{1,49},{2,50},{3,51},{4,52},{5,53},{6,54},{7,55},{8,56},{9,... | collective-permute-start | bytes 2654216 | tf_op jit(solution)/shard_map/ppermute | solution.py:46
  75.8 10.9 %collective-permute-start.13 = (bf16[192,768]{1,0:T(8,128)(2,1)S(1)}, bf16[192,768]{1,0:T(8,128)(2,1)S(1)}, u32[]{:S(2)}, u32[]{:S(2)}) collective-permute-start(bf16[192,768]{1,0:T(8,128)(2,1)S(1)} %get-tuple-element.110), channel_id=1, source_target_pairs={{2,4},{3,5},{6,8},{7,9},{10,12},{11,13},{14,16},{15,17},{18,20},{1... | collective-permute-start | bytes 884744 | tf_op jit(solution)/shard_map/ppermute | solution.py:46
  77.7 10.0 %collective-permute-start.14 = (bf16[192,768]{1,0:T(8,128)(2,1)S(1)}, bf16[192,768]{1,0:T(8,128)(2,1)S(1)}, u32[]{:S(2)}, u32[]{:S(2)}) collective-permute-start(bf16[192,768]{1,0:T(8,128)(2,1)S(1)} %get-tuple-element.109), channel_id=1, source_target_pairs={{0,2},{1,3},{2,0},{3,1},{4,6},{5,7},{6,4},{7,5},{8,10},{9,11},{10,... | collective-permute-start | bytes 884744 | tf_op jit(solution)/shard_map/ppermute | solution.py:46
  79.7 27.5 %collective-permute-start.18 = (bf16[1,384,1408]{2,1,0:T(8,128)(2,1)S(1)}, bf16[1,384,1408]{2,1,0:T(8,128)(2,1)S(1)}, u32[]{:S(2)}, u32[]{:S(2)}) collective-permute-start(bf16[1,384,1408]{2,1,0:T(8,128)(2,1)S(1)} %dynamic-slice_bitcast_fusion), channel_id=1, source_target_pairs={{0,64},{1,65},{2,66},{3,67},{4,68},{5,69},{6,70},{7,71},{8,72},{9,... | collective-permute-start | bytes 3244040 | tf_op jit(solution)/shard_map/ppermute | solution.py:46
  101.2 40.8 %collective-permute-start.19 = (bf16[2,2,288,384]{3,2,1,0:T(8,128)(2,1)}, bf16[2,2,288,384]{3,2,1,0:T(8,128)(2,1)}, u32[]{:S(2)}, u32[]{:S(2)}) collective-permute-start(bf16[2,2,288,384]{3,2,1,0:T(8,128)(2,1)} %pad_maximum_fusion.3), channel_id=1, source_target_pairs={{0,16},{1,17},{2,18},{3,19},{4,20},{5,21},{6,22},{7,23},{8,24},{9,... | collective-permute-start | bytes 2654216 | tf_op jit(solution)/shard_map/ppermute | solution.py:46
  102.0 38.9 %collective-permute-start.21 = (bf16[2,288,384]{2,1,0:T(8,128)(2,1)}, bf16[2,288,384]{2,1,0:T(8,128)(2,1)}, u32[]{:S(2)}, u32[]{:S(2)}) collective-permute-start(bf16[2,288,384]{2,1,0:T(8,128)(2,1)} %dynamic-slice_bitcast_fusion.3), channel_id=1, source_target_pairs={{0,16},{1,17},{2,18},{3,19},{4,20},{5,21},{6,22},{7,23},{8,24},{9,... | collective-permute-start | bytes 1327112 | tf_op jit(solution)/shard_map/ppermute | solution.py:46
  107.2 46.0 %collective-permute-start.25 = (bf16[1,1152,384]{2,1,0:T(8,128)(2,1)}, bf16[1,1152,384]{2,1,0:T(8,128)(2,1)}, u32[]{:S(2)}, u32[]{:S(2)}) collective-permute-start(bf16[1,1152,384]{2,1,0:T(8,128)(2,1)} %dynamic-slice_bitcast_fusion.1), channel_id=1, source_target_pairs={{0,64},{1,65},{2,66},{3,67},{4,68},{5,69},{6,70},{7,71},{8,72},{9,... | collective-permute-start | bytes 2654216 | tf_op jit(solution)/shard_map/ppermute | solution.py:46
  108.5 42.6 %all-to-all-start = ((bf16[16,24,1408]{2,1,0:T(8,128)(2,1)}), bf16[16,24,1408]{2,1,0:T(8,128)(2,1)}, u32[]{:S(2)}, u32[]{:S(2)}) async-start(bf16[16,24,1408]{2,1,0:T(8,128)(2,1)} %bitcast.145), calls=%async_computation | async-start | bytes 2162688 | tf_op jit(solution)/shard_map/all_to_all | solution.py:226
  146.0 13.6 %collective-permute-start.20 = (bf16[2,288,384]{2,1,0:T(8,128)(2,1)}, bf16[2,288,384]{2,1,0:T(8,128)(2,1)}, u32[]{:S(2)}, u32[]{:S(2)}) collective-permute-start(bf16[2,288,384]{2,1,0:T(8,128)(2,1)} %slice_bitcast_fusion), channel_id=1, source_target_pairs={{0,48},{1,49},{2,50},{3,51},{4,52},{5,53},{6,54},{7,55},{8,56},{9,... | collective-permute-start | bytes 1327112 | tf_op jit(solution)/shard_map/ppermute | solution.py:46
  155.5 24.9 %all-to-all-start.1 = ((bf16[16,72,384]{2,1,0:T(8,128)(2,1)}), bf16[16,72,384]{2,1,0:T(8,128)(2,1)S(1)}, u32[]{:S(2)}, u32[]{:S(2)}) async-start(bf16[16,72,384]{2,1,0:T(8,128)(2,1)} %bitcast.47), calls=%async_computation.1 | async-start | bytes 1769472 | tf_op jit(solution)/shard_map/all_to_all | solution.py:226
  160.8 13.5 %collective-permute-start.22 = (bf16[2,144,384]{2,1,0:T(8,128)(2,1)S(1)}, bf16[2,144,384]{2,1,0:T(8,128)(2,1)S(1)}, u32[]{:S(2)}, u32[]{:S(2)}) collective-permute-start(bf16[2,144,384]{2,1,0:T(8,128)(2,1)S(1)} %get-tuple-element.92), channel_id=1, source_target_pairs={{0,4},{1,5},{2,6},{3,7},{4,0},{5,1},{6,2},{7,3},{8,12},{9,13},{10,... | collective-permute-start | bytes 663560 | tf_op jit(solution)/shard_map/ppermute | solution.py:46
  162.3 16.3 %collective-permute-start.23 = (bf16[2,144,384]{2,1,0:T(8,128)(2,1)S(1)}, bf16[2,144,384]{2,1,0:T(8,128)(2,1)S(1)}, u32[]{:S(2)}, u32[]{:S(2)}) collective-permute-start(bf16[2,144,384]{2,1,0:T(8,128)(2,1)S(1)} %get-tuple-element.93), channel_id=1, source_target_pairs={{0,12},{1,13},{2,14},{3,15},{4,8},{5,9},{6,10},{7,11},{8,4},{9,5},... | collective-permute-start | bytes 663560 | tf_op jit(solution)/shard_map/ppermute | solution.py:46
  164.1 16.2 %collective-permute-start.24 = (bf16[2,144,384]{2,1,0:T(8,128)(2,1)S(1)}, bf16[2,144,384]{2,1,0:T(8,128)(2,1)S(1)}, u32[]{:S(2)}, u32[]{:S(2)}) collective-permute-start(bf16[2,144,384]{2,1,0:T(8,128)(2,1)S(1)} %get-tuple-element.94), channel_id=1, source_target_pairs={{0,8},{1,9},{2,10},{3,11},{4,12},{5,13},{6,14},{7,15},{8,0},{9,1},... | collective-permute-start | bytes 663560 | tf_op jit(solution)/shard_map/ppermute | solution.py:46
  180.6 8.0 %collective-permute-start.26 = (bf16[312,384]{1,0:T(8,128)(2,1)S(1)}, bf16[312,384]{1,0:T(8,128)(2,1)S(1)}, u32[]{:S(2)}, u32[]{:S(2)}) collective-permute-start(bf16[312,384]{1,0:T(8,128)(2,1)S(1)} %fusion.88), channel_id=1, source_target_pairs={{0,0},{1,2},{2,1},{3,3},{4,4},{5,6},{6,5},{7,7},{8,8},{9,10},{10,9... | collective-permute-start | bytes 718856 | tf_op jit(solution)/shard_map/ppermute | solution.py:46
  181.3 15.6 %collective-permute-start.27 = (bf16[312,384]{1,0:T(8,128)(2,1)S(1)}, bf16[312,384]{1,0:T(8,128)(2,1)S(1)}, u32[]{:S(2)}, u32[]{:S(2)}) collective-permute-start(bf16[312,384]{1,0:T(8,128)(2,1)S(1)} %fusion.88), channel_id=1, source_target_pairs={{0,2},{1,0},{2,3},{3,1},{4,6},{5,4},{6,7},{7,5},{8,10},{9,8},{10,1... | collective-permute-start | bytes 718856 | tf_op jit(solution)/shard_map/ppermute | solution.py:46
  185.7 14.3 %collective-permute-start.28 = (bf16[144,384]{1,0:T(8,128)(2,1)S(1)}, bf16[144,384]{1,0:T(8,128)(2,1)S(1)}, u32[]{:S(2)}, u32[]{:S(2)}) collective-permute-start(bf16[144,384]{1,0:T(8,128)(2,1)S(1)} %dynamic-slice_bitcast_fusion.8), channel_id=1, source_target_pairs={{0,64},{1,66},{2,65},{3,67},{4,68},{5,70},{6,69},{7,71},{8,72},{9,... | collective-permute-start | bytes 331784 | tf_op jit(solution)/shard_map/ppermute | solution.py:46
  185.8 14.2 %collective-permute-start.29 = (bf16[144,384]{1,0:T(8,128)(2,1)S(1)}, bf16[144,384]{1,0:T(8,128)(2,1)S(1)}, u32[]{:S(2)}, u32[]{:S(2)}) collective-permute-start(bf16[144,384]{1,0:T(8,128)(2,1)S(1)} %dynamic-slice_bitcast_fusion.8), channel_id=1, source_target_pairs={{0,66},{1,64},{2,67},{3,65},{4,70},{5,68},{6,71},{7,69},{8,74},{9,... | collective-permute-start | bytes 331784 | tf_op jit(solution)/shard_map/ppermute | solution.py:46
  (24 other events, 192.1 us)

commit v8 on v7

--- a/solution.py
+++ b/solution.py
@@ -158,26 +158,6 @@
         out_bf[:, cols] = total.astype(BF)
 
 
-def back1_kernel(flags, before, own, after, stream, grad, w_ref, out, out_bf, wide, g_in, weights, sems):
-    made = copies_in(w_ref, weights, sems, (1,))
-    wide[0:192, :] = before[...]
-    wide[192:448, :] = own[...]
-    wide[448:640, :] = after[...]
-    g_in[0:64, :] = before[128:192, :].astype(F32)
-    g_in[64:320, :] = grad[...]
-    g_in[320:384, :] = after[0:64, :].astype(F32)
-    for tap in (1, 0, 2):
-        made[0, tap].wait()
-    for start in (0, 192):
-        for cols in COLS:
-            act_grad = three_taps(wide, weights, 0, 128, start, 192, cols, True)
-            slope = tanh_gelu_slope(stream[start + 64 : start + 256, cols].astype(F32))
-            total = g_in[start : start + 192, cols] + slope * act_grad
-            g_in[start : start + 192, cols] = total
-            out_bf[start : start + 192, cols] = zero_outside(total, flags, start, 64, 384).astype(BF)
-    out[...] = g_in[64:320, :]
-
-
 def on_core(kernel, outs, scratch, count, flops, *operands):
     def place(v):
         if v.ndim == 4:
@@ -240,6 +220,11 @@
     bin_weight = jnp.where(error_mask == 1, upweight, 1).astype(F32).reshape(positions, 1)
     weight_part = jnp.sum(bin_weight)
     first, last = (xl + z + y + c == 0), (xl == 1) & (z == 3) & (y == 3) & (c == 1)
+
+    def inside(v, width):
+        row = lax.broadcasted_iota(jnp.int32, (v.shape[0], 1), 0)
+        out = (first & (row < width)) | (last & (row >= v.shape[0] - width))
+        return jnp.where(out, jnp.zeros_like(v), v)
 
     def conv_back(rows, weights, d, count):
         total = jnp.dot(rows[d : d + count], weights[1].T, preferred_element_type=F32)
@@ -343,14 +328,11 @@
     half1 = half1.reshape(2, 4, 288, 384)
     got1 = send(jnp.stack([pick(half1, z ^ 1, 1), pick(half1, z ^ 2, 1)]), ALONG_Z[1])
     before, half1 = lax.optimization_barrier((before, half1))
-    g1, gb0 = on_core(
-        back1_kernel,
-        [(256, F32), (384, BF)],
-        [(640, BF), (384, F32)],
-        1,
-        384 * tap_flops,
-        *(flags, before, gb1, after, wide1, g2, conv_weight),
-    )
+    wide = jnp.concatenate([before, gb1, after], axis=0)
+    g_in = jnp.concatenate([before[128:].astype(F32), g2, after[:64].astype(F32)], axis=0)
+    g1 = g_in + through(wide1[64:448], conv_back(wide, conv_weight[1], 128, 384))
+    gb0 = inside(g1.astype(BF), 64)
+    g1 = g1[64:320]
     part2_z = take(half2, got2, z // 2)
     got2 = give(part2_z, z % 2, ALONG_Z[1], 2)
     gb0, part2_z = lax.optimization_barrier((gb0, part2_z))
@@ -360,17 +342,17 @@
     head_x = take(head_half, head_got, xl)
     head_x, half1, part2_z = lax.optimization_barrier((head_x, half1, part2_z))
     head_plane = plane_sum(head_x.reshape(16, 24, 1408))
+    g0 = g1 + through(trunk[0], conv_back(gb0, conv_weight[0], 64, 256))
+    g0, half1, part2_z = lax.optimization_barrier((g0, half1, part2_z))
     keep1 = jnp.stack([pick(half1, z, 1), pick(half1, z ^ 3, 1)])
     keep1 = (keep1.astype(F32) + got1.astype(F32)).astype(BF)
     got1 = send(keep1[1], ALONG_Z[3])
-    keep1, gb0 = lax.optimization_barrier((keep1, gb0))
-    g0 = g1 + through(trunk[0], conv_back(gb0, conv_weight[0], 64, 256))
-    g0, half0, head_plane = lax.optimization_barrier((g0, half0, head_plane))
-    plane0 = plane_sum(take(half0, got0, xl).reshape(16, 72, 384))
+    part2 = take(part2_z, got2, z % 2)
     part1 = (keep1[0].astype(F32) + got1.astype(F32)).astype(BF)
-    part2 = take(part2_z, got2, z % 2)
     early = jnp.concatenate([part1.reshape(2, 4, 72, 384), part2.reshape(2, 4, 72, 384)], axis=2)
     got = [send(pick(early, y ^ k, 1), ALONG_Y[k]) for k in (1, 3, 2)]
+    half0, head_plane, early = lax.optimization_barrier((half0, head_plane, early))
+    plane0 = plane_sum(take(half0, got0, xl).reshape(16, 72, 384))
     early = sum((g.astype(F32) for g in got), pick(early, y, 1).astype(F32)).astype(BF)
     head_plane = jnp.pad(head_plane, ((0, 0), (0, 128)))
     near = [pick(early, xl), plane0] + [head_plane[:, 384 * k : 384 * k + 384] for k in range(4)]

time: 204 us -> 195 us (0.956)
  the two profiles are of different devices: /device:TPU:7 before, /device:TPU:1 now
where the time goes in v8:
time: 195 us; the launch traced here: 194 us
  starting transfers between devices  64.1 us (33%)
  waiting for transfers between devices  53.4 us (27%)
  other arithmetic  24.4 us (13%)
  matrix products  22.8 us (12%)
  local copies, waits for them, and re-layouts  13.6 us (7%)
  Pallas kernels  10.8 us (6%)
  between operations  4.64 us (2%)
    ppermute x30, starting transfers between devices, send(): return lax.ppermute(v, AXES, pairs)  55.1 us
    ppermute x30, waiting for transfers between devices, send(): return lax.ppermute(v, AXES, pairs)  53.4 us
    pallas_call x3, Pallas kernels, on_core(): pl.pallas_call(kernel, out_shape=[jax.ShapeDtypeStruct((rows, 768), kind)...  10.8 us
    unnamed x35, local copies, waits for them, and re-layouts  9.72 us
    all_to_all x2, starting transfers between devices, plane_sum(): got = lax.all_to_all(blocks, ('z', 'y'), 0, 0, tiled=True)  9.07 us
    dot_general x10, matrix products, pair_dot(): jnp.dot(far_a.T, far_b, preferred_element_type=F32)  7.3 us
    convert_element_type x3, other arithmetic, take(): return total.astype(BF).reshape(rows // 2, lanes)  4.89 us
    dot_general x1, matrix products, per_device(): logits = jnp.dot(stream, head_weight, preferred_element_type=F32)  4.48 us
  transfers between devices with their start and end apart: 32, of which 9 were waited for; matrix products, arithmetic and copies ran while one was open for 24% of the time, Pallas kernels for 1%

profile of v8, /device:TPU:1, one launch (start us, length us, event | category | flops | bytes accessed | tf_op | source)
XLA Modules:
  0.0 193.8 jit_solution(9181165112237276099)
XLA Ops:
  1.8 4.6 %collective-permute-start = (bf16[192,768]{1,0:T(8,128)(2,1)S(1)}, bf16[192,768]{1,0:T(8,128)(2,1)S(1)}, u32[]{:S(2)}, u32[]{:S(2)}) collective-permute-start(bf16[192,768]{1,0:T(8,128)(2,1)S(1)} %get-tuple-element.114), channel_id=1, source_target_pairs={{2,4},{3,5},{6,8},{7,9},{10,12},{11,13},{14,16},{15,17},{18,20},{1... | collective-permute-start | bytes 884744 | tf_op jit(solution)/shard_map/ppermute | solution.py:46
  6.6 4.2 %collective-permute-done = bf16[192,768]{1,0:T(8,128)(2,1)S(1)} collective-permute-done((bf16[192,768]{1,0:T(8,128)(2,1)S(1)}, bf16[192,768]{1,0:T(8,128)(2,1)S(1)}, u32[]{:S(2)}, u32[]{:S(2)}) %collective-permute-start) | collective-permute-done | bytes 294944 | tf_op jit(solution)/shard_map/ppermute | solution.py:46
  10.9 4.0 %copy-done = bf16[3,3,768,768]{3,2,1,0:T(8,128)(2,1)S(1)} copy-done((bf16[3,3,768,768]{3,2,1,0:T(8,128)(2,1)S(1)}, bf16[3,3,768,768]{3,2,1,0:T(8,128)(2,1)}, u32[]{:S(2)}) %copy-start) | copy-done | bytes 10616856
  14.9 6.7 %shard_map.93 = (bf16[384,768]{1,0:T(8,128)(2,1)S(1)}, bf16[512,768]{1,0:T(8,128)(2,1)S(1)}, bf16[512,768]{1,0:T(8,128)(2,1)S(1)}, bf16[256,768]{1,0:T(8,128)(2,1)S(1)}, bf16[256,768]{1,0:T(8,128)(2,1)S(1)}) custom-call(s32[2]{0:T(128)S(1)} %add_convert_fusion.1.flags, bf16[192,768]{1,0:T(8,128)(2,1)S(1)} %get-tuple-element.102.before, ...), custom_call_target="tpu_custom_call" | custom-call | flops 2717908992 | bytes 7077888 | tf_op jit(solution)/shard_map/pallas_call | solution.py:169
  21.8 3.7 %collective-permute-start.2 = (bf16[256,768]{1,0:T(8,128)(2,1)S(1)}, bf16[256,768]{1,0:T(8,128)(2,1)S(1)}, u32[]{:S(2)}, u32[]{:S(2)}) collective-permute-start(bf16[256,768]{1,0:T(8,128)(2,1)S(1)} %get-tuple-element.43.own), channel_id=1, source_target_pairs={{2,4},{3,5},{6,8},{7,9},{10,12},{11,13},{14,16},{15,17},{18,20},{1... | collective-permute-start | bytes 1179656 | tf_op jit(solution)/shard_map/ppermute | solution.py:46
  26.8 4.1 %collective-permute-done.2 = bf16[256,768]{1,0:T(8,128)(2,1)S(1)} collective-permute-done((bf16[256,768]{1,0:T(8,128)(2,1)S(1)}, bf16[256,768]{1,0:T(8,128)(2,1)S(1)}, u32[]{:S(2)}, u32[]{:S(2)}) %collective-permute-start.2) | collective-permute-done | bytes 393248 | tf_op jit(solution)/shard_map/ppermute | solution.py:46
  31.0 4.0 %copy-done.1 = bf16[3,3,768,768]{3,2,1,0:T(8,128)(2,1)S(1)} copy-done((bf16[3,3,768,768]{3,2,1,0:T(8,128)(2,1)S(1)}, bf16[3,3,768,768]{3,2,1,0:T(8,128)(2,1)}, u32[]{:S(2)}) %copy-start.1) | copy-done | bytes 10616856
  38.0 4.5 %fusion.5 = (f32[]{:T(128)}, bf16[256,2688]{1,0:T(8,128)(2,1)S(1)}) fusion(s32[1,256,2688]{2,1,0:T(8,128)S(1)} %copy-done.14, f32[256]{0:T(256)S(1)} %bitcast.170, bf16[256,768]{1,0:T(8,128)(2,1)S(1)} %get-tuple-element.47, bf16[768,2688]{1,0:T(8,128)(2,1)S(1)} %copy-done.13), kind=kOutput, calls=%fused_computation.9 | convolution fusion | flops 1070039040 | bytes 8651780 | tf_op jit(solution)/shard_map/dot_general | solution.py:263
  43.9 3.6 %collective-permute-start.8 = (bf16[256,768]{1,0:T(8,128)(2,1)S(1)}, bf16[256,768]{1,0:T(8,128)(2,1)S(1)}, u32[]{:S(2)}, u32[]{:S(2)}) collective-permute-start(bf16[256,768]{1,0:T(8,128)(2,1)S(1)} %get-tuple-element.50.own), channel_id=1, source_target_pairs={{2,4},{3,5},{6,8},{7,9},{10,12},{11,13},{14,16},{15,17},{18,20},{1... | collective-permute-start | bytes 1179656 | tf_op jit(solution)/shard_map/ppermute | solution.py:46
  57.6 8.8 %collective-permute-start.16 = (bf16[2,576,384]{2,1,0:T(8,128)(2,1)}, bf16[2,576,384]{2,1,0:T(8,128)(2,1)}, u32[]{:S(2)}, u32[]{:S(2)}) collective-permute-start(bf16[2,576,384]{2,1,0:T(8,128)(2,1)} %dynamic-slice_bitcast_fusion.2), channel_id=1, source_target_pairs={{0,48},{1,49},{2,50},{3,51},{4,52},{5,53},{6,54},{7,55},{8,56},{9,... | collective-permute-start | bytes 2654216 | tf_op jit(solution)/shard_map/ppermute | solution.py:46
  68.0 2.1 %shard_map.95 = (f32[256,768]{1,0:T(8,128)S(1)}, bf16[256,768]{1,0:T(8,128)(2,1)S(1)}) custom-call(bf16[256,768]{1,0:T(8,128)(2,1)S(1)} %get-tuple-element.55.before, bf16[256,768]{1,0:T(8,128)(2,1)S(1)} %get-tuple-element.50.own, bf16[256,768]{1,0:T(8,128)(2,1)S(1)} %get-tuple-element.93.after, bf16[256,768]{1,0:T(8,128)(2,1)S(1)} %get-tuple-element.46.stream, ...), custom_call_target="tpu_custom_call" | custom-call | flops 905969664 | bytes 3538944 | tf_op jit(solution)/shard_map/pallas_call | solution.py:169
  72.9 6.7 %collective-permute-start.18 = (bf16[1,384,1408]{2,1,0:T(8,128)(2,1)S(1)}, bf16[1,384,1408]{2,1,0:T(8,128)(2,1)S(1)}, u32[]{:S(2)}, u32[]{:S(2)}) collective-permute-start(bf16[1,384,1408]{2,1,0:T(8,128)(2,1)S(1)} %dynamic-slice_bitcast_fusion), channel_id=1, source_target_pairs={{0,64},{1,65},{2,66},{3,67},{4,68},{5,69},{6,70},{7,71},{8,72},{9,... | collective-permute-start | bytes 3244040 | tf_op jit(solution)/shard_map/ppermute | solution.py:46
  100.8 6.5 %collective-permute-start.25 = (bf16[1,1152,384]{2,1,0:T(8,128)(2,1)}, bf16[1,1152,384]{2,1,0:T(8,128)(2,1)}, u32[]{:S(2)}, u32[]{:S(2)}) collective-permute-start(bf16[1,1152,384]{2,1,0:T(8,128)(2,1)} %dynamic-slice_bitcast_fusion.1), channel_id=1, source_target_pairs={{0,64},{1,65},{2,66},{3,67},{4,68},{5,69},{6,70},{7,71},{8,72},{9,... | collective-permute-start | bytes 2654216 | tf_op jit(solution)/shard_map/ppermute | solution.py:46
  108.5 5.3 %all-to-all-start = ((bf16[16,24,1408]{2,1,0:T(8,128)(2,1)}), bf16[16,24,1408]{2,1,0:T(8,128)(2,1)}, u32[]{:S(2)}, u32[]{:S(2)}) async-start(bf16[16,24,1408]{2,1,0:T(8,128)(2,1)} %bitcast.160), calls=%async_computation | async-start | bytes 2162688 | tf_op jit(solution)/shard_map/all_to_all | solution.py:206
  116.5 2.6 %collective-permute-start.20 = (bf16[2,288,384]{2,1,0:T(8,128)(2,1)S(1)}, bf16[2,288,384]{2,1,0:T(8,128)(2,1)}, u32[]{:S(2)}, u32[]{:S(2)}) collective-permute-start(bf16[2,288,384]{2,1,0:T(8,128)(2,1)S(1)} %slice_bitcast_fusion), channel_id=1, source_target_pairs={{0,48},{1,49},{2,50},{3,51},{4,52},{5,53},{6,54},{7,55},{8,56},{9,... | collective-permute-start | bytes 1327112 | tf_op jit(solution)/shard_map/ppermute | solution.py:46
  120.3 19.1 %collective-permute-done.20 = bf16[2,288,384]{2,1,0:T(8,128)(2,1)} collective-permute-done((bf16[2,288,384]{2,1,0:T(8,128)(2,1)S(1)}, bf16[2,288,384]{2,1,0:T(8,128)(2,1)}, u32[]{:S(2)}, u32[]{:S(2)}) %collective-permute-start.20) | collective-permute-done | bytes 442400 | tf_op jit(solution)/shard_map/ppermute | solution.py:46
  143.7 2.3 %fusion.8 = bf16[1,1152,384]{2,1,0:T(8,128)(2,1)} fusion(bf16[1,1152,384]{2,1,0:T(8,128)(2,1)} %collective-permute-done.25, bf16[1,2,1152,384]{3,2,1,0:T(8,128)(2,1)S(1)} %bitcast.159, s32[]{:T(128)S(6)} %select_n.280), kind=kLoop, calls=%fused_computation.21 | loop fusion | flops 1769472 | bytes 2654212 | tf_op jit(solution)/shard_map/convert_element_type | solution.py:202
  146.0 3.8 %all-to-all-start.1 = ((bf16[16,72,384]{2,1,0:T(8,128)(2,1)}), bf16[16,72,384]{2,1,0:T(8,128)(2,1)S(1)}, u32[]{:S(2)}, u32[]{:S(2)}) async-start(bf16[16,72,384]{2,1,0:T(8,128)(2,1)} %bitcast.167), calls=%async_computation.1 | async-start | bytes 1769472 | tf_op jit(solution)/shard_map/all_to_all | solution.py:206
  153.7 11.9 %collective-permute-done.22 = bf16[2,144,384]{2,1,0:T(8,128)(2,1)S(1)} collective-permute-done((bf16[2,144,384]{2,1,0:T(8,128)(2,1)S(1)}, bf16[2,144,384]{2,1,0:T(8,128)(2,1)S(1)}, u32[]{:S(2)}, u32[]{:S(2)}) %collective-permute-start.22) | collective-permute-done | bytes 221216 | tf_op jit(solution)/shard_map/ppermute | solution.py:46
  165.6 2.5 %collective-permute-done.23 = bf16[2,144,384]{2,1,0:T(8,128)(2,1)S(1)} collective-permute-done((bf16[2,144,384]{2,1,0:T(8,128)(2,1)S(1)}, bf16[2,144,384]{2,1,0:T(8,128)(2,1)S(1)}, u32[]{:S(2)}, u32[]{:S(2)}) %collective-permute-start.23) | collective-permute-done | bytes 221216 | tf_op jit(solution)/shard_map/ppermute | solution.py:46
  168.1 3.8 %collective-permute-done.24 = bf16[2,144,384]{2,1,0:T(8,128)(2,1)S(1)} collective-permute-done((bf16[2,144,384]{2,1,0:T(8,128)(2,1)S(1)}, bf16[2,144,384]{2,1,0:T(8,128)(2,1)S(1)}, u32[]{:S(2)}, u32[]{:S(2)}) %collective-permute-start.24) | collective-permute-done | bytes 221216 | tf_op jit(solution)/shard_map/ppermute | solution.py:46
  173.2 6.3 %collective-permute-start.26 = (bf16[312,384]{1,0:T(8,128)(2,1)S(1)}, bf16[312,384]{1,0:T(8,128)(2,1)S(1)}, u32[]{:S(2)}, u32[]{:S(2)}) collective-permute-start(bf16[312,384]{1,0:T(8,128)(2,1)S(1)} %fusion.109), channel_id=1, source_target_pairs={{0,0},{1,2},{2,1},{3,3},{4,4},{5,6},{6,5},{7,7},{8,8},{9,10},{10,9... | collective-permute-start | bytes 718856 | tf_op jit(solution)/shard_map/ppermute | solution.py:46
  180.1 4.5 %collective-permute-done.26 = bf16[312,384]{1,0:T(8,128)(2,1)S(1)} collective-permute-done((bf16[312,384]{1,0:T(8,128)(2,1)S(1)}, bf16[312,384]{1,0:T(8,128)(2,1)S(1)}, u32[]{:S(2)}, u32[]{:S(2)}) %collective-permute-start.26) | collective-permute-done | bytes 239648 | tf_op jit(solution)/shard_map/ppermute | solution.py:46
  184.6 3.0 %collective-permute-done.27 = bf16[312,384]{1,0:T(8,128)(2,1)S(1)} collective-permute-done((bf16[312,384]{1,0:T(8,128)(2,1)S(1)}, bf16[312,384]{1,0:T(8,128)(2,1)S(1)}, u32[]{:S(2)}, u32[]{:S(2)}) %collective-permute-start.27) | collective-permute-done | bytes 239648 | tf_op jit(solution)/shard_map/ppermute | solution.py:46
  (161 shorter events, 60.7 us)
Async XLA Ops:
  1.8 9.0 %collective-permute-start = (bf16[192,768]{1,0:T(8,128)(2,1)S(1)}, bf16[192,768]{1,0:T(8,128)(2,1)S(1)}, u32[]{:S(2)}, u32[]{:S(2)}) collective-permute-start(bf16[192,768]{1,0:T(8,128)(2,1)S(1)} %get-tuple-element.114), channel_id=1, source_target_pairs={{2,4},{3,5},{6,8},{7,9},{10,12},{11,13},{14,16},{15,17},{18,20},{1... | collective-permute-start | bytes 884744 | tf_op jit(solution)/shard_map/ppermute | solution.py:46
  21.6 9.4 %collective-permute-start.5 = (bf16[512,768]{1,0:T(8,128)(2,1)S(1)}, bf16[512,768]{1,0:T(8,128)(2,1)}, u32[]{:S(2)}, u32[]{:S(2)}) collective-permute-start(bf16[512,768]{1,0:T(8,128)(2,1)S(1)} %get-tuple-element.44), channel_id=1, source_target_pairs={{0,2},{1,3},{2,0},{3,1},{4,6},{5,7},{6,4},{7,5},{8,10},{9,11},{10,... | collective-permute-start | bytes 2359304 | tf_op jit(solution)/shard_map/ppermute | solution.py:46
  21.8 9.1 %collective-permute-start.2 = (bf16[256,768]{1,0:T(8,128)(2,1)S(1)}, bf16[256,768]{1,0:T(8,128)(2,1)S(1)}, u32[]{:S(2)}, u32[]{:S(2)}) collective-permute-start(bf16[256,768]{1,0:T(8,128)(2,1)S(1)} %get-tuple-element.43.own), channel_id=1, source_target_pairs={{2,4},{3,5},{6,8},{7,9},{10,12},{11,13},{14,16},{15,17},{18,20},{1... | collective-permute-start | bytes 1179656 | tf_op jit(solution)/shard_map/ppermute | solution.py:46
  43.9 22.4 %collective-permute-start.8 = (bf16[256,768]{1,0:T(8,128)(2,1)S(1)}, bf16[256,768]{1,0:T(8,128)(2,1)S(1)}, u32[]{:S(2)}, u32[]{:S(2)}) collective-permute-start(bf16[256,768]{1,0:T(8,128)(2,1)S(1)} %get-tuple-element.50.own), channel_id=1, source_target_pairs={{2,4},{3,5},{6,8},{7,9},{10,12},{11,13},{14,16},{15,17},{18,20},{1... | collective-permute-start | bytes 1179656 | tf_op jit(solution)/shard_map/ppermute | solution.py:46
  47.6 18.7 %collective-permute-start.9 = (bf16[256,768]{1,0:T(8,128)(2,1)S(1)}, bf16[256,768]{1,0:T(8,128)(2,1)S(1)}, u32[]{:S(2)}, u32[]{:S(2)}) collective-permute-start(bf16[256,768]{1,0:T(8,128)(2,1)S(1)} %get-tuple-element.50.own), channel_id=1, source_target_pairs={{0,2},{1,3},{2,0},{3,1},{4,6},{5,7},{6,4},{7,5},{8,10},{9,11},{10,... | collective-permute-start | bytes 1179656 | tf_op jit(solution)/shard_map/ppermute | solution.py:46
  49.7 16.6 %collective-permute-start.11 = (bf16[256,1408]{1,0:T(8,128)(2,1)S(1)}, bf16[256,1408]{1,0:T(8,128)(2,1)S(1)}, u32[]{:S(2)}, u32[]{:S(2)}) collective-permute-start(bf16[256,1408]{1,0:T(8,128)(2,1)S(1)} %broadcast_select_fusion), channel_id=1, source_target_pairs={{0,2},{1,3},{2,0},{3,1},{4,6},{5,7},{6,4},{7,5},{8,10},{9,11},{10,... | collective-permute-start | bytes 2162696 | tf_op jit(solution)/shard_map/ppermute | solution.py:46
  57.6 32.0 %collective-permute-start.16 = (bf16[2,576,384]{2,1,0:T(8,128)(2,1)}, bf16[2,576,384]{2,1,0:T(8,128)(2,1)}, u32[]{:S(2)}, u32[]{:S(2)}) collective-permute-start(bf16[2,576,384]{2,1,0:T(8,128)(2,1)} %dynamic-slice_bitcast_fusion.2), channel_id=1, source_target_pairs={{0,48},{1,49},{2,50},{3,51},{4,52},{5,53},{6,54},{7,55},{8,56},{9,... | collective-permute-start | bytes 2654216 | tf_op jit(solution)/shard_map/ppermute | solution.py:46
  70.3 16.5 %collective-permute-start.13 = (bf16[192,768]{1,0:T(8,128)(2,1)S(1)}, bf16[192,768]{1,0:T(8,128)(2,1)S(1)}, u32[]{:S(2)}, u32[]{:S(2)}) collective-permute-start(bf16[192,768]{1,0:T(8,128)(2,1)S(1)} %get-tuple-element.107), channel_id=1, source_target_pairs={{2,4},{3,5},{6,8},{7,9},{10,12},{11,13},{14,16},{15,17},{18,20},{1... | collective-permute-start | bytes 884744 | tf_op jit(solution)/shard_map/ppermute | solution.py:46
  72.2 14.6 %collective-permute-start.14 = (bf16[192,768]{1,0:T(8,128)(2,1)S(1)}, bf16[192,768]{1,0:T(8,128)(2,1)S(1)}, u32[]{:S(2)}, u32[]{:S(2)}) collective-permute-start(bf16[192,768]{1,0:T(8,128)(2,1)S(1)} %get-tuple-element.108), channel_id=1, source_target_pairs={{0,2},{1,3},{2,0},{3,1},{4,6},{5,7},{6,4},{7,5},{8,10},{9,11},{10,... | collective-permute-start | bytes 884744 | tf_op jit(solution)/shard_map/ppermute | solution.py:46
  72.3 7.2 %collective-permute-start.15 = (bf16[256,384]{1,0:T(8,128)(2,1)S(1)}, bf16[256,384]{1,0:T(8,128)(2,1)S(1)}, u32[]{:S(2)}, u32[]{:S(2)}) collective-permute-start(bf16[256,384]{1,0:T(8,128)(2,1)S(1)} %get-tuple-element.110), channel_id=1, source_target_pairs={{0,2},{1,3},{2,0},{3,1},{4,6},{5,7},{6,4},{7,5},{8,10},{9,11},{10,... | collective-permute-start | bytes 589832 | tf_op jit(solution)/shard_map/ppermute | solution.py:46
  72.9 34.4 %collective-permute-start.18 = (bf16[1,384,1408]{2,1,0:T(8,128)(2,1)S(1)}, bf16[1,384,1408]{2,1,0:T(8,128)(2,1)S(1)}, u32[]{:S(2)}, u32[]{:S(2)}) collective-permute-start(bf16[1,384,1408]{2,1,0:T(8,128)(2,1)S(1)} %dynamic-slice_bitcast_fusion), channel_id=1, source_target_pairs={{0,64},{1,65},{2,66},{3,67},{4,68},{5,69},{6,70},{7,71},{8,72},{9,... | collective-permute-start | bytes 3244040 | tf_op jit(solution)/shard_map/ppermute | solution.py:46
  86.7 27.3 %collective-permute-start.19 = (bf16[2,2,288,384]{3,2,1,0:T(8,128)(2,1)}, bf16[2,2,288,384]{3,2,1,0:T(8,128)(2,1)}, u32[]{:S(2)}, u32[]{:S(2)}) collective-permute-start(bf16[2,2,288,384]{3,2,1,0:T(8,128)(2,1)} %pad_maximum_fusion.4), channel_id=1, source_target_pairs={{0,16},{1,17},{2,18},{3,19},{4,20},{5,21},{6,22},{7,23},{8,24},{9,... | collective-permute-start | bytes 2654216 | tf_op jit(solution)/shard_map/ppermute | solution.py:46
  93.8 25.3 %collective-permute-start.21 = (bf16[2,288,384]{2,1,0:T(8,128)(2,1)}, bf16[2,288,384]{2,1,0:T(8,128)(2,1)}, u32[]{:S(2)}, u32[]{:S(2)}) collective-permute-start(bf16[2,288,384]{2,1,0:T(8,128)(2,1)} %dynamic-slice_bitcast_fusion.3), channel_id=1, source_target_pairs={{0,16},{1,17},{2,18},{3,19},{4,20},{5,21},{6,22},{7,23},{8,24},{9,... | collective-permute-start | bytes 1327112 | tf_op jit(solution)/shard_map/ppermute | solution.py:46
  100.8 42.9 %collective-permute-start.25 = (bf16[1,1152,384]{2,1,0:T(8,128)(2,1)}, bf16[1,1152,384]{2,1,0:T(8,128)(2,1)}, u32[]{:S(2)}, u32[]{:S(2)}) collective-permute-start(bf16[1,1152,384]{2,1,0:T(8,128)(2,1)} %dynamic-slice_bitcast_fusion.1), channel_id=1, source_target_pairs={{0,64},{1,65},{2,66},{3,67},{4,68},{5,69},{6,70},{7,71},{8,72},{9,... | collective-permute-start | bytes 2654216 | tf_op jit(solution)/shard_map/ppermute | solution.py:46
  108.5 33.1 %all-to-all-start = ((bf16[16,24,1408]{2,1,0:T(8,128)(2,1)}), bf16[16,24,1408]{2,1,0:T(8,128)(2,1)}, u32[]{:S(2)}, u32[]{:S(2)}) async-start(bf16[16,24,1408]{2,1,0:T(8,128)(2,1)} %bitcast.160), calls=%async_computation | async-start | bytes 2162688 | tf_op jit(solution)/shard_map/all_to_all | solution.py:206
  116.5 23.0 %collective-permute-start.20 = (bf16[2,288,384]{2,1,0:T(8,128)(2,1)S(1)}, bf16[2,288,384]{2,1,0:T(8,128)(2,1)}, u32[]{:S(2)}, u32[]{:S(2)}) collective-permute-start(bf16[2,288,384]{2,1,0:T(8,128)(2,1)S(1)} %slice_bitcast_fusion), channel_id=1, source_target_pairs={{0,48},{1,49},{2,50},{3,51},{4,52},{5,53},{6,54},{7,55},{8,56},{9,... | collective-permute-start | bytes 1327112 | tf_op jit(solution)/shard_map/ppermute | solution.py:46
  146.0 26.9 %all-to-all-start.1 = ((bf16[16,72,384]{2,1,0:T(8,128)(2,1)}), bf16[16,72,384]{2,1,0:T(8,128)(2,1)S(1)}, u32[]{:S(2)}, u32[]{:S(2)}) async-start(bf16[16,72,384]{2,1,0:T(8,128)(2,1)} %bitcast.167), calls=%async_computation.1 | async-start | bytes 1769472 | tf_op jit(solution)/shard_map/all_to_all | solution.py:206
  149.9 15.7 %collective-permute-start.22 = (bf16[2,144,384]{2,1,0:T(8,128)(2,1)S(1)}, bf16[2,144,384]{2,1,0:T(8,128)(2,1)S(1)}, u32[]{:S(2)}, u32[]{:S(2)}) collective-permute-start(bf16[2,144,384]{2,1,0:T(8,128)(2,1)S(1)} %get-tuple-element.90), channel_id=1, source_target_pairs={{0,4},{1,5},{2,6},{3,7},{4,0},{5,1},{6,2},{7,3},{8,12},{9,13},{10,... | collective-permute-start | bytes 663560 | tf_op jit(solution)/shard_map/ppermute | solution.py:46
  151.3 16.8 %collective-permute-start.23 = (bf16[2,144,384]{2,1,0:T(8,128)(2,1)S(1)}, bf16[2,144,384]{2,1,0:T(8,128)(2,1)S(1)}, u32[]{:S(2)}, u32[]{:S(2)}) collective-permute-start(bf16[2,144,384]{2,1,0:T(8,128)(2,1)S(1)} %get-tuple-element.91), channel_id=1, source_target_pairs={{0,12},{1,13},{2,14},{3,15},{4,8},{5,9},{6,10},{7,11},{8,4},{9,5},... | collective-permute-start | bytes 663560 | tf_op jit(solution)/shard_map/ppermute | solution.py:46
  153.1 18.8 %collective-permute-start.24 = (bf16[2,144,384]{2,1,0:T(8,128)(2,1)S(1)}, bf16[2,144,384]{2,1,0:T(8,128)(2,1)S(1)}, u32[]{:S(2)}, u32[]{:S(2)}) collective-permute-start(bf16[2,144,384]{2,1,0:T(8,128)(2,1)S(1)} %get-tuple-element.92), channel_id=1, source_target_pairs={{0,8},{1,9},{2,10},{3,11},{4,12},{5,13},{6,14},{7,15},{8,0},{9,1},... | collective-permute-start | bytes 663560 | tf_op jit(solution)/shard_map/ppermute | solution.py:46
  173.2 11.4 %collective-permute-start.26 = (bf16[312,384]{1,0:T(8,128)(2,1)S(1)}, bf16[312,384]{1,0:T(8,128)(2,1)S(1)}, u32[]{:S(2)}, u32[]{:S(2)}) collective-permute-start(bf16[312,384]{1,0:T(8,128)(2,1)S(1)} %fusion.109), channel_id=1, source_target_pairs={{0,0},{1,2},{2,1},{3,3},{4,4},{5,6},{6,5},{7,7},{8,8},{9,10},{10,9... | collective-permute-start | bytes 718856 | tf_op jit(solution)/shard_map/ppermute | solution.py:46
  179.5 8.0 %collective-permute-start.27 = (bf16[312,384]{1,0:T(8,128)(2,1)S(1)}, bf16[312,384]{1,0:T(8,128)(2,1)S(1)}, u32[]{:S(2)}, u32[]{:S(2)}) collective-permute-start(bf16[312,384]{1,0:T(8,128)(2,1)S(1)} %fusion.109), channel_id=1, source_target_pairs={{0,2},{1,0},{2,3},{3,1},{4,6},{5,4},{6,7},{7,5},{8,10},{9,8},{10,1... | collective-permute-start | bytes 718856 | tf_op jit(solution)/shard_map/ppermute | solution.py:46
  179.6 11.0 %collective-permute-start.28 = (bf16[144,384]{1,0:T(8,128)(2,1)S(1)}, bf16[144,384]{1,0:T(8,128)(2,1)S(1)}, u32[]{:S(2)}, u32[]{:S(2)}) collective-permute-start(bf16[144,384]{1,0:T(8,128)(2,1)S(1)} %dynamic-slice_bitcast_fusion.8), channel_id=1, source_target_pairs={{0,64},{1,66},{2,65},{3,67},{4,68},{5,70},{6,69},{7,71},{8,72},{9,... | collective-permute-start | bytes 331784 | tf_op jit(solution)/shard_map/ppermute | solution.py:46
  179.7 10.9 %collective-permute-start.29 = (bf16[144,384]{1,0:T(8,128)(2,1)S(1)}, bf16[144,384]{1,0:T(8,128)(2,1)S(1)}, u32[]{:S(2)}, u32[]{:S(2)}) collective-permute-start(bf16[144,384]{1,0:T(8,128)(2,1)S(1)} %dynamic-slice_bitcast_fusion.8), channel_id=1, source_target_pairs={{0,66},{1,64},{2,67},{3,65},{4,70},{5,68},{6,71},{7,69},{8,74},{9,... | collective-permute-start | bytes 331784 | tf_op jit(solution)/shard_map/ppermute | solution.py:46
  (23 other events, 158.0 us)

commit v9 on v8

--- a/solution.py
+++ b/solution.py
@@ -173,7 +173,7 @@
         out_specs=[pl.BlockSpec(memory_space=pltpu.VMEM) for _ in outs],
         scratch_shapes=[pltpu.VMEM((rows, 768), kind) for rows, kind in scratch]
         + [pltpu.VMEM((count, 3, 768, 768), BF), pltpu.SemaphoreType.DMA((count, 3))],
-        compiler_params=pltpu.CompilerParams(vmem_limit_bytes=36 * 2**20),
+        compiler_params=pltpu.CompilerParams(vmem_limit_bytes=56 * 2**20),
         cost_estimate=pl.CostEstimate(
             flops=flops, bytes_accessed=count * 3 * 768 * 768 * 2, transcendentals=0
         ),
@@ -348,16 +348,23 @@
     keep1 = (keep1.astype(F32) + got1.astype(F32)).astype(BF)
     got1 = send(keep1[1], ALONG_Z[3])
     part2 = take(part2_z, got2, z % 2)
+    half0, head_plane = lax.optimization_barrier((half0, head_plane))
+    half0 = take(half0, got0, xl)
+    half0, keep1 = lax.optimization_barrier((half0, keep1))
+    plane0 = plane_sum(half0.reshape(16, 72, 384))
     part1 = (keep1[0].astype(F32) + got1.astype(F32)).astype(BF)
     early = jnp.concatenate([part1.reshape(2, 4, 72, 384), part2.reshape(2, 4, 72, 384)], axis=2)
     got = [send(pick(early, y ^ k, 1), ALONG_Y[k]) for k in (1, 3, 2)]
-    half0, head_plane, early = lax.optimization_barrier((half0, head_plane, early))
-    plane0 = plane_sum(take(half0, got0, xl).reshape(16, 72, 384))
     early = sum((g.astype(F32) for g in got), pick(early, y, 1).astype(F32)).astype(BF)
     head_plane = jnp.pad(head_plane, ((0, 0), (0, 128)))
-    near = [pick(early, xl), plane0] + [head_plane[:, 384 * k : 384 * k + 384] for k in range(4)]
-    early, late = last_sum(jnp.concatenate(near, axis=0), pick(early, 1 - xl))
-    conv_sum, head_sum = [late[:72], early[:72], early[72:]], late[72:]
+    head_plane = jnp.concatenate(
+        [head_plane[:, 384 * k : 384 * k + 384] for k in range(4)], axis=0
+    )
+    head_sum = sum(send(head_plane, last_hop(0, m)).astype(F32) for m in range(2))
+    early, late = last_sum(
+        jnp.concatenate([pick(early, xl), plane0], axis=0), pick(early, 1 - xl)
+    )
+    conv_sum = [late, early[:72], early[72:]]
 
     def own(v):
         half = v.shape[0] // 2

time: 195 us -> 189 us (0.969)
  waiting for transfers between devices: 53.4 us -> 37.6 us
  Pallas kernels: 10.8 us -> 20.2 us
  local copies, waits for them, and re-layouts: 13.6 us -> 6 us
  starting transfers between devices: 64.1 us -> 69.5 us
  other arithmetic: 24.4 us -> 26.9 us
    ppermute x30 -> x32, waiting for transfers between devices: 53.4 us -> 24.1 us  [send(): return lax.ppermute(v, AXES, pairs)]
    all_to_all x2, waiting for transfers between devices: 0.01 us -> 13.5 us  [plane_sum(): got = lax.all_to_all(blocks, ('z', 'y'), 0, 0, tiled=True)]
    pallas_call x3, Pallas kernels: 10.8 us -> 20.2 us  [on_core(): pl.pallas_call(kernel, out_shape=[jax.ShapeDtypeStruct((rows, 768), kind)...]
    unnamed x35 -> x44, local copies, waits for them, and re-layouts: 9.72 us -> 2.09 us
    ppermute x30 -> x32, starting transfers between devices: 55.1 us -> 59.5 us  [send(): return lax.ppermute(v, AXES, pairs)]
    dot_general x10, matrix products: 7.3 us -> 4.36 us  [pair_dot(): jnp.dot(far_a.T, far_b, preferred_element_type=F32)]
    convert_element_type x3 -> x2, other arithmetic: 4.89 us -> 2.13 us  [take(): return total.astype(BF).reshape(rows // 2, lanes)]
    select_n x4, other arithmetic: 0.2 us -> 2.83 us  [edges(): return (jnp.where(c == 0, outer, inner), jnp.where(c == 0, inner, outer))]
  transfers between devices with their start and end apart: 32 -> 34, of which waited for: 9 -> 10; matrix products, arithmetic and copies ran while one was open for 24% -> 27% of each run, Pallas kernels for 1% -> 4%
where the time goes in v9:
time: 189 us; the launch traced here: 188 us
  starting transfers between devices  69.5 us (37%)
  waiting for transfers between devices  37.6 us (20%)
  other arithmetic  26.9 us (14%)
  matrix products  23 us (12%)
  Pallas kernels  20.2 us (11%)
  local copies, waits for them, and re-layouts  6 us (3%)
  between operations  4.63 us (2%)
    ppermute x32, starting transfers between devices, send(): return lax.ppermute(v, AXES, pairs)  59.5 us
    ppermute x32, waiting for transfers between devices, send(): return lax.ppermute(v, AXES, pairs)  24.1 us
    pallas_call x3, Pallas kernels, on_core(): pl.pallas_call(kernel, out_shape=[jax.ShapeDtypeStruct((rows, 768), kind)...  20.2 us
    all_to_all x2, waiting for transfers between devices, plane_sum(): got = lax.all_to_all(blocks, ('z', 'y'), 0, 0, tiled=True)  13.5 us
    all_to_all x2, starting transfers between devices, plane_sum(): got = lax.all_to_all(blocks, ('z', 'y'), 0, 0, tiled=True)  10 us
    dot_general x1, matrix products, per_device(): logits = jnp.dot(stream, head_weight, preferred_element_type=F32)  6.52 us
    dot_general x10, matrix products, pair_dot(): jnp.dot(a.T, b, preferred_element_type=F32)  4.39 us
    dot_general x10, matrix products, pair_dot(): jnp.dot(far_a.T, far_b, preferred_element_type=F32)  4.36 us
  transfers between devices with their start and end apart: 34, of which 10 were waited for; matrix products, arithmetic and copies ran while one was open for 27% of the time, Pallas kernels for 4%

profile of v9, /device:TPU:1, one launch (start us, length us, event | category | flops | bytes accessed | tf_op | source)
XLA Modules:
  0.0 187.8 jit_solution(12043293999882511165)
XLA Ops:
  1.7 4.6 %collective-permute-start = (bf16[192,768]{1,0:T(8,128)(2,1)S(1)}, bf16[192,768]{1,0:T(8,128)(2,1)S(1)}, u32[]{:S(2)}, u32[]{:S(2)}) collective-permute-start(bf16[192,768]{1,0:T(8,128)(2,1)S(1)} %get-tuple-element.112), channel_id=1, source_target_pairs={{2,4},{3,5},{6,8},{7,9},{10,12},{11,13},{14,16},{15,17},{18,20},{1... | collective-permute-start | bytes 884744 | tf_op jit(solution)/shard_map/ppermute | solution.py:46
  7.1 3.6 %collective-permute-done = bf16[192,768]{1,0:T(8,128)(2,1)S(1)} collective-permute-done((bf16[192,768]{1,0:T(8,128)(2,1)S(1)}, bf16[192,768]{1,0:T(8,128)(2,1)S(1)}, u32[]{:S(2)}, u32[]{:S(2)}) %collective-permute-start) | collective-permute-done | bytes 294944 | tf_op jit(solution)/shard_map/ppermute | solution.py:46
  11.6 8.1 %shard_map.93 = (bf16[384,768]{1,0:T(8,128)(2,1)}, bf16[512,768]{1,0:T(8,128)(2,1)}, bf16[512,768]{1,0:T(8,128)(2,1)}, bf16[256,768]{1,0:T(8,128)(2,1)}, bf16[256,768]{1,0:T(8,128)(2,1)}) custom-call(s32[2]{0:T(128)} %add_convert_fusion.1.flags, bf16[192,768]{1,0:T(8,128)(2,1)} %get-tuple-element.104.before, bf16[256,768]{1,0:T(8,128)(2,1)} %bitcast.170, ...), custom_call_target="tpu_custom_call" | custom-call | flops 2717908992 | bytes 7077888 | tf_op jit(solution)/shard_map/pallas_call | solution.py:169
  19.8 3.7 %collective-permute-start.2 = (bf16[256,768]{1,0:T(8,128)(2,1)}, bf16[256,768]{1,0:T(8,128)(2,1)S(1)}, u32[]{:S(2)}, u32[]{:S(2)}) collective-permute-start(bf16[256,768]{1,0:T(8,128)(2,1)} %get-tuple-element.44.own), channel_id=1, source_target_pairs={{2,4},{3,5},{6,8},{7,9},{10,12},{11,13},{14,16},{15,17},{18,20},{1... | collective-permute-start | bytes 1179656 | tf_op jit(solution)/shard_map/ppermute | solution.py:46
  24.8 4.4 %collective-permute-done.2 = bf16[256,768]{1,0:T(8,128)(2,1)S(1)} collective-permute-done((bf16[256,768]{1,0:T(8,128)(2,1)}, bf16[256,768]{1,0:T(8,128)(2,1)S(1)}, u32[]{:S(2)}, u32[]{:S(2)}) %collective-permute-start.2) | collective-permute-done | bytes 393248 | tf_op jit(solution)/shard_map/ppermute | solution.py:46
  30.2 5.4 %shard_map.94 = (bf16[768,768]{1,0:T(8,128)(2,1)}, bf16[256,768]{1,0:T(8,128)(2,1)}) custom-call(bf16[256,768]{1,0:T(8,128)(2,1)} %get-tuple-element.46.before, bf16[256,768]{1,0:T(8,128)(2,1)} %get-tuple-element.44.own, bf16[256,768]{1,0:T(8,128)(2,1)} %get-tuple-element.97.after, bf16[256,768]{1,0:T(8,128)(2,1)} %get-tuple-element.47.stream, ...), custom_call_target="tpu_custom_call" | custom-call | flops 905969664 | bytes 3538944 | tf_op jit(solution)/shard_map/pallas_call | solution.py:169
  36.1 6.5 %fusion.5 = (f32[]{:T(128)}, bf16[256,2688]{1,0:T(8,128)(2,1)S(1)}) fusion(s32[1,256,2688]{2,1,0:T(8,128)S(1)} %copy-done.15, f32[256]{0:T(256)S(1)} %bitcast.173, bf16[256,768]{1,0:T(8,128)(2,1)} %get-tuple-element.48, bf16[768,2688]{1,0:T(8,128)(2,1)} %param.8), kind=kOutput, calls=%fused_computation.9 | convolution fusion | flops 1070039040 | bytes 8651780 | tf_op jit(solution)/shard_map/dot_general | solution.py:263
  44.9 3.6 %collective-permute-start.8 = (bf16[256,768]{1,0:T(8,128)(2,1)S(1)}, bf16[256,768]{1,0:T(8,128)(2,1)S(1)}, u32[]{:S(2)}, u32[]{:S(2)}) collective-permute-start(bf16[256,768]{1,0:T(8,128)(2,1)S(1)} %get-tuple-element.51.own), channel_id=1, source_target_pairs={{2,4},{3,5},{6,8},{7,9},{10,12},{11,13},{14,16},{15,17},{18,20},{1... | collective-permute-start | bytes 1179656 | tf_op jit(solution)/shard_map/ppermute | solution.py:46
  58.6 8.8 %collective-permute-start.16 = (bf16[2,576,384]{2,1,0:T(8,128)(2,1)}, bf16[2,576,384]{2,1,0:T(8,128)(2,1)S(1)}, u32[]{:S(2)}, u32[]{:S(2)}) collective-permute-start(bf16[2,576,384]{2,1,0:T(8,128)(2,1)} %dynamic-slice_bitcast_fusion.2), channel_id=1, source_target_pairs={{0,48},{1,49},{2,50},{3,51},{4,52},{5,53},{6,54},{7,55},{8,56},{9,... | collective-permute-start | bytes 2654216 | tf_op jit(solution)/shard_map/ppermute | solution.py:46
  70.2 6.7 %shard_map.95 = (f32[256,768]{1,0:T(8,128)}, bf16[256,768]{1,0:T(8,128)(2,1)}) custom-call(bf16[256,768]{1,0:T(8,128)(2,1)} %get-tuple-element.56.before, bf16[256,768]{1,0:T(8,128)(2,1)} %copy-done.9, bf16[256,768]{1,0:T(8,128)(2,1)} %get-tuple-element.95.after, bf16[256,768]{1,0:T(8,128)(2,1)} %get-tuple-element.47.stream, ...), custom_call_target="tpu_custom_call" | custom-call | flops 905969664 | bytes 3538944 | tf_op jit(solution)/shard_map/pallas_call | solution.py:169
  80.8 6.5 %collective-permute-start.18 = (bf16[1,384,1408]{2,1,0:T(8,128)(2,1)S(1)}, bf16[1,384,1408]{2,1,0:T(8,128)(2,1)S(1)}, u32[]{:S(2)}, u32[]{:S(2)}) collective-permute-start(bf16[1,384,1408]{2,1,0:T(8,128)(2,1)S(1)} %dynamic-slice_bitcast_fusion), channel_id=1, source_target_pairs={{0,64},{1,65},{2,66},{3,67},{4,68},{5,69},{6,70},{7,71},{8,72},{9,... | collective-permute-start | bytes 3244040 | tf_op jit(solution)/shard_map/ppermute | solution.py:46
  104.4 7.4 %collective-permute-done.18 = bf16[1,384,1408]{2,1,0:T(8,128)(2,1)S(1)} collective-permute-done((bf16[1,384,1408]{2,1,0:T(8,128)(2,1)S(1)}, bf16[1,384,1408]{2,1,0:T(8,128)(2,1)S(1)}, u32[]{:S(2)}, u32[]{:S(2)}) %collective-permute-start.18) | collective-permute-done | bytes 1081376 | tf_op jit(solution)/shard_map/ppermute | solution.py:46
  113.1 6.4 %all-to-all-start = ((bf16[16,24,1408]{2,1,0:T(8,128)(2,1)}), bf16[16,24,1408]{2,1,0:T(8,128)(2,1)}, u32[]{:S(2)}, u32[]{:S(2)}) async-start(bf16[16,24,1408]{2,1,0:T(8,128)(2,1)} %bitcast.163), calls=%async_computation | async-start | bytes 2162688 | tf_op jit(solution)/shard_map/all_to_all | solution.py:206
  120.6 2.3 %collective-permute-start.21 = (bf16[1,1152,384]{2,1,0:T(8,128)(2,1)}, bf16[1,1152,384]{2,1,0:T(8,128)(2,1)}, u32[]{:S(2)}, u32[]{:S(2)}) collective-permute-start(bf16[1,1152,384]{2,1,0:T(8,128)(2,1)} %dynamic-slice_bitcast_fusion.1), channel_id=1, source_target_pairs={{0,64},{1,65},{2,66},{3,67},{4,68},{5,69},{6,70},{7,71},{8,72},{9,... | collective-permute-start | bytes 2654216 | tf_op jit(solution)/shard_map/ppermute | solution.py:46
  126.4 2.6 %collective-permute-start.23 = (bf16[2,288,384]{2,1,0:T(8,128)(2,1)S(1)}, bf16[2,288,384]{2,1,0:T(8,128)(2,1)}, u32[]{:S(2)}, u32[]{:S(2)}) collective-permute-start(bf16[2,288,384]{2,1,0:T(8,128)(2,1)S(1)} %slice_bitcast_fusion), channel_id=1, source_target_pairs={{0,48},{1,49},{2,50},{3,51},{4,52},{5,53},{6,54},{7,55},{8,56},{9,... | collective-permute-start | bytes 1327112 | tf_op jit(solution)/shard_map/ppermute | solution.py:46
  129.0 6.7 %all-to-all-done = bf16[16,24,1408]{2,1,0:T(8,128)(2,1)} async-done(((bf16[16,24,1408]{2,1,0:T(8,128)(2,1)}), bf16[16,24,1408]{2,1,0:T(8,128)(2,1)}, u32[]{:S(2)}, u32[]{:S(2)}) %all-to-all-start) | async-done | bytes 1081376 | tf_op jit(solution)/shard_map/all_to_all | solution.py:206
  137.7 7.5 %collective-permute-start.19 = (bf16[96,384]{1,0:T(8,128)(2,1)}, bf16[96,384]{1,0:T(8,128)(2,1)}, u32[]{:S(2)}, u32[]{:S(2)}) collective-permute-start(bf16[96,384]{1,0:T(8,128)(2,1)} %pad_maximum_fusion.14), channel_id=1, source_target_pairs={{0,0},{1,2},{2,1},{3,3},{4,4},{5,6},{6,5},{7,7},{8,8},{9,10},{10,9... | collective-permute-start | bytes 221192 | tf_op jit(solution)/shard_map/ppermute | solution.py:46
  145.4 2.4 %fusion.46 = bf16[1152,384]{1,0:T(8,128)(2,1)} fusion(bf16[1,1152,384]{2,1,0:T(8,128)(2,1)} %collective-permute-done.21, bf16[1,2,1152,384]{3,2,1,0:T(8,128)(2,1)S(1)} %bitcast.162, s32[]{:T(128)S(6)} %select_n.280), kind=kLoop, calls=%fused_computation.86 | loop fusion | flops 1769472 | bytes 2654212 | tf_op jit(solution)/shard_map/reshape | solution.py:202
  149.8 2.6 %collective-permute-start.27 = (bf16[2,144,384]{2,1,0:T(8,128)(2,1)S(1)}, bf16[2,144,384]{2,1,0:T(8,128)(2,1)S(1)}, u32[]{:S(2)}, u32[]{:S(2)}) collective-permute-start(bf16[2,144,384]{2,1,0:T(8,128)(2,1)S(1)} %get-tuple-element.94), channel_id=1, source_target_pairs={{0,8},{1,9},{2,10},{3,11},{4,12},{5,13},{6,14},{7,15},{8,0},{9,1},... | collective-permute-start | bytes 663560 | tf_op jit(solution)/shard_map/ppermute | solution.py:46
  152.4 3.6 %all-to-all-start.1 = ((bf16[16,72,384]{2,1,0:T(8,128)(2,1)}), bf16[16,72,384]{2,1,0:T(8,128)(2,1)S(1)}, u32[]{:S(2)}, u32[]{:S(2)}) async-start(bf16[16,72,384]{2,1,0:T(8,128)(2,1)} %bitcast.51), calls=%async_computation.1 | async-start | bytes 1769472 | tf_op jit(solution)/shard_map/all_to_all | solution.py:206
  160.5 3.0 %collective-permute-done.26 = bf16[2,144,384]{2,1,0:T(8,128)(2,1)S(1)} collective-permute-done((bf16[2,144,384]{2,1,0:T(8,128)(2,1)S(1)}, bf16[2,144,384]{2,1,0:T(8,128)(2,1)S(1)}, u32[]{:S(2)}, u32[]{:S(2)}) %collective-permute-start.26) | collective-permute-done | bytes 221216 | tf_op jit(solution)/shard_map/ppermute | solution.py:46
  163.8 6.8 %all-to-all-done.1 = bf16[16,72,384]{2,1,0:T(8,128)(2,1)S(1)} async-done(((bf16[16,72,384]{2,1,0:T(8,128)(2,1)}), bf16[16,72,384]{2,1,0:T(8,128)(2,1)S(1)}, u32[]{:S(2)}, u32[]{:S(2)}) %all-to-all-start.1) | async-done | bytes 884768 | tf_op jit(solution)/shard_map/all_to_all | solution.py:206
  170.7 6.6 %collective-permute-start.28 = (bf16[216,384]{1,0:T(8,128)(2,1)S(1)}, bf16[216,384]{1,0:T(8,128)(2,1)S(1)}, u32[]{:S(2)}, u32[]{:S(2)}) collective-permute-start(bf16[216,384]{1,0:T(8,128)(2,1)S(1)} %pad_maximum_fusion.12), channel_id=1, source_target_pairs={{0,0},{1,2},{2,1},{3,3},{4,4},{5,6},{6,5},{7,7},{8,8},{9,10},{10,9... | collective-permute-start | bytes 497672 | tf_op jit(solution)/shard_map/ppermute | solution.py:46
  178.3 2.5 %collective-permute-start.30 = (bf16[144,384]{1,0:T(8,128)(2,1)S(1)}, bf16[144,384]{1,0:T(8,128)(2,1)S(1)}, u32[]{:S(2)}, u32[]{:S(2)}) collective-permute-start(bf16[144,384]{1,0:T(8,128)(2,1)S(1)} %get-tuple-element.115), channel_id=1, source_target_pairs={{0,64},{1,66},{2,65},{3,67},{4,68},{5,70},{6,69},{7,71},{8,72},{9,... | collective-permute-start | bytes 331784 | tf_op jit(solution)/shard_map/ppermute | solution.py:46
  (178 shorter events, 60.6 us)
Async XLA Ops:
  1.7 9.0 %collective-permute-start = (bf16[192,768]{1,0:T(8,128)(2,1)S(1)}, bf16[192,768]{1,0:T(8,128)(2,1)S(1)}, u32[]{:S(2)}, u32[]{:S(2)}) collective-permute-start(bf16[192,768]{1,0:T(8,128)(2,1)S(1)} %get-tuple-element.112), channel_id=1, source_target_pairs={{2,4},{3,5},{6,8},{7,9},{10,12},{11,13},{14,16},{15,17},{18,20},{1... | collective-permute-start | bytes 884744 | tf_op jit(solution)/shard_map/ppermute | solution.py:46
  19.7 10.5 %collective-permute-start.5 = (bf16[512,768]{1,0:T(8,128)(2,1)}, bf16[512,768]{1,0:T(8,128)(2,1)S(1)}, u32[]{:S(2)}, u32[]{:S(2)}) collective-permute-start(bf16[512,768]{1,0:T(8,128)(2,1)} %get-tuple-element.45), channel_id=1, source_target_pairs={{0,2},{1,3},{2,0},{3,1},{4,6},{5,7},{6,4},{7,5},{8,10},{9,11},{10,... | collective-permute-start | bytes 2359304 | tf_op jit(solution)/shard_map/ppermute | solution.py:46
  19.8 9.4 %collective-permute-start.2 = (bf16[256,768]{1,0:T(8,128)(2,1)}, bf16[256,768]{1,0:T(8,128)(2,1)S(1)}, u32[]{:S(2)}, u32[]{:S(2)}) collective-permute-start(bf16[256,768]{1,0:T(8,128)(2,1)} %get-tuple-element.44.own), channel_id=1, source_target_pairs={{2,4},{3,5},{6,8},{7,9},{10,12},{11,13},{14,16},{15,17},{18,20},{1... | collective-permute-start | bytes 1179656 | tf_op jit(solution)/shard_map/ppermute | solution.py:46
  35.6 9.3 %collective-permute-start.7 = (bf16[256,768]{1,0:T(8,128)(2,1)}, bf16[256,768]{1,0:T(8,128)(2,1)S(1)}, u32[]{:S(2)}, u32[]{:S(2)}) collective-permute-start(bf16[256,768]{1,0:T(8,128)(2,1)} %get-tuple-element.48), channel_id=1, source_target_pairs={{0,2},{1,3},{2,0},{3,1},{4,6},{5,7},{6,4},{7,5},{8,10},{9,11},{10,... | collective-permute-start | bytes 1179656 | tf_op jit(solution)/shard_map/ppermute | solution.py:46
  44.9 22.4 %collective-permute-start.8 = (bf16[256,768]{1,0:T(8,128)(2,1)S(1)}, bf16[256,768]{1,0:T(8,128)(2,1)S(1)}, u32[]{:S(2)}, u32[]{:S(2)}) collective-permute-start(bf16[256,768]{1,0:T(8,128)(2,1)S(1)} %get-tuple-element.51.own), channel_id=1, source_target_pairs={{2,4},{3,5},{6,8},{7,9},{10,12},{11,13},{14,16},{15,17},{18,20},{1... | collective-permute-start | bytes 1179656 | tf_op jit(solution)/shard_map/ppermute | solution.py:46
  48.6 18.8 %collective-permute-start.9 = (bf16[256,768]{1,0:T(8,128)(2,1)S(1)}, bf16[256,768]{1,0:T(8,128)(2,1)S(1)}, u32[]{:S(2)}, u32[]{:S(2)}) collective-permute-start(bf16[256,768]{1,0:T(8,128)(2,1)S(1)} %get-tuple-element.51.own), channel_id=1, source_target_pairs={{0,2},{1,3},{2,0},{3,1},{4,6},{5,7},{6,4},{7,5},{8,10},{9,11},{10,... | collective-permute-start | bytes 1179656 | tf_op jit(solution)/shard_map/ppermute | solution.py:46
  50.9 17.4 %collective-permute-start.11 = (bf16[256,1408]{1,0:T(8,128)(2,1)S(1)}, bf16[256,1408]{1,0:T(8,128)(2,1)S(1)}, u32[]{:S(2)}, u32[]{:S(2)}) collective-permute-start(bf16[256,1408]{1,0:T(8,128)(2,1)S(1)} %broadcast_select_fusion), channel_id=1, source_target_pairs={{0,2},{1,3},{2,0},{3,1},{4,6},{5,7},{6,4},{7,5},{8,10},{9,11},{10,... | collective-permute-start | bytes 2162696 | tf_op jit(solution)/shard_map/ppermute | solution.py:46
  58.6 36.7 %collective-permute-start.16 = (bf16[2,576,384]{2,1,0:T(8,128)(2,1)}, bf16[2,576,384]{2,1,0:T(8,128)(2,1)S(1)}, u32[]{:S(2)}, u32[]{:S(2)}) collective-permute-start(bf16[2,576,384]{2,1,0:T(8,128)(2,1)} %dynamic-slice_bitcast_fusion.2), channel_id=1, source_target_pairs={{0,48},{1,49},{2,50},{3,51},{4,52},{5,53},{6,54},{7,55},{8,56},{9,... | collective-permute-start | bytes 2654216 | tf_op jit(solution)/shard_map/ppermute | solution.py:46
  78.2 13.1 %collective-permute-start.13 = (bf16[192,768]{1,0:T(8,128)(2,1)S(1)}, bf16[192,768]{1,0:T(8,128)(2,1)S(1)}, u32[]{:S(2)}, u32[]{:S(2)}) collective-permute-start(bf16[192,768]{1,0:T(8,128)(2,1)S(1)} %get-tuple-element.107), channel_id=1, source_target_pairs={{2,4},{3,5},{6,8},{7,9},{10,12},{11,13},{14,16},{15,17},{18,20},{1... | collective-permute-start | bytes 884744 | tf_op jit(solution)/shard_map/ppermute | solution.py:46
  80.1 11.2 %collective-permute-start.14 = (bf16[192,768]{1,0:T(8,128)(2,1)S(1)}, bf16[192,768]{1,0:T(8,128)(2,1)S(1)}, u32[]{:S(2)}, u32[]{:S(2)}) collective-permute-start(bf16[192,768]{1,0:T(8,128)(2,1)S(1)} %get-tuple-element.108), channel_id=1, source_target_pairs={{0,2},{1,3},{2,0},{3,1},{4,6},{5,7},{6,4},{7,5},{8,10},{9,11},{10,... | collective-permute-start | bytes 884744 | tf_op jit(solution)/shard_map/ppermute | solution.py:46
  80.2 7.1 %collective-permute-start.15 = (bf16[256,384]{1,0:T(8,128)(2,1)S(1)}, bf16[256,384]{1,0:T(8,128)(2,1)S(1)}, u32[]{:S(2)}, u32[]{:S(2)}) collective-permute-start(bf16[256,384]{1,0:T(8,128)(2,1)S(1)} %get-tuple-element.106), channel_id=1, source_target_pairs={{0,2},{1,3},{2,0},{3,1},{4,6},{5,7},{6,4},{7,5},{8,10},{9,11},{10,... | collective-permute-start | bytes 589832 | tf_op jit(solution)/shard_map/ppermute | solution.py:46
  80.8 31.1 %collective-permute-start.18 = (bf16[1,384,1408]{2,1,0:T(8,128)(2,1)S(1)}, bf16[1,384,1408]{2,1,0:T(8,128)(2,1)S(1)}, u32[]{:S(2)}, u32[]{:S(2)}) collective-permute-start(bf16[1,384,1408]{2,1,0:T(8,128)(2,1)S(1)} %dynamic-slice_bitcast_fusion), channel_id=1, source_target_pairs={{0,64},{1,65},{2,66},{3,67},{4,68},{5,69},{6,70},{7,71},{8,72},{9,... | collective-permute-start | bytes 3244040 | tf_op jit(solution)/shard_map/ppermute | solution.py:46
  91.1 33.8 %collective-permute-start.22 = (bf16[2,2,288,384]{3,2,1,0:T(8,128)(2,1)}, bf16[2,2,288,384]{3,2,1,0:T(8,128)(2,1)}, u32[]{:S(2)}, u32[]{:S(2)}) collective-permute-start(bf16[2,2,288,384]{3,2,1,0:T(8,128)(2,1)} %pad_maximum_fusion.3), channel_id=1, source_target_pairs={{0,16},{1,17},{2,18},{3,19},{4,20},{5,21},{6,22},{7,23},{8,24},{9,... | collective-permute-start | bytes 2654216 | tf_op jit(solution)/shard_map/ppermute | solution.py:46
  98.2 24.7 %collective-permute-start.24 = (bf16[2,288,384]{2,1,0:T(8,128)(2,1)}, bf16[2,288,384]{2,1,0:T(8,128)(2,1)}, u32[]{:S(2)}, u32[]{:S(2)}) collective-permute-start(bf16[2,288,384]{2,1,0:T(8,128)(2,1)} %dynamic-slice_bitcast_fusion.3), channel_id=1, source_target_pairs={{0,16},{1,17},{2,18},{3,19},{4,20},{5,21},{6,22},{7,23},{8,24},{9,... | collective-permute-start | bytes 1327112 | tf_op jit(solution)/shard_map/ppermute | solution.py:46
  113.1 22.6 %all-to-all-start = ((bf16[16,24,1408]{2,1,0:T(8,128)(2,1)}), bf16[16,24,1408]{2,1,0:T(8,128)(2,1)}, u32[]{:S(2)}, u32[]{:S(2)}) async-start(bf16[16,24,1408]{2,1,0:T(8,128)(2,1)} %bitcast.163), calls=%async_computation | async-start | bytes 2162688 | tf_op jit(solution)/shard_map/all_to_all | solution.py:206
  120.6 24.8 %collective-permute-start.21 = (bf16[1,1152,384]{2,1,0:T(8,128)(2,1)}, bf16[1,1152,384]{2,1,0:T(8,128)(2,1)}, u32[]{:S(2)}, u32[]{:S(2)}) collective-permute-start(bf16[1,1152,384]{2,1,0:T(8,128)(2,1)} %dynamic-slice_bitcast_fusion.1), channel_id=1, source_target_pairs={{0,64},{1,65},{2,66},{3,67},{4,68},{5,69},{6,70},{7,71},{8,72},{9,... | collective-permute-start | bytes 2654216 | tf_op jit(solution)/shard_map/ppermute | solution.py:46
  126.4 21.4 %collective-permute-start.23 = (bf16[2,288,384]{2,1,0:T(8,128)(2,1)S(1)}, bf16[2,288,384]{2,1,0:T(8,128)(2,1)}, u32[]{:S(2)}, u32[]{:S(2)}) collective-permute-start(bf16[2,288,384]{2,1,0:T(8,128)(2,1)S(1)} %slice_bitcast_fusion), channel_id=1, source_target_pairs={{0,48},{1,49},{2,50},{3,51},{4,52},{5,53},{6,54},{7,55},{8,56},{9,... | collective-permute-start | bytes 1327112 | tf_op jit(solution)/shard_map/ppermute | solution.py:46
  137.7 18.3 %collective-permute-start.19 = (bf16[96,384]{1,0:T(8,128)(2,1)}, bf16[96,384]{1,0:T(8,128)(2,1)}, u32[]{:S(2)}, u32[]{:S(2)}) collective-permute-start(bf16[96,384]{1,0:T(8,128)(2,1)} %pad_maximum_fusion.14), channel_id=1, source_target_pairs={{0,0},{1,2},{2,1},{3,3},{4,4},{5,6},{6,5},{7,7},{8,8},{9,10},{10,9... | collective-permute-start | bytes 221192 | tf_op jit(solution)/shard_map/ppermute | solution.py:46
  145.3 10.8 %collective-permute-start.20 = (bf16[96,384]{1,0:T(8,128)(2,1)}, bf16[96,384]{1,0:T(8,128)(2,1)}, u32[]{:S(2)}, u32[]{:S(2)}) collective-permute-start(bf16[96,384]{1,0:T(8,128)(2,1)} %pad_maximum_fusion.14), channel_id=1, source_target_pairs={{0,2},{1,0},{2,3},{3,1},{4,6},{5,4},{6,7},{7,5},{8,10},{9,8},{10,1... | collective-permute-start | bytes 221192 | tf_op jit(solution)/shard_map/ppermute | solution.py:46
  149.1 11.5 %collective-permute-start.25 = (bf16[2,144,384]{2,1,0:T(8,128)(2,1)S(1)}, bf16[2,144,384]{2,1,0:T(8,128)(2,1)S(1)}, u32[]{:S(2)}, u32[]{:S(2)}) collective-permute-start(bf16[2,144,384]{2,1,0:T(8,128)(2,1)S(1)} %get-tuple-element.92), channel_id=1, source_target_pairs={{0,4},{1,5},{2,6},{3,7},{4,0},{5,1},{6,2},{7,3},{8,12},{9,13},{10,... | collective-permute-start | bytes 663560 | tf_op jit(solution)/shard_map/ppermute | solution.py:46
  149.1 14.4 %collective-permute-start.26 = (bf16[2,144,384]{2,1,0:T(8,128)(2,1)S(1)}, bf16[2,144,384]{2,1,0:T(8,128)(2,1)S(1)}, u32[]{:S(2)}, u32[]{:S(2)}) collective-permute-start(bf16[2,144,384]{2,1,0:T(8,128)(2,1)S(1)} %get-tuple-element.93), channel_id=1, source_target_pairs={{0,12},{1,13},{2,14},{3,15},{4,8},{5,9},{6,10},{7,11},{8,4},{9,5},... | collective-permute-start | bytes 663560 | tf_op jit(solution)/shard_map/ppermute | solution.py:46
  149.8 13.8 %collective-permute-start.27 = (bf16[2,144,384]{2,1,0:T(8,128)(2,1)S(1)}, bf16[2,144,384]{2,1,0:T(8,128)(2,1)S(1)}, u32[]{:S(2)}, u32[]{:S(2)}) collective-permute-start(bf16[2,144,384]{2,1,0:T(8,128)(2,1)S(1)} %get-tuple-element.94), channel_id=1, source_target_pairs={{0,8},{1,9},{2,10},{3,11},{4,12},{5,13},{6,14},{7,15},{8,0},{9,1},... | collective-permute-start | bytes 663560 | tf_op jit(solution)/shard_map/ppermute | solution.py:46
  152.4 18.2 %all-to-all-start.1 = ((bf16[16,72,384]{2,1,0:T(8,128)(2,1)}), bf16[16,72,384]{2,1,0:T(8,128)(2,1)S(1)}, u32[]{:S(2)}, u32[]{:S(2)}) async-start(bf16[16,72,384]{2,1,0:T(8,128)(2,1)} %bitcast.51), calls=%async_computation.1 | async-start | bytes 1769472 | tf_op jit(solution)/shard_map/all_to_all | solution.py:206
  170.7 10.1 %collective-permute-start.28 = (bf16[216,384]{1,0:T(8,128)(2,1)S(1)}, bf16[216,384]{1,0:T(8,128)(2,1)S(1)}, u32[]{:S(2)}, u32[]{:S(2)}) collective-permute-start(bf16[216,384]{1,0:T(8,128)(2,1)S(1)} %pad_maximum_fusion.12), channel_id=1, source_target_pairs={{0,0},{1,2},{2,1},{3,3},{4,4},{5,6},{6,5},{7,7},{8,8},{9,10},{10,9... | collective-permute-start | bytes 497672 | tf_op jit(solution)/shard_map/ppermute | solution.py:46
  (32 other events, 168.9 us)

commit v10 on v9

--- a/solution.py
+++ b/solution.py
@@ -59,15 +59,19 @@
 
 
 def copies_in(w_ref, scratch, sems, layers):
-    order = [(n, layer, tap) for n, layer in enumerate(layers) for tap in (1, 0, 2)]
-    made = {
-        (n, tap): pltpu.make_async_copy(
-            w_ref.at[layer, tap], scratch.at[n, tap], sems.at[n, tap]
-        )
-        for n, layer, tap in order
-    }
-    for n, layer, tap in order:
-        made[n, tap].start()
+    made = []
+    for n, layer in enumerate(layers):
+        made.append([])
+        for tap in (1, 0, 2):
+            for part in range(4):
+                rows = slice(192 * part, 192 * part + 192)
+                copy = pltpu.make_async_copy(
+                    w_ref.at[layer, tap, rows, :],
+                    scratch.at[n, tap, rows, :],
+                    sems.at[n, tap, part],
+                )
+                copy.start()
+                made[n].append(copy)
     return made
 
 
@@ -114,8 +118,8 @@
     for r in range(0, 640, 64):
         acts[r : r + 64, :] = tanh_gelu(wide[r : r + 64, :].astype(F32)).astype(BF)
     act0[...] = acts[128:512, :]
-    for tap in (1, 0, 2):
-        made[0, tap].wait()
+    for copy in made[0]:
+        copy.wait()
     for start in (0, 256):
         for cols in COLS:
             conv = three_taps(acts, weights, 0, 64, start, 256, cols, False)
@@ -123,8 +127,8 @@
             stream = zero_outside(stream.astype(F32), flags, start, 128, 512)
             wide1[start : start + 256, cols] = stream.astype(BF)
             act1[start : start + 256, cols] = tanh_gelu(stream).astype(BF)
-    for tap in (1, 0, 2):
-        made[1, tap].wait()
+    for copy in made[1]:
+        copy.wait()
     for cols in COLS:
         conv = three_taps(act1, weights, 1, 128, 0, 256, cols, False)
         stream = (wide1[128:384, cols].astype(F32) + conv).astype(BF)
@@ -137,8 +141,8 @@
     padded[0:256, :] = before[...]
     padded[256:512, :] = own[...]
     padded[512:768, :] = after[...]
-    for tap in (1, 0, 2):
-        made[0, tap].wait()
+    for copy in made[0]:
+        copy.wait()
     for cols in COLS:
         conv = three_taps(padded, weights, 0, 256, 0, 256, cols, False)
         out[:, cols] = (stream[:, cols].astype(F32) + conv).astype(BF)
@@ -149,8 +153,8 @@
     wide[0:256, :] = before[...]
     wide[256:512, :] = own[...]
     wide[512:768, :] = after[...]
-    for tap in (1, 0, 2):
-        made[0, tap].wait()
+    for copy in made[0]:
+        copy.wait()
     for cols in COLS:
         act_grad = three_taps(wide, weights, 0, 256, 0, 256, cols, True)
         total = grad[:, cols] + tanh_gelu_slope(stream[:, cols].astype(F32)) * act_grad
@@ -158,7 +162,7 @@
         out_bf[:, cols] = total.astype(BF)
 
 
-def on_core(kernel, outs, scratch, count, flops, *operands):
+def on_core(kernel, room, outs, scratch, count, flops, *operands):
     def place(v):
         if v.ndim == 4:
             return pl.BlockSpec(memory_space=pltpu.HBM)
@@ -172,8 +176,8 @@
         in_specs=[place(v) for v in operands],
         out_specs=[pl.BlockSpec(memory_space=pltpu.VMEM) for _ in outs],
         scratch_shapes=[pltpu.VMEM((rows, 768), kind) for rows, kind in scratch]
-        + [pltpu.VMEM((count, 3, 768, 768), BF), pltpu.SemaphoreType.DMA((count, 3))],
-        compiler_params=pltpu.CompilerParams(vmem_limit_bytes=56 * 2**20),
+        + [pltpu.VMEM((count, 3, 768, 768), BF), pltpu.SemaphoreType.DMA((count, 3, 4))],
+        compiler_params=pltpu.CompilerParams(vmem_limit_bytes=room * 2**20),
         cost_estimate=pl.CostEstimate(
             flops=flops, bytes_accessed=count * 3 * 768 * 768 * 2, transcendentals=0
         ),
@@ -200,11 +204,6 @@
     halves = part.reshape(outer, 2, rows // (2 * outer), lanes)
     total = pick(halves, bit, 1).astype(F32) + got.astype(F32)
     return total.astype(BF).reshape(rows // 2, lanes)
-
-
-def plane_sum(blocks):
-    got = lax.all_to_all(blocks, ("z", "y"), 0, 0, tiled=True)
-    return jnp.sum(got.astype(F32), axis=0).astype(BF)
 
 
 def last_sum(near, rest):
@@ -241,6 +240,7 @@
     before, after = edges(trunk[0], 192, c)
     act0, wide1, act1, stream2, act2 = on_core(
         front_kernel,
+        56,
         [(384, BF), (512, BF), (512, BF), (256, BF), (256, BF)],
         [(640, BF), (640, BF)],
         2,
@@ -252,6 +252,7 @@
     before, far_acts[0], far_acts[1] = lax.optimization_barrier((before, *far_acts))
     act2, stream = on_core(
         middle_kernel,
+        46,
         [(768, BF), (256, BF)],
         [],
         1,
@@ -317,6 +318,7 @@
     before, head_half, half2 = lax.optimization_barrier((before, head_half, half2))
     g2, gb1 = on_core(
         back2_kernel,
+        46,
         [(256, F32), (256, BF)],
         [(768, BF)],
         1,
@@ -341,29 +343,34 @@
     half0, half1, head_half, part2_z = lax.optimization_barrier((half0, half1, head_half, part2_z))
     head_x = take(head_half, head_got, xl)
     head_x, half1, part2_z = lax.optimization_barrier((head_x, half1, part2_z))
-    head_plane = plane_sum(head_x.reshape(16, 24, 1408))
+    head_plane = lax.all_to_all(head_x.reshape(16, 24, 1408), ("z", "y"), 0, 0, tiled=True)
     g0 = g1 + through(trunk[0], conv_back(gb0, conv_weight[0], 64, 256))
     g0, half1, part2_z = lax.optimization_barrier((g0, half1, part2_z))
     keep1 = jnp.stack([pick(half1, z, 1), pick(half1, z ^ 3, 1)])
     keep1 = (keep1.astype(F32) + got1.astype(F32)).astype(BF)
     got1 = send(keep1[1], ALONG_Z[3])
     part2 = take(part2_z, got2, z % 2)
-    half0, head_plane = lax.optimization_barrier((half0, head_plane))
-    half0 = take(half0, got0, xl)
+    half0 = take(half0, got0, xl).reshape(4, 288, 384)
+    got0 = [send(pick(half0, z ^ k), ALONG_Z[k]) for k in (1, 3, 2)]
     half0, keep1 = lax.optimization_barrier((half0, keep1))
-    plane0 = plane_sum(half0.reshape(16, 72, 384))
     part1 = (keep1[0].astype(F32) + got1.astype(F32)).astype(BF)
-    early = jnp.concatenate([part1.reshape(2, 4, 72, 384), part2.reshape(2, 4, 72, 384)], axis=2)
+    part0 = sum((g.astype(F32) for g in got0), pick(half0, z).astype(F32)).astype(BF)
+    early = jnp.concatenate(
+        [v.reshape(-1, 4, 72, 384) for v in (part1[0], part1[1], part2[:288], part2[288:], part0)],
+        axis=0,
+    )
     got = [send(pick(early, y ^ k, 1), ALONG_Y[k]) for k in (1, 3, 2)]
-    early = sum((g.astype(F32) for g in got), pick(early, y, 1).astype(F32)).astype(BF)
+    head_plane = jnp.sum(head_plane.astype(F32), axis=0).astype(BF)
     head_plane = jnp.pad(head_plane, ((0, 0), (0, 128)))
     head_plane = jnp.concatenate(
         [head_plane[:, 384 * k : 384 * k + 384] for k in range(4)], axis=0
     )
     head_sum = sum(send(head_plane, last_hop(0, m)).astype(F32) for m in range(2))
-    early, late = last_sum(
-        jnp.concatenate([pick(early, xl), plane0], axis=0), pick(early, 1 - xl)
-    )
+    early, head_sum = lax.optimization_barrier((early, head_sum))
+    early = sum((g.astype(F32) for g in got), pick(early, y, 1).astype(F32)).astype(BF)
+    both = early[:4].reshape(2, 2, 72, 384)
+    near = jnp.concatenate([pick(both, xl, 1), early[4:]], axis=0).reshape(216, 384)
+    early, late = last_sum(near, pick(both, 1 - xl, 1).reshape(144, 384))
     conv_sum = [late, early[:72], early[72:]]
 
     def own(v):

time: 189 us -> 183 us (0.968)
  waiting for transfers between devices: 37.6 us -> 47.3 us
  other arithmetic: 26.9 us -> 19.7 us
  Pallas kernels: 20.2 us -> 15.6 us
  matrix products: 23 us -> 20.1 us
    ppermute x32 -> x35, waiting for transfers between devices: 24.1 us -> 47.3 us  [send(): return lax.ppermute(v, AXES, pairs)]
    all_to_all x2 -> x1, waiting for transfers between devices: 13.5 us -> 0.01 us  [per_device(): lax.all_to_all(head_x.reshape(16, 24, 1408), ('z', 'y'), 0, 0, tiled=True)]
    pallas_call x3, Pallas kernels: 20.2 us -> 15.6 us  [on_core(): pl.pallas_call(kernel, out_shape=[jax.ShapeDtypeStruct((rows, 768), kind)...]
    all_to_all x2 -> x1, starting transfers between devices: 10 us -> 7.66 us  [per_device(): lax.all_to_all(head_x.reshape(16, 24, 1408), ('z', 'y'), 0, 0, tiled=True)]
    reshape x2 -> x1, other arithmetic: 3.64 us -> 1.28 us  [take(): return total.astype(BF).reshape(rows // 2, lanes)]
    dot_general x1, matrix products: 6.52 us -> 4.54 us  [per_device(): logits = jnp.dot(stream, head_weight, preferred_element_type=F32)]
    ppermute x32 -> x35, starting transfers between devices: 59.5 us -> 61.4 us  [send(): return lax.ppermute(v, AXES, pairs)]
  transfers between devices with their start and end apart: 34 -> 36, of which waited for: 10 -> 13; matrix products, arithmetic and copies ran while one was open for 27% -> 21% of each run, Pallas kernels for 4% -> 2%
where the time goes in v10:
time: 183 us; the launch traced here: 182 us
  starting transfers between devices  69.1 us (38%)
  waiting for transfers between devices  47.3 us (26%)
  matrix products  20.1 us (11%)
  other arithmetic  19.7 us (11%)
  Pallas kernels  15.6 us (9%)
  local copies, waits for them, and re-layouts  5.56 us (3%)
  between operations  4.76 us (3%)
    ppermute x35, starting transfers between devices, send(): return lax.ppermute(v, AXES, pairs)  61.4 us
    ppermute x35, waiting for transfers between devices, send(): return lax.ppermute(v, AXES, pairs)  47.3 us
    pallas_call x3, Pallas kernels, on_core(): pl.pallas_call(kernel, out_shape=[jax.ShapeDtypeStruct((rows, 768), kind)...  15.6 us
    all_to_all x1, starting transfers between devices, per_device(): lax.all_to_all(head_x.reshape(16, 24, 1408), ('z', 'y'), 0, 0, tiled=True)  7.66 us
    dot_general x1, matrix products, per_device(): logits = jnp.dot(stream, head_weight, preferred_element_type=F32)  4.54 us
    dot_general x10, matrix products, pair_dot(): jnp.dot(a.T, b, preferred_element_type=F32)  4.41 us
    dot_general x10, matrix products, pair_dot(): jnp.dot(far_a.T, far_b, preferred_element_type=F32)  4.38 us
  transfers between devices with their start and end apart: 36, of which 13 were waited for; matrix products, arithmetic and copies ran while one was open for 21% of the time, Pallas kernels for 2%

profile of v10, /device:TPU:1, one launch (start us, length us, event | category | flops | bytes accessed | tf_op | source)
XLA Modules:
  0.0 182.2 jit_solution(10015549970022305285)
XLA Ops:
  1.7 4.6 %collective-permute-start = (bf16[192,768]{1,0:T(8,128)(2,1)S(1)}, bf16[192,768]{1,0:T(8,128)(2,1)S(1)}, u32[]{:S(2)}, u32[]{:S(2)}) collective-permute-start(bf16[192,768]{1,0:T(8,128)(2,1)S(1)} %get-tuple-element.119), channel_id=1, source_target_pairs={{2,4},{3,5},{6,8},{7,9},{10,12},{11,13},{14,16},{15,17},{18,20},{1... | collective-permute-start | bytes 884744 | tf_op jit(solution)/shard_map/ppermute | solution.py:46
  7.1 3.6 %collective-permute-done = bf16[192,768]{1,0:T(8,128)(2,1)S(1)} collective-permute-done((bf16[192,768]{1,0:T(8,128)(2,1)S(1)}, bf16[192,768]{1,0:T(8,128)(2,1)S(1)}, u32[]{:S(2)}, u32[]{:S(2)}) %collective-permute-start) | collective-permute-done | bytes 294944 | tf_op jit(solution)/shard_map/ppermute | solution.py:46
  11.6 8.2 %shard_map.93 = (bf16[384,768]{1,0:T(8,128)(2,1)}, bf16[512,768]{1,0:T(8,128)(2,1)}, bf16[512,768]{1,0:T(8,128)(2,1)}, bf16[256,768]{1,0:T(8,128)(2,1)}, bf16[256,768]{1,0:T(8,128)(2,1)}) custom-call(s32[2]{0:T(128)} %add_convert_fusion.1.flags, bf16[192,768]{1,0:T(8,128)(2,1)} %get-tuple-element.107.before, bf16[256,768]{1,0:T(8,128)(2,1)} %bitcast.179, ...), custom_call_target="tpu_custom_call" | custom-call | flops 2717908992 | bytes 7077888 | tf_op jit(solution)/shard_map/pallas_call | solution.py:173
  20.0 3.9 %collective-permute-start.2 = (bf16[256,768]{1,0:T(8,128)(2,1)}, bf16[256,768]{1,0:T(8,128)(2,1)S(1)}, u32[]{:S(2)}, u32[]{:S(2)}) collective-permute-start(bf16[256,768]{1,0:T(8,128)(2,1)} %get-tuple-element.44.own), channel_id=1, source_target_pairs={{2,4},{3,5},{6,8},{7,9},{10,12},{11,13},{14,16},{15,17},{18,20},{1... | collective-permute-start | bytes 1179656 | tf_op jit(solution)/shard_map/ppermute | solution.py:46
  25.0 4.4 %collective-permute-done.2 = bf16[256,768]{1,0:T(8,128)(2,1)S(1)} collective-permute-done((bf16[256,768]{1,0:T(8,128)(2,1)}, bf16[256,768]{1,0:T(8,128)(2,1)S(1)}, u32[]{:S(2)}, u32[]{:S(2)}) %collective-permute-start.2) | collective-permute-done | bytes 393248 | tf_op jit(solution)/shard_map/ppermute | solution.py:46
  29.6 3.3 %shard_map.94 = (bf16[768,768]{1,0:T(8,128)(2,1)S(1)}, bf16[256,768]{1,0:T(8,128)(2,1)S(1)}) custom-call(bf16[256,768]{1,0:T(8,128)(2,1)S(1)} %get-tuple-element.46.before, bf16[256,768]{1,0:T(8,128)(2,1)S(1)} %copy-done.1, bf16[256,768]{1,0:T(8,128)(2,1)S(1)} %get-tuple-element.100.after, bf16[256,768]{1,0:T(8,128)(2,1)S(1)} %copy-done, ...), custom_call_target="tpu_custom_call" | custom-call | flops 905969664 | bytes 3538944 | tf_op jit(solution)/shard_map/pallas_call | solution.py:173
  33.7 4.5 %fusion.5 = (f32[]{:T(128)}, bf16[256,2688]{1,0:T(8,128)(2,1)S(1)}) fusion(s32[1,256,2688]{2,1,0:T(8,128)S(1)} %copy-done.12, f32[256]{0:T(256)S(1)} %bitcast.192, bf16[256,768]{1,0:T(8,128)(2,1)S(1)} %get-tuple-element.48, bf16[768,2688]{1,0:T(8,128)(2,1)S(1)} %copy-done.11), kind=kOutput, calls=%fused_computation.9 | convolution fusion | flops 1070039040 | bytes 8651780 | tf_op jit(solution)/shard_map/dot_general | solution.py:264
  39.6 3.6 %collective-permute-start.8 = (bf16[256,768]{1,0:T(8,128)(2,1)S(1)}, bf16[256,768]{1,0:T(8,128)(2,1)S(1)}, u32[]{:S(2)}, u32[]{:S(2)}) collective-permute-start(bf16[256,768]{1,0:T(8,128)(2,1)S(1)} %get-tuple-element.51.own), channel_id=1, source_target_pairs={{2,4},{3,5},{6,8},{7,9},{10,12},{11,13},{14,16},{15,17},{18,20},{1... | collective-permute-start | bytes 1179656 | tf_op jit(solution)/shard_map/ppermute | solution.py:46
  52.4 8.8 %collective-permute-start.16 = (bf16[2,576,384]{2,1,0:T(8,128)(2,1)S(1)}, bf16[2,576,384]{2,1,0:T(8,128)(2,1)S(1)}, u32[]{:S(2)}, u32[]{:S(2)}) collective-permute-start(bf16[2,576,384]{2,1,0:T(8,128)(2,1)S(1)} %dynamic-slice_bitcast_fusion.2), channel_id=1, source_target_pairs={{0,48},{1,49},{2,50},{3,51},{4,52},{5,53},{6,54},{7,55},{8,56},{9,... | collective-permute-start | bytes 2654216 | tf_op jit(solution)/shard_map/ppermute | solution.py:46
  62.9 4.2 %shard_map.95 = (f32[256,768]{1,0:T(8,128)S(1)}, bf16[256,768]{1,0:T(8,128)(2,1)S(1)}) custom-call(bf16[256,768]{1,0:T(8,128)(2,1)S(1)} %get-tuple-element.56.before, bf16[256,768]{1,0:T(8,128)(2,1)S(1)} %get-tuple-element.51.own, bf16[256,768]{1,0:T(8,128)(2,1)S(1)} %get-tuple-element.98.after, bf16[256,768]{1,0:T(8,128)(2,1)S(1)} %copy-done, ...), custom_call_target="tpu_custom_call" | custom-call | flops 905969664 | bytes 3538944 | tf_op jit(solution)/shard_map/pallas_call | solution.py:173
  67.2 1.9 %collective-permute-start.13 = (bf16[192,768]{1,0:T(8,128)(2,1)S(1)}, bf16[192,768]{1,0:T(8,128)(2,1)S(1)}, u32[]{:S(2)}, u32[]{:S(2)}) collective-permute-start(bf16[192,768]{1,0:T(8,128)(2,1)S(1)} %get-tuple-element.112), channel_id=1, source_target_pairs={{2,4},{3,5},{6,8},{7,9},{10,12},{11,13},{14,16},{15,17},{18,20},{1... | collective-permute-start | bytes 884744 | tf_op jit(solution)/shard_map/ppermute | solution.py:46
  69.8 7.5 %collective-permute-start.19 = (bf16[1,384,1408]{2,1,0:T(8,128)(2,1)S(1)}, bf16[1,384,1408]{2,1,0:T(8,128)(2,1)S(1)}, u32[]{:S(2)}, u32[]{:S(2)}) collective-permute-start(bf16[1,384,1408]{2,1,0:T(8,128)(2,1)S(1)} %dynamic-slice_bitcast_fusion), channel_id=1, source_target_pairs={{0,64},{1,65},{2,66},{3,67},{4,68},{5,69},{6,70},{7,71},{8,72},{9,... | collective-permute-start | bytes 3244040 | tf_op jit(solution)/shard_map/ppermute | solution.py:46
  95.4 6.1 %collective-permute-start.18 = (bf16[1,1152,384]{2,1,0:T(8,128)(2,1)}, bf16[1,1152,384]{2,1,0:T(8,128)(2,1)}, u32[]{:S(2)}, u32[]{:S(2)}) collective-permute-start(bf16[1,1152,384]{2,1,0:T(8,128)(2,1)} %dynamic-slice_bitcast_fusion.1), channel_id=1, source_target_pairs={{0,64},{1,65},{2,66},{3,67},{4,68},{5,69},{6,70},{7,71},{8,72},{9,... | collective-permute-start | bytes 2654216 | tf_op jit(solution)/shard_map/ppermute | solution.py:46
  103.0 7.7 %all-to-all-start = ((bf16[16,24,1408]{2,1,0:T(8,128)(2,1)}), bf16[16,24,1408]{2,1,0:T(8,128)(2,1)}, u32[]{:S(2)}, u32[]{:S(2)}) async-start(bf16[16,24,1408]{2,1,0:T(8,128)(2,1)} %bitcast.174), calls=%async_computation | async-start | bytes 2162688 | tf_op jit(solution)/shard_map/all_to_all | solution.py:346
  114.2 2.0 %collective-permute-start.21 = (bf16[2,288,384]{2,1,0:T(8,128)(2,1)S(1)}, bf16[2,288,384]{2,1,0:T(8,128)(2,1)S(1)}, u32[]{:S(2)}, u32[]{:S(2)}) collective-permute-start(bf16[2,288,384]{2,1,0:T(8,128)(2,1)S(1)} %slice_bitcast_fusion), channel_id=1, source_target_pairs={{0,48},{1,49},{2,50},{3,51},{4,52},{5,53},{6,54},{7,55},{8,56},{9,... | collective-permute-start | bytes 1327112 | tf_op jit(solution)/shard_map/ppermute | solution.py:46
  116.3 5.8 %collective-permute-done.18 = bf16[1,1152,384]{2,1,0:T(8,128)(2,1)} collective-permute-done((bf16[1,1152,384]{2,1,0:T(8,128)(2,1)}, bf16[1,1152,384]{2,1,0:T(8,128)(2,1)}, u32[]{:S(2)}, u32[]{:S(2)}) %collective-permute-start.18) | collective-permute-done | bytes 884768 | tf_op jit(solution)/shard_map/ppermute | solution.py:46
  124.7 2.3 %collective-permute-start.25 = (bf16[288,384]{1,0:T(8,128)(2,1)S(1)}, bf16[288,384]{1,0:T(8,128)(2,1)S(1)}, u32[]{:S(2)}, u32[]{:S(2)}) collective-permute-start(bf16[288,384]{1,0:T(8,128)(2,1)S(1)} %get-tuple-element.96), channel_id=1, source_target_pairs={{0,32},{1,33},{2,34},{3,35},{4,36},{5,37},{6,38},{7,39},{8,40},{9,... | collective-permute-start | bytes 663560 | tf_op jit(solution)/shard_map/ppermute | solution.py:46
  126.9 13.9 %collective-permute-done.21 = bf16[2,288,384]{2,1,0:T(8,128)(2,1)S(1)} collective-permute-done((bf16[2,288,384]{2,1,0:T(8,128)(2,1)S(1)}, bf16[2,288,384]{2,1,0:T(8,128)(2,1)S(1)}, u32[]{:S(2)}, u32[]{:S(2)}) %collective-permute-start.21) | collective-permute-done | bytes 442400 | tf_op jit(solution)/shard_map/ppermute | solution.py:46
  141.2 4.4 %collective-permute-done.24 = bf16[288,384]{1,0:T(8,128)(2,1)S(1)} collective-permute-done((bf16[288,384]{1,0:T(8,128)(2,1)S(1)}, bf16[288,384]{1,0:T(8,128)(2,1)S(1)}, u32[]{:S(2)}, u32[]{:S(2)}) %collective-permute-start.24) | collective-permute-done | bytes 221216 | tf_op jit(solution)/shard_map/ppermute | solution.py:46
  147.2 5.1 %collective-permute-start.26 = (bf16[96,384]{1,0:T(8,128)(2,1)S(1)}, bf16[96,384]{1,0:T(8,128)(2,1)S(1)}, u32[]{:S(2)}, u32[]{:S(2)}) collective-permute-start(bf16[96,384]{1,0:T(8,128)(2,1)S(1)} %pad_maximum_fusion.14), channel_id=1, source_target_pairs={{0,0},{1,2},{2,1},{3,3},{4,4},{5,6},{6,5},{7,7},{8,8},{9,10},{10,9... | collective-permute-start | bytes 221192 | tf_op jit(solution)/shard_map/ppermute | solution.py:46
  155.9 4.4 %collective-permute-done.28 = bf16[5,72,384]{2,1,0:T(8,128)(2,1)S(1)} collective-permute-done((bf16[5,72,384]{2,1,0:T(8,128)(2,1)S(1)}, bf16[5,72,384]{2,1,0:T(8,128)(2,1)S(1)}, u32[]{:S(2)}, u32[]{:S(2)}) %collective-permute-start.28) | collective-permute-done | bytes 276512 | tf_op jit(solution)/shard_map/ppermute | solution.py:46
  160.3 1.9 %collective-permute-done.29 = bf16[5,72,384]{2,1,0:T(8,128)(2,1)S(1)} collective-permute-done((bf16[5,72,384]{2,1,0:T(8,128)(2,1)S(1)}, bf16[5,72,384]{2,1,0:T(8,128)(2,1)S(1)}, u32[]{:S(2)}, u32[]{:S(2)}) %collective-permute-start.29) | collective-permute-done | bytes 276512 | tf_op jit(solution)/shard_map/ppermute | solution.py:46
  162.1 5.9 %collective-permute-done.30 = bf16[5,72,384]{2,1,0:T(8,128)(2,1)S(1)} collective-permute-done((bf16[5,72,384]{2,1,0:T(8,128)(2,1)S(1)}, bf16[5,72,384]{2,1,0:T(8,128)(2,1)S(1)}, u32[]{:S(2)}, u32[]{:S(2)}) %collective-permute-start.30) | collective-permute-done | bytes 276512 | tf_op jit(solution)/shard_map/ppermute | solution.py:46
  168.3 3.7 %collective-permute-start.31 = (bf16[216,384]{1,0:T(8,128)(2,1)S(1)}, bf16[216,384]{1,0:T(8,128)(2,1)S(1)}, u32[]{:S(2)}, u32[]{:S(2)}) collective-permute-start(bf16[216,384]{1,0:T(8,128)(2,1)S(1)} %bitcast.188), channel_id=1, source_target_pairs={{0,0},{1,2},{2,1},{3,3},{4,4},{5,6},{6,5},{7,7},{8,8},{9,10},{10,9... | collective-permute-start | bytes 497672 | tf_op jit(solution)/shard_map/ppermute | solution.py:46
  (182 shorter events, 55.8 us)
Async XLA Ops:
  1.7 9.0 %collective-permute-start = (bf16[192,768]{1,0:T(8,128)(2,1)S(1)}, bf16[192,768]{1,0:T(8,128)(2,1)S(1)}, u32[]{:S(2)}, u32[]{:S(2)}) collective-permute-start(bf16[192,768]{1,0:T(8,128)(2,1)S(1)} %get-tuple-element.119), channel_id=1, source_target_pairs={{2,4},{3,5},{6,8},{7,9},{10,12},{11,13},{14,16},{15,17},{18,20},{1... | collective-permute-start | bytes 884744 | tf_op jit(solution)/shard_map/ppermute | solution.py:46
  19.8 9.7 %collective-permute-start.5 = (bf16[512,768]{1,0:T(8,128)(2,1)}, bf16[512,768]{1,0:T(8,128)(2,1)S(1)}, u32[]{:S(2)}, u32[]{:S(2)}) collective-permute-start(bf16[512,768]{1,0:T(8,128)(2,1)} %get-tuple-element.45), channel_id=1, source_target_pairs={{0,2},{1,3},{2,0},{3,1},{4,6},{5,7},{6,4},{7,5},{8,10},{9,11},{10,... | collective-permute-start | bytes 2359304 | tf_op jit(solution)/shard_map/ppermute | solution.py:46
  20.0 9.5 %collective-permute-start.2 = (bf16[256,768]{1,0:T(8,128)(2,1)}, bf16[256,768]{1,0:T(8,128)(2,1)S(1)}, u32[]{:S(2)}, u32[]{:S(2)}) collective-permute-start(bf16[256,768]{1,0:T(8,128)(2,1)} %get-tuple-element.44.own), channel_id=1, source_target_pairs={{2,4},{3,5},{6,8},{7,9},{10,12},{11,13},{14,16},{15,17},{18,20},{1... | collective-permute-start | bytes 1179656 | tf_op jit(solution)/shard_map/ppermute | solution.py:46
  39.6 21.5 %collective-permute-start.8 = (bf16[256,768]{1,0:T(8,128)(2,1)S(1)}, bf16[256,768]{1,0:T(8,128)(2,1)S(1)}, u32[]{:S(2)}, u32[]{:S(2)}) collective-permute-start(bf16[256,768]{1,0:T(8,128)(2,1)S(1)} %get-tuple-element.51.own), channel_id=1, source_target_pairs={{2,4},{3,5},{6,8},{7,9},{10,12},{11,13},{14,16},{15,17},{18,20},{1... | collective-permute-start | bytes 1179656 | tf_op jit(solution)/shard_map/ppermute | solution.py:46
  43.3 17.9 %collective-permute-start.9 = (bf16[256,768]{1,0:T(8,128)(2,1)S(1)}, bf16[256,768]{1,0:T(8,128)(2,1)S(1)}, u32[]{:S(2)}, u32[]{:S(2)}) collective-permute-start(bf16[256,768]{1,0:T(8,128)(2,1)S(1)} %get-tuple-element.51.own), channel_id=1, source_target_pairs={{0,2},{1,3},{2,0},{3,1},{4,6},{5,7},{6,4},{7,5},{8,10},{9,11},{10,... | collective-permute-start | bytes 1179656 | tf_op jit(solution)/shard_map/ppermute | solution.py:46
  45.4 15.8 %collective-permute-start.11 = (bf16[256,1408]{1,0:T(8,128)(2,1)S(1)}, bf16[256,1408]{1,0:T(8,128)(2,1)S(1)}, u32[]{:S(2)}, u32[]{:S(2)}) collective-permute-start(bf16[256,1408]{1,0:T(8,128)(2,1)S(1)} %broadcast_select_fusion), channel_id=1, source_target_pairs={{0,2},{1,3},{2,0},{3,1},{4,6},{5,7},{6,4},{7,5},{8,10},{9,11},{10,... | collective-permute-start | bytes 2162696 | tf_op jit(solution)/shard_map/ppermute | solution.py:46
  52.4 32.6 %collective-permute-start.16 = (bf16[2,576,384]{2,1,0:T(8,128)(2,1)S(1)}, bf16[2,576,384]{2,1,0:T(8,128)(2,1)S(1)}, u32[]{:S(2)}, u32[]{:S(2)}) collective-permute-start(bf16[2,576,384]{2,1,0:T(8,128)(2,1)S(1)} %dynamic-slice_bitcast_fusion.2), channel_id=1, source_target_pairs={{0,48},{1,49},{2,50},{3,51},{4,52},{5,53},{6,54},{7,55},{8,56},{9,... | collective-permute-start | bytes 2654216 | tf_op jit(solution)/shard_map/ppermute | solution.py:46
  67.2 13.9 %collective-permute-start.13 = (bf16[192,768]{1,0:T(8,128)(2,1)S(1)}, bf16[192,768]{1,0:T(8,128)(2,1)S(1)}, u32[]{:S(2)}, u32[]{:S(2)}) collective-permute-start(bf16[192,768]{1,0:T(8,128)(2,1)S(1)} %get-tuple-element.112), channel_id=1, source_target_pairs={{2,4},{3,5},{6,8},{7,9},{10,12},{11,13},{14,16},{15,17},{18,20},{1... | collective-permute-start | bytes 884744 | tf_op jit(solution)/shard_map/ppermute | solution.py:46
  69.1 12.0 %collective-permute-start.14 = (bf16[192,768]{1,0:T(8,128)(2,1)S(1)}, bf16[192,768]{1,0:T(8,128)(2,1)S(1)}, u32[]{:S(2)}, u32[]{:S(2)}) collective-permute-start(bf16[192,768]{1,0:T(8,128)(2,1)S(1)} %get-tuple-element.113), channel_id=1, source_target_pairs={{0,2},{1,3},{2,0},{3,1},{4,6},{5,7},{6,4},{7,5},{8,10},{9,11},{10,... | collective-permute-start | bytes 884744 | tf_op jit(solution)/shard_map/ppermute | solution.py:46
  69.2 8.0 %collective-permute-start.15 = (bf16[256,384]{1,0:T(8,128)(2,1)S(1)}, bf16[256,384]{1,0:T(8,128)(2,1)S(1)}, u32[]{:S(2)}, u32[]{:S(2)}) collective-permute-start(bf16[256,384]{1,0:T(8,128)(2,1)S(1)} %get-tuple-element.115), channel_id=1, source_target_pairs={{0,2},{1,3},{2,0},{3,1},{4,6},{5,7},{6,4},{7,5},{8,10},{9,11},{10,... | collective-permute-start | bytes 589832 | tf_op jit(solution)/shard_map/ppermute | solution.py:46
  69.8 32.0 %collective-permute-start.19 = (bf16[1,384,1408]{2,1,0:T(8,128)(2,1)S(1)}, bf16[1,384,1408]{2,1,0:T(8,128)(2,1)S(1)}, u32[]{:S(2)}, u32[]{:S(2)}) collective-permute-start(bf16[1,384,1408]{2,1,0:T(8,128)(2,1)S(1)} %dynamic-slice_bitcast_fusion), channel_id=1, source_target_pairs={{0,64},{1,65},{2,66},{3,67},{4,68},{5,69},{6,70},{7,71},{8,72},{9,... | collective-permute-start | bytes 3244040 | tf_op jit(solution)/shard_map/ppermute | solution.py:46
  81.0 31.7 %collective-permute-start.20 = (bf16[2,2,288,384]{3,2,1,0:T(8,128)(2,1)}, bf16[2,2,288,384]{3,2,1,0:T(8,128)(2,1)}, u32[]{:S(2)}, u32[]{:S(2)}) collective-permute-start(bf16[2,2,288,384]{3,2,1,0:T(8,128)(2,1)} %pad_maximum_fusion.3), channel_id=1, source_target_pairs={{0,16},{1,17},{2,18},{3,19},{4,20},{5,21},{6,22},{7,23},{8,24},{9,... | collective-permute-start | bytes 2654216 | tf_op jit(solution)/shard_map/ppermute | solution.py:46
  88.2 23.1 %collective-permute-start.22 = (bf16[2,288,384]{2,1,0:T(8,128)(2,1)}, bf16[2,288,384]{2,1,0:T(8,128)(2,1)}, u32[]{:S(2)}, u32[]{:S(2)}) collective-permute-start(bf16[2,288,384]{2,1,0:T(8,128)(2,1)} %dynamic-slice_bitcast_fusion.3), channel_id=1, source_target_pairs={{0,16},{1,17},{2,18},{3,19},{4,20},{5,21},{6,22},{7,23},{8,24},{9,... | collective-permute-start | bytes 1327112 | tf_op jit(solution)/shard_map/ppermute | solution.py:46
  95.4 26.7 %collective-permute-start.18 = (bf16[1,1152,384]{2,1,0:T(8,128)(2,1)}, bf16[1,1152,384]{2,1,0:T(8,128)(2,1)}, u32[]{:S(2)}, u32[]{:S(2)}) collective-permute-start(bf16[1,1152,384]{2,1,0:T(8,128)(2,1)} %dynamic-slice_bitcast_fusion.1), channel_id=1, source_target_pairs={{0,64},{1,65},{2,66},{3,67},{4,68},{5,69},{6,70},{7,71},{8,72},{9,... | collective-permute-start | bytes 2654216 | tf_op jit(solution)/shard_map/ppermute | solution.py:46
  103.0 42.7 %all-to-all-start = ((bf16[16,24,1408]{2,1,0:T(8,128)(2,1)}), bf16[16,24,1408]{2,1,0:T(8,128)(2,1)}, u32[]{:S(2)}, u32[]{:S(2)}) async-start(bf16[16,24,1408]{2,1,0:T(8,128)(2,1)} %bitcast.174), calls=%async_computation | async-start | bytes 2162688 | tf_op jit(solution)/shard_map/all_to_all | solution.py:346
  114.2 26.6 %collective-permute-start.21 = (bf16[2,288,384]{2,1,0:T(8,128)(2,1)S(1)}, bf16[2,288,384]{2,1,0:T(8,128)(2,1)S(1)}, u32[]{:S(2)}, u32[]{:S(2)}) collective-permute-start(bf16[2,288,384]{2,1,0:T(8,128)(2,1)S(1)} %slice_bitcast_fusion), channel_id=1, source_target_pairs={{0,48},{1,49},{2,50},{3,51},{4,52},{5,53},{6,54},{7,55},{8,56},{9,... | collective-permute-start | bytes 1327112 | tf_op jit(solution)/shard_map/ppermute | solution.py:46
  123.6 17.6 %collective-permute-start.23 = (bf16[288,384]{1,0:T(8,128)(2,1)S(1)}, bf16[288,384]{1,0:T(8,128)(2,1)S(1)}, u32[]{:S(2)}, u32[]{:S(2)}) collective-permute-start(bf16[288,384]{1,0:T(8,128)(2,1)S(1)} %get-tuple-element.95), channel_id=1, source_target_pairs={{0,16},{1,17},{2,18},{3,19},{4,20},{5,21},{6,22},{7,23},{8,24},{9,... | collective-permute-start | bytes 663560 | tf_op jit(solution)/shard_map/ppermute | solution.py:46
  124.7 20.9 %collective-permute-start.24 = (bf16[288,384]{1,0:T(8,128)(2,1)S(1)}, bf16[288,384]{1,0:T(8,128)(2,1)S(1)}, u32[]{:S(2)}, u32[]{:S(2)}) collective-permute-start(bf16[288,384]{1,0:T(8,128)(2,1)S(1)} %get-tuple-element.97), channel_id=1, source_target_pairs={{0,48},{1,49},{2,50},{3,51},{4,52},{5,53},{6,54},{7,55},{8,56},{9,... | collective-permute-start | bytes 663560 | tf_op jit(solution)/shard_map/ppermute | solution.py:46
  124.7 20.9 %collective-permute-start.25 = (bf16[288,384]{1,0:T(8,128)(2,1)S(1)}, bf16[288,384]{1,0:T(8,128)(2,1)S(1)}, u32[]{:S(2)}, u32[]{:S(2)}) collective-permute-start(bf16[288,384]{1,0:T(8,128)(2,1)S(1)} %get-tuple-element.96), channel_id=1, source_target_pairs={{0,32},{1,33},{2,34},{3,35},{4,36},{5,37},{6,38},{7,39},{8,40},{9,... | collective-permute-start | bytes 663560 | tf_op jit(solution)/shard_map/ppermute | solution.py:46
  147.2 8.7 %collective-permute-start.26 = (bf16[96,384]{1,0:T(8,128)(2,1)S(1)}, bf16[96,384]{1,0:T(8,128)(2,1)S(1)}, u32[]{:S(2)}, u32[]{:S(2)}) collective-permute-start(bf16[96,384]{1,0:T(8,128)(2,1)S(1)} %pad_maximum_fusion.14), channel_id=1, source_target_pairs={{0,0},{1,2},{2,1},{3,3},{4,4},{5,6},{6,5},{7,7},{8,8},{9,10},{10,9... | collective-permute-start | bytes 221192 | tf_op jit(solution)/shard_map/ppermute | solution.py:46
  152.5 7.8 %collective-permute-start.28 = (bf16[5,72,384]{2,1,0:T(8,128)(2,1)S(1)}, bf16[5,72,384]{2,1,0:T(8,128)(2,1)S(1)}, u32[]{:S(2)}, u32[]{:S(2)}) collective-permute-start(bf16[5,72,384]{2,1,0:T(8,128)(2,1)S(1)} %get-tuple-element.92), channel_id=1, source_target_pairs={{0,4},{1,5},{2,6},{3,7},{4,0},{5,1},{6,2},{7,3},{8,12},{9,13},{10,... | collective-permute-start | bytes 829448 | tf_op jit(solution)/shard_map/ppermute | solution.py:46
  153.5 8.6 %collective-permute-start.29 = (bf16[5,72,384]{2,1,0:T(8,128)(2,1)S(1)}, bf16[5,72,384]{2,1,0:T(8,128)(2,1)S(1)}, u32[]{:S(2)}, u32[]{:S(2)}) collective-permute-start(bf16[5,72,384]{2,1,0:T(8,128)(2,1)S(1)} %get-tuple-element.94), channel_id=1, source_target_pairs={{0,12},{1,13},{2,14},{3,15},{4,8},{5,9},{6,10},{7,11},{8,4},{9,5},... | collective-permute-start | bytes 829448 | tf_op jit(solution)/shard_map/ppermute | solution.py:46
  155.1 13.0 %collective-permute-start.30 = (bf16[5,72,384]{2,1,0:T(8,128)(2,1)S(1)}, bf16[5,72,384]{2,1,0:T(8,128)(2,1)S(1)}, u32[]{:S(2)}, u32[]{:S(2)}) collective-permute-start(bf16[5,72,384]{2,1,0:T(8,128)(2,1)S(1)} %get-tuple-element.93), channel_id=1, source_target_pairs={{0,8},{1,9},{2,10},{3,11},{4,12},{5,13},{6,14},{7,15},{8,0},{9,1},... | collective-permute-start | bytes 829448 | tf_op jit(solution)/shard_map/ppermute | solution.py:46
  168.3 10.1 %collective-permute-start.31 = (bf16[216,384]{1,0:T(8,128)(2,1)S(1)}, bf16[216,384]{1,0:T(8,128)(2,1)S(1)}, u32[]{:S(2)}, u32[]{:S(2)}) collective-permute-start(bf16[216,384]{1,0:T(8,128)(2,1)S(1)} %bitcast.188), channel_id=1, source_target_pairs={{0,0},{1,2},{2,1},{3,3},{4,4},{5,6},{6,5},{7,7},{8,8},{9,10},{10,9... | collective-permute-start | bytes 497672 | tf_op jit(solution)/shard_map/ppermute | solution.py:46
  (29 other events, 173.2 us)

commit v11 on v10

--- a/solution.py
+++ b/solution.py
@@ -272,9 +272,8 @@
     spare = lanes - 1344 * (1 - c)
 
     def with_scalars(v, scalars):
-        for n, s in enumerate(scalars):
-            inside = (spare >= 32 * n) & (spare < 32 * n + 32)
-            v = jnp.where(inside, s * (1.0 + (spare - 32 * n).astype(F32) / 32), v)
+        mark = jnp.where(spare < 32, scalars[0], scalars[1]) * (1.0 + (spare % 32).astype(F32) / 32)
+        v = jnp.where((spare >= 0) & (spare < 64), mark, v)
         return v
 
     def halves(v, width):
@@ -292,10 +291,11 @@
         (gb2, logit_grad, partial_loss, send(stream, CORE))
     )
     near, far = halves(logit_grad, 1408)
-    scal = jnp.stack([weight_part, partial_loss])
+    lane = lax.broadcasted_iota(jnp.int32, (1, 128), 1)
+    scal = jnp.where(lane == 0, weight_part, partial_loss)
     scal = scal + send(scal, CORE)
     head_half = pair_dot(stream, near, far_stream, send(far, CORE))
-    head_half = with_scalars(head_half, (scal[0], scal[1])).astype(BF)
+    head_half = with_scalars(head_half, (scal[0, 0], scal[0, 1])).astype(BF)
     head_got = give(head_half, xl, ALONG_X)
 
     def conv_grad(layer, grad_bf):
@@ -343,7 +343,8 @@
     half0, half1, head_half, part2_z = lax.optimization_barrier((half0, half1, head_half, part2_z))
     head_x = take(head_half, head_got, xl)
     head_x, half1, part2_z = lax.optimization_barrier((head_x, half1, part2_z))
-    head_plane = lax.all_to_all(head_x.reshape(16, 24, 1408), ("z", "y"), 0, 0, tiled=True)
+    head_y = lax.all_to_all(head_x.reshape(4, 4, 24, 1408), "y", 1, 1, tiled=True)
+    head_y = jnp.sum(head_y.astype(F32), axis=1).astype(BF)
     g0 = g1 + through(trunk[0], conv_back(gb0, conv_weight[0], 64, 256))
     g0, half1, part2_z = lax.optimization_barrier((g0, half1, part2_z))
     keep1 = jnp.stack([pick(half1, z, 1), pick(half1, z ^ 3, 1)])
@@ -352,7 +353,8 @@
     part2 = take(part2_z, got2, z % 2)
     half0 = take(half0, got0, xl).reshape(4, 288, 384)
     got0 = [send(pick(half0, z ^ k), ALONG_Z[k]) for k in (1, 3, 2)]
-    half0, keep1 = lax.optimization_barrier((half0, keep1))
+    half0, keep1, head_y = lax.optimization_barrier((half0, keep1, head_y))
+    head_plane = lax.all_to_all(head_y, "z", 0, 0, tiled=True)
     part1 = (keep1[0].astype(F32) + got1.astype(F32)).astype(BF)
     part0 = sum((g.astype(F32) for g in got0), pick(half0, z).astype(F32)).astype(BF)
     early = jnp.concatenate(

time: 183 us -> 180 us (0.984)
  waiting for transfers between devices: 47.3 us -> 32.8 us
  local copies, waits for them, and re-layouts: 5.56 us -> 9.73 us
  other arithmetic: 19.7 us -> 22.5 us
  starting transfers between devices: 69.1 us -> 71.8 us
    ppermute x35, waiting for transfers between devices: 47.3 us -> 31.8 us  [send(): return lax.ppermute(v, AXES, pairs)]
    ppermute x35, starting transfers between devices: 61.4 us -> 64.1 us  [send(): return lax.ppermute(v, AXES, pairs)]
    reduce_sum x0 -> x1, other arithmetic: none -> 2.17 us  [per_device(): head_y = jnp.sum(head_y.astype(F32), axis=1).astype(BF)]
    all_to_all x1 -> x2, starting transfers between devices: 7.66 us -> 7.7 us  [the longest x1 4.25 us: per_device(): lax.all_to_all(head_x.reshape(4, 4, 24, 1408), 'y', 1, 1, tiled=True)]
  transfers between devices with their start and end apart: 36 -> 37, of which waited for: 13 -> 12; matrix products, arithmetic and copies ran while one was open for 21% -> 27% of each run, Pallas kernels for 2% -> 2%
where the time goes in v11:
time: 180 us; the launch traced here: 178 us
  starting transfers between devices  71.8 us (40%)
  waiting for transfers between devices  32.8 us (18%)
  other arithmetic  22.5 us (12%)
  matrix products  21.3 us (12%)
  Pallas kernels  15 us (8%)
  local copies, waits for them, and re-layouts  9.73 us (5%)
  between operations  4.78 us (3%)
    ppermute x35, starting transfers between devices, send(): return lax.ppermute(v, AXES, pairs)  64.1 us
    ppermute x35, waiting for transfers between devices, send(): return lax.ppermute(v, AXES, pairs)  31.8 us
    pallas_call x3, Pallas kernels, on_core(): pl.pallas_call(kernel, out_shape=[jax.ShapeDtypeStruct((rows, 768), kind)...  15 us
    dot_general x1, matrix products, per_device(): logits = jnp.dot(stream, head_weight, preferred_element_type=F32)  5.81 us
    dot_general x10, matrix products, pair_dot(): jnp.dot(a.T, b, preferred_element_type=F32)  4.37 us
    dot_general x10, matrix products, pair_dot(): jnp.dot(far_a.T, far_b, preferred_element_type=F32)  4.31 us
    all_to_all x1, starting transfers between devices, per_device(): lax.all_to_all(head_x.reshape(4, 4, 24, 1408), 'y', 1, 1, tiled=True)  4.25 us
    convert_element_type x3, other arithmetic, take(): return total.astype(BF).reshape(rows // 2, lanes)  4.04 us
  transfers between devices with their start and end apart: 37, of which 12 were waited for; matrix products, arithmetic and copies ran while one was open for 27% of the time, Pallas kernels for 2%

profile of v11, /device:TPU:1, one launch (start us, length us, event | category | flops | bytes accessed | tf_op | source)
XLA Modules:
  0.0 178.0 jit_solution(1724652050617817629)
XLA Ops:
  1.7 4.6 %collective-permute-start = (bf16[192,768]{1,0:T(8,128)(2,1)S(1)}, bf16[192,768]{1,0:T(8,128)(2,1)S(1)}, u32[]{:S(2)}, u32[]{:S(2)}) collective-permute-start(bf16[192,768]{1,0:T(8,128)(2,1)S(1)} %get-tuple-element.121), channel_id=1, source_target_pairs={{2,4},{3,5},{6,8},{7,9},{10,12},{11,13},{14,16},{15,17},{18,20},{1... | collective-permute-start | bytes 884744 | tf_op jit(solution)/shard_map/ppermute | solution.py:46
  7.0 3.7 %collective-permute-done = bf16[192,768]{1,0:T(8,128)(2,1)S(1)} collective-permute-done((bf16[192,768]{1,0:T(8,128)(2,1)S(1)}, bf16[192,768]{1,0:T(8,128)(2,1)S(1)}, u32[]{:S(2)}, u32[]{:S(2)}) %collective-permute-start) | collective-permute-done | bytes 294944 | tf_op jit(solution)/shard_map/ppermute | solution.py:46
  11.6 8.2 %shard_map.93 = (bf16[384,768]{1,0:T(8,128)(2,1)}, bf16[512,768]{1,0:T(8,128)(2,1)}, bf16[512,768]{1,0:T(8,128)(2,1)}, bf16[256,768]{1,0:T(8,128)(2,1)}, bf16[256,768]{1,0:T(8,128)(2,1)}) custom-call(s32[2]{0:T(128)} %add_convert_fusion.1.flags, bf16[192,768]{1,0:T(8,128)(2,1)} %get-tuple-element.109.before, bf16[256,768]{1,0:T(8,128)(2,1)} %bitcast.179, ...), custom_call_target="tpu_custom_call" | custom-call | flops 2717908992 | bytes 7077888 | tf_op jit(solution)/shard_map/pallas_call | solution.py:173
  20.0 3.8 %collective-permute-start.2 = (bf16[256,768]{1,0:T(8,128)(2,1)}, bf16[256,768]{1,0:T(8,128)(2,1)S(1)}, u32[]{:S(2)}, u32[]{:S(2)}) collective-permute-start(bf16[256,768]{1,0:T(8,128)(2,1)} %get-tuple-element.45.own), channel_id=1, source_target_pairs={{2,4},{3,5},{6,8},{7,9},{10,12},{11,13},{14,16},{15,17},{18,20},{1... | collective-permute-start | bytes 1179656 | tf_op jit(solution)/shard_map/ppermute | solution.py:46
  25.0 4.4 %collective-permute-done.2 = bf16[256,768]{1,0:T(8,128)(2,1)S(1)} collective-permute-done((bf16[256,768]{1,0:T(8,128)(2,1)}, bf16[256,768]{1,0:T(8,128)(2,1)S(1)}, u32[]{:S(2)}, u32[]{:S(2)}) %collective-permute-start.2) | collective-permute-done | bytes 393248 | tf_op jit(solution)/shard_map/ppermute | solution.py:46
  29.6 3.4 %shard_map.94 = (bf16[768,768]{1,0:T(8,128)(2,1)S(1)}, bf16[256,768]{1,0:T(8,128)(2,1)S(1)}) custom-call(bf16[256,768]{1,0:T(8,128)(2,1)S(1)} %get-tuple-element.47.before, bf16[256,768]{1,0:T(8,128)(2,1)S(1)} %copy-done.1, bf16[256,768]{1,0:T(8,128)(2,1)S(1)} %get-tuple-element.102.after, bf16[256,768]{1,0:T(8,128)(2,1)S(1)} %copy-done, ...), custom_call_target="tpu_custom_call" | custom-call | flops 905969664 | bytes 3538944 | tf_op jit(solution)/shard_map/pallas_call | solution.py:173
  33.7 5.8 %fusion.5 = (f32[]{:T(128)}, bf16[256,2688]{1,0:T(8,128)(2,1)S(1)}) fusion(s32[1,256,2688]{2,1,0:T(8,128)} %param.9, f32[256]{0:T(256)S(1)} %bitcast.190, bf16[256,768]{1,0:T(8,128)(2,1)S(1)} %get-tuple-element.49, bf16[768,2688]{1,0:T(8,128)(2,1)S(1)} %copy-done.13), kind=kOutput, calls=%fused_computation.9 | convolution fusion | flops 1070039040 | bytes 8651780 | tf_op jit(solution)/shard_map/dot_general | solution.py:264
  40.9 3.7 %collective-permute-start.8 = (bf16[256,768]{1,0:T(8,128)(2,1)S(1)}, bf16[256,768]{1,0:T(8,128)(2,1)S(1)}, u32[]{:S(2)}, u32[]{:S(2)}) collective-permute-start(bf16[256,768]{1,0:T(8,128)(2,1)S(1)} %get-tuple-element.52.own), channel_id=1, source_target_pairs={{2,4},{3,5},{6,8},{7,9},{10,12},{11,13},{14,16},{15,17},{18,20},{1... | collective-permute-start | bytes 1179656 | tf_op jit(solution)/shard_map/ppermute | solution.py:46
  54.5 8.8 %collective-permute-start.16 = (bf16[2,576,384]{2,1,0:T(8,128)(2,1)}, bf16[2,576,384]{2,1,0:T(8,128)(2,1)}, u32[]{:S(2)}, u32[]{:S(2)}) collective-permute-start(bf16[2,576,384]{2,1,0:T(8,128)(2,1)} %dynamic-slice_bitcast_fusion.2), channel_id=1, source_target_pairs={{0,48},{1,49},{2,50},{3,51},{4,52},{5,53},{6,54},{7,55},{8,56},{9,... | collective-permute-start | bytes 2654216 | tf_op jit(solution)/shard_map/ppermute | solution.py:46
  64.9 3.4 %shard_map.95 = (f32[256,768]{1,0:T(8,128)S(1)}, bf16[256,768]{1,0:T(8,128)(2,1)S(1)}) custom-call(bf16[256,768]{1,0:T(8,128)(2,1)S(1)} %get-tuple-element.57.before, bf16[256,768]{1,0:T(8,128)(2,1)S(1)} %get-tuple-element.52.own, bf16[256,768]{1,0:T(8,128)(2,1)S(1)} %get-tuple-element.100.after, bf16[256,768]{1,0:T(8,128)(2,1)S(1)} %copy-done, ...), custom_call_target="tpu_custom_call" | custom-call | flops 905969664 | bytes 3538944 | tf_op jit(solution)/shard_map/pallas_call | solution.py:173
  68.4 2.1 %collective-permute-start.13 = (bf16[192,768]{1,0:T(8,128)(2,1)S(1)}, bf16[192,768]{1,0:T(8,128)(2,1)S(1)}, u32[]{:S(2)}, u32[]{:S(2)}) collective-permute-start(bf16[192,768]{1,0:T(8,128)(2,1)S(1)} %get-tuple-element.114), channel_id=1, source_target_pairs={{2,4},{3,5},{6,8},{7,9},{10,12},{11,13},{14,16},{15,17},{18,20},{1... | collective-permute-start | bytes 884744 | tf_op jit(solution)/shard_map/ppermute | solution.py:46
  71.2 6.7 %collective-permute-start.19 = (bf16[1,384,1408]{2,1,0:T(8,128)(2,1)S(1)}, bf16[1,384,1408]{2,1,0:T(8,128)(2,1)S(1)}, u32[]{:S(2)}, u32[]{:S(2)}) collective-permute-start(bf16[1,384,1408]{2,1,0:T(8,128)(2,1)S(1)} %dynamic-slice_bitcast_fusion), channel_id=1, source_target_pairs={{0,64},{1,65},{2,66},{3,67},{4,68},{5,69},{6,70},{7,71},{8,72},{9,... | collective-permute-start | bytes 3244040 | tf_op jit(solution)/shard_map/ppermute | solution.py:46
  97.2 7.8 %collective-permute-start.18 = (bf16[1,1152,384]{2,1,0:T(8,128)(2,1)}, bf16[1,1152,384]{2,1,0:T(8,128)(2,1)}, u32[]{:S(2)}, u32[]{:S(2)}) collective-permute-start(bf16[1,1152,384]{2,1,0:T(8,128)(2,1)} %dynamic-slice_bitcast_fusion.1), channel_id=1, source_target_pairs={{0,64},{1,65},{2,66},{3,67},{4,68},{5,69},{6,70},{7,71},{8,72},{9,... | collective-permute-start | bytes 2654216 | tf_op jit(solution)/shard_map/ppermute | solution.py:46
  106.4 4.3 %all-to-all-start = ((bf16[4,4,24,1408]{3,2,0,1:T(8,128)(2,1)}), bf16[4,4,24,1408]{3,2,0,1:T(8,128)(2,1)}, u32[]{:S(2)}, u32[]{:S(2)}) async-start(bf16[4,4,24,1408]{3,2,0,1:T(8,128)(2,1)} %copy.17), calls=%async_computation | async-start | bytes 2162688 | tf_op jit(solution)/shard_map/all_to_all | solution.py:346
  118.0 7.4 %collective-permute-done.18 = bf16[1,1152,384]{2,1,0:T(8,128)(2,1)} collective-permute-done((bf16[1,1152,384]{2,1,0:T(8,128)(2,1)}, bf16[1,1152,384]{2,1,0:T(8,128)(2,1)}, u32[]{:S(2)}, u32[]{:S(2)}) %collective-permute-start.18) | collective-permute-done | bytes 884768 | tf_op jit(solution)/shard_map/ppermute | solution.py:46
  130.2 2.2 %reduce_sum.62 = bf16[4,24,1408]{2,1,0:T(8,128)(2,1)} reduce(bf16[4,4,24,1408]{3,2,0,1:T(8,128)(2,1)} %all-to-all-done, bf16[]{:T(256)} %constant.163.clone.1), dimensions={1}, to_apply=%region_2.3 | reduce | flops 405504 | bytes 1351682 | tf_op jit(solution)/shard_map/reduce_sum | solution.py:347
  132.4 3.4 %all-to-all-start.1 = ((bf16[4,24,1408]{2,1,0:T(8,128)(2,1)}), bf16[4,24,1408]{2,1,0:T(8,128)(2,1)S(1)}, u32[]{:S(2)}, u32[]{:S(2)}) async-start(bf16[4,24,1408]{2,1,0:T(8,128)(2,1)} %reduce_sum.62), calls=%async_computation.1 | async-start | bytes 540672 | tf_op jit(solution)/shard_map/all_to_all | solution.py:357
  138.0 2.6 %collective-permute-done.24 = bf16[288,384]{1,0:T(8,128)(2,1)S(1)} collective-permute-done((bf16[288,384]{1,0:T(8,128)(2,1)S(1)}, bf16[288,384]{1,0:T(8,128)(2,1)S(1)}, u32[]{:S(2)}, u32[]{:S(2)}) %collective-permute-start.24) | collective-permute-done | bytes 221216 | tf_op jit(solution)/shard_map/ppermute | solution.py:46
  142.8 7.1 %collective-permute-start.26 = (bf16[96,384]{1,0:T(8,128)(2,1)S(1)}, bf16[96,384]{1,0:T(8,128)(2,1)S(1)}, u32[]{:S(2)}, u32[]{:S(2)}) collective-permute-start(bf16[96,384]{1,0:T(8,128)(2,1)S(1)} %pad_maximum_fusion.14), channel_id=1, source_target_pairs={{0,0},{1,2},{2,1},{3,3},{4,4},{5,6},{6,5},{7,7},{8,8},{9,10},{10,9... | collective-permute-start | bytes 221192 | tf_op jit(solution)/shard_map/ppermute | solution.py:46
  151.0 2.5 %collective-permute-start.30 = (bf16[5,72,384]{2,1,0:T(8,128)(2,1)S(1)}, bf16[5,72,384]{2,1,0:T(8,128)(2,1)S(1)}, u32[]{:S(2)}, u32[]{:S(2)}) collective-permute-start(bf16[5,72,384]{2,1,0:T(8,128)(2,1)S(1)} %get-tuple-element.95), channel_id=1, source_target_pairs={{0,8},{1,9},{2,10},{3,11},{4,12},{5,13},{6,14},{7,15},{8,0},{9,1},... | collective-permute-start | bytes 829448 | tf_op jit(solution)/shard_map/ppermute | solution.py:46
  153.5 4.4 %collective-permute-done.28 = bf16[5,72,384]{2,1,0:T(8,128)(2,1)S(1)} collective-permute-done((bf16[5,72,384]{2,1,0:T(8,128)(2,1)S(1)}, bf16[5,72,384]{2,1,0:T(8,128)(2,1)S(1)}, u32[]{:S(2)}, u32[]{:S(2)}) %collective-permute-start.28) | collective-permute-done | bytes 276512 | tf_op jit(solution)/shard_map/ppermute | solution.py:46
  158.0 2.2 %collective-permute-done.29 = bf16[5,72,384]{2,1,0:T(8,128)(2,1)S(1)} collective-permute-done((bf16[5,72,384]{2,1,0:T(8,128)(2,1)S(1)}, bf16[5,72,384]{2,1,0:T(8,128)(2,1)S(1)}, u32[]{:S(2)}, u32[]{:S(2)}) %collective-permute-start.29) | collective-permute-done | bytes 276512 | tf_op jit(solution)/shard_map/ppermute | solution.py:46
  160.1 4.2 %collective-permute-done.30 = bf16[5,72,384]{2,1,0:T(8,128)(2,1)S(1)} collective-permute-done((bf16[5,72,384]{2,1,0:T(8,128)(2,1)S(1)}, bf16[5,72,384]{2,1,0:T(8,128)(2,1)S(1)}, u32[]{:S(2)}, u32[]{:S(2)}) %collective-permute-start.30) | collective-permute-done | bytes 276512 | tf_op jit(solution)/shard_map/ppermute | solution.py:46
  164.6 4.2 %collective-permute-start.31 = (bf16[216,384]{1,0:T(8,128)(2,1)S(1)}, bf16[216,384]{1,0:T(8,128)(2,1)S(1)}, u32[]{:S(2)}, u32[]{:S(2)}) collective-permute-start(bf16[216,384]{1,0:T(8,128)(2,1)S(1)} %bitcast.186), channel_id=1, source_target_pairs={{0,0},{1,2},{2,1},{3,3},{4,4},{5,6},{6,5},{7,7},{8,8},{9,10},{10,9... | collective-permute-start | bytes 497672 | tf_op jit(solution)/shard_map/ppermute | solution.py:46
  (186 shorter events, 62.3 us)
Async XLA Ops:
  1.7 9.0 %collective-permute-start = (bf16[192,768]{1,0:T(8,128)(2,1)S(1)}, bf16[192,768]{1,0:T(8,128)(2,1)S(1)}, u32[]{:S(2)}, u32[]{:S(2)}) collective-permute-start(bf16[192,768]{1,0:T(8,128)(2,1)S(1)} %get-tuple-element.121), channel_id=1, source_target_pairs={{2,4},{3,5},{6,8},{7,9},{10,12},{11,13},{14,16},{15,17},{18,20},{1... | collective-permute-start | bytes 884744 | tf_op jit(solution)/shard_map/ppermute | solution.py:46
  19.9 9.7 %collective-permute-start.5 = (bf16[512,768]{1,0:T(8,128)(2,1)}, bf16[512,768]{1,0:T(8,128)(2,1)S(1)}, u32[]{:S(2)}, u32[]{:S(2)}) collective-permute-start(bf16[512,768]{1,0:T(8,128)(2,1)} %get-tuple-element.46), channel_id=1, source_target_pairs={{0,2},{1,3},{2,0},{3,1},{4,6},{5,7},{6,4},{7,5},{8,10},{9,11},{10,... | collective-permute-start | bytes 2359304 | tf_op jit(solution)/shard_map/ppermute | solution.py:46
  20.0 9.4 %collective-permute-start.2 = (bf16[256,768]{1,0:T(8,128)(2,1)}, bf16[256,768]{1,0:T(8,128)(2,1)S(1)}, u32[]{:S(2)}, u32[]{:S(2)}) collective-permute-start(bf16[256,768]{1,0:T(8,128)(2,1)} %get-tuple-element.45.own), channel_id=1, source_target_pairs={{2,4},{3,5},{6,8},{7,9},{10,12},{11,13},{14,16},{15,17},{18,20},{1... | collective-permute-start | bytes 1179656 | tf_op jit(solution)/shard_map/ppermute | solution.py:46
  40.9 22.4 %collective-permute-start.8 = (bf16[256,768]{1,0:T(8,128)(2,1)S(1)}, bf16[256,768]{1,0:T(8,128)(2,1)S(1)}, u32[]{:S(2)}, u32[]{:S(2)}) collective-permute-start(bf16[256,768]{1,0:T(8,128)(2,1)S(1)} %get-tuple-element.52.own), channel_id=1, source_target_pairs={{2,4},{3,5},{6,8},{7,9},{10,12},{11,13},{14,16},{15,17},{18,20},{1... | collective-permute-start | bytes 1179656 | tf_op jit(solution)/shard_map/ppermute | solution.py:46
  44.5 18.7 %collective-permute-start.9 = (bf16[256,768]{1,0:T(8,128)(2,1)S(1)}, bf16[256,768]{1,0:T(8,128)(2,1)S(1)}, u32[]{:S(2)}, u32[]{:S(2)}) collective-permute-start(bf16[256,768]{1,0:T(8,128)(2,1)S(1)} %get-tuple-element.52.own), channel_id=1, source_target_pairs={{0,2},{1,3},{2,0},{3,1},{4,6},{5,7},{6,4},{7,5},{8,10},{9,11},{10,... | collective-permute-start | bytes 1179656 | tf_op jit(solution)/shard_map/ppermute | solution.py:46
  46.7 16.6 %collective-permute-start.11 = (bf16[256,1408]{1,0:T(8,128)(2,1)S(1)}, bf16[256,1408]{1,0:T(8,128)(2,1)S(1)}, u32[]{:S(2)}, u32[]{:S(2)}) collective-permute-start(bf16[256,1408]{1,0:T(8,128)(2,1)S(1)} %broadcast_select_fusion), channel_id=1, source_target_pairs={{0,2},{1,3},{2,0},{3,1},{4,6},{5,7},{6,4},{7,5},{8,10},{9,11},{10,... | collective-permute-start | bytes 2162696 | tf_op jit(solution)/shard_map/ppermute | solution.py:46
  54.5 31.1 %collective-permute-start.16 = (bf16[2,576,384]{2,1,0:T(8,128)(2,1)}, bf16[2,576,384]{2,1,0:T(8,128)(2,1)}, u32[]{:S(2)}, u32[]{:S(2)}) collective-permute-start(bf16[2,576,384]{2,1,0:T(8,128)(2,1)} %dynamic-slice_bitcast_fusion.2), channel_id=1, source_target_pairs={{0,48},{1,49},{2,50},{3,51},{4,52},{5,53},{6,54},{7,55},{8,56},{9,... | collective-permute-start | bytes 2654216 | tf_op jit(solution)/shard_map/ppermute | solution.py:46
  68.4 13.3 %collective-permute-start.13 = (bf16[192,768]{1,0:T(8,128)(2,1)S(1)}, bf16[192,768]{1,0:T(8,128)(2,1)S(1)}, u32[]{:S(2)}, u32[]{:S(2)}) collective-permute-start(bf16[192,768]{1,0:T(8,128)(2,1)S(1)} %get-tuple-element.114), channel_id=1, source_target_pairs={{2,4},{3,5},{6,8},{7,9},{10,12},{11,13},{14,16},{15,17},{18,20},{1... | collective-permute-start | bytes 884744 | tf_op jit(solution)/shard_map/ppermute | solution.py:46
  70.5 11.3 %collective-permute-start.14 = (bf16[192,768]{1,0:T(8,128)(2,1)S(1)}, bf16[192,768]{1,0:T(8,128)(2,1)S(1)}, u32[]{:S(2)}, u32[]{:S(2)}) collective-permute-start(bf16[192,768]{1,0:T(8,128)(2,1)S(1)} %get-tuple-element.115), channel_id=1, source_target_pairs={{0,2},{1,3},{2,0},{3,1},{4,6},{5,7},{6,4},{7,5},{8,10},{9,11},{10,... | collective-permute-start | bytes 884744 | tf_op jit(solution)/shard_map/ppermute | solution.py:46
  71.2 33.9 %collective-permute-start.19 = (bf16[1,384,1408]{2,1,0:T(8,128)(2,1)S(1)}, bf16[1,384,1408]{2,1,0:T(8,128)(2,1)S(1)}, u32[]{:S(2)}, u32[]{:S(2)}) collective-permute-start(bf16[1,384,1408]{2,1,0:T(8,128)(2,1)S(1)} %dynamic-slice_bitcast_fusion), channel_id=1, source_target_pairs={{0,64},{1,65},{2,66},{3,67},{4,68},{5,69},{6,70},{7,71},{8,72},{9,... | collective-permute-start | bytes 3244040 | tf_op jit(solution)/shard_map/ppermute | solution.py:46
  81.7 32.5 %collective-permute-start.20 = (bf16[2,2,288,384]{3,2,1,0:T(8,128)(2,1)}, bf16[2,2,288,384]{3,2,1,0:T(8,128)(2,1)}, u32[]{:S(2)}, u32[]{:S(2)}) collective-permute-start(bf16[2,2,288,384]{3,2,1,0:T(8,128)(2,1)} %pad_maximum_fusion.3), channel_id=1, source_target_pairs={{0,16},{1,17},{2,18},{3,19},{4,20},{5,21},{6,22},{7,23},{8,24},{9,... | collective-permute-start | bytes 2654216 | tf_op jit(solution)/shard_map/ppermute | solution.py:46
  90.0 21.9 %collective-permute-start.22 = (bf16[2,288,384]{2,1,0:T(8,128)(2,1)}, bf16[2,288,384]{2,1,0:T(8,128)(2,1)}, u32[]{:S(2)}, u32[]{:S(2)}) collective-permute-start(bf16[2,288,384]{2,1,0:T(8,128)(2,1)} %dynamic-slice_bitcast_fusion.3), channel_id=1, source_target_pairs={{0,16},{1,17},{2,18},{3,19},{4,20},{5,21},{6,22},{7,23},{8,24},{9,... | collective-permute-start | bytes 1327112 | tf_op jit(solution)/shard_map/ppermute | solution.py:46
  97.2 28.2 %collective-permute-start.18 = (bf16[1,1152,384]{2,1,0:T(8,128)(2,1)}, bf16[1,1152,384]{2,1,0:T(8,128)(2,1)}, u32[]{:S(2)}, u32[]{:S(2)}) collective-permute-start(bf16[1,1152,384]{2,1,0:T(8,128)(2,1)} %dynamic-slice_bitcast_fusion.1), channel_id=1, source_target_pairs={{0,64},{1,65},{2,66},{3,67},{4,68},{5,69},{6,70},{7,71},{8,72},{9,... | collective-permute-start | bytes 2654216 | tf_op jit(solution)/shard_map/ppermute | solution.py:46
  106.4 23.8 %all-to-all-start = ((bf16[4,4,24,1408]{3,2,0,1:T(8,128)(2,1)}), bf16[4,4,24,1408]{3,2,0,1:T(8,128)(2,1)}, u32[]{:S(2)}, u32[]{:S(2)}) async-start(bf16[4,4,24,1408]{3,2,0,1:T(8,128)(2,1)} %copy.17), calls=%async_computation | async-start | bytes 2162688 | tf_op jit(solution)/shard_map/all_to_all | solution.py:346
  116.4 19.4 %collective-permute-start.21 = (bf16[2,288,384]{2,1,0:T(8,128)(2,1)}, bf16[2,288,384]{2,1,0:T(8,128)(2,1)}, u32[]{:S(2)}, u32[]{:S(2)}) collective-permute-start(bf16[2,288,384]{2,1,0:T(8,128)(2,1)} %slice_bitcast_fusion), channel_id=1, source_target_pairs={{0,48},{1,49},{2,50},{3,51},{4,52},{5,53},{6,54},{7,55},{8,56},{9,... | collective-permute-start | bytes 1327112 | tf_op jit(solution)/shard_map/ppermute | solution.py:46
  126.9 11.1 %collective-permute-start.23 = (bf16[288,384]{1,0:T(8,128)(2,1)S(1)}, bf16[288,384]{1,0:T(8,128)(2,1)S(1)}, u32[]{:S(2)}, u32[]{:S(2)}) collective-permute-start(bf16[288,384]{1,0:T(8,128)(2,1)S(1)} %get-tuple-element.97), channel_id=1, source_target_pairs={{0,16},{1,17},{2,18},{3,19},{4,20},{5,21},{6,22},{7,23},{8,24},{9,... | collective-permute-start | bytes 663560 | tf_op jit(solution)/shard_map/ppermute | solution.py:46
  128.2 12.4 %collective-permute-start.24 = (bf16[288,384]{1,0:T(8,128)(2,1)S(1)}, bf16[288,384]{1,0:T(8,128)(2,1)S(1)}, u32[]{:S(2)}, u32[]{:S(2)}) collective-permute-start(bf16[288,384]{1,0:T(8,128)(2,1)S(1)} %get-tuple-element.99), channel_id=1, source_target_pairs={{0,48},{1,49},{2,50},{3,51},{4,52},{5,53},{6,54},{7,55},{8,56},{9,... | collective-permute-start | bytes 663560 | tf_op jit(solution)/shard_map/ppermute | solution.py:46
  128.2 12.4 %collective-permute-start.25 = (bf16[288,384]{1,0:T(8,128)(2,1)S(1)}, bf16[288,384]{1,0:T(8,128)(2,1)}, u32[]{:S(2)}, u32[]{:S(2)}) collective-permute-start(bf16[288,384]{1,0:T(8,128)(2,1)S(1)} %get-tuple-element.98), channel_id=1, source_target_pairs={{0,32},{1,33},{2,34},{3,35},{4,36},{5,37},{6,38},{7,39},{8,40},{9,... | collective-permute-start | bytes 663560 | tf_op jit(solution)/shard_map/ppermute | solution.py:46
  132.4 10.4 %all-to-all-start.1 = ((bf16[4,24,1408]{2,1,0:T(8,128)(2,1)}), bf16[4,24,1408]{2,1,0:T(8,128)(2,1)S(1)}, u32[]{:S(2)}, u32[]{:S(2)}) async-start(bf16[4,24,1408]{2,1,0:T(8,128)(2,1)} %reduce_sum.62), calls=%async_computation.1 | async-start | bytes 540672 | tf_op jit(solution)/shard_map/all_to_all | solution.py:357
  142.8 10.7 %collective-permute-start.26 = (bf16[96,384]{1,0:T(8,128)(2,1)S(1)}, bf16[96,384]{1,0:T(8,128)(2,1)S(1)}, u32[]{:S(2)}, u32[]{:S(2)}) collective-permute-start(bf16[96,384]{1,0:T(8,128)(2,1)S(1)} %pad_maximum_fusion.14), channel_id=1, source_target_pairs={{0,0},{1,2},{2,1},{3,3},{4,4},{5,6},{6,5},{7,7},{8,8},{9,10},{10,9... | collective-permute-start | bytes 221192 | tf_op jit(solution)/shard_map/ppermute | solution.py:46
  150.2 7.8 %collective-permute-start.28 = (bf16[5,72,384]{2,1,0:T(8,128)(2,1)S(1)}, bf16[5,72,384]{2,1,0:T(8,128)(2,1)S(1)}, u32[]{:S(2)}, u32[]{:S(2)}) collective-permute-start(bf16[5,72,384]{2,1,0:T(8,128)(2,1)S(1)} %get-tuple-element.94), channel_id=1, source_target_pairs={{0,4},{1,5},{2,6},{3,7},{4,0},{5,1},{6,2},{7,3},{8,12},{9,13},{10,... | collective-permute-start | bytes 829448 | tf_op jit(solution)/shard_map/ppermute | solution.py:46
  150.3 9.9 %collective-permute-start.29 = (bf16[5,72,384]{2,1,0:T(8,128)(2,1)S(1)}, bf16[5,72,384]{2,1,0:T(8,128)(2,1)S(1)}, u32[]{:S(2)}, u32[]{:S(2)}) collective-permute-start(bf16[5,72,384]{2,1,0:T(8,128)(2,1)S(1)} %get-tuple-element.96), channel_id=1, source_target_pairs={{0,12},{1,13},{2,14},{3,15},{4,8},{5,9},{6,10},{7,11},{8,4},{9,5},... | collective-permute-start | bytes 829448 | tf_op jit(solution)/shard_map/ppermute | solution.py:46
  151.0 13.3 %collective-permute-start.30 = (bf16[5,72,384]{2,1,0:T(8,128)(2,1)S(1)}, bf16[5,72,384]{2,1,0:T(8,128)(2,1)S(1)}, u32[]{:S(2)}, u32[]{:S(2)}) collective-permute-start(bf16[5,72,384]{2,1,0:T(8,128)(2,1)S(1)} %get-tuple-element.95), channel_id=1, source_target_pairs={{0,8},{1,9},{2,10},{3,11},{4,12},{5,13},{6,14},{7,15},{8,0},{9,1},... | collective-permute-start | bytes 829448 | tf_op jit(solution)/shard_map/ppermute | solution.py:46
  164.6 10.1 %collective-permute-start.31 = (bf16[216,384]{1,0:T(8,128)(2,1)S(1)}, bf16[216,384]{1,0:T(8,128)(2,1)S(1)}, u32[]{:S(2)}, u32[]{:S(2)}) collective-permute-start(bf16[216,384]{1,0:T(8,128)(2,1)S(1)} %bitcast.186), channel_id=1, source_target_pairs={{0,0},{1,2},{2,1},{3,3},{4,4},{5,6},{6,5},{7,7},{8,8},{9,10},{10,9... | collective-permute-start | bytes 497672 | tf_op jit(solution)/shard_map/ppermute | solution.py:46
  (31 other events, 180.7 us)

commit v12 on v11

--- a/solution.py
+++ b/solution.py
@@ -351,14 +351,15 @@
     keep1 = (keep1.astype(F32) + got1.astype(F32)).astype(BF)
     got1 = send(keep1[1], ALONG_Z[3])
     part2 = take(part2_z, got2, z % 2)
-    half0 = take(half0, got0, xl).reshape(4, 288, 384)
-    got0 = [send(pick(half0, z ^ k), ALONG_Z[k]) for k in (1, 3, 2)]
+    half0 = take(half0, got0, xl).reshape(4, 4, 72, 384)
+    got0 = [send(pick(half0, y ^ k, 1), ALONG_Y[k]) for k in (1, 3, 2)]
     half0, keep1, head_y = lax.optimization_barrier((half0, keep1, head_y))
     head_plane = lax.all_to_all(head_y, "z", 0, 0, tiled=True)
     part1 = (keep1[0].astype(F32) + got1.astype(F32)).astype(BF)
-    part0 = sum((g.astype(F32) for g in got0), pick(half0, z).astype(F32)).astype(BF)
+    part0 = sum((g.astype(F32) for g in got0), pick(half0, y, 1).astype(F32)).astype(BF)
+    got0 = [send(pick(part0, z ^ k), ALONG_Z[k]) for k in (1, 3, 2)]
     early = jnp.concatenate(
-        [v.reshape(-1, 4, 72, 384) for v in (part1[0], part1[1], part2[:288], part2[288:], part0)],
+        [v.reshape(-1, 4, 72, 384) for v in (part1[0], part1[1], part2)],
         axis=0,
     )
     got = [send(pick(early, y ^ k, 1), ALONG_Y[k]) for k in (1, 3, 2)]
@@ -367,13 +368,13 @@
     head_plane = jnp.concatenate(
         [head_plane[:, 384 * k : 384 * k + 384] for k in range(4)], axis=0
     )
-    head_sum = sum(send(head_plane, last_hop(0, m)).astype(F32) for m in range(2))
-    early, head_sum = lax.optimization_barrier((early, head_sum))
+    early, head_plane = lax.optimization_barrier((early, head_plane))
+    part0 = sum((g.astype(F32) for g in got0), pick(part0, z).astype(F32)).astype(BF)
     early = sum((g.astype(F32) for g in got), pick(early, y, 1).astype(F32)).astype(BF)
-    both = early[:4].reshape(2, 2, 72, 384)
-    near = jnp.concatenate([pick(both, xl, 1), early[4:]], axis=0).reshape(216, 384)
+    both = early.reshape(2, 2, 72, 384)
+    near = jnp.concatenate([pick(both, xl, 1).reshape(144, 384), part0, head_plane], axis=0)
     early, late = last_sum(near, pick(both, 1 - xl, 1).reshape(144, 384))
-    conv_sum = [late, early[:72], early[72:]]
+    conv_sum, head_sum = [late[:72], early[:72], early[72:]], late[72:]
 
     def own(v):
         half = v.shape[0] // 2

time: 180 us -> 178 us (0.989)
  waiting for transfers between devices: 32.8 us -> 35 us
    all_to_all x1, waiting for transfers between devices: 1.02 us -> 2.87 us  [per_device(): head_plane = lax.all_to_all(head_y, 'z', 0, 0, tiled=True)]
    ppermute x35 -> x36, starting transfers between devices: 64.1 us -> 62.8 us  [send(): return lax.ppermute(v, AXES, pairs)]
    ppermute x35 -> x36, waiting for transfers between devices: 31.8 us -> 32.1 us  [send(): return lax.ppermute(v, AXES, pairs)]
  transfers between devices with their start and end apart: 37 -> 38, of which waited for: 12 -> 10; matrix products, arithmetic and copies ran while one was open for 27% -> 26% of each run, Pallas kernels for 2% -> 2%
where the time goes in v12:
time: 178 us; the launch traced here: 177 us
  starting transfers between devices  70.5 us (40%)
  waiting for transfers between devices  35 us (20%)
  other arithmetic  22.3 us (13%)
  matrix products  21.3 us (12%)
  Pallas kernels  15 us (8%)
  local copies, waits for them, and re-layouts  7.99 us (4%)
  between operations  4.74 us (3%)
    ppermute x36, starting transfers between devices, send(): return lax.ppermute(v, AXES, pairs)  62.8 us
    ppermute x36, waiting for transfers between devices, send(): return lax.ppermute(v, AXES, pairs)  32.1 us
    pallas_call x3, Pallas kernels, on_core(): pl.pallas_call(kernel, out_shape=[jax.ShapeDtypeStruct((rows, 768), kind)...  15 us
    dot_general x1, matrix products, per_device(): logits = jnp.dot(stream, head_weight, preferred_element_type=F32)  5.82 us
    convert_element_type x3, other arithmetic, take(): return total.astype(BF).reshape(rows // 2, lanes)  4.68 us
    dot_general x10, matrix products, pair_dot(): jnp.dot(a.T, b, preferred_element_type=F32)  4.36 us
    dot_general x10, matrix products, pair_dot(): jnp.dot(far_a.T, far_b, preferred_element_type=F32)  4.31 us
    all_to_all x1, starting transfers between devices, per_device(): lax.all_to_all(head_x.reshape(4, 4, 24, 1408), 'y', 1, 1, tiled=True)  4.25 us
  transfers between devices with their start and end apart: 38, of which 10 were waited for; matrix products, arithmetic and copies ran while one was open for 26% of the time, Pallas kernels for 2%

profile of v12, /device:TPU:1, one launch (start us, length us, event | category | flops | bytes accessed | tf_op | source)
XLA Modules:
  0.0 176.9 jit_solution(5642892081394696248)
XLA Ops:
  1.7 4.6 %collective-permute-start = (bf16[192,768]{1,0:T(8,128)(2,1)S(1)}, bf16[192,768]{1,0:T(8,128)(2,1)S(1)}, u32[]{:S(2)}, u32[]{:S(2)}) collective-permute-start(bf16[192,768]{1,0:T(8,128)(2,1)S(1)} %get-tuple-element.123), channel_id=1, source_target_pairs={{2,4},{3,5},{6,8},{7,9},{10,12},{11,13},{14,16},{15,17},{18,20},{1... | collective-permute-start | bytes 884744 | tf_op jit(solution)/shard_map/ppermute | solution.py:46
  7.0 3.7 %collective-permute-done = bf16[192,768]{1,0:T(8,128)(2,1)S(1)} collective-permute-done((bf16[192,768]{1,0:T(8,128)(2,1)S(1)}, bf16[192,768]{1,0:T(8,128)(2,1)S(1)}, u32[]{:S(2)}, u32[]{:S(2)}) %collective-permute-start) | collective-permute-done | bytes 294944 | tf_op jit(solution)/shard_map/ppermute | solution.py:46
  11.6 8.2 %shard_map.93 = (bf16[384,768]{1,0:T(8,128)(2,1)}, bf16[512,768]{1,0:T(8,128)(2,1)}, bf16[512,768]{1,0:T(8,128)(2,1)}, bf16[256,768]{1,0:T(8,128)(2,1)}, bf16[256,768]{1,0:T(8,128)(2,1)}) custom-call(s32[2]{0:T(128)} %add_convert_fusion.1.flags, bf16[192,768]{1,0:T(8,128)(2,1)} %get-tuple-element.109.before, bf16[256,768]{1,0:T(8,128)(2,1)} %bitcast.182, ...), custom_call_target="tpu_custom_call" | custom-call | flops 2717908992 | bytes 7077888 | tf_op jit(solution)/shard_map/pallas_call | solution.py:173
  20.0 3.8 %collective-permute-start.2 = (bf16[256,768]{1,0:T(8,128)(2,1)}, bf16[256,768]{1,0:T(8,128)(2,1)S(1)}, u32[]{:S(2)}, u32[]{:S(2)}) collective-permute-start(bf16[256,768]{1,0:T(8,128)(2,1)} %get-tuple-element.45.own), channel_id=1, source_target_pairs={{2,4},{3,5},{6,8},{7,9},{10,12},{11,13},{14,16},{15,17},{18,20},{1... | collective-permute-start | bytes 1179656 | tf_op jit(solution)/shard_map/ppermute | solution.py:46
  25.0 4.4 %collective-permute-done.2 = bf16[256,768]{1,0:T(8,128)(2,1)S(1)} collective-permute-done((bf16[256,768]{1,0:T(8,128)(2,1)}, bf16[256,768]{1,0:T(8,128)(2,1)S(1)}, u32[]{:S(2)}, u32[]{:S(2)}) %collective-permute-start.2) | collective-permute-done | bytes 393248 | tf_op jit(solution)/shard_map/ppermute | solution.py:46
  29.6 3.4 %shard_map.94 = (bf16[768,768]{1,0:T(8,128)(2,1)S(1)}, bf16[256,768]{1,0:T(8,128)(2,1)S(1)}) custom-call(bf16[256,768]{1,0:T(8,128)(2,1)S(1)} %get-tuple-element.47.before, bf16[256,768]{1,0:T(8,128)(2,1)S(1)} %copy-done.1, bf16[256,768]{1,0:T(8,128)(2,1)S(1)} %get-tuple-element.102.after, bf16[256,768]{1,0:T(8,128)(2,1)S(1)} %copy-done, ...), custom_call_target="tpu_custom_call" | custom-call | flops 905969664 | bytes 3538944 | tf_op jit(solution)/shard_map/pallas_call | solution.py:173
  33.6 5.8 %fusion.5 = (f32[]{:T(128)}, bf16[256,2688]{1,0:T(8,128)(2,1)S(1)}) fusion(s32[1,256,2688]{2,1,0:T(8,128)} %param.9, f32[256]{0:T(256)S(1)} %bitcast.190, bf16[256,768]{1,0:T(8,128)(2,1)S(1)} %get-tuple-element.49, bf16[768,2688]{1,0:T(8,128)(2,1)S(1)} %copy-done.13), kind=kOutput, calls=%fused_computation.9 | convolution fusion | flops 1070039040 | bytes 8651780 | tf_op jit(solution)/shard_map/dot_general | solution.py:264
  40.8 3.6 %collective-permute-start.8 = (bf16[256,768]{1,0:T(8,128)(2,1)S(1)}, bf16[256,768]{1,0:T(8,128)(2,1)S(1)}, u32[]{:S(2)}, u32[]{:S(2)}) collective-permute-start(bf16[256,768]{1,0:T(8,128)(2,1)S(1)} %get-tuple-element.52.own), channel_id=1, source_target_pairs={{2,4},{3,5},{6,8},{7,9},{10,12},{11,13},{14,16},{15,17},{18,20},{1... | collective-permute-start | bytes 1179656 | tf_op jit(solution)/shard_map/ppermute | solution.py:46
  54.1 8.9 %collective-permute-start.16 = (bf16[2,576,384]{2,1,0:T(8,128)(2,1)}, bf16[2,576,384]{2,1,0:T(8,128)(2,1)}, u32[]{:S(2)}, u32[]{:S(2)}) collective-permute-start(bf16[2,576,384]{2,1,0:T(8,128)(2,1)} %dynamic-slice_bitcast_fusion.2), channel_id=1, source_target_pairs={{0,48},{1,49},{2,50},{3,51},{4,52},{5,53},{6,54},{7,55},{8,56},{9,... | collective-permute-start | bytes 2654216 | tf_op jit(solution)/shard_map/ppermute | solution.py:46
  64.7 3.4 %shard_map.95 = (f32[256,768]{1,0:T(8,128)S(1)}, bf16[256,768]{1,0:T(8,128)(2,1)S(1)}) custom-call(bf16[256,768]{1,0:T(8,128)(2,1)S(1)} %get-tuple-element.57.before, bf16[256,768]{1,0:T(8,128)(2,1)S(1)} %get-tuple-element.52.own, bf16[256,768]{1,0:T(8,128)(2,1)S(1)} %get-tuple-element.100.after, bf16[256,768]{1,0:T(8,128)(2,1)S(1)} %copy-done, ...), custom_call_target="tpu_custom_call" | custom-call | flops 905969664 | bytes 3538944 | tf_op jit(solution)/shard_map/pallas_call | solution.py:173
  70.9 6.9 %collective-permute-start.19 = (bf16[1,384,1408]{2,1,0:T(8,128)(2,1)S(1)}, bf16[1,384,1408]{2,1,0:T(8,128)(2,1)S(1)}, u32[]{:S(2)}, u32[]{:S(2)}) collective-permute-start(bf16[1,384,1408]{2,1,0:T(8,128)(2,1)S(1)} %dynamic-slice_bitcast_fusion), channel_id=1, source_target_pairs={{0,64},{1,65},{2,66},{3,67},{4,68},{5,69},{6,70},{7,71},{8,72},{9,... | collective-permute-start | bytes 3244040 | tf_op jit(solution)/shard_map/ppermute | solution.py:46
  97.1 7.7 %collective-permute-start.18 = (bf16[1,1152,384]{2,1,0:T(8,128)(2,1)}, bf16[1,1152,384]{2,1,0:T(8,128)(2,1)}, u32[]{:S(2)}, u32[]{:S(2)}) collective-permute-start(bf16[1,1152,384]{2,1,0:T(8,128)(2,1)} %dynamic-slice_bitcast_fusion.1), channel_id=1, source_target_pairs={{0,64},{1,65},{2,66},{3,67},{4,68},{5,69},{6,70},{7,71},{8,72},{9,... | collective-permute-start | bytes 2654216 | tf_op jit(solution)/shard_map/ppermute | solution.py:46
  106.1 4.2 %all-to-all-start = ((bf16[4,4,24,1408]{3,2,0,1:T(8,128)(2,1)}), bf16[4,4,24,1408]{3,2,0,1:T(8,128)(2,1)}, u32[]{:S(2)}, u32[]{:S(2)}) async-start(bf16[4,4,24,1408]{3,2,0,1:T(8,128)(2,1)} %copy.17), calls=%async_computation | async-start | bytes 2162688 | tf_op jit(solution)/shard_map/all_to_all | solution.py:346
  117.2 7.9 %collective-permute-done.18 = bf16[1,1152,384]{2,1,0:T(8,128)(2,1)} collective-permute-done((bf16[1,1152,384]{2,1,0:T(8,128)(2,1)}, bf16[1,1152,384]{2,1,0:T(8,128)(2,1)}, u32[]{:S(2)}, u32[]{:S(2)}) %collective-permute-start.18) | collective-permute-done | bytes 884768 | tf_op jit(solution)/shard_map/ppermute | solution.py:46
  126.8 3.1 %collective-permute-start.28 = (bf16[4,72,384]{2,1,0:T(8,128)(2,1)S(1)}, bf16[4,72,384]{2,1,0:T(8,128)(2,1)S(1)}, u32[]{:S(2)}, u32[]{:S(2)}) collective-permute-start(bf16[4,72,384]{2,1,0:T(8,128)(2,1)S(1)} %get-tuple-element.98), channel_id=1, source_target_pairs={{0,8},{1,9},{2,10},{3,11},{4,12},{5,13},{6,14},{7,15},{8,0},{9,1},... | collective-permute-start | bytes 663560 | tf_op jit(solution)/shard_map/ppermute | solution.py:46
  129.9 2.2 %reduce_sum.62 = bf16[4,24,1408]{2,1,0:T(8,128)(2,1)} reduce(bf16[4,4,24,1408]{3,2,0,1:T(8,128)(2,1)} %all-to-all-done, bf16[]{:T(256)} %constant.171.clone.1), dimensions={1}, to_apply=%region_2.3 | reduce | flops 405504 | bytes 1351682 | tf_op jit(solution)/shard_map/reduce_sum | solution.py:347
  133.3 6.3 %collective-permute-done.27 = bf16[4,72,384]{2,1,0:T(8,128)(2,1)S(1)} collective-permute-done((bf16[4,72,384]{2,1,0:T(8,128)(2,1)S(1)}, bf16[4,72,384]{2,1,0:T(8,128)(2,1)S(1)}, u32[]{:S(2)}, u32[]{:S(2)}) %collective-permute-start.27) | collective-permute-done | bytes 221216 | tf_op jit(solution)/shard_map/ppermute | solution.py:46
  140.9 2.1 %collective-permute-start.31 = (bf16[72,384]{1,0:T(8,128)(2,1)S(1)}, bf16[72,384]{1,0:T(8,128)(2,1)S(1)}, u32[]{:S(2)}, u32[]{:S(2)}) collective-permute-start(bf16[72,384]{1,0:T(8,128)(2,1)S(1)} %get-tuple-element.129), channel_id=1, source_target_pairs={{0,32},{1,33},{2,34},{3,35},{4,36},{5,37},{6,38},{7,39},{8,40},{9,... | collective-permute-start | bytes 165896 | tf_op jit(solution)/shard_map/ppermute | solution.py:46
  144.1 3.4 %all-to-all-start.1 = ((bf16[4,24,1408]{2,1,0:T(8,128)(2,1)}), bf16[4,24,1408]{2,1,0:T(8,128)(2,1)S(1)}, u32[]{:S(2)}, u32[]{:S(2)}) async-start(bf16[4,24,1408]{2,1,0:T(8,128)(2,1)} %reduce_sum.62), calls=%async_computation.1 | async-start | bytes 540672 | tf_op jit(solution)/shard_map/all_to_all | solution.py:357
  147.5 2.6 %collective-permute-start.25 = (bf16[4,72,384]{2,1,0:T(8,128)(2,1)S(1)}, bf16[4,72,384]{2,1,0:T(8,128)(2,1)S(1)}, u32[]{:S(2)}, u32[]{:S(2)}) collective-permute-start(bf16[4,72,384]{2,1,0:T(8,128)(2,1)S(1)} %get-tuple-element.95), channel_id=1, source_target_pairs={{0,8},{1,9},{2,10},{3,11},{4,12},{5,13},{6,14},{7,15},{8,0},{9,1},... | collective-permute-start | bytes 663560 | tf_op jit(solution)/shard_map/ppermute | solution.py:46
  150.2 2.9 %all-to-all-done.1 = bf16[4,24,1408]{2,1,0:T(8,128)(2,1)S(1)} async-done(((bf16[4,24,1408]{2,1,0:T(8,128)(2,1)}), bf16[4,24,1408]{2,1,0:T(8,128)(2,1)S(1)}, u32[]{:S(2)}, u32[]{:S(2)}) %all-to-all-start.1) | async-done | bytes 270368 | tf_op jit(solution)/shard_map/all_to_all | solution.py:357
  154.2 8.3 %collective-permute-start.32 = (bf16[312,384]{1,0:T(8,128)(2,1)S(1)}, bf16[312,384]{1,0:T(8,128)(2,1)S(1)}, u32[]{:S(2)}, u32[]{:S(2)}) collective-permute-start(bf16[312,384]{1,0:T(8,128)(2,1)S(1)} %pad_maximum_fusion.13), channel_id=1, source_target_pairs={{0,0},{1,2},{2,1},{3,3},{4,4},{5,6},{6,5},{7,7},{8,8},{9,10},{10,9... | collective-permute-start | bytes 718856 | tf_op jit(solution)/shard_map/ppermute | solution.py:46
  163.0 4.6 %collective-permute-done.32 = bf16[312,384]{1,0:T(8,128)(2,1)S(1)} collective-permute-done((bf16[312,384]{1,0:T(8,128)(2,1)S(1)}, bf16[312,384]{1,0:T(8,128)(2,1)S(1)}, u32[]{:S(2)}, u32[]{:S(2)}) %collective-permute-start.32) | collective-permute-done | bytes 239648 | tf_op jit(solution)/shard_map/ppermute | solution.py:46
  167.6 3.0 %collective-permute-done.33 = bf16[312,384]{1,0:T(8,128)(2,1)S(1)} collective-permute-done((bf16[312,384]{1,0:T(8,128)(2,1)S(1)}, bf16[312,384]{1,0:T(8,128)(2,1)S(1)}, u32[]{:S(2)}, u32[]{:S(2)}) %collective-permute-start.33) | collective-permute-done | bytes 239648 | tf_op jit(solution)/shard_map/ppermute | solution.py:46
  (182 shorter events, 57.1 us)
Async XLA Ops:
  1.7 9.0 %collective-permute-start = (bf16[192,768]{1,0:T(8,128)(2,1)S(1)}, bf16[192,768]{1,0:T(8,128)(2,1)S(1)}, u32[]{:S(2)}, u32[]{:S(2)}) collective-permute-start(bf16[192,768]{1,0:T(8,128)(2,1)S(1)} %get-tuple-element.123), channel_id=1, source_target_pairs={{2,4},{3,5},{6,8},{7,9},{10,12},{11,13},{14,16},{15,17},{18,20},{1... | collective-permute-start | bytes 884744 | tf_op jit(solution)/shard_map/ppermute | solution.py:46
  19.8 9.7 %collective-permute-start.5 = (bf16[512,768]{1,0:T(8,128)(2,1)}, bf16[512,768]{1,0:T(8,128)(2,1)S(1)}, u32[]{:S(2)}, u32[]{:S(2)}) collective-permute-start(bf16[512,768]{1,0:T(8,128)(2,1)} %get-tuple-element.46), channel_id=1, source_target_pairs={{0,2},{1,3},{2,0},{3,1},{4,6},{5,7},{6,4},{7,5},{8,10},{9,11},{10,... | collective-permute-start | bytes 2359304 | tf_op jit(solution)/shard_map/ppermute | solution.py:46
  20.0 9.4 %collective-permute-start.2 = (bf16[256,768]{1,0:T(8,128)(2,1)}, bf16[256,768]{1,0:T(8,128)(2,1)S(1)}, u32[]{:S(2)}, u32[]{:S(2)}) collective-permute-start(bf16[256,768]{1,0:T(8,128)(2,1)} %get-tuple-element.45.own), channel_id=1, source_target_pairs={{2,4},{3,5},{6,8},{7,9},{10,12},{11,13},{14,16},{15,17},{18,20},{1... | collective-permute-start | bytes 1179656 | tf_op jit(solution)/shard_map/ppermute | solution.py:46
  40.8 22.2 %collective-permute-start.8 = (bf16[256,768]{1,0:T(8,128)(2,1)S(1)}, bf16[256,768]{1,0:T(8,128)(2,1)S(1)}, u32[]{:S(2)}, u32[]{:S(2)}) collective-permute-start(bf16[256,768]{1,0:T(8,128)(2,1)S(1)} %get-tuple-element.52.own), channel_id=1, source_target_pairs={{2,4},{3,5},{6,8},{7,9},{10,12},{11,13},{14,16},{15,17},{18,20},{1... | collective-permute-start | bytes 1179656 | tf_op jit(solution)/shard_map/ppermute | solution.py:46
  44.4 18.5 %collective-permute-start.9 = (bf16[256,768]{1,0:T(8,128)(2,1)S(1)}, bf16[256,768]{1,0:T(8,128)(2,1)S(1)}, u32[]{:S(2)}, u32[]{:S(2)}) collective-permute-start(bf16[256,768]{1,0:T(8,128)(2,1)S(1)} %get-tuple-element.52.own), channel_id=1, source_target_pairs={{0,2},{1,3},{2,0},{3,1},{4,6},{5,7},{6,4},{7,5},{8,10},{9,11},{10,... | collective-permute-start | bytes 1179656 | tf_op jit(solution)/shard_map/ppermute | solution.py:46
  46.6 16.5 %collective-permute-start.11 = (bf16[256,1408]{1,0:T(8,128)(2,1)S(1)}, bf16[256,1408]{1,0:T(8,128)(2,1)S(1)}, u32[]{:S(2)}, u32[]{:S(2)}) collective-permute-start(bf16[256,1408]{1,0:T(8,128)(2,1)S(1)} %broadcast_select_fusion), channel_id=1, source_target_pairs={{0,2},{1,3},{2,0},{3,1},{4,6},{5,7},{6,4},{7,5},{8,10},{9,11},{10,... | collective-permute-start | bytes 2162696 | tf_op jit(solution)/shard_map/ppermute | solution.py:46
  54.1 31.4 %collective-permute-start.16 = (bf16[2,576,384]{2,1,0:T(8,128)(2,1)}, bf16[2,576,384]{2,1,0:T(8,128)(2,1)}, u32[]{:S(2)}, u32[]{:S(2)}) collective-permute-start(bf16[2,576,384]{2,1,0:T(8,128)(2,1)} %dynamic-slice_bitcast_fusion.2), channel_id=1, source_target_pairs={{0,48},{1,49},{2,50},{3,51},{4,52},{5,53},{6,54},{7,55},{8,56},{9,... | collective-permute-start | bytes 2654216 | tf_op jit(solution)/shard_map/ppermute | solution.py:46
  68.2 13.4 %collective-permute-start.13 = (bf16[192,768]{1,0:T(8,128)(2,1)S(1)}, bf16[192,768]{1,0:T(8,128)(2,1)S(1)}, u32[]{:S(2)}, u32[]{:S(2)}) collective-permute-start(bf16[192,768]{1,0:T(8,128)(2,1)S(1)} %get-tuple-element.118), channel_id=1, source_target_pairs={{2,4},{3,5},{6,8},{7,9},{10,12},{11,13},{14,16},{15,17},{18,20},{1... | collective-permute-start | bytes 884744 | tf_op jit(solution)/shard_map/ppermute | solution.py:46
  70.2 11.4 %collective-permute-start.14 = (bf16[192,768]{1,0:T(8,128)(2,1)S(1)}, bf16[192,768]{1,0:T(8,128)(2,1)S(1)}, u32[]{:S(2)}, u32[]{:S(2)}) collective-permute-start(bf16[192,768]{1,0:T(8,128)(2,1)S(1)} %get-tuple-element.119), channel_id=1, source_target_pairs={{0,2},{1,3},{2,0},{3,1},{4,6},{5,7},{6,4},{7,5},{8,10},{9,11},{10,... | collective-permute-start | bytes 884744 | tf_op jit(solution)/shard_map/ppermute | solution.py:46
  70.9 33.9 %collective-permute-start.19 = (bf16[1,384,1408]{2,1,0:T(8,128)(2,1)S(1)}, bf16[1,384,1408]{2,1,0:T(8,128)(2,1)S(1)}, u32[]{:S(2)}, u32[]{:S(2)}) collective-permute-start(bf16[1,384,1408]{2,1,0:T(8,128)(2,1)S(1)} %dynamic-slice_bitcast_fusion), channel_id=1, source_target_pairs={{0,64},{1,65},{2,66},{3,67},{4,68},{5,69},{6,70},{7,71},{8,72},{9,... | collective-permute-start | bytes 3244040 | tf_op jit(solution)/shard_map/ppermute | solution.py:46
  81.6 32.2 %collective-permute-start.20 = (bf16[2,2,288,384]{3,2,1,0:T(8,128)(2,1)}, bf16[2,2,288,384]{3,2,1,0:T(8,128)(2,1)}, u32[]{:S(2)}, u32[]{:S(2)}) collective-permute-start(bf16[2,2,288,384]{3,2,1,0:T(8,128)(2,1)} %pad_maximum_fusion.3), channel_id=1, source_target_pairs={{0,16},{1,17},{2,18},{3,19},{4,20},{5,21},{6,22},{7,23},{8,24},{9,... | collective-permute-start | bytes 2654216 | tf_op jit(solution)/shard_map/ppermute | solution.py:46
  89.9 22.0 %collective-permute-start.22 = (bf16[2,288,384]{2,1,0:T(8,128)(2,1)}, bf16[2,288,384]{2,1,0:T(8,128)(2,1)}, u32[]{:S(2)}, u32[]{:S(2)}) collective-permute-start(bf16[2,288,384]{2,1,0:T(8,128)(2,1)} %dynamic-slice_bitcast_fusion.3), channel_id=1, source_target_pairs={{0,16},{1,17},{2,18},{3,19},{4,20},{5,21},{6,22},{7,23},{8,24},{9,... | collective-permute-start | bytes 1327112 | tf_op jit(solution)/shard_map/ppermute | solution.py:46
  97.1 28.0 %collective-permute-start.18 = (bf16[1,1152,384]{2,1,0:T(8,128)(2,1)}, bf16[1,1152,384]{2,1,0:T(8,128)(2,1)}, u32[]{:S(2)}, u32[]{:S(2)}) collective-permute-start(bf16[1,1152,384]{2,1,0:T(8,128)(2,1)} %dynamic-slice_bitcast_fusion.1), channel_id=1, source_target_pairs={{0,64},{1,65},{2,66},{3,67},{4,68},{5,69},{6,70},{7,71},{8,72},{9,... | collective-permute-start | bytes 2654216 | tf_op jit(solution)/shard_map/ppermute | solution.py:46
  106.1 23.8 %all-to-all-start = ((bf16[4,4,24,1408]{3,2,0,1:T(8,128)(2,1)}), bf16[4,4,24,1408]{3,2,0,1:T(8,128)(2,1)}, u32[]{:S(2)}, u32[]{:S(2)}) async-start(bf16[4,4,24,1408]{3,2,0,1:T(8,128)(2,1)} %copy.17), calls=%async_computation | async-start | bytes 2162688 | tf_op jit(solution)/shard_map/all_to_all | solution.py:346
  116.0 16.1 %collective-permute-start.21 = (bf16[2,288,384]{2,1,0:T(8,128)(2,1)}, bf16[2,288,384]{2,1,0:T(8,128)(2,1)}, u32[]{:S(2)}, u32[]{:S(2)}) collective-permute-start(bf16[2,288,384]{2,1,0:T(8,128)(2,1)} %slice_bitcast_fusion), channel_id=1, source_target_pairs={{0,48},{1,49},{2,50},{3,51},{4,52},{5,53},{6,54},{7,55},{8,56},{9,... | collective-permute-start | bytes 1327112 | tf_op jit(solution)/shard_map/ppermute | solution.py:46
  126.7 12.9 %collective-permute-start.27 = (bf16[4,72,384]{2,1,0:T(8,128)(2,1)S(1)}, bf16[4,72,384]{2,1,0:T(8,128)(2,1)S(1)}, u32[]{:S(2)}, u32[]{:S(2)}) collective-permute-start(bf16[4,72,384]{2,1,0:T(8,128)(2,1)S(1)} %get-tuple-element.99), channel_id=1, source_target_pairs={{0,12},{1,13},{2,14},{3,15},{4,8},{5,9},{6,10},{7,11},{8,4},{9,5},... | collective-permute-start | bytes 663560 | tf_op jit(solution)/shard_map/ppermute | solution.py:46
  126.8 12.8 %collective-permute-start.28 = (bf16[4,72,384]{2,1,0:T(8,128)(2,1)S(1)}, bf16[4,72,384]{2,1,0:T(8,128)(2,1)S(1)}, u32[]{:S(2)}, u32[]{:S(2)}) collective-permute-start(bf16[4,72,384]{2,1,0:T(8,128)(2,1)S(1)} %get-tuple-element.98), channel_id=1, source_target_pairs={{0,8},{1,9},{2,10},{3,11},{4,12},{5,13},{6,14},{7,15},{8,0},{9,1},... | collective-permute-start | bytes 663560 | tf_op jit(solution)/shard_map/ppermute | solution.py:46
  140.9 9.2 %collective-permute-start.30 = (bf16[72,384]{1,0:T(8,128)(2,1)S(1)}, bf16[72,384]{1,0:T(8,128)(2,1)S(1)}, u32[]{:S(2)}, u32[]{:S(2)}) collective-permute-start(bf16[72,384]{1,0:T(8,128)(2,1)S(1)} %get-tuple-element.130), channel_id=1, source_target_pairs={{0,48},{1,49},{2,50},{3,51},{4,52},{5,53},{6,54},{7,55},{8,56},{9,... | collective-permute-start | bytes 165896 | tf_op jit(solution)/shard_map/ppermute | solution.py:46
  140.9 9.2 %collective-permute-start.31 = (bf16[72,384]{1,0:T(8,128)(2,1)S(1)}, bf16[72,384]{1,0:T(8,128)(2,1)S(1)}, u32[]{:S(2)}, u32[]{:S(2)}) collective-permute-start(bf16[72,384]{1,0:T(8,128)(2,1)S(1)} %get-tuple-element.129), channel_id=1, source_target_pairs={{0,32},{1,33},{2,34},{3,35},{4,36},{5,37},{6,38},{7,39},{8,40},{9,... | collective-permute-start | bytes 165896 | tf_op jit(solution)/shard_map/ppermute | solution.py:46
  143.3 9.9 %collective-permute-start.23 = (bf16[4,72,384]{2,1,0:T(8,128)(2,1)S(1)}, bf16[4,72,384]{2,1,0:T(8,128)(2,1)S(1)}, u32[]{:S(2)}, u32[]{:S(2)}) collective-permute-start(bf16[4,72,384]{2,1,0:T(8,128)(2,1)S(1)} %get-tuple-element.94), channel_id=1, source_target_pairs={{0,4},{1,5},{2,6},{3,7},{4,0},{5,1},{6,2},{7,3},{8,12},{9,13},{10,... | collective-permute-start | bytes 663560 | tf_op jit(solution)/shard_map/ppermute | solution.py:46
  143.4 9.8 %collective-permute-start.24 = (bf16[4,72,384]{2,1,0:T(8,128)(2,1)S(1)}, bf16[4,72,384]{2,1,0:T(8,128)(2,1)S(1)}, u32[]{:S(2)}, u32[]{:S(2)}) collective-permute-start(bf16[4,72,384]{2,1,0:T(8,128)(2,1)S(1)} %get-tuple-element.96), channel_id=1, source_target_pairs={{0,12},{1,13},{2,14},{3,15},{4,8},{5,9},{6,10},{7,11},{8,4},{9,5},... | collective-permute-start | bytes 663560 | tf_op jit(solution)/shard_map/ppermute | solution.py:46
  154.2 13.4 %collective-permute-start.32 = (bf16[312,384]{1,0:T(8,128)(2,1)S(1)}, bf16[312,384]{1,0:T(8,128)(2,1)S(1)}, u32[]{:S(2)}, u32[]{:S(2)}) collective-permute-start(bf16[312,384]{1,0:T(8,128)(2,1)S(1)} %pad_maximum_fusion.13), channel_id=1, source_target_pairs={{0,0},{1,2},{2,1},{3,3},{4,4},{5,6},{6,5},{7,7},{8,8},{9,10},{10,9... | collective-permute-start | bytes 718856 | tf_op jit(solution)/shard_map/ppermute | solution.py:46
  162.6 11.0 %collective-permute-start.34 = (bf16[144,384]{1,0:T(8,128)(2,1)S(1)}, bf16[144,384]{1,0:T(8,128)(2,1)S(1)}, u32[]{:S(2)}, u32[]{:S(2)}) collective-permute-start(bf16[144,384]{1,0:T(8,128)(2,1)S(1)} %bitcast.188), channel_id=1, source_target_pairs={{0,64},{1,66},{2,65},{3,67},{4,68},{5,70},{6,69},{7,71},{8,72},{9,... | collective-permute-start | bytes 331784 | tf_op jit(solution)/shard_map/ppermute | solution.py:46
  162.8 10.9 %collective-permute-start.35 = (bf16[144,384]{1,0:T(8,128)(2,1)S(1)}, bf16[144,384]{1,0:T(8,128)(2,1)S(1)}, u32[]{:S(2)}, u32[]{:S(2)}) collective-permute-start(bf16[144,384]{1,0:T(8,128)(2,1)S(1)} %bitcast.189), channel_id=1, source_target_pairs={{0,66},{1,64},{2,67},{3,65},{4,70},{5,68},{6,71},{7,69},{8,74},{9,... | collective-permute-start | bytes 331784 | tf_op jit(solution)/shard_map/ppermute | solution.py:46
  (32 other events, 209.2 us)
